TPU v7x, 256 devices: a whole 4x4x8 slice. The times are simulated.
256 devices in a mesh: grp: 4 (over y), gz: 64 (over x, z, core).
Axes of the slice: x: 4, y: 4, z: 8, core: 2. Of those that a mesh axis runs over, the one named last changes fastest.
Arguments:
- features: bfloat16 [32768, 256], P(('grp', 'gz')), may hold values from -6 to 6
- hilbert_rank: int32 [32768], P(('grp', 'gz')), may hold values from 0 to 8191, as said below
- neighbours: int32 [32768, 27], P(('grp', 'gz')), may hold values from -1 to 159, as said below
- halo_rows: int32 [256, 32], P(('grp', 'gz')), may hold values from 0 to 127, as said below
- cotangent: bfloat16 [32768, 256], P(('grp', 'gz')), may hold values from -6 to 6
- conv_weight: bfloat16 [6912, 256], replicated, may hold values from -0.078125 to 0.078125
- qkv_weight: bfloat16 [256, 768], replicated, may hold values from -0.375 to 0.375
- proj_weight: bfloat16 [256, 256], replicated, may hold values from -0.375 to 0.375
- norm_gain: float32 [256], replicated, may hold values from 0.25 to 1.75
Outputs:
- block_out: bfloat16 [32768, 256], P(('grp', 'gz'))
- grad_features: bfloat16 [32768, 256], P(('grp', 'gz'))
- grad_conv: float32 [6912, 256], P('gz')
- grad_qkv: float32 [256, 768], replicated
- grad_proj: float32 [256, 256], replicated
- grad_gain: float32 [256], replicated
Inputs may be any that keep to these rules, and one draw needn't show every extreme that they name: `hilbert_rank`: within each group the 8192 ranks are a permutation. Ranks k * 128 to (k + 1) * 128 - 1 are held in Hilbert order by index k of gz, and indices 2i and 2i + 1 hold patch i. At most 4 points of one device have ranks in one such range, and every device has exactly 4 in some range. `neighbours`: -1 marks an absent neighbour. Otherwise the entry indexes the device's extended rows: its 128 own rows, then 16 rows from the previous index of gz, then 16 from the next; entries of the last two kinds occur only where that device exists. Offset 13 is the point itself. `halo_rows`: row indices of the device's own points: the first 16 entries go to the previous index of gz, the last 16 to the next; repeats may occur.
All inputs are finite; a program needn't handle non-finite values.
Results may differ from a plain program's by a relative error of at most 0.014.
Values may be sent and summed in bfloat16 or wider, within the bound.
No kernel may reach another device: no remote copies, remote signals or barrier semaphores. Data moves between devices by JAX's collectives and lax.ppermute only.
A program may use at most 64 MiB of HBM per device.

v0:
```python
import math

import jax
import jax.numpy as jnp
from jax import lax
from jax.sharding import PartitionSpec as P

HEADS = 16


norm_eps = 1e-05


def padded_2(x, sides, width):
    for axis, dim in sides:
        size, length = (lax.axis_size(axis), x.shape[dim])
        up = [(i, (i + 1) % size) for i in range(size - 1)]
        down = [(j, i) for i, j in up]
        last = lax.slice_in_dim(x, length - width, length, axis=dim)
        leading = lax.slice_in_dim(x, 0, width, axis=dim)
        before = lax.ppermute(last, axis, up)
        after = lax.ppermute(leading, axis, down)
        x = jnp.concatenate([before, x, after], axis=dim)
    return x


def swapped(block, axis, apart):
    count = lax.axis_size(axis)
    route = []
    for low in range(count):
        high = low | 1 << apart
        if high != low and high < count:
            route += [(low, high), (high, low)]
    return lax.ppermute(block, axis, route)


def neighbour_rows(extended, neighbours):
    present = neighbours >= 0
    picked = extended[jnp.where(present, neighbours, 0)]
    picked = jnp.where(present[:, :, None], picked, jnp.zeros((), extended.dtype))
    return picked.reshape(neighbours.shape[0], -1)


def contract_rows(left_side, right_side):
    return lax.dot_general(
        left_side, right_side, (((0,), (0,)), ((), ())), preferred_element_type=jnp.float32
    )


def contract_cols(left_side, right_side):
    return lax.dot_general(
        left_side, right_side, (((1,), (1,)), ((), ())), preferred_element_type=jnp.float32
    )


def head_major(values, head_count):
    rows = values.shape[0]
    return values.reshape(rows, head_count, -1).transpose(1, 0, 2)


def row_major(values):
    return values.transpose(1, 0, 2).reshape(values.shape[1], -1)


def shards(
    features,
    hilbert_rank,
    neighbours,
    halo_rows,
    cotangent,
    conv_weight,
    qkv_weight,
    proj_weight,
    norm_gain,
):
    point_count, feat_width = features.shape
    shard_count = lax.axis_size("gz")
    group_count = lax.axis_size("grp")
    halo_width = halo_rows.shape[1] // 2
    pick_rows = halo_rows[0]
    head_count = HEADS
    head_dim = feat_width // head_count
    score_scale = head_dim ** (-0.5)
    capacity = 2 * point_count // shard_count
    factor = 1.0 / math.sqrt(point_count * shard_count * group_count)
    padded = padded_2(features[pick_rows], (("gz", 0),), halo_width)
    extended = jnp.concatenate([features, padded[:halo_width], padded[3 * halo_width :]], 0)
    flat_rows = neighbour_rows(extended, neighbours)
    mixed_rows = (
        features.astype(jnp.float32)
        + jnp.dot(flat_rows, conv_weight, preferred_element_type=jnp.float32)
    ).astype(jnp.bfloat16)
    owner_index = hilbert_rank // point_count
    place_index = hilbert_rank % point_count
    owner_hits = (owner_index[:, None] == jnp.arange(shard_count)[None, :]).astype(jnp.int32)
    slot_index = jnp.sum(jnp.cumsum(owner_hits, 0) * owner_hits, 1) - 1
    target = owner_index * capacity + slot_index
    send_rows = (
        jnp.zeros((shard_count * capacity, feat_width), jnp.bfloat16)
        .at[target]
        .set(mixed_rows)
        .reshape(shard_count, capacity, feat_width)
    )
    send_cot = (
        jnp.zeros((shard_count * capacity, feat_width), jnp.bfloat16)
        .at[target]
        .set(cotangent)
        .reshape(shard_count, capacity, feat_width)
    )
    send_place = (
        jnp.full((shard_count * capacity,), -1, jnp.int32)
        .at[target]
        .set(place_index)
        .reshape(shard_count, capacity)
    )
    got_rows, got_cot, got_place = (
        lax.all_to_all(send_rows, "gz", split_axis=0, concat_axis=0, tiled=True),
        lax.all_to_all(send_cot, "gz", split_axis=0, concat_axis=0, tiled=True),
        lax.all_to_all(send_place, "gz", split_axis=0, concat_axis=0, tiled=True),
    )
    got_place = got_place.reshape(-1)
    filled = got_place >= 0
    where_to = jnp.where(filled, got_place, point_count)
    local_rows = (
        jnp.zeros((point_count, feat_width), jnp.bfloat16)
        .at[where_to]
        .set(got_rows.reshape(-1, feat_width), mode="drop")
    )
    local_cot = (
        jnp.zeros((point_count, feat_width), jnp.bfloat16)
        .at[where_to]
        .set(got_cot.reshape(-1, feat_width), mode="drop")
    )
    hidden = local_rows.astype(jnp.float32)
    centred = hidden - jnp.mean(hidden, -1, keepdims=True)
    inverse = lax.rsqrt(jnp.mean(centred * centred, -1, keepdims=True) + norm_eps)
    normed = centred * inverse
    scaled = (normed * norm_gain).astype(jnp.bfloat16)
    w_query = qkv_weight[:, :feat_width]
    w_keyval = qkv_weight[:, feat_width:]
    query_rows = jnp.dot(scaled, w_query, preferred_element_type=jnp.float32).astype(jnp.bfloat16)
    keyval = jnp.dot(scaled, w_keyval, preferred_element_type=jnp.float32).astype(jnp.bfloat16)
    partner_kv = swapped(keyval, "gz", 0)
    all_kv = jnp.concatenate([keyval, partner_kv], 0)
    grad_attended = contract_cols(local_cot, proj_weight).astype(jnp.bfloat16)

    def one_head(inputs):
        query_h, key_h, value_h, grad_att_h = inputs
        scores = contract_cols(query_h, key_h) * score_scale
        exp_scores = jnp.exp(scores)
        probs = (exp_scores / jnp.sum(exp_scores, -1, keepdims=True)).astype(jnp.bfloat16)
        attended_h = jnp.dot(probs, value_h, preferred_element_type=jnp.float32).astype(
            jnp.bfloat16
        )
        grad_probs = contract_cols(grad_att_h, value_h)
        probs_wide = probs.astype(jnp.float32)
        row_delta = jnp.sum(probs_wide * grad_probs, -1, keepdims=True)
        grad_scores = (probs_wide * (grad_probs - row_delta) * score_scale).astype(jnp.bfloat16)
        grad_query_h = jnp.dot(grad_scores, key_h, preferred_element_type=jnp.float32).astype(
            jnp.bfloat16
        )
        grad_key_h = contract_rows(grad_scores, query_h).astype(jnp.bfloat16)
        grad_value_h = contract_rows(probs, grad_att_h).astype(jnp.bfloat16)
        return (attended_h, grad_query_h, grad_key_h, grad_value_h)

    head_inputs = (
        head_major(query_rows, head_count),
        head_major(all_kv[:, :feat_width], head_count),
        head_major(all_kv[:, feat_width:], head_count),
        head_major(grad_attended, head_count),
    )
    attended_heads, grad_query_heads, grad_key_heads, grad_value_heads = lax.map(
        one_head, head_inputs
    )
    attended = row_major(attended_heads)
    grad_query = row_major(grad_query_heads)
    grad_keyval = jnp.concatenate([row_major(grad_key_heads), row_major(grad_value_heads)], 1)
    out_local = (
        hidden + jnp.dot(attended, proj_weight, preferred_element_type=jnp.float32)
    ).astype(jnp.bfloat16)
    grad_proj = contract_rows(attended, local_cot)
    own_grads = grad_keyval[:point_count]
    far_grads = grad_keyval[point_count:]
    grad_q_part = contract_rows(scaled, grad_query)
    grad_scaled = contract_cols(grad_query, w_query) + contract_cols(own_grads, w_keyval)
    near_grads = swapped(far_grads, "gz", 0)
    grad_kv_part = contract_rows(scaled, own_grads) + contract_rows(scaled, near_grads)
    grad_scaled = grad_scaled + contract_cols(near_grads, w_keyval)
    grad_qkv = jnp.concatenate([grad_q_part, grad_kv_part], 1)
    grad_gain = jnp.sum(grad_scaled * normed, 0)
    grad_normed = grad_scaled * norm_gain
    grad_hidden = (
        grad_normed
        - jnp.mean(grad_normed, -1, keepdims=True)
        - normed * jnp.mean(grad_normed * normed, -1, keepdims=True)
    ) * inverse
    grad_local = (local_cot.astype(jnp.float32) + grad_hidden).astype(jnp.bfloat16)
    source_rows = jnp.where(filled, got_place, 0)
    back_out, back_grad = (
        lax.all_to_all(
            out_local[source_rows].reshape(shard_count, capacity, feat_width),
            "gz",
            split_axis=0,
            concat_axis=0,
            tiled=True,
        ),
        lax.all_to_all(
            grad_local[source_rows].reshape(shard_count, capacity, feat_width),
            "gz",
            split_axis=0,
            concat_axis=0,
            tiled=True,
        ),
    )
    block_out = back_out.reshape(-1, feat_width)[target]
    grad_mixed = back_grad.reshape(-1, feat_width)[target]
    present = neighbours >= 0
    grad_flat = contract_cols(grad_mixed, conv_weight).reshape(
        point_count, neighbours.shape[1], feat_width
    )
    grad_flat = jnp.where(present[:, :, None], grad_flat, jnp.zeros((), jnp.float32))
    spread = (
        jnp.zeros((point_count + 2 * halo_width, feat_width), jnp.float32)
        .at[jnp.where(present, neighbours, 0)]
        .add(grad_flat)
    )
    returned_rims = padded_2(
        spread[point_count:].astype(jnp.bfloat16), (("gz", 0),), halo_width
    ).astype(jnp.float32)
    own_part = (
        spread[:point_count]
        .at[pick_rows[:halo_width]]
        .add(returned_rims[:halo_width])
        .at[pick_rows[halo_width:]]
        .add(returned_rims[3 * halo_width :])
    )
    grad_features = (grad_mixed.astype(jnp.float32) + own_part).astype(jnp.bfloat16)
    shard_part = lax.psum_scatter(
        contract_rows(flat_rows, grad_mixed), "gz", scatter_dimension=0, tiled=True
    )
    grad_conv = lax.psum(shard_part.astype(jnp.bfloat16), "grp").astype(jnp.float32)
    summed_qkv, summed_proj, summed_gain = lax.psum((grad_qkv, grad_proj, grad_gain), ("grp", "gz"))
    return (
        block_out,
        grad_features,
        grad_conv * factor,
        summed_qkv * factor,
        summed_proj * factor,
        summed_gain * factor,
    )


def solution(mesh):
    return jax.shard_map(
        shards,
        mesh=mesh,
        in_specs=(
            P(("grp", "gz"), None),
            P(("grp", "gz")),
            P(("grp", "gz"), None),
            P(("grp", "gz"), None),
            P(("grp", "gz"), None),
            P(),
            P(),
            P(),
            P(),
        ),
        out_specs=(P(("grp", "gz"), None), P(("grp", "gz"), None), P("gz", None), P(), P(), P()),
        check_vma=False,
    )
```

profile of v0, /device:TPU:1, one launch (start us, length us, event | category | flops | bytes accessed | tf_op | source)
XLA Modules:
  0.0 641.6 jit_solution(11806615439661929906)
XLA Ops:
  10.8 4.9 collective-permute-start
  15.7 2.1 collective-permute-start.1
  19.2 1.6 reduce_window_sum.11
  23.5 12.9 %all-to-all-start = ((s32[64,1,4]{2,1,0:T(1,128)}), s32[64,1,4]{2,1,0:T(1,128)}, u32[]{:S(2)}, u32[]{:S(2)}) async-start(s32[64,1,4]{2,1,0:T(1,128)} %bitcast.156), calls=%async_computation | async-start | bytes 65536 | tf_op jit(solution)/shard_map/all_to_all | solution.py:119
  40.6 1.6 reshape.266
  45.6 2.0 scatter_custom_fusion.3
  51.1 10.5 %all-to-all-start.2 = ((bf16[64,4,256]{2,1,0:T(4,128)(2,1)}), bf16[64,4,256]{2,1,0:T(4,128)(2,1)}, u32[]{:S(2)}, u32[]{:S(2)}) async-start(bf16[64,4,256]{2,1,0:T(4,128)(2,1)} %reshape.244), calls=%async_computation.2 | async-start | bytes 262144 | tf_op jit(solution)/shard_map/all_to_all | solution.py:118
  62.1 2.1 reduce.3
  68.4 10.0 %gather_fusion.1 = bf16[3456,256]{1,0:T(8,128)(2,1)} fusion(bf16[160,256]{1,0:T(8,128)(2,1)} %pad_maximum_fusion.3, s32[4096]{0:T(1024)S(1)} %pad_clamp_fusion), kind=kCustom, calls=%fused_computation.1 | custom fusion | bytes 3552768 | tf_op jit(solution)/shard_map/gather | solution.py:39
  78.4 3.8 reshape.265
  82.2 3.0 broadcast_select_fusion.1
  85.2 4.4 copy.34
  89.6 2.9 fusion.36
  92.5 2.0 scatter_custom_fusion.1
  94.5 1.6 reshape.239
  96.1 10.5 %all-to-all-start.1 = ((bf16[64,4,256]{2,1,0:T(4,128)(2,1)}), bf16[64,4,256]{2,1,0:T(4,128)(2,1)}, u32[]{:S(2)}, u32[]{:S(2)}) async-start(bf16[64,4,256]{2,1,0:T(4,128)(2,1)} %reshape.239), calls=%async_computation.1 | async-start | bytes 262144 | tf_op jit(solution)/shard_map/all_to_all | solution.py:117
  107.9 1.6 reshape.340
  109.5 2.4 scatter_custom_fusion.4
  111.8 1.8 convolution_convert_fusion.5
  115.2 1.7 all-to-all-done.1
  116.9 1.6 reshape.324
  118.5 2.4 scatter_custom_fusion.2
  122.9 1.9 convolution_convert_fusion.4
  125.2 1.8 convolution_convert_fusion.6
  128.5 1.6 pad_maximum_fusion.2
  130.2 1.7 copy.36
  131.9 1.7 copy.37
  133.5 124.6 %while.16 = (s32[]{:T(128)}, bf16[16,128,16]{1,2,0:T(8,128)(2,1)}, bf16[16,128,16]{1,2,0:T(8,128)(2,1)}, bf16[16,256,16]{1,2,0:T(8,128)(2,1)}, bf16[16,256,16]{1...) while((s32[]{:T(128)}, bf16[16,128,16]{1,2,0:T(8,128)(2,1)}, ...), condition=%wide.region_12.13_spmd, body=%wide.region_9.12_spmd.sunk | while | flops 6696706 | bytes 1065061 | solution.py:172
  258.1 2.1 fusion.86
  261.7 1.9 fusion.91
  264.9 1.9 convolution_add_fusion.2
  266.8 1.8 fusion.37
  268.6 2.6 gather_fusion.2
  272.8 8.8 %all-to-all-start.3 = ((bf16[64,4,256]{2,1,0:T(4,128)(2,1)}), bf16[64,4,256]{2,1,0:T(4,128)(2,1)}, u32[]{:S(2)}, u32[]{:S(2)}) async-start(bf16[64,4,256]{2,1,0:T(4,128)(2,1)} %reshape.248), calls=%async_computation.3 | async-start | bytes 262144 | tf_op jit(solution)/shard_map/all_to_all | solution.py:200
  281.6 1.7 fusion.101
  283.3 2.0 fusion.53
  285.3 1.6 fusion.52
  287.0 2.6 gather_fusion.4
  291.1 2.3 convolution_add_fusion
  293.4 10.5 %all-to-all-start.4 = ((bf16[64,4,256]{2,1,0:T(4,128)(2,1)}), bf16[64,4,256]{2,1,0:T(4,128)(2,1)}, u32[]{:S(2)}, u32[]{:S(2)}) async-start(bf16[64,4,256]{2,1,0:T(4,128)(2,1)} %reshape.253), calls=%async_computation.4 | async-start | bytes 262144 | tf_op jit(solution)/shard_map/all_to_all | solution.py:207
  304.0 2.0 pad_maximum_fusion
  306.1 77.9 %psum.31 = f32[256]{0:T(256)} all-reduce(f32[256]{0:T(256)} %get-tuple-element.60), channel_id=1, replica_groups=mesh['grp'=4,'gz'=64] {'grp','gz'}, use_global_device_ids=true, to_apply=%region_23.24 | all-reduce | flops 256 | bytes 2048 | tf_op jit(solution)/shard_map/psum | solution.py:242
  385.2 1.6 reshape.249
  386.8 2.4 gather_fusion.3
  389.3 1.6 reshape.254
  390.9 2.4 gather_fusion.5
  393.3 5.5 fusion.100
  398.7 149.5 %fusion = f32[112,256]{1,0:T(8,128)} fusion(f32[6912,256]{1,0:T(8,128)} %fusion.100), kind=kCustom, calls=%all-reduce-scatter | all-reduce-scatter fusion | flops 1835009 | bytes 7193600
  549.8 1.9 collective-permute-start.6
  551.7 1.9 collective-permute-start.7
  555.0 3.7 fusion.99
  558.7 1.9 collective-permute-start.8
  560.6 5.5 copy.40
  566.1 3.9 broadcast_select_fusion
  569.9 4.9 reshape.348
  574.8 19.0 %scatter_custom_fusion.5 = f32[160,256]{1,0:T(8,128)} fusion(s32[3456]{0:T(1024)} %reshape.266, f32[3456,256]{1,0:T(8,128)} %reshape.348, f32[]{:T(128)} %constant.89.clone.1), kind=kCustom, calls=%fused_computation.107 | custom fusion | flops 884736 | bytes 164352 | tf_op jit(solution)/shard_map/scatter-add | solution.py:225
  594.7 1.9 collective-permute-start.4
  596.7 4.0 collective-permute-start.5
  602.2 2.3 scatter_custom_fusion.6
  604.5 2.3 scatter_custom_fusion.7
  608.4 5.8 concatenate.20
  615.7 13.9 %psum.28 = bf16[108,256]{1,0:T(8,128)(2,1)} all-reduce(bf16[108,256]{1,0:T(8,128)(2,1)} %dynamic-slice_convert_fusion), channel_id=1, replica_groups=mesh['grp'=4,'gz'=64] {'grp'}, use_global_device_ids=true, to_apply=%region_19.20 | all-reduce | flops 27648 | bytes 110592 | tf_op jit(solution)/shard_map/psum | solution.py:241
  631.0 2.1 broadcast_multiply_fusion
  633.1 1.7 broadcast_multiply_fusion.1
  (189 shorter events, 170.9 us)
Async XLA Ops:
  7.2 82.4 %copy-start = (bf16[6912,256]{1,0:T(8,128)(2,1)S(1)}, bf16[6912,256]{1,0:T(8,128)(2,1)}, u32[]{:S(2)}) copy-start(bf16[6912,256]{1,0:T(8,128)(2,1)} %param.16) | copy-start | bytes 10616836
  10.8 56.2 %collective-permute-start = (bf16[16,256]{1,0:T(8,128)(2,1)}, bf16[16,256]{1,0:T(8,128)(2,1)}, u32[]{:S(2)}, u32[]{:S(2)}) collective-permute-start(bf16[16,256]{1,0:T(8,128)(2,1)} %get-tuple-element.94), channel_id=1, source_target_pairs={{0,1},{1,2},{2,3},{3,4},{4,5},{5,6},{6,7},{7,8},{8,9},{9,10},{10,1... | collective-permute-start | bytes 24584 | tf_op jit(solution)/shard_map/ppermute | solution.py:21
  15.7 51.2 %collective-permute-start.1 = (bf16[16,256]{1,0:T(8,128)(2,1)}, bf16[16,256]{1,0:T(8,128)(2,1)}, u32[]{:S(2)}, u32[]{:S(2)}) collective-permute-start(bf16[16,256]{1,0:T(8,128)(2,1)} %get-tuple-element.95), channel_id=1, source_target_pairs={{1,0},{2,1},{3,2},{4,3},{5,4},{6,5},{7,6},{8,7},{9,8},{10,9},{11,1... | collective-permute-start | bytes 24584 | tf_op jit(solution)/shard_map/ppermute | solution.py:22
  21.8 1.7 copy-start.4
  23.5 27.5 %all-to-all-start = ((s32[64,1,4]{2,1,0:T(1,128)}), s32[64,1,4]{2,1,0:T(1,128)}, u32[]{:S(2)}, u32[]{:S(2)}) async-start(s32[64,1,4]{2,1,0:T(1,128)} %bitcast.156), calls=%async_computation | async-start | bytes 65536 | tf_op jit(solution)/shard_map/all_to_all | solution.py:119
  51.1 45.0 %all-to-all-start.2 = ((bf16[64,4,256]{2,1,0:T(4,128)(2,1)}), bf16[64,4,256]{2,1,0:T(4,128)(2,1)}, u32[]{:S(2)}, u32[]{:S(2)}) async-start(bf16[64,4,256]{2,1,0:T(4,128)(2,1)} %reshape.244), calls=%async_computation.2 | async-start | bytes 262144 | tf_op jit(solution)/shard_map/all_to_all | solution.py:118
  78.4 3.9 copy-start.1
  96.1 20.8 %all-to-all-start.1 = ((bf16[64,4,256]{2,1,0:T(4,128)(2,1)}), bf16[64,4,256]{2,1,0:T(4,128)(2,1)}, u32[]{:S(2)}, u32[]{:S(2)}) async-start(bf16[64,4,256]{2,1,0:T(4,128)(2,1)} %reshape.239), calls=%async_computation.1 | async-start | bytes 262144 | tf_op jit(solution)/shard_map/all_to_all | solution.py:117
  121.8 3.3 copy-start.2
  122.9 2.3 copy-start.3
  124.8 3.8 collective-permute-start.2
  264.7 18.6 %collective-permute-start.3 = (bf16[128,512]{0,1:T(8,128)(2,1)}, bf16[128,512]{0,1:T(8,128)(2,1)}, u32[]{:S(2)}, u32[]{:S(2)}) collective-permute-start(bf16[128,512]{0,1:T(8,128)(2,1)} %pad_maximum_fusion.1), channel_id=1, source_target_pairs={{0,1},{1,0},{2,3},{3,2},{4,5},{5,4},{6,7},{7,6},{8,9},{9,8},{10,11... | collective-permute-start | bytes 393224 | tf_op jit(solution)/shard_map/ppermute | solution.py:34
  272.8 20.7 %all-to-all-start.3 = ((bf16[64,4,256]{2,1,0:T(4,128)(2,1)}), bf16[64,4,256]{2,1,0:T(4,128)(2,1)}, u32[]{:S(2)}, u32[]{:S(2)}) async-start(bf16[64,4,256]{2,1,0:T(4,128)(2,1)} %reshape.248), calls=%async_computation.3 | async-start | bytes 262144 | tf_op jit(solution)/shard_map/all_to_all | solution.py:200
  293.4 95.8 %all-to-all-start.4 = ((bf16[64,4,256]{2,1,0:T(4,128)(2,1)}), bf16[64,4,256]{2,1,0:T(4,128)(2,1)}, u32[]{:S(2)}, u32[]{:S(2)}) async-start(bf16[64,4,256]{2,1,0:T(4,128)(2,1)} %reshape.253), calls=%async_computation.4 | async-start | bytes 262144 | tf_op jit(solution)/shard_map/all_to_all | solution.py:207
  303.9 327.0 %all-reduce.5.cloned.1.call-start = ((), (), s32[]{:S(2)}) async-start(), calls=%async_computation.5 | async-start | bytes 2097152 | tf_op jit(solution)/shard_map/psum | solution.py:242
  549.8 58.6 %collective-permute-start.6 = (bf16[112,256]{1,0:T(8,128)(2,1)}, bf16[112,256]{1,0:T(8,128)(2,1)}, u32[]{:S(2)}, u32[]{:S(2)}) collective-permute-start(bf16[112,256]{1,0:T(8,128)(2,1)} %convert.14), channel_id=1, source_target_pairs={{0,1},{1,2},{2,3},{3,4},{4,5},{5,6},{6,7},{7,8},{8,9},{9,10},{10,1... | collective-permute-start | bytes 172040
  551.7 56.7 %collective-permute-start.7 = (bf16[112,256]{1,0:T(8,128)(2,1)}, bf16[112,256]{1,0:T(8,128)(2,1)}, u32[]{:S(2)}, u32[]{:S(2)}) collective-permute-start(bf16[112,256]{1,0:T(8,128)(2,1)} %convert.14), channel_id=1, source_target_pairs={{0,2},{1,3},{2,4},{3,5},{4,6},{5,7},{6,8},{7,9},{8,10},{9,11},{10,... | collective-permute-start | bytes 172040
  558.7 49.7 %collective-permute-start.8 = (bf16[28,256]{1,0:T(8,128)(2,1)}, bf16[28,256]{1,0:T(8,128)(2,1)}, u32[]{:S(2)}, u32[]{:S(2)}) collective-permute-start(bf16[28,256]{1,0:T(8,128)(2,1)} %slice.97), channel_id=1, source_target_pairs={{0,3},{1,4},{2,5},{3,6},{4,7},{5,8},{6,9},{7,10},{8,11},{9,12},{10... | collective-permute-start | bytes 43016
  594.7 7.5 %collective-permute-start.4 = (bf16[16,256]{1,0:T(8,128)(2,1)S(1)}, bf16[16,256]{1,0:T(8,128)(2,1)}, u32[]{:S(2)}, u32[]{:S(2)}) collective-permute-start(bf16[16,256]{1,0:T(8,128)(2,1)S(1)} %get-tuple-element.92), channel_id=1, source_target_pairs={{0,1},{1,2},{2,3},{3,4},{4,5},{5,6},{6,7},{7,8},{8,9},{9,10},{10,1... | collective-permute-start | bytes 24584 | tf_op jit(solution)/shard_map/ppermute | solution.py:21
  596.7 5.5 collective-permute-start.5
Sparse Core Ops, SparseCore 0:
  311.0 256.2 all-reduce.4
where the time goes:
time: 649 us; the launch traced here: 642 us
  blocking collectives  241 us (37%)
  matrix products  155 us (24%)
  local copies, waits for them, and re-layouts  86 us (13%)
  starting transfers between devices  72.5 us (11%)
  other arithmetic  69.7 us (11%)
  between operations  14.9 us (2%)
    unnamed x1, blocking collectives  150 us
    psum x1, blocking collectives, shards(): lax.psum((grad_qkv, grad_proj, grad_gain), ('grp', 'gz'))  77.9 us
    dot_general x37, matrix products, contract_rows(): lax.dot_general(left_side, right_side, (((0,), (0,)), ((), ())), preferre...  58.5 us
    dot_general x37, matrix products, contract_cols(): lax.dot_general(left_side, right_side, (((1,), (1,)), ((), ())), preferre...  42.1 us
    dot_general x16, matrix products, one_head(): jnp.dot(grad_scores, key_h, preferred_element_type=jnp.float32)  23 us
    dot_general x16, matrix products, one_head(): jnp.dot(probs, value_h, preferred_element_type=jnp.float32)  23 us
    scatter-add x1, other arithmetic, shards(): spread = jnp.zeros((point_count + 2 * halo_width, feat_width), jnp.float3...  19 us
    psum x1, blocking collectives, shards(): lax.psum(shard_part.astype(jnp.bfloat16), 'grp').astype(jnp.float32)  13.9 us
  transfers between devices with their start and end apart: 15, of which 1 were waited for; matrix products, arithmetic and copies ran while one was open for 48% of the time, Pallas kernels for 0%

commit v1 on v0

v1 whole, which is shorter than its diff:
```python
import math

import jax
import jax.numpy as jnp
from jax import lax
from jax.experimental import pallas as pl
from jax.experimental.pallas import tpu as pltpu
from jax.sharding import PartitionSpec as P

HEADS = 16
NORM_EPS = 1e-05
BF = jnp.bfloat16
F32 = jnp.float32
I32 = jnp.int32

PTS = 128
FEAT = 256
OFFS = 27
RIM = 16
EXT = PTS + 2 * RIM
SLOTS = 512
PAY = 304
VMEM_LIMIT = 48 * 1024 * 1024

NX, NZ, NC = 4, 8, 2
Z_GROUPS = [[x * 16 + z * 2 + c for z in range(NZ)] for x in range(NX) for c in range(NC)]
XC_GROUPS = [[x * 16 + z * 2 + c for x in range(NX) for c in range(NC)] for z in range(NZ)]
SWAP = [(i, i ^ 1) for i in range(NX * NZ * NC)]
UP = [(i, i + 1) for i in range(NX * NZ * NC - 1)]
DOWN = [(i + 1, i) for i in range(NX * NZ * NC - 1)]


def mm(a, b):
    return jnp.dot(a, b, preferred_element_type=F32)


def mm_t(a, b):
    return lax.dot_general(a, b, (((1,), (1,)), ((), ())), preferred_element_type=F32)


def t_mm(a, b):
    return lax.dot_general(a, b, (((0,), (0,)), ((), ())), preferred_element_type=F32)


def one_hot(cond):
    return jnp.where(cond, 1.0, 0.0).astype(BF)


def iota(shape, dim):
    return lax.broadcasted_iota(I32, shape, dim)


def call(body, out_shape, *args, scratch=(), flops=1 << 26, nbytes=1 << 20, smem=0):
    specs = [pl.BlockSpec(memory_space=pltpu.SMEM)] * smem
    specs += [pl.BlockSpec(memory_space=pltpu.VMEM)] * (len(args) - smem)
    single = not isinstance(out_shape, (list, tuple))
    outs = [out_shape] if single else list(out_shape)
    got = pl.pallas_call(
        body,
        out_shape=outs,
        in_specs=specs,
        out_specs=[pl.BlockSpec(memory_space=pltpu.VMEM)] * len(outs),
        scratch_shapes=list(scratch),
        compiler_params=pltpu.CompilerParams(vmem_limit_bytes=VMEM_LIMIT),
        cost_estimate=pl.CostEstimate(flops=flops, bytes_accessed=nbytes, transcendentals=0),
    )(*args)
    return got[0] if single else got


def sds(shape, dtype=BF):
    return jax.ShapeDtypeStruct(shape, dtype)


def pick_body(pick_ref, feat_ref, down_ref, up_ref):
    rows = jnp.broadcast_to(pick_ref[...], (PTS, 2 * RIM))
    hit = one_hot(rows == iota((PTS, 2 * RIM), 0))
    got = t_mm(hit, feat_ref[...]).astype(BF)
    down_ref[...] = got[:RIM]
    up_ref[...] = got[RIM:]


def slot_hits(rank_row):
    owner = lax.shift_right_logical(rank_row, 7)
    wide = jnp.broadcast_to(owner, (PTS, PTS))
    tall = jnp.transpose(wide)
    earlier = (wide == tall) & (iota((PTS, PTS), 0) < iota((PTS, PTS), 1))
    slot = jnp.sum(jnp.where(earlier, 1, 0), axis=0, keepdims=True)
    target = owner * 8 + slot
    rows = iota((SLOTS, PTS), 0)
    return one_hot(rows == target), one_hot(rows == target + 4)


def conv_body(feat_ref, prev_ref, next_ref, nbr_ref, rank_ref, cot_ref, weight_ref, send_ref, ext, wide):
    ext[:PTS] = feat_ref[...]
    ext[PTS : PTS + RIM] = prev_ref[...]
    ext[PTS + RIM : EXT] = next_ref[...]
    ext[EXT:] = jnp.zeros((FEAT - EXT, FEAT), BF)
    rows = ext[...]
    lanes = iota((PTS, FEAT), 1)
    for k in range(OFFS):
        hit = one_hot(nbr_ref[:, k : k + 1] == lanes)
        wide[:, k * FEAT : (k + 1) * FEAT] = mm(hit, rows).astype(BF)
    mixed = (feat_ref[...].astype(F32) + mm(wide[...], weight_ref[...])).astype(BF)
    rank_row = rank_ref[...]
    first, second = slot_hits(rank_row)
    place = jnp.transpose(jnp.broadcast_to(rank_row & (PTS - 1), (PTS, PTS))).astype(F32)
    send_ref[:, :FEAT] = (mm(first, mixed) + mm(second, cot_ref[...])).astype(BF)
    marks = mm(first, (place + 1.0).astype(BF)) + mm(second, (place + (PTS + 1.0)).astype(BF))
    send_ref[:, FEAT:] = marks.astype(BF)


def place_hits(marks):
    marks = marks.astype(F32)
    lanes = iota((SLOTS, PTS), 1).astype(F32)
    return one_hot(marks == lanes + 1.0), one_hot(marks == lanes + (PTS + 1.0))


def layer_norm(hidden):
    centred = hidden - jnp.mean(hidden, -1, keepdims=True)
    inverse = lax.rsqrt(jnp.mean(centred * centred, -1, keepdims=True) + NORM_EPS)
    return centred * inverse, inverse


def keyval_body(got_ref, qkv_ref, gain_ref, local_ref, kv_ref):
    first, second = place_hits(got_ref[:, FEAT:])
    rows = got_ref[:, :FEAT]
    hidden = t_mm(first, rows)
    local_ref[:PTS] = hidden.astype(BF)
    local_ref[PTS:] = t_mm(second, rows).astype(BF)
    normed, _ = layer_norm(hidden)
    scaled = (normed * gain_ref[...]).astype(BF)
    kv_ref[...] = mm(scaled, qkv_ref[:, FEAT:]).astype(BF)


def attend_body(
    local_ref, own_ref, far_ref, qkv_ref, proj_ref, gain_ref,
    out_ref, far_grad_ref, own_grad_ref, gq_ref, gp_ref,
    qm, am, pr, ds,
):
    head_dim = FEAT // HEADS
    hidden = local_ref[:PTS].astype(F32)
    cot = local_ref[PTS:]
    normed, _ = layer_norm(hidden)
    scaled = (normed * gain_ref[...]).astype(BF)
    query = mm(scaled, qkv_ref[:, :FEAT]).astype(BF)
    grad_att = mm_t(cot, proj_ref[...]).astype(BF)
    keys = jnp.concatenate([own_ref[:, :FEAT], far_ref[:, :FEAT]], 0)
    values = jnp.concatenate([own_ref[:, FEAT:], far_ref[:, FEAT:]], 0)
    head_of = iota((PTS, FEAT), 1) // head_dim
    zero = jnp.zeros((PTS, FEAT), BF)
    att = jnp.zeros((PTS, FEAT), F32)
    gq = jnp.zeros((PTS, FEAT), F32)
    scale = head_dim ** (-0.5)
    for h in range(HEADS):
        mine = head_of == h
        span = slice(h * PTS, (h + 1) * PTS)
        q_h = jnp.where(mine, query, zero)
        a_h = jnp.where(mine, grad_att, zero)
        qm[span] = q_h
        am[span] = a_h
        e = jnp.exp(mm_t(q_h, keys) * scale)
        probs = (e * (1.0 / jnp.sum(e, -1, keepdims=True))).astype(BF)
        pr[span] = probs
        att = jnp.where(mine, mm(probs, values), att)
        grad_probs = mm_t(a_h, values)
        wide = probs.astype(F32)
        delta = jnp.sum(wide * grad_probs, -1, keepdims=True)
        grad_scores = (wide * (grad_probs - delta) * scale).astype(BF)
        ds[span] = grad_scores
        gq = jnp.where(mine, mm(grad_scores, keys), gq)
    grad_key = t_mm(ds[...], qm[...]).astype(BF)
    grad_value = t_mm(pr[...], am[...]).astype(BF)
    own_grad_ref[:, :FEAT] = grad_key[:PTS]
    own_grad_ref[:, FEAT:] = grad_value[:PTS]
    far_grad_ref[:, :FEAT] = grad_key[PTS:]
    far_grad_ref[:, FEAT:] = grad_value[PTS:]
    attended = att.astype(BF)
    out_ref[...] = (hidden + mm(attended, proj_ref[...])).astype(BF)
    gq_ref[...] = gq.astype(BF)
    gp_ref[...] = t_mm(attended, cot).astype(BF)


def norm_body(
    got_ref, local_ref, out_ref, gq_ref, own_ref, near_ref, gp_ref, qkv_ref, gain_ref,
    back_ref, dense_ref, gg_ref,
):
    hidden = local_ref[:PTS].astype(F32)
    cot = local_ref[PTS:].astype(F32)
    gain = gain_ref[...]
    normed, inverse = layer_norm(hidden)
    scaled = (normed * gain).astype(BF)
    gq, own, near = gq_ref[...], own_ref[...], near_ref[...]
    w_query, w_keyval = qkv_ref[:, :FEAT], qkv_ref[:, FEAT:]
    grad_scaled = mm_t(gq, w_query) + mm_t(own, w_keyval) + mm_t(near, w_keyval)
    grad_kv = t_mm(scaled, own) + t_mm(scaled, near)
    dense_ref[:FEAT] = t_mm(scaled, gq).astype(BF)
    dense_ref[FEAT : 2 * FEAT] = grad_kv[:, :FEAT].astype(BF)
    dense_ref[2 * FEAT : 3 * FEAT] = grad_kv[:, FEAT:].astype(BF)
    dense_ref[3 * FEAT :] = gp_ref[...]
    gg_ref[...] = jnp.sum(grad_scaled * normed, 0, keepdims=True)
    grad_normed = grad_scaled * gain
    grad_hidden = (
        grad_normed
        - jnp.mean(grad_normed, -1, keepdims=True)
        - normed * jnp.mean(grad_normed * normed, -1, keepdims=True)
    ) * inverse
    grad_local = (cot + grad_hidden).astype(BF)
    first, second = place_hits(got_ref[:, FEAT:])
    back_ref[...] = (mm(first, out_ref[...]) + mm(second, grad_local)).astype(BF)


def spread_body(
    back_ref, rank_ref, feat_ref, prev_ref, next_ref, nbr_ref, gg_ref, weight_ref,
    block_ref, pay_ref, own_ref, down_ref, up_ref,
    acc,
):
    first, second = slot_hits(rank_ref[...])
    rows = back_ref[...]
    block_ref[...] = t_mm(first, rows).astype(BF)
    grad_f32 = t_mm(second, rows)
    grad = grad_f32.astype(BF)
    eye = one_hot(iota((PTS, PTS), 0) == iota((PTS, PTS), 1))
    table = t_mm(nbr_ref[...].astype(F32).astype(BF), eye)
    points = iota((EXT, PTS), 0).astype(F32)
    acc[...] = jnp.zeros((EXT, FEAT), F32)
    for k in range(OFFS):
        hit = one_hot(points == table[k : k + 1])
        term = mm(hit, grad).astype(BF)
        acc[...] += mm_t(term, weight_ref[k * FEAT : (k + 1) * FEAT])
    own_ref[...] = acc[:PTS] + grad_f32
    down_ref[...] = acc[PTS : PTS + RIM].astype(BF)
    up_ref[...] = acc[PTS + RIM :].astype(BF)
    pay_ref[:PTS] = grad
    pay_ref[PTS : 2 * PTS] = feat_ref[...]
    pay_ref[2 * PTS : 2 * PTS + RIM] = prev_ref[...]
    pay_ref[2 * PTS + RIM : 2 * PTS + 2 * RIM] = next_ref[...]
    gg = gg_ref[...]
    pay_ref[PTS + EXT :, :PTS] = table[:16].astype(BF)
    low = jnp.concatenate([table[16:27], jnp.zeros((5, PTS), F32)], 0)
    at = iota((16, PTS), 0)
    low = jnp.where(at == 12, gg[:, :PTS], jnp.where(at == 14, gg[:, PTS:], low))
    pay_ref[PTS + EXT :, PTS:] = low.astype(BF)


def rim_body(own_ref, down_ref, up_ref, pick_ref, out_ref):
    rows = jnp.broadcast_to(pick_ref[...], (PTS, 2 * RIM))
    hit = one_hot(rows == iota((PTS, 2 * RIM), 0))
    rims = jnp.concatenate([down_ref[...], up_ref[...]], 0)
    out_ref[...] = (own_ref[...] + mm(hit, rims)).astype(BF)


def kernel_grad_body(where_ref, all_ref, dense_ref, out_ref, tab, terms, total):
    first_offset = where_ref[0]
    first_row = where_ref[1]
    odd = where_ref[2]
    sources = NX * NC
    gain = jnp.zeros((1, FEAT), F32)
    exts = []
    for s in range(sources):
        at = s * PAY
        rows = all_ref[at + PTS + EXT : at + PAY].astype(F32)
        tab[s * 32 : s * 32 + 16] = rows[:, :PTS]
        tab[s * 32 + 16 : s * 32 + 32] = rows[:, PTS:]
        gain += jnp.concatenate([rows[12:13, PTS:], rows[14:15, PTS:]], 1)
        exts.append(all_ref[at + PTS : at + PTS + EXT])
    ext_t = jnp.transpose(jnp.concatenate(exts, 0))
    points = iota((EXT, PTS), 0).astype(F32)
    for k in range(8):
        for s in range(sources):
            hit = one_hot(points == tab[pl.ds(first_offset + (s * 32 + k), 1), :])
            terms[s * EXT : (s + 1) * EXT] = mm(hit, all_ref[s * PAY : s * PAY + PTS]).astype(BF)
        total[k * FEAT : (k + 1) * FEAT] = mm(ext_t, terms[...])
    total[8 * FEAT :] = jnp.zeros((16, FEAT), F32)
    dense = jnp.zeros((PTS, FEAT), F32)
    for s in range(sources):
        dense += dense_ref[s].astype(F32)
    at = iota((112, FEAT), 0)
    for z in range(NZ):
        wide = total[pl.ds(pl.multiple_of(first_row + z * 216, 8), 120), :]
        rows = jnp.where(odd == 1, wide[4:116], wide[:112])
        rows = jnp.where(at < 108, rows, jnp.where(at == 108, gain, 0.0))
        out_ref[z, :112] = rows.astype(BF)
        out_ref[z, 112:] = dense[z * 16 : (z + 1) * 16].astype(BF)


def sum_body(got_ref, out_ref):
    total = got_ref[0].astype(F32)
    for i in range(1, got_ref.shape[0]):
        total += got_ref[i].astype(F32)
    out_ref[...] = total.astype(BF)


def group_sum_body(factor, got_ref, conv_ref, gain_ref, dense_ref):
    total = got_ref[0].astype(F32)
    for i in range(1, got_ref.shape[0]):
        total += got_ref[i].astype(F32)
    conv_ref[...] = total[:108] * factor
    gain_ref[...] = total[108:109] * factor
    dense_ref[...] = total[112:]


def unfold_body(factor, got_ref, qkv_ref, proj_ref):
    for x in range(NX):
        for c in range(NC):
            for z in range(NZ):
                row = (x * 2 + c) * 128 + z * 16
                block = got_ref[pl.ds((x * 16 + z * 2 + c) * 16, 16), :] * factor
                part, at = row // FEAT, row % FEAT
                if part < 3:
                    qkv_ref[at : at + 16, part * FEAT : (part + 1) * FEAT] = block
                else:
                    proj_ref[at : at + 16] = block


def shards(
    features,
    hilbert_rank,
    neighbours,
    halo_rows,
    cotangent,
    conv_weight,
    qkv_weight,
    proj_weight,
    norm_gain,
):
    factor = 1.0 / math.sqrt(PTS * NX * NZ * NC * lax.axis_size("grp"))
    rank_row = hilbert_rank.reshape(1, PTS)
    gain_row = norm_gain.reshape(1, FEAT)
    to_prev, to_next = call(pick_body, [sds((RIM, FEAT))] * 2, halo_rows, features)
    from_prev = lax.ppermute(to_next, "gz", UP)
    from_next = lax.ppermute(to_prev, "gz", DOWN)
    send = call(
        conv_body,
        sds((SLOTS, FEAT + PTS)),
        features, from_prev, from_next, neighbours, rank_row, cotangent, conv_weight,
        scratch=[pltpu.VMEM((FEAT, FEAT), BF), pltpu.VMEM((PTS, OFFS * FEAT), BF)],
    )
    got = lax.all_to_all(
        send.reshape(64, 8, FEAT + PTS), "gz", split_axis=0, concat_axis=0, tiled=True
    ).reshape(SLOTS, FEAT + PTS)
    local, own_kv = call(
        keyval_body, [sds((2 * PTS, FEAT)), sds((PTS, 2 * FEAT))], got, qkv_weight, gain_row
    )
    far_kv = lax.ppermute(own_kv, "gz", SWAP)
    out_local, far_grad, own_grad, grad_query, grad_proj = call(
        attend_body,
        [sds((PTS, FEAT)), sds((PTS, 2 * FEAT)), sds((PTS, 2 * FEAT)), sds((PTS, FEAT)), sds((FEAT, FEAT))],
        local, own_kv, far_kv, qkv_weight, proj_weight, gain_row,
        scratch=[pltpu.VMEM((HEADS * PTS, FEAT), BF)] * 4,
    )
    near_grad = lax.ppermute(far_grad, "gz", SWAP)
    back, dense, grad_gain = call(
        norm_body,
        [sds((SLOTS, FEAT)), sds((4 * FEAT, FEAT)), sds((1, FEAT), F32)],
        got, local, out_local, grad_query, own_grad, near_grad, grad_proj, qkv_weight, gain_row,
    )
    returned = lax.all_to_all(
        back.reshape(64, 8, FEAT), "gz", split_axis=0, concat_axis=0, tiled=True
    ).reshape(SLOTS, FEAT)
    dense_parts = lax.all_to_all(
        dense.reshape(8, PTS, FEAT), "gz", split_axis=0, concat_axis=0,
        axis_index_groups=XC_GROUPS, tiled=True,
    )
    block_out, payload, own_part, rim_down, rim_up = call(
        spread_body,
        [sds((PTS, FEAT)), sds((PAY, FEAT)), sds((PTS, FEAT), F32), sds((RIM, FEAT)), sds((RIM, FEAT))],
        returned, rank_row, features, from_prev, from_next, neighbours, grad_gain, conv_weight,
        scratch=[pltpu.VMEM((EXT, FEAT), F32)],
    )
    got_down = lax.ppermute(rim_down, "gz", DOWN)
    got_up = lax.ppermute(rim_up, "gz", UP)
    grad_features = call(rim_body, sds((PTS, FEAT)), own_part, got_up, got_down, halo_rows)
    everyone = lax.all_gather(payload, "gz", axis_index_groups=XC_GROUPS, tiled=True)
    me = lax.axis_index("gz")
    odd = me % 2
    base = (me // 16) * 1728 + odd * 108
    first_offset = jnp.minimum(base // FEAT, OFFS - 8)
    where = jnp.stack([first_offset, base - first_offset * FEAT - odd * 4, odd]).astype(I32)
    parts = call(
        kernel_grad_body,
        sds((NZ, 128, FEAT)),
        where, everyone, dense_parts,
        scratch=[
            pltpu.VMEM((NX * NC * 32, PTS), F32),
            pltpu.VMEM((NX * NC * EXT, FEAT), BF),
            pltpu.VMEM((8 * FEAT + 16, FEAT), F32),
        ],
        smem=1,
    )
    z_parts = lax.all_to_all(
        parts, "gz", split_axis=0, concat_axis=0, axis_index_groups=Z_GROUPS, tiled=True
    )
    mine = call(sum_body, sds((128, FEAT)), z_parts)
    groups = lax.all_gather(mine, "grp")
    grad_conv, gain_sum, dense_rows = call(
        lambda *refs: group_sum_body(factor, *refs),
        [sds((108, FEAT), F32), sds((1, FEAT), F32), sds((16, FEAT), F32)],
        groups,
    )
    dense_all = lax.all_gather(dense_rows, "gz", tiled=True)
    grad_qkv, grad_proj_sum = call(
        lambda *refs: unfold_body(factor, *refs),
        [sds((FEAT, 3 * FEAT), F32), sds((FEAT, FEAT), F32)],
        dense_all,
    )
    return (
        block_out,
        grad_features,
        grad_conv,
        grad_qkv,
        grad_proj_sum,
        gain_sum.reshape(FEAT),
    )


def solution(mesh):
    return jax.shard_map(
        shards,
        mesh=mesh,
        in_specs=(
            P(("grp", "gz"), None),
            P(("grp", "gz")),
            P(("grp", "gz"), None),
            P(("grp", "gz"), None),
            P(("grp", "gz"), None),
            P(),
            P(),
            P(),
            P(),
        ),
        out_specs=(P(("grp", "gz"), None), P(("grp", "gz"), None), P("gz", None), P(), P(), P()),
        check_vma=False,
    )
```

time: 649 us -> 235 us (0.36)
  blocking collectives: 241 us -> 77.2 us
  matrix products: 155 us -> 0 us
  waiting for transfers between devices: 1.76 us -> 90.3 us
  local copies, waits for them, and re-layouts: 86 us -> 9.18 us
  other arithmetic: 69.7 us -> 0.08 us
  starting transfers between devices: 72.5 us -> 19.6 us
  Pallas kernels: 0 us -> 23.6 us
    dot_general x110 -> x0, matrix products: 155 us -> none  [the longest x37 58.5 us: contract_rows(): lax.dot_general(left_side, right_side, (((0,), (0,)), ((), ())), preferre...]
    unnamed x1 -> x0, blocking collectives: 150 us -> none
    psum x2 -> x0, blocking collectives: 91.8 us -> none  [the longest x1 77.9 us: shards(): lax.psum((grad_qkv, grad_proj, grad_gain), ('grp', 'gz'))]
    all_gather x0 -> x2, waiting for transfers between devices: none -> 73.2 us  [the longest x1 62.7 us: shards(): dense_all = lax.all_gather(dense_rows, 'gz', tiled=True)]
    all_to_all x0 -> x3, blocking collectives: none -> 66.7 us  [the longest x1 25.9 us: shards(): lax.all_to_all(send.reshape(64, 8, FEAT + PTS), 'gz', split_axis=0, conca...]
    all_to_all x5 -> x1, starting transfers between devices: 53.3 us -> 4.47 us  [shards(): lax.all_to_all(dense.reshape(8, PTS, FEAT), 'gz', split_axis=0, concat_ax...]
    gather x7 -> x0, local copies, waits for them, and re-layouts: 25.4 us -> none  [the longest x2 13.8 us: neighbour_rows(): picked = extended[jnp.where(present, neighbours, 0)]]
    scatter-add x3 -> x0, other arithmetic: 23.6 us -> none  [the longest x1 19 us: shards(): spread = jnp.zeros((point_count + 2 * halo_width, feat_width), jnp.float3...]
  transfers between devices with their start and end apart: 15 -> 9, of which waited for: 1 -> 7; matrix products, arithmetic and copies ran while one was open for 48% -> 0% of each run, Pallas kernels for 0% -> 0%
where the time goes in v1:
time: 235 us; the launch traced here: 234 us
  waiting for transfers between devices  90.3 us (38%)
  blocking collectives  77.2 us (33%)
  Pallas kernels  23.6 us (10%)
  starting transfers between devices  19.6 us (8%)
  between operations  14.1 us (6%)
  local copies, waits for them, and re-layouts  9.18 us (4%)
    all_gather x1, waiting for transfers between devices, shards(): dense_all = lax.all_gather(dense_rows, 'gz', tiled=True)  62.7 us
    all_to_all x1, blocking collectives, shards(): lax.all_to_all(send.reshape(64, 8, FEAT + PTS), 'gz', split_axis=0, conca...  25.9 us
    pallas_call x11, Pallas kernels, call(): pl.pallas_call(body, out_shape=outs, in_specs=specs, out_specs=[pl.BlockS...  23.6 us
    all_to_all x1, blocking collectives, shards(): lax.all_to_all(parts, 'gz', split_axis=0, concat_axis=0, axis_index_group...  22.9 us
    all_to_all x1, blocking collectives, shards(): lax.all_to_all(back.reshape(64, 8, FEAT), 'gz', split_axis=0, concat_axis...  18 us
    all_gather x1, waiting for transfers between devices, shards(): lax.all_gather(payload, 'gz', axis_index_groups=XC_GROUPS, tiled=True)  10.5 us
    all_gather x1, blocking collectives, shards(): groups = lax.all_gather(mine, 'grp')  10.5 us
    all_to_all x1, waiting for transfers between devices, shards(): lax.all_to_all(dense.reshape(8, PTS, FEAT), 'gz', split_axis=0, concat_ax...  9.84 us
  transfers between devices with their start and end apart: 9, of which 7 were waited for; matrix products, arithmetic and copies ran while one was open for 0% of the time, Pallas kernels for 0%

profile of v1, /device:TPU:1, one launch (start us, length us, event | category | flops | bytes accessed | tf_op | source)
XLA Modules:
  0.0 234.1 jit_solution(12119865625654993301)
XLA Ops:
  7.2 0.0 all-gather.4.cloned.1.call-start
  7.2 0.0 copy-start.5
  7.2 0.8 copy-done.5
  8.1 0.0 copy-start.12
  8.1 0.7 copy-done.12
  8.7 0.0 copy-start.9
  8.7 0.0 copy-start.7
  8.7 0.2 shard_map.136
  8.9 4.9 %collective-permute-start = (bf16[16,256]{1,0:T(8,128)(2,1)S(1)}, bf16[16,256]{1,0:T(8,128)(2,1)S(1)}, u32[]{:S(2)}, u32[]{:S(2)}) collective-permute-start(bf16[16,256]{1,0:T(8,128)(2,1)S(1)} %get-tuple-element.28), channel_id=1, source_target_pairs={{0,1},{1,2},{2,3},{3,4},{4,5},{5,6},{6,7},{7,8},{8,9},{9,10},{10,1... | collective-permute-start | bytes 24584 | tf_op jit(solution)/shard_map/ppermute | solution.py:330
  13.8 1.9 collective-permute-start.1
  15.8 0.8 copy.15.nbr_ref
  16.6 0.0 collective-permute-done.prev_ref
  16.6 2.2 collective-permute-done.1.next_ref
  18.8 0.0 copy-start
  18.8 2.0 copy-done
  20.8 0.0 copy-start.6
  20.8 0.8 copy-done.6
  21.6 0.0 copy-start.8
  21.6 0.8 copy-done.8
  22.5 0.0 copy-start.10
  22.5 0.7 copy-done.10
  23.1 0.0 copy-start.2
  23.1 0.0 copy-start.1
  23.1 0.0 copy-start.11
  23.1 1.7 shard_map.137
  24.9 25.9 %all_to_all.20 = bf16[64,8,384]{2,1,0:T(8,128)(2,1)S(1)} all-to-all(bf16[64,8,384]{2,1,0:T(8,128)(2,1)S(1)} %bitcast.14), channel_id=1, replica_groups=mesh['grp'=4,'gz'=64] {'gz'}, dimensions={0} | all-to-all | bytes 786432 | tf_op jit(solution)/shard_map/all_to_all | solution.py:338
  50.8 0.0 copy-done.9
  50.8 0.0 copy-done.2
  50.8 0.5 shard_map.138
  51.3 0.5 collective-permute-start.2
  51.8 1.0 collective-permute-done.2.far_ref
  52.8 0.0 copy-done.7
  52.8 9.6 %shard_map.139 = (bf16[128,256]{1,0:T(8,128)(2,1)S(1)}, bf16[128,512]{1,0:T(8,128)(2,1)S(1)}, bf16[128,512]{1,0:T(8,128)(2,1)S(1)}, bf16[128,256]{1,0:T(8,128)(2,1)S(1)}, bf16[256,256]{1,0:T(8,128)(2,1)S(1)}) custom-call(bf16[256,256]{1,0:T(8,128)(2,1)S(1)} %get-tuple-element.30.local_ref, bf16[128,512]{1,0:T(8,128)(2,1)S(1)} %get-tuple-element.31.own_ref, ...), custom_call_target="tpu_custom_call" | custom-call | flops 67108864 | bytes 1048576 | tf_op jit(solution)/shard_map/pallas_call | solution.py:58
  62.4 0.4 collective-permute-start.3
  62.9 1.0 collective-permute-done.3.near_ref
  63.9 1.6 shard_map.140
  65.4 18.0 %all_to_all.21 = bf16[64,8,256]{2,1,0:T(8,128)(2,1)S(1)} all-to-all(bf16[64,8,256]{2,1,0:T(8,128)(2,1)S(1)} %bitcast.17), channel_id=1, replica_groups=mesh['grp'=4,'gz'=64] {'gz'}, dimensions={0} | all-to-all | bytes 524288 | tf_op jit(solution)/shard_map/all_to_all | solution.py:357
  83.4 0.0 copy-done.1
  83.4 0.0 copy-done.11
  83.4 3.5 %shard_map.141 = (bf16[128,256]{1,0:T(8,128)(2,1)}, bf16[304,256]{1,0:T(8,128)(2,1)}, f32[128,256]{1,0:T(8,128)S(1)}, bf16[16,256]{1,0:T(8,128)(2,1)S(1)}, bf16[16,256]{1,0:T(8,128)(2,1)S(1)}) custom-call(bf16[512,256]{1,0:T(8,128)(2,1)S(1)} %bitcast.15, s32[1,128]{1,0:T(1,128)S(1)} %bitcast.22, bf16[128,256]{1,0:T(8,128)(2,1)S(1)} %copy-done.6, ...), custom_call_target="tpu_custom_call" | custom-call | flops 67108864 | bytes 1048576 | tf_op jit(solution)/shard_map/pallas_call | solution.py:58
  86.9 0.0 copy-start.13
  86.9 0.0 all-gather.4.cloned.1.call-update
  86.9 4.5 %all-to-all-start.2 = ((bf16[8,128,256]{2,1,0:T(8,128)(2,1)}), bf16[8,128,256]{2,1,0:T(8,128)(2,1)S(1)}, u32[]{:S(2)}, u32[]{:S(2)}) async-start(bf16[8,128,256]{2,1,0:T(8,128)(2,1)} %bitcast.9), calls=%async_computation.2 | async-start | bytes 1048576 | tf_op jit(solution)/shard_map/all_to_all | solution.py:360
  91.4 0.0 all-gather.6.cloned.1.call-start
  91.4 0.1 pad_add_fusion.where_ref
  91.4 9.8 %all-to-all-done.2.dense_ref = bf16[8,128,256]{2,1,0:T(8,128)(2,1)S(1)} async-done(((bf16[8,128,256]{2,1,0:T(8,128)(2,1)}), bf16[8,128,256]{2,1,0:T(8,128)(2,1)S(1)}, u32[]{:S(2)}, u32[]{:S(2)}) %all-to-all-start.2) | async-done | bytes 524320 | tf_op jit(solution)/shard_map/all_to_all | solution.py:360
  101.3 10.5 %all-gather.4.cloned.1.call-done.all_ref = bf16[2432,256]{1,0:T(8,128)(2,1)} async-done(((bf16[304,256]{1,0:T(8,128)(2,1)}), bf16[2432,256]{1,0:T(8,128)(2,1)}) %all-gather.4.cloned.1.call-update) | async-done | bytes 1245200 | tf_op jit(solution)/shard_map/all_gather | solution.py:373
  111.8 0.0 copy-start.3
  111.8 1.3 copy-done.3
  113.1 3.9 %shard_map.143 = bf16[8,128,256]{2,1,0:T(8,128)(2,1)S(1)} custom-call(s32[3]{0:T(128)S(1)} %pad_add_fusion.where_ref, bf16[2432,256]{1,0:T(8,128)(2,1)S(1)} %copy-done.3, bf16[8,128,256]{2,1,0:T(8,128)(2,1)S(1)} %all-to-all-done.2.dense_ref), custom_call_target="tpu_custom_call" | custom-call | flops 67108864 | bytes 1048576 | tf_op jit(solution)/shard_map/pallas_call | solution.py:58
  117.0 22.9 %all_to_all.22.got_ref = bf16[8,128,256]{2,1,0:T(8,128)(2,1)S(1)} all-to-all(bf16[8,128,256]{2,1,0:T(8,128)(2,1)S(1)} %shard_map.143), channel_id=1, replica_groups={{0,2,4,6,8,10,12,14},{1,3,5,7,9,11,13,15},{16,18,20,22,24,26,28,30},{17..., dimensions={0} | all-to-all | bytes 1048576 | tf_op jit(solution)/shard_map/all_to_all | solution.py:390
  139.9 0.1 shard_map.144
  139.9 10.5 %all-gather = bf16[512,256]{1,0:T(8,128)(2,1)S(1)} all-gather(bf16[128,256]{1,0:T(8,128)(2,1)S(1)} %shard_map.144), channel_id=2, replica_groups=mesh['grp'=4,'gz'=64] {'grp'}, dimensions={0}, use_global_device_ids=true | all-gather | bytes 327680 | tf_op jit(solution)/shard_map/all_gather | solution.py:394
  150.4 0.7 shard_map.145
  151.1 0.0 all-gather.6.cloned.1.call-update
  151.1 5.4 %collective-permute-start.4 = (bf16[16,256]{1,0:T(8,128)(2,1)S(1)}, bf16[16,256]{1,0:T(8,128)(2,1)S(1)}, u32[]{:S(2)}, u32[]{:S(2)}) collective-permute-start(bf16[16,256]{1,0:T(8,128)(2,1)S(1)} %get-tuple-element.41), channel_id=1, source_target_pairs={{0,1},{1,2},{2,3},{3,4},{4,5},{5,6},{6,7},{7,8},{8,9},{9,10},{10,1... | collective-permute-start | bytes 24584 | tf_op jit(solution)/shard_map/ppermute | solution.py:371
  156.5 1.9 collective-permute-start.5
  158.5 0.0 collective-permute-done.4.down_ref
  158.5 3.0 %collective-permute-done.5.up_ref = bf16[16,256]{1,0:T(8,128)(2,1)S(1)} collective-permute-done((bf16[16,256]{1,0:T(8,128)(2,1)S(1)}, bf16[16,256]{1,0:T(8,128)(2,1)S(1)}, u32[]{:S(2)}, u32[]{:S(2)}) %collective-permute-start.5) | collective-permute-done | bytes 8224 | tf_op jit(solution)/shard_map/ppermute | solution.py:370
  161.5 0.0 copy-done.13
  161.5 0.8 shard_map.142
  162.3 62.7 %all-gather.6.cloned.1.call-done.refs_0_ = f32[1024,256]{1,0:T(8,128)} async-done(((f32[16,256]{1,0:T(8,128)}), f32[1024,256]{1,0:T(8,128)}) %all-gather.6.cloned.1.call-update) | async-done | bytes 1048592 | tf_op jit(solution)/shard_map/all_gather | solution.py:400
  225.0 1.2 copy-done.4
  226.2 1.1 shard_map.146
  (1 shorter events, 0.0 us)
Async XLA Ops:
  7.2 104.6 %all-gather.4.cloned.1.call-start = ((), (), s32[]{:S(2)}) async-start(), calls=%async_computation.4 | async-start | bytes 1400832 | tf_op jit(solution)/shard_map/all_gather | solution.py:373
  7.2 0.8 copy-start.5
  8.1 0.7 copy-start.12
  8.7 42.0 %copy-start.9 = (f32[256]{0:T(256)S(1)}, f32[256]{0:T(256)}, u32[]{:S(2)}) copy-start(f32[256]{0:T(256)} %param.17) | copy-start | bytes 3076
  8.7 44.1 %copy-start.7 = (bf16[256,256]{1,0:T(8,128)(2,1)S(1)}, bf16[256,256]{1,0:T(8,128)(2,1)}, u32[]{:S(2)}) copy-start(bf16[256,256]{1,0:T(8,128)(2,1)} %proj_ref.1) | copy-start | bytes 393220
  8.9 7.7 %collective-permute-start = (bf16[16,256]{1,0:T(8,128)(2,1)S(1)}, bf16[16,256]{1,0:T(8,128)(2,1)S(1)}, u32[]{:S(2)}, u32[]{:S(2)}) collective-permute-start(bf16[16,256]{1,0:T(8,128)(2,1)S(1)} %get-tuple-element.28), channel_id=1, source_target_pairs={{0,1},{1,2},{2,3},{3,4},{4,5},{5,6},{6,7},{7,8},{8,9},{9,10},{10,1... | collective-permute-start | bytes 24584 | tf_op jit(solution)/shard_map/ppermute | solution.py:330
  13.8 5.0 %collective-permute-start.1 = (bf16[16,256]{1,0:T(8,128)(2,1)S(1)}, bf16[16,256]{1,0:T(8,128)(2,1)S(1)}, u32[]{:S(2)}, u32[]{:S(2)}) collective-permute-start(bf16[16,256]{1,0:T(8,128)(2,1)S(1)} %get-tuple-element.29), channel_id=1, source_target_pairs={{1,0},{2,1},{3,2},{4,3},{5,4},{6,5},{7,6},{8,7},{9,8},{10,9},{11,1... | collective-permute-start | bytes 24584 | tf_op jit(solution)/shard_map/ppermute | solution.py:331
  18.8 2.0 copy-start
  20.8 0.8 copy-start.6
  21.6 0.8 copy-start.8
  22.5 0.7 copy-start.10
  23.1 27.6 %copy-start.2 = (bf16[256,768]{1,0:T(8,128)(2,1)S(1)}, bf16[256,768]{1,0:T(8,128)(2,1)}, u32[]{:S(2)}) copy-start(bf16[256,768]{1,0:T(8,128)(2,1)} %qkv_ref.5) | copy-start | bytes 1179652
  23.1 60.3 %copy-start.1 = (bf16[6912,256]{1,0:T(8,128)(2,1)S(1)}, bf16[6912,256]{1,0:T(8,128)(2,1)}, u32[]{:S(2)}) copy-start(bf16[6912,256]{1,0:T(8,128)(2,1)} %weight_ref.3) | copy-start | bytes 10616836
  23.1 60.3 %copy-start.11 = (s32[128]{0:T(128)S(1)}, s32[128]{0:T(128)}, u32[]{:S(2)}) copy-start(s32[128]{0:T(128)} %param.10) | copy-start | bytes 1540
  51.3 1.5 collective-permute-start.2
  62.4 1.4 collective-permute-start.3
  86.9 74.6 %copy-start.13 = (s32[1,32]{1,0:T(1,128)S(1)}, s32[1,32]{1,0:T(1,128)}, u32[]{:S(2)}) copy-start(s32[1,32]{1,0:T(1,128)} %pick_ref.3) | copy-start | bytes 388
  86.9 14.4 %all-to-all-start.2 = ((bf16[8,128,256]{2,1,0:T(8,128)(2,1)}), bf16[8,128,256]{2,1,0:T(8,128)(2,1)S(1)}, u32[]{:S(2)}, u32[]{:S(2)}) async-start(bf16[8,128,256]{2,1,0:T(8,128)(2,1)} %bitcast.9), calls=%async_computation.2 | async-start | bytes 1048576 | tf_op jit(solution)/shard_map/all_to_all | solution.py:360
  91.4 133.6 %all-gather.6.cloned.1.call-start = ((), (), s32[]{:S(2)}) async-start(), calls=%async_computation.5 | async-start | bytes 1064960 | tf_op jit(solution)/shard_map/all_gather | solution.py:400
  111.8 1.3 copy-start.3
  151.1 7.3 %collective-permute-start.4 = (bf16[16,256]{1,0:T(8,128)(2,1)S(1)}, bf16[16,256]{1,0:T(8,128)(2,1)S(1)}, u32[]{:S(2)}, u32[]{:S(2)}) collective-permute-start(bf16[16,256]{1,0:T(8,128)(2,1)S(1)} %get-tuple-element.41), channel_id=1, source_target_pairs={{0,1},{1,2},{2,3},{3,4},{4,5},{5,6},{6,7},{7,8},{8,9},{9,10},{10,1... | collective-permute-start | bytes 24584 | tf_op jit(solution)/shard_map/ppermute | solution.py:371
  156.5 5.0 %collective-permute-start.5 = (bf16[16,256]{1,0:T(8,128)(2,1)S(1)}, bf16[16,256]{1,0:T(8,128)(2,1)S(1)}, u32[]{:S(2)}, u32[]{:S(2)}) collective-permute-start(bf16[16,256]{1,0:T(8,128)(2,1)S(1)} %get-tuple-element.42), channel_id=1, source_target_pairs={{1,0},{2,1},{3,2},{4,3},{5,4},{6,5},{7,6},{8,7},{9,8},{10,9},{11,1... | collective-permute-start | bytes 24584 | tf_op jit(solution)/shard_map/ppermute | solution.py:370
  225.0 1.2 copy-start.4
Sparse Core Ops, SparseCore 0:
  87.0 24.7 all-gather.3
  151.3 73.6 all-gather.5

commit v2 on v1

v2 whole, which is shorter than its diff:
```python
import math

import jax
import jax.numpy as jnp
from jax import lax
from jax.experimental import pallas as pl
from jax.experimental.pallas import tpu as pltpu
from jax.sharding import PartitionSpec as P

HEADS = 16
NORM_EPS = 1e-05
BF = jnp.bfloat16
F32 = jnp.float32
I32 = jnp.int32

PTS = 128
FEAT = 256
OFFS = 27
RIM = 16
EXT = PTS + 2 * RIM
SLOTS = 512
PAY = 256
VMEM_LIMIT = 48 * 1024 * 1024

NX, NZ, NC = 4, 8, 2
Z_GROUPS = [[x * 16 + z * 2 + c for z in range(NZ)] for x in range(NX) for c in range(NC)]
XC_GROUPS = [[x * 16 + z * 2 + c for x in range(NX) for c in range(NC)] for z in range(NZ)]
SWAP = [(i, i ^ 1) for i in range(NX * NZ * NC)]
UP = [(i, i + 1) for i in range(NX * NZ * NC - 1)]
DOWN = [(i + 1, i) for i in range(NX * NZ * NC - 1)]


def along_x(value, d):
    n = NX * NZ * NC
    return lax.ppermute(value, "gz", [(i, (i + 16 * d) % n) for i in range(n)])


def over_chips(value):
    near = [value] + [along_x(value, d) for d in range(1, NX)]
    return near + [lax.ppermute(v, "gz", SWAP) for v in near]


def mm(a, b):
    return jnp.dot(a, b, preferred_element_type=F32)


def mm_t(a, b):
    return lax.dot_general(a, b, (((1,), (1,)), ((), ())), preferred_element_type=F32)


def t_mm(a, b):
    return lax.dot_general(a, b, (((0,), (0,)), ((), ())), preferred_element_type=F32)


def one_hot(cond):
    return jnp.where(cond, 1.0, 0.0).astype(BF)


def iota(shape, dim):
    return lax.broadcasted_iota(I32, shape, dim)


def call(body, out_shape, *args, scratch=(), flops=1 << 26, nbytes=1 << 20, smem=0, fetched=(), late=()):
    fetched = tuple(fetched) + tuple(late)
    specs = []
    for i in range(len(args)):
        space = pltpu.SMEM if i < smem else pl.ANY if i in fetched else pltpu.VMEM
        specs.append(pl.BlockSpec(memory_space=space))
    single = not isinstance(out_shape, (list, tuple))
    outs = [out_shape] if single else list(out_shape)
    held = [pltpu.VMEM(args[i].shape, args[i].dtype) for i in fetched]
    held += [pltpu.SemaphoreType.DMA] * len(fetched)

    def outer(*refs):
        base = len(args) + len(outs) + len(scratch)
        views = list(refs[: len(args)])
        copies = {}
        for n, i in enumerate(fetched):
            copies[i] = pltpu.make_async_copy(refs[i], refs[base + n], refs[base + len(fetched) + n])
            copies[i].start()
            views[i] = refs[base + n]
        for i in fetched:
            if i in late:
                views[i] = (views[i], copies[i].wait)
            else:
                copies[i].wait()
        body(*views, *refs[len(args) : base])

    got = pl.pallas_call(
        outer,
        out_shape=outs,
        in_specs=specs,
        out_specs=[pl.BlockSpec(memory_space=pltpu.VMEM)] * len(outs),
        scratch_shapes=list(scratch) + held,
        compiler_params=pltpu.CompilerParams(vmem_limit_bytes=VMEM_LIMIT),
        cost_estimate=pl.CostEstimate(flops=flops, bytes_accessed=nbytes, transcendentals=0),
    )(*args)
    return got[0] if single else got


def sds(shape, dtype=BF):
    return jax.ShapeDtypeStruct(shape, dtype)


def pick_body(pick_ref, feat_ref, down_ref, up_ref):
    rows = jnp.broadcast_to(pick_ref[...], (PTS, 2 * RIM))
    hit = one_hot(rows == iota((PTS, 2 * RIM), 0))
    got = t_mm(hit, feat_ref[...]).astype(BF)
    down_ref[...] = got[:RIM]
    up_ref[...] = got[RIM:]


def slot_hits(rank_row):
    owner = lax.shift_right_logical(rank_row, 7)
    wide = jnp.broadcast_to(owner, (PTS, PTS))
    tall = jnp.transpose(wide)
    earlier = (wide == tall) & (iota((PTS, PTS), 0) < iota((PTS, PTS), 1))
    slot = jnp.sum(jnp.where(earlier, 1, 0), axis=0, keepdims=True)
    target = owner * 8 + slot
    rows = iota((SLOTS, PTS), 0)
    return one_hot(rows == target), one_hot(rows == target + 4)


def conv_body(feat_ref, prev_ref, next_ref, nbr_ref, rank_ref, cot_ref, weight, send_ref, ext, tab, wide):
    weight_ref, weight_here = weight
    ext[:PTS] = feat_ref[...]
    ext[PTS : PTS + RIM] = prev_ref[...]
    ext[PTS + RIM : EXT] = next_ref[...]
    ext[EXT:] = jnp.zeros((FEAT - EXT, FEAT), BF)
    rows = ext[...]
    tab[:OFFS] = nbr_ref[...].astype(F32)
    tab[OFFS:] = jnp.zeros((PTS - OFFS, PTS), F32)
    table = jnp.transpose(tab[...])
    lanes = iota((PTS, FEAT), 1).astype(F32)
    for k in range(OFFS):
        hit = one_hot(table[:, k : k + 1] == lanes)
        wide[:, k * FEAT : (k + 1) * FEAT] = mm(hit, rows).astype(BF)
    weight_here()
    mixed = (feat_ref[...].astype(F32) + mm(wide[...], weight_ref[...])).astype(BF)
    rank_row = rank_ref[...]
    first, second = slot_hits(rank_row)
    place = jnp.transpose(jnp.broadcast_to(rank_row & (PTS - 1), (PTS, PTS))).astype(F32)
    send_ref[:, :FEAT] = (mm(first, mixed) + mm(second, cot_ref[...])).astype(BF)
    marks = mm(first, (place + 1.0).astype(BF)) + mm(second, (place + (PTS + 1.0)).astype(BF))
    send_ref[:, FEAT:] = marks.astype(BF)


def place_hits(marks):
    marks = marks.astype(F32)
    lanes = iota((SLOTS, PTS), 1).astype(F32)
    return one_hot(marks == lanes + 1.0), one_hot(marks == lanes + (PTS + 1.0))


def layer_norm(hidden):
    centred = hidden - jnp.mean(hidden, -1, keepdims=True)
    inverse = lax.rsqrt(jnp.mean(centred * centred, -1, keepdims=True) + NORM_EPS)
    return centred * inverse, inverse


def keyval_body(got_ref, qkv_ref, gain_ref, local_ref, kv_ref):
    first, second = place_hits(got_ref[:, FEAT:])
    rows = got_ref[:, :FEAT]
    hidden = t_mm(first, rows)
    local_ref[:PTS] = hidden.astype(BF)
    local_ref[PTS:] = t_mm(second, rows).astype(BF)
    normed, _ = layer_norm(hidden)
    scaled = (normed * gain_ref[...]).astype(BF)
    kv_ref[...] = mm(scaled, qkv_ref[:, FEAT:]).astype(BF)


def attend_body(
    local_ref, own_ref, far_ref, qkv_ref, proj_ref, gain_ref,
    out_ref, far_grad_ref, own_grad_ref, gq_ref, gp_ref,
    qm, am, pr, ds, sc, gs,
):
    head_dim = FEAT // HEADS
    scale = head_dim ** (-0.5)
    hidden = local_ref[:PTS].astype(F32)
    cot = local_ref[PTS:]
    normed, _ = layer_norm(hidden)
    scaled = (normed * gain_ref[...]).astype(BF)
    query = mm(scaled, qkv_ref[:, :FEAT]).astype(BF)
    grad_att = mm_t(cot, proj_ref[...]).astype(BF)
    keys = jnp.concatenate([own_ref[:, :FEAT], far_ref[:, :FEAT]], 0)
    values = jnp.concatenate([own_ref[:, FEAT:], far_ref[:, FEAT:]], 0)
    head_of = iota((PTS, FEAT), 1) // head_dim
    zero = jnp.zeros((PTS, FEAT), BF)
    spans = [slice(h * PTS, (h + 1) * PTS) for h in range(HEADS)]
    for h in range(HEADS):
        qm[spans[h]] = jnp.where(head_of == h, query, zero)
        am[spans[h]] = jnp.where(head_of == h, grad_att, zero)
    sc[...] = mm_t(qm[...], keys)
    gs[...] = mm_t(am[...], values)
    for h in range(HEADS):
        e = jnp.exp(sc[spans[h]] * scale)
        probs = (e * (1.0 / jnp.sum(e, -1, keepdims=True))).astype(BF)
        pr[spans[h]] = probs
        wide = probs.astype(F32)
        grad_probs = gs[spans[h]]
        delta = jnp.sum(wide * grad_probs, -1, keepdims=True)
        ds[spans[h]] = (wide * (grad_probs - delta) * scale).astype(BF)
    sc[...] = mm(pr[...], values)
    gs[...] = mm(ds[...], keys)
    att = sc[spans[0]]
    gq = gs[spans[0]]
    for h in range(1, HEADS):
        att = jnp.where(head_of == h, sc[spans[h]], att)
        gq = jnp.where(head_of == h, gs[spans[h]], gq)
    grad_key = t_mm(ds[...], qm[...]).astype(BF)
    grad_value = t_mm(pr[...], am[...]).astype(BF)
    own_grad_ref[:, :FEAT] = grad_key[:PTS]
    own_grad_ref[:, FEAT:] = grad_value[:PTS]
    far_grad_ref[:, :FEAT] = grad_key[PTS:]
    far_grad_ref[:, FEAT:] = grad_value[PTS:]
    attended = att.astype(BF)
    out_ref[...] = (hidden + mm(attended, proj_ref[...])).astype(BF)
    gq_ref[...] = gq.astype(BF)
    gp_ref[...] = t_mm(attended, cot).astype(BF)


def attend(*args):
    return call(
        attend_body,
        [sds((PTS, FEAT)), sds((PTS, 2 * FEAT)), sds((PTS, 2 * FEAT)), sds((PTS, FEAT)), sds((FEAT, FEAT))],
        *args,
        scratch=[pltpu.VMEM((HEADS * PTS, FEAT), BF)] * 4 + [pltpu.VMEM((HEADS * PTS, FEAT), F32)] * 2,
    )


def norm_body(
    got_ref, local_ref, out_ref, gq_ref, own_ref, near_ref, gp_ref, qkv_ref, gain_ref,
    back_ref, dense_ref, gg_ref,
):
    hidden = local_ref[:PTS].astype(F32)
    cot = local_ref[PTS:].astype(F32)
    gain = gain_ref[...]
    normed, inverse = layer_norm(hidden)
    scaled = (normed * gain).astype(BF)
    gq, own, near = gq_ref[...], own_ref[...], near_ref[...]
    w_query, w_keyval = qkv_ref[:, :FEAT], qkv_ref[:, FEAT:]
    grad_scaled = mm_t(gq, w_query) + mm_t(own, w_keyval) + mm_t(near, w_keyval)
    grad_kv = t_mm(scaled, own) + t_mm(scaled, near)
    dense_ref[:FEAT] = t_mm(scaled, gq).astype(BF)
    dense_ref[FEAT : 2 * FEAT] = grad_kv[:, :FEAT].astype(BF)
    dense_ref[2 * FEAT : 3 * FEAT] = grad_kv[:, FEAT:].astype(BF)
    dense_ref[3 * FEAT :] = gp_ref[...]
    gg_ref[...] = jnp.sum(grad_scaled * normed, 0, keepdims=True)
    grad_normed = grad_scaled * gain
    grad_hidden = (
        grad_normed
        - jnp.mean(grad_normed, -1, keepdims=True)
        - normed * jnp.mean(grad_normed * normed, -1, keepdims=True)
    ) * inverse
    grad_local = (cot + grad_hidden).astype(BF)
    first, second = place_hits(got_ref[:, FEAT:])
    back_ref[...] = (mm(first, out_ref[...]) + mm(second, grad_local)).astype(BF)


def table_body(feat_ref, prev_ref, next_ref, nbr_ref, pay_ref):
    pay_ref[:PTS] = feat_ref[...]
    pay_ref[PTS : PTS + RIM] = prev_ref[...]
    pay_ref[PTS + RIM : EXT] = next_ref[...]
    table = nbr_ref[...].astype(F32)
    pay_ref[EXT : EXT + 16, :PTS] = table[:16].astype(BF)
    pay_ref[EXT : EXT + 16, PTS:] = jnp.concatenate([table[16:], jnp.zeros((5, PTS), F32)], 0).astype(BF)
    pay_ref[EXT + 16 :] = jnp.zeros((PAY - EXT - 16, FEAT), BF)


def unpack_body(back_ref, rank_ref, gg_ref, block_ref, grad_ref):
    first, second = slot_hits(rank_ref[...])
    rows = back_ref[...]
    grad_ref[:PTS] = t_mm(second, rows).astype(BF)
    grad_ref[PTS:] = jnp.broadcast_to(gg_ref[...], (16, FEAT)).astype(BF)
    block_ref[...] = t_mm(first, rows).astype(BF)


def spread_body(grad_ref, nbr_ref, weight_ref, own_ref, down_ref, up_ref, acc):
    grad = grad_ref[:PTS]
    table = nbr_ref[...].astype(F32)
    points = iota((EXT, PTS), 0).astype(F32)
    acc[...] = jnp.zeros((EXT, FEAT), F32)
    for k in range(OFFS):
        hit = one_hot(points == table[k : k + 1])
        term = mm(hit, grad).astype(BF)
        acc[...] += mm_t(term, weight_ref[k * FEAT : (k + 1) * FEAT])
    own_ref[...] = acc[:PTS] + grad.astype(F32)
    down_ref[...] = acc[PTS : PTS + RIM].astype(BF)
    up_ref[...] = acc[PTS + RIM :].astype(BF)


def rim_body(own_ref, down_ref, up_ref, pick_ref, out_ref):
    rows = jnp.broadcast_to(pick_ref[...], (PTS, 2 * RIM))
    hit = one_hot(rows == iota((PTS, 2 * RIM), 0))
    rims = jnp.concatenate([down_ref[...], up_ref[...]], 0)
    out_ref[...] = (own_ref[...] + mm(hit, rims)).astype(BF)


def kernel_grad_body(where_ref, all_ref, dense_ref, *refs):
    grads, (out_ref, tab, exts, terms, total) = refs[: NX * NC], refs[NX * NC :]
    first_offset = where_ref[0]
    first_row = where_ref[1]
    core = where_ref[2]
    x = where_ref[3]
    gain = jnp.zeros((1, FEAT), F32)
    for s in range(NX * NC):
        source = ((x + NX - s % NX) & (NX - 1)) * NC + (core if s < NX else 1 - core)
        rows = all_ref[source, EXT : EXT + 16].astype(F32)
        tab[s * 32 : s * 32 + 16] = rows[:, :PTS]
        tab[s * 32 + 16 : s * 32 + 32] = rows[:, PTS:]
        exts[s * EXT : (s + 1) * EXT] = all_ref[source, :EXT]
        gain += grads[s][PTS : PTS + 1].astype(F32)
    ext_t = jnp.transpose(exts[...])
    points = iota((EXT, PTS), 0).astype(F32)
    for k in range(8):
        for s in range(NX * NC):
            hit = one_hot(points == tab[pl.ds(first_offset + (s * 32 + k), 1), :])
            terms[s * EXT : (s + 1) * EXT] = mm(hit, grads[s][:PTS]).astype(BF)
        total[k * FEAT : (k + 1) * FEAT] = mm(ext_t, terms[...])
    total[8 * FEAT :] = jnp.zeros((16, FEAT), F32)
    at = iota((112, FEAT), 0)
    for z in range(NZ):
        wide = total[pl.ds(pl.multiple_of(first_row + z * 216, 8), 120), :]
        rows = jnp.where(core == 1, wide[4:116], wide[:112])
        rows = jnp.where(at < 108, rows, jnp.where(at == 108, gain, 0.0))
        out_ref[z, :112] = rows.astype(BF)
        out_ref[z, 112:] = dense_ref[...]


def sum_body(got_ref, out_ref):
    total = got_ref[0].astype(F32)
    for i in range(1, got_ref.shape[0]):
        total += got_ref[i].astype(F32)
    out_ref[...] = total.astype(BF)


def group_sum_body(factor, *refs):
    parts, (conv_ref, gain_ref, dense_ref) = refs[:4], refs[4:]
    total = parts[0][...].astype(F32)
    for part in parts[1:]:
        total += part[...].astype(F32)
    dense_ref[...] = total[112:].astype(BF)
    conv_ref[...] = total[:108] * factor
    gain_ref[...] = total[108:109] * factor


def unfold_body(factor, where_ref, *refs):
    parts, (qkv_ref, proj_ref, rows) = refs[: NX * NC], refs[NX * NC :]
    core = where_ref[2]
    x = where_ref[3]
    for s in range(NX * NC):
        source = ((x + NX - s % NX) & (NX - 1)) * NC + (core if s < NX else 1 - core)
        rows[source] = parts[s][...].astype(F32) * factor
    for b in range(NX * NC):
        part, at = b // 2, b % 2 * PTS
        if part < 3:
            qkv_ref[at : at + PTS, part * FEAT : (part + 1) * FEAT] = rows[b]
        else:
            proj_ref[at : at + PTS] = rows[b]


def shards(
    features,
    hilbert_rank,
    neighbours,
    halo_rows,
    cotangent,
    conv_weight,
    qkv_weight,
    proj_weight,
    norm_gain,
):
    factor = 1.0 / math.sqrt(PTS * NX * NZ * NC * lax.axis_size("grp"))
    rank_row = hilbert_rank.reshape(1, PTS)
    gain_row = norm_gain.reshape(1, FEAT)
    table = neighbours.T
    to_prev, to_next = call(
        pick_body, [sds((RIM, FEAT))] * 2, halo_rows, features, fetched=(0, 1)
    )
    from_prev = lax.ppermute(to_next, "gz", UP)
    from_next = lax.ppermute(to_prev, "gz", DOWN)
    me = lax.axis_index("gz")
    core = me % 2
    base = (me // 16) * 1728 + core * 108
    first_offset = jnp.minimum(base // FEAT, OFFS - 8)
    where = jnp.stack([first_offset, base - first_offset * FEAT - core * 4, core, me // 16]).astype(I32)
    payload = call(table_body, sds((PAY, FEAT)), features, from_prev, from_next, table)
    everyone = lax.all_gather(payload, "gz", axis_index_groups=XC_GROUPS)
    send = call(
        conv_body,
        sds((SLOTS, FEAT + PTS)),
        features, from_prev, from_next, table, rank_row, cotangent, conv_weight,
        scratch=[pltpu.VMEM((FEAT, FEAT), BF), pltpu.VMEM((PTS, PTS), F32), pltpu.VMEM((PTS, OFFS * FEAT), BF)],
        fetched=(0, 3, 4, 5), late=(6,),
    )
    got = lax.all_to_all(
        send.reshape(64, 8, FEAT + PTS), "gz", split_axis=0, concat_axis=0, tiled=True
    ).reshape(SLOTS, FEAT + PTS)
    local, own_kv = call(
        keyval_body, [sds((2 * PTS, FEAT)), sds((PTS, 2 * FEAT))], got, qkv_weight, gain_row
    )
    far_kv = lax.ppermute(own_kv, "gz", SWAP)
    out_local, far_grad, own_grad, grad_query, grad_proj = attend(
        local, own_kv, far_kv, qkv_weight, proj_weight, gain_row
    )
    near_grad = lax.ppermute(far_grad, "gz", SWAP)
    back, dense, grad_gain = call(
        norm_body,
        [sds((SLOTS, FEAT)), sds((4 * FEAT, FEAT)), sds((1, FEAT), F32)],
        got, local, out_local, grad_query, own_grad, near_grad, grad_proj, qkv_weight, gain_row,
    )
    dense_part = lax.psum_scatter(
        dense, "gz", scatter_dimension=0, axis_index_groups=XC_GROUPS, tiled=True
    )
    returned = lax.all_to_all(
        back.reshape(64, 8, FEAT), "gz", split_axis=0, concat_axis=0, tiled=True
    ).reshape(SLOTS, FEAT)
    block_out, grad = call(
        unpack_body, [sds((PTS, FEAT)), sds((PTS + 16, FEAT))], returned, rank_row, grad_gain
    )
    grads = over_chips(grad)
    own_part, rim_down, rim_up = call(
        spread_body,
        [sds((PTS, FEAT), F32), sds((RIM, FEAT)), sds((RIM, FEAT))],
        grad, table, conv_weight,
        scratch=[pltpu.VMEM((EXT, FEAT), F32)],
    )
    got_down = lax.ppermute(rim_down, "gz", DOWN)
    got_up = lax.ppermute(rim_up, "gz", UP)
    grad_features = call(rim_body, sds((PTS, FEAT)), own_part, got_up, got_down, halo_rows)
    parts = call(
        kernel_grad_body,
        sds((NZ, 240, FEAT)),
        where, everyone, dense_part, *grads,
        scratch=[
            pltpu.VMEM((NX * NC * 32, PTS), F32),
            pltpu.VMEM((NX * NC * EXT, FEAT), BF),
            pltpu.VMEM((NX * NC * EXT, FEAT), BF),
            pltpu.VMEM((8 * FEAT + 16, FEAT), F32),
        ],
        smem=1,
    )
    z_parts = lax.all_to_all(
        parts, "gz", split_axis=0, concat_axis=0, axis_index_groups=Z_GROUPS, tiled=True
    )
    mine = call(sum_body, sds((240, FEAT)), z_parts)
    groups = [mine] + [
        lax.ppermute(mine, "grp", [(i, (i + d) % 4) for i in range(4)]) for d in range(1, 4)
    ]
    grad_conv, gain_sum, dense_rows = call(
        lambda *refs: group_sum_body(factor, *refs),
        [sds((108, FEAT), F32), sds((1, FEAT), F32), sds((PTS, FEAT))],
        *groups,
    )
    grad_qkv, grad_proj_sum = call(
        lambda *refs: unfold_body(factor, *refs),
        [sds((FEAT, 3 * FEAT), F32), sds((FEAT, FEAT), F32)],
        where, *over_chips(dense_rows),
        scratch=[pltpu.VMEM((NX * NC, PTS, FEAT), F32)],
        smem=1,
    )
    return (
        block_out,
        grad_features,
        grad_conv,
        grad_qkv,
        grad_proj_sum,
        gain_sum.reshape(FEAT),
    )


def solution(mesh):
    return jax.shard_map(
        shards,
        mesh=mesh,
        in_specs=(
            P(("grp", "gz"), None),
            P(("grp", "gz")),
            P(("grp", "gz"), None),
            P(("grp", "gz"), None),
            P(("grp", "gz"), None),
            P(),
            P(),
            P(),
            P(),
        ),
        out_specs=(P(("grp", "gz"), None), P(("grp", "gz"), None), P("gz", None), P(), P(), P()),
        check_vma=False,
    )
```

time: 235 us -> 179 us (0.76)
  waiting for transfers between devices: 90.3 us -> 12.9 us
  starting transfers between devices: 19.6 us -> 39.6 us
  local copies, waits for them, and re-layouts: 9.18 us -> 18.2 us
  blocking collectives: 77.2 us -> 72.3 us
  Pallas kernels: 23.6 us -> 20.5 us
    all_gather x2 -> x1, waiting for transfers between devices: 73.2 us -> 0.01 us  [shards(): everyone = lax.all_gather(payload, 'gz', axis_index_groups=XC_GROUPS)]
    ppermute x0 -> x17, starting transfers between devices: none -> 27.7 us  [the longest x6 12.3 us: along_x(): return lax.ppermute(value, 'gz', [(i, (i + 16 * d) % n) for i in range(n)])]
    all_gather x1 -> x0, blocking collectives: 10.5 us -> none  [shards(): groups = lax.all_gather(mine, 'grp')]
    all_to_all x1 -> x0, waiting for transfers between devices: 9.84 us -> none  [shards(): lax.all_to_all(dense.reshape(8, PTS, FEAT), 'gz', split_axis=0, concat_ax...]
    unnamed x29 -> x58, local copies, waits for them, and re-layouts: 9.18 us -> 18.2 us
    all_to_all x1, blocking collectives: 22.9 us -> 28 us  [shards(): lax.all_to_all(parts, 'gz', split_axis=0, concat_axis=0, axis_index_group...]
    all_to_all x1 -> x0, starting transfers between devices: 4.47 us -> none  [shards(): lax.all_to_all(dense.reshape(8, PTS, FEAT), 'gz', split_axis=0, concat_ax...]
    ppermute x0 -> x17, waiting for transfers between devices: none -> 3.68 us  [the longest x3 2.93 us: shards(): lax.ppermute(mine, 'grp', [(i, (i + d) % 4) for i in range(4)])]
  transfers between devices with their start and end apart: 9 -> 25, of which waited for: 7 -> 8; matrix products, arithmetic and copies ran while one was open for 0% -> 0% of each run, Pallas kernels for 0% -> 7%
where the time goes in v2:
time: 179 us; the launch traced here: 178 us
  blocking collectives  72.3 us (40%)
  starting transfers between devices  39.6 us (22%)
  Pallas kernels  20.5 us (11%)
  local copies, waits for them, and re-layouts  18.2 us (10%)
  between operations  14.2 us (8%)
  waiting for transfers between devices  12.9 us (7%)
    all_to_all x1, blocking collectives, shards(): lax.all_to_all(parts, 'gz', split_axis=0, concat_axis=0, axis_index_group...  28 us
    all_to_all x1, blocking collectives, shards(): lax.all_to_all(send.reshape(64, 8, FEAT + PTS), 'gz', split_axis=0, conca...  25.9 us
    pallas_call x13, Pallas kernels, call(): pl.pallas_call(outer, out_shape=outs, in_specs=specs, out_specs=[pl.Block...  20.5 us
    all_to_all x1, blocking collectives, shards(): lax.all_to_all(back.reshape(64, 8, FEAT), 'gz', split_axis=0, concat_axis...  18.4 us
    unnamed x58, local copies, waits for them, and re-layouts  18.2 us
    ppermute x6, starting transfers between devices, along_x(): return lax.ppermute(value, 'gz', [(i, (i + 16 * d) % n) for i in range(n)])  12.3 us
    ppermute x8, starting transfers between devices, over_chips(): return near + [lax.ppermute(v, 'gz', SWAP) for v in near]  9.93 us
    ppermute x3, starting transfers between devices, shards(): lax.ppermute(mine, 'grp', [(i, (i + d) % 4) for i in range(4)])  5.5 us
  transfers between devices with their start and end apart: 25, of which 8 were waited for; matrix products, arithmetic and copies ran while one was open for 0% of the time, Pallas kernels for 7%

profile of v2, /device:TPU:1, one launch (start us, length us, event | category | flops | bytes accessed | tf_op | source)
XLA Modules:
  0.0 178.5 jit_solution(13462363631546914936)
XLA Ops:
  7.2 0.9 copy-done.14
  8.1 0.7 copy-done.27
  9.0 4.9 %collective-permute-start = (bf16[16,256]{1,0:T(8,128)(2,1)S(1)}, bf16[16,256]{1,0:T(8,128)(2,1)S(1)}, u32[]{:S(2)}, u32[]{:S(2)}) collective-permute-start(bf16[16,256]{1,0:T(8,128)(2,1)S(1)} %get-tuple-element.28), channel_id=1, source_target_pairs={{0,1},{1,2},{2,3},{3,4},{4,5},{5,6},{6,7},{7,8},{8,9},{9,10},{10,1... | collective-permute-start | bytes 24584 | tf_op jit(solution)/shard_map/ppermute | solution.py:379
  14.0 1.9 %collective-permute-start.1 = (bf16[16,256]{1,0:T(8,128)(2,1)S(1)}, bf16[16,256]{1,0:T(8,128)(2,1)S(1)}, u32[]{:S(2)}, u32[]{:S(2)}) collective-permute-start(bf16[16,256]{1,0:T(8,128)(2,1)S(1)} %get-tuple-element.29), channel_id=1, source_target_pairs={{1,0},{2,1},{3,2},{4,3},{5,4},{6,5},{7,6},{8,7},{9,8},{10,9},{11,1... | collective-permute-start | bytes 24584 | tf_op jit(solution)/shard_map/ppermute | solution.py:380
  15.9 3.0 %collective-permute-done.1.refs_2_ = bf16[16,256]{1,0:T(8,128)(2,1)S(1)} collective-permute-done((bf16[16,256]{1,0:T(8,128)(2,1)S(1)}, bf16[16,256]{1,0:T(8,128)(2,1)S(1)}, u32[]{:S(2)}, u32[]{:S(2)}) %collective-permute-start.1) | collective-permute-done | bytes 8224 | tf_op jit(solution)/shard_map/ppermute | solution.py:380
  19.0 0.8 copy-done.15
  19.8 0.7 copy-done.18
  20.5 0.7 shard_map.144
  21.3 2.0 %copy-done = bf16[6912,256]{1,0:T(8,128)(2,1)S(1)} copy-done((bf16[6912,256]{1,0:T(8,128)(2,1)S(1)}, bf16[6912,256]{1,0:T(8,128)(2,1)}, u32[]{:S(2)}) %copy-start) | copy-done | bytes 3538968
  23.3 0.8 copy-done.16
  24.1 0.8 copy-done.17
  24.9 0.7 copy-done.23
  25.6 3.0 %shard_map.137 = bf16[512,384]{1,0:T(8,128)(2,1)S(1)} custom-call(bf16[128,256]{1,0:T(8,128)(2,1)S(1)} %copy-done.16, bf16[16,256]{1,0:T(8,128)(2,1)S(1)} %collective-permute-done.refs_1_, bf16[16,256]{1,0:T(8,128)(2,1)S(1)} %collective-permute-done.1.refs_2_, s32[27,128]{1,0:T(8,128)S(1)} %bitcast.20, s32[1,128]{1,0:T(1,128)S(1)} %bitcast.25, ...), custom_call_target="tpu_custom_call" | custom-call | flops 67108864 | bytes 1048576 | tf_op jit(solution)/shard_map/pallas_call | solution.py:89
  28.6 25.9 %all_to_all.15 = bf16[64,8,384]{2,1,0:T(8,128)(2,1)S(1)} all-to-all(bf16[64,8,384]{2,1,0:T(8,128)(2,1)S(1)} %bitcast.15), channel_id=1, replica_groups=mesh['grp'=4,'gz'=64] {'gz'}, dimensions={0} | all-to-all | bytes 786432 | tf_op jit(solution)/shard_map/all_to_all | solution.py:395
  54.5 0.5 shard_map.138
  55.0 0.5 collective-permute-start.2
  55.5 1.0 collective-permute-done.2.refs_2_
  56.5 2.4 %shard_map.139 = (bf16[128,256]{1,0:T(8,128)(2,1)S(1)}, bf16[128,512]{1,0:T(8,128)(2,1)S(1)}, bf16[128,512]{1,0:T(8,128)(2,1)S(1)}, bf16[128,256]{1,0:T(8,128)(2,1)S(1)}, bf16[256,256]{1,0:T(8,128)(2,1)S(1)}) custom-call(bf16[256,256]{1,0:T(8,128)(2,1)S(1)} %get-tuple-element.30.refs_0_.refs_1_, bf16[128,512]{1,0:T(8,128)(2,1)S(1)} %get-tuple-element.31.refs_1_, ...), custom_call_target="tpu_custom_call" | custom-call | flops 67108864 | bytes 1048576 | tf_op jit(solution)/shard_map/pallas_call | solution.py:89
  59.3 1.0 collective-permute-done.3.refs_5_
  60.3 1.6 shard_map.140
  61.9 0.7 copy-done.4
  62.6 18.4 %all_to_all.16 = bf16[64,8,256]{2,1,0:T(8,128)(2,1)S(1)} all-to-all(bf16[64,8,256]{2,1,0:T(8,128)(2,1)} %bitcast.18), channel_id=1, replica_groups=mesh['grp'=4,'gz'=64] {'gz'}, dimensions={0} | all-to-all | bytes 524288 | tf_op jit(solution)/shard_map/all_to_all | solution.py:414
  81.0 0.7 copy-done.24
  81.7 0.7 copy-done.26
  82.4 1.1 shard_map.141
  83.4 0.9 collective-permute-start.6
  84.4 2.6 %collective-permute-start.7 = (bf16[144,256]{1,0:T(8,128)(2,1)}, bf16[144,256]{1,0:T(8,128)(2,1)}, u32[]{:S(2)}, u32[]{:S(2)}) collective-permute-start(bf16[144,256]{1,0:T(8,128)(2,1)} %get-tuple-element.40.refs_0_.refs_3_), channel_id=1, source_target_pairs={{0,32},{1,33},{2,34},{3,35},{4,36},{5,37},{6,38},{7,39},{8,40},{9,... | collective-permute-start | bytes 221192 | tf_op jit(solution)/shard_map/ppermute | solution.py:35
  87.0 1.1 collective-permute-start.8
  88.0 1.2 collective-permute-start.9
  89.3 1.0 collective-permute-start.10
  90.2 0.7 collective-permute-done.7.refs_5_
  90.9 1.6 collective-permute-start.11
  92.6 0.7 pad_add_fusion.refs_0_
  93.2 0.6 copy-done.6
  93.9 0.6 copy-done.8
  94.5 0.6 copy-done.10
  95.1 0.6 copy-done.12
  95.8 1.2 copy-done.3
  97.0 0.9 copy-done.7
  97.9 0.9 copy-done.9
  98.8 0.9 copy-done.11
  99.6 0.9 copy-done.13
  100.5 0.8 copy-done.20
  101.4 0.7 copy-done.22
  102.1 4.3 %shard_map.145 = bf16[8,240,256]{2,1,0:T(8,128)(2,1)S(1)} custom-call(s32[4]{0:T(128)S(1)} %copy-done.22, bf16[8,256,256]{2,1,0:T(8,128)(2,1)S(1)} %bitcast.16, bf16[128,256]{1,0:T(8,128)(2,1)S(1)} %copy-done.20, bf16[144,256]{1,0:T(8,128)(2,1)} %get-tuple-element.40.refs_0_.refs_3_, bf16[144,256]{1,0:T(8,128)(2,1)} %collective-permute-done.6.refs_4_, ...), custom_call_target="tpu_custom_call" | custom-call | flops 67108864 | bytes 1048576 | tf_op jit(solution)/shard_map/pallas_call | solution.py:89
  106.3 28.0 %all_to_all.17.refs_0_ = bf16[8,240,256]{2,1,0:T(8,128)(2,1)S(1)} all-to-all(bf16[8,240,256]{2,1,0:T(8,128)(2,1)S(1)} %shard_map.145), channel_id=1, replica_groups={{0,2,4,6,8,10,12,14},{1,3,5,7,9,11,13,15},{16,18,20,22,24,26,28,30},{17..., dimensions={0} | all-to-all | bytes 1966080 | tf_op jit(solution)/shard_map/all_to_all | solution.py:442
  134.5 1.4 collective-permute-start.13
  135.9 3.0 %collective-permute-start.14 = (bf16[240,256]{1,0:T(8,128)(2,1)S(1)}, bf16[240,256]{1,0:T(8,128)(2,1)S(1)}, u32[]{:S(2)}, u32[]{:S(2)}) collective-permute-start(bf16[240,256]{1,0:T(8,128)(2,1)S(1)} %shard_map.146.refs_0_), channel_id=1, source_target_pairs={{0,128},{64,192},{128,0},{192,64},{1,129},{65,193},{129,1},{193,65... | collective-permute-start | bytes 368648 | tf_op jit(solution)/shard_map/ppermute | solution.py:447
  138.9 1.1 collective-permute-start.15
  140.0 2.5 %collective-permute-done.14.refs_2_ = bf16[240,256]{1,0:T(8,128)(2,1)S(1)} collective-permute-done((bf16[240,256]{1,0:T(8,128)(2,1)S(1)}, bf16[240,256]{1,0:T(8,128)(2,1)S(1)}, u32[]{:S(2)}, u32[]{:S(2)}) %collective-permute-start.14) | collective-permute-done | bytes 122912 | tf_op jit(solution)/shard_map/ppermute | solution.py:447
  142.9 0.7 shard_map.147
  143.6 4.9 %collective-permute-start.16 = (bf16[128,256]{1,0:T(8,128)(2,1)S(1)}, bf16[128,256]{1,0:T(8,128)(2,1)S(1)}, u32[]{:S(2)}, u32[]{:S(2)}) collective-permute-start(bf16[128,256]{1,0:T(8,128)(2,1)S(1)} %get-tuple-element.46.refs_1_), channel_id=1, source_target_pairs={{0,16},{1,17},{2,18},{3,19},{4,20},{5,21},{6,22},{7,23},{8,24},{9,... | collective-permute-start | bytes 196616 | tf_op jit(solution)/shard_map/ppermute | solution.py:35
  148.5 2.8 %collective-permute-start.17 = (bf16[128,256]{1,0:T(8,128)(2,1)S(1)}, bf16[128,256]{1,0:T(8,128)(2,1)S(1)}, u32[]{:S(2)}, u32[]{:S(2)}) collective-permute-start(bf16[128,256]{1,0:T(8,128)(2,1)S(1)} %get-tuple-element.46.refs_1_), channel_id=1, source_target_pairs={{0,32},{1,33},{2,34},{3,35},{4,36},{5,37},{6,38},{7,39},{8,40},{9,... | collective-permute-start | bytes 196616 | tf_op jit(solution)/shard_map/ppermute | solution.py:35
  151.3 2.1 %collective-permute-start.19 = (bf16[128,256]{1,0:T(8,128)(2,1)S(1)}, bf16[128,256]{1,0:T(8,128)(2,1)S(1)}, u32[]{:S(2)}, u32[]{:S(2)}) collective-permute-start(bf16[128,256]{1,0:T(8,128)(2,1)S(1)} %get-tuple-element.46.refs_1_), channel_id=1, source_target_pairs={{0,1},{1,0},{2,3},{3,2},{4,5},{5,4},{6,7},{7,6},{8,9},{9,8},{10,11... | collective-permute-start | bytes 196616 | tf_op jit(solution)/shard_map/ppermute | solution.py:40
  153.4 1.3 collective-permute-start.20
  154.7 1.5 collective-permute-start.21
  156.1 1.3 collective-permute-start.22
  157.5 3.5 %shard_map.142 = (f32[128,256]{1,0:T(8,128)S(1)}, bf16[16,256]{1,0:T(8,128)(2,1)S(1)}, bf16[16,256]{1,0:T(8,128)(2,1)S(1)}) custom-call(bf16[144,256]{1,0:T(8,128)(2,1)} %get-tuple-element.40.refs_0_.refs_3_, s32[27,128]{1,0:T(8,128)S(1)} %bitcast.21, bf16[6912,256]{1,0:T(8,128)(2,1)S(1)} %copy-done.1), custom_call_target="tpu_custom_call" | custom-call | flops 67108864 | bytes 1048576 | tf_op jit(solution)/shard_map/pallas_call | solution.py:89
  161.0 1.9 %collective-permute-start.4 = (bf16[16,256]{1,0:T(8,128)(2,1)S(1)}, bf16[16,256]{1,0:T(8,128)(2,1)S(1)}, u32[]{:S(2)}, u32[]{:S(2)}) collective-permute-start(bf16[16,256]{1,0:T(8,128)(2,1)S(1)} %get-tuple-element.42), channel_id=1, source_target_pairs={{0,1},{1,2},{2,3},{3,4},{4,5},{5,6},{6,7},{7,8},{8,9},{9,10},{10,1... | collective-permute-start | bytes 24584 | tf_op jit(solution)/shard_map/ppermute | solution.py:428
  162.9 1.1 collective-permute-done.4.refs_1_
  164.0 2.1 %collective-permute-start.5 = (bf16[16,256]{1,0:T(8,128)(2,1)S(1)}, bf16[16,256]{1,0:T(8,128)(2,1)S(1)}, u32[]{:S(2)}, u32[]{:S(2)}) collective-permute-start(bf16[16,256]{1,0:T(8,128)(2,1)S(1)} %get-tuple-element.43), channel_id=1, source_target_pairs={{1,0},{2,1},{3,2},{4,3},{5,4},{6,5},{7,6},{8,7},{9,8},{10,9},{11,1... | collective-permute-start | bytes 24584 | tf_op jit(solution)/shard_map/ppermute | solution.py:427
  166.1 3.1 %collective-permute-done.5.refs_2_ = bf16[16,256]{1,0:T(8,128)(2,1)S(1)} collective-permute-done((bf16[16,256]{1,0:T(8,128)(2,1)S(1)}, bf16[16,256]{1,0:T(8,128)(2,1)S(1)}, u32[]{:S(2)}, u32[]{:S(2)}) %collective-permute-start.5) | collective-permute-done | bytes 8224 | tf_op jit(solution)/shard_map/ppermute | solution.py:427
  169.2 0.8 shard_map.143
  170.0 1.6 shard_map.148
  (63 shorter events, 1.6 us)
Async XLA Ops:
  7.2 47.3 %copy-start.2 = (bf16[256,768]{1,0:T(8,128)(2,1)S(1)}, bf16[256,768]{1,0:T(8,128)(2,1)}, u32[]{:S(2)}) copy-start(bf16[256,768]{1,0:T(8,128)(2,1)} %refs_7_.1) | copy-start | bytes 1179652
  7.2 49.3 %copy-start.5 = (bf16[256,256]{1,0:T(8,128)(2,1)S(1)}, bf16[256,256]{1,0:T(8,128)(2,1)}, u32[]{:S(2)}) copy-start(bf16[256,256]{1,0:T(8,128)(2,1)} %refs_4_.1) | copy-start | bytes 393220
  7.2 88.6 %all-gather.3.cloned.1.call-start = ((), (), s32[]{:S(2)}) async-start(), calls=%async_computation.5 | async-start | bytes 1179648 | tf_op jit(solution)/shard_map/all_gather | solution.py:387
  7.2 0.9 copy-start.14
  8.1 0.7 copy-start.27
  9.0 6.9 %collective-permute-start = (bf16[16,256]{1,0:T(8,128)(2,1)S(1)}, bf16[16,256]{1,0:T(8,128)(2,1)S(1)}, u32[]{:S(2)}, u32[]{:S(2)}) collective-permute-start(bf16[16,256]{1,0:T(8,128)(2,1)S(1)} %get-tuple-element.28), channel_id=1, source_target_pairs={{0,1},{1,2},{2,3},{3,4},{4,5},{5,6},{6,7},{7,8},{8,9},{9,10},{10,1... | collective-permute-start | bytes 24584 | tf_op jit(solution)/shard_map/ppermute | solution.py:379
  14.0 5.0 %collective-permute-start.1 = (bf16[16,256]{1,0:T(8,128)(2,1)S(1)}, bf16[16,256]{1,0:T(8,128)(2,1)S(1)}, u32[]{:S(2)}, u32[]{:S(2)}) collective-permute-start(bf16[16,256]{1,0:T(8,128)(2,1)S(1)} %get-tuple-element.29), channel_id=1, source_target_pairs={{1,0},{2,1},{3,2},{4,3},{5,4},{6,5},{7,6},{8,7},{9,8},{10,9},{11,1... | collective-permute-start | bytes 24584 | tf_op jit(solution)/shard_map/ppermute | solution.py:380
  19.0 0.8 copy-start.15
  19.8 0.7 copy-start.18
  20.5 34.0 %copy-start.21 = (f32[256]{0:T(256)S(1)}, f32[256]{0:T(256)}, u32[]{:S(2)}) copy-start(f32[256]{0:T(256)} %param.17) | copy-start | bytes 3076
  21.2 74.6 %reduce-scatter.2.cloned.1.call-start = ((), (), s32[]{:S(2)}) async-start(), calls=%async_computation.4 | async-start | bytes 589824 | tf_op jit(solution)/shard_map/reduce_scatter | solution.py:411
  21.3 2.0 %copy-start = (bf16[6912,256]{1,0:T(8,128)(2,1)S(1)}, bf16[6912,256]{1,0:T(8,128)(2,1)}, u32[]{:S(2)}) copy-start(bf16[6912,256]{1,0:T(8,128)(2,1)} %refs_2_.1) | copy-start | bytes 10616836
  23.3 0.8 copy-start.16
  24.1 0.8 copy-start.17
  24.9 0.7 copy-start.23
  55.0 1.5 collective-permute-start.2
  58.9 1.4 collective-permute-start.3
  61.9 0.7 copy-start.4
  61.9 0.7 copy-start.25
  61.9 95.6 %copy-start.19 = (s32[128,27]{0,1:T(8,128)S(1)}, s32[128,27]{0,1:T(8,128)}, u32[]{:S(2)}) copy-start(s32[128,27]{0,1:T(8,128)} %param.11) | copy-start | bytes 41476
  62.6 94.9 %copy-start.1 = (bf16[6912,256]{1,0:T(8,128)(2,1)S(1)}, bf16[6912,256]{1,0:T(8,128)(2,1)}, u32[]{:S(2)}) copy-start(bf16[6912,256]{1,0:T(8,128)(2,1)} %refs_2_.1) | copy-start | bytes 10616836
  81.0 0.7 copy-start.24
  81.7 0.7 copy-start.26
  83.4 5.8 %collective-permute-start.6 = (bf16[144,256]{1,0:T(8,128)(2,1)}, bf16[144,256]{1,0:T(8,128)(2,1)}, u32[]{:S(2)}, u32[]{:S(2)}) collective-permute-start(bf16[144,256]{1,0:T(8,128)(2,1)} %get-tuple-element.40.refs_0_.refs_3_), channel_id=1, source_target_pairs={{0,16},{1,17},{2,18},{3,19},{4,20},{5,21},{6,22},{7,23},{8,24},{9,... | collective-permute-start | bytes 221192 | tf_op jit(solution)/shard_map/ppermute | solution.py:35
  84.4 6.6 %collective-permute-start.7 = (bf16[144,256]{1,0:T(8,128)(2,1)}, bf16[144,256]{1,0:T(8,128)(2,1)}, u32[]{:S(2)}, u32[]{:S(2)}) collective-permute-start(bf16[144,256]{1,0:T(8,128)(2,1)} %get-tuple-element.40.refs_0_.refs_3_), channel_id=1, source_target_pairs={{0,32},{1,33},{2,34},{3,35},{4,36},{5,37},{6,38},{7,39},{8,40},{9,... | collective-permute-start | bytes 221192 | tf_op jit(solution)/shard_map/ppermute | solution.py:35
  87.0 5.5 %collective-permute-start.8 = (bf16[144,256]{1,0:T(8,128)(2,1)}, bf16[144,256]{1,0:T(8,128)(2,1)}, u32[]{:S(2)}, u32[]{:S(2)}) collective-permute-start(bf16[144,256]{1,0:T(8,128)(2,1)} %get-tuple-element.40.refs_0_.refs_3_), channel_id=1, source_target_pairs={{0,48},{1,49},{2,50},{3,51},{4,52},{5,53},{6,54},{7,55},{8,56},{9,... | collective-permute-start | bytes 221192 | tf_op jit(solution)/shard_map/ppermute | solution.py:35
  88.0 5.2 %collective-permute-start.9 = (bf16[144,256]{1,0:T(8,128)(2,1)}, bf16[144,256]{1,0:T(8,128)(2,1)S(1)}, u32[]{:S(2)}, u32[]{:S(2)}) collective-permute-start(bf16[144,256]{1,0:T(8,128)(2,1)} %get-tuple-element.40.refs_0_.refs_3_), channel_id=1, source_target_pairs={{0,1},{1,0},{2,3},{3,2},{4,5},{5,4},{6,7},{7,6},{8,9},{9,8},{10,11... | collective-permute-start | bytes 221192 | tf_op jit(solution)/shard_map/ppermute | solution.py:40
  89.3 4.6 %collective-permute-start.10 = (bf16[144,256]{1,0:T(8,128)(2,1)}, bf16[144,256]{1,0:T(8,128)(2,1)S(1)}, u32[]{:S(2)}, u32[]{:S(2)}) collective-permute-start(bf16[144,256]{1,0:T(8,128)(2,1)} %collective-permute-done.6.refs_4_), channel_id=1, source_target_pairs={{0,1},{1,0},{2,3},{3,2},{4,5},{5,4},{6,7},{7,6},{8,9},{9,8},{10,11... | collective-permute-start | bytes 221192 | tf_op jit(solution)/shard_map/ppermute | solution.py:40
  90.9 3.6 %collective-permute-start.11 = (bf16[144,256]{1,0:T(8,128)(2,1)}, bf16[144,256]{1,0:T(8,128)(2,1)S(1)}, u32[]{:S(2)}, u32[]{:S(2)}) collective-permute-start(bf16[144,256]{1,0:T(8,128)(2,1)} %collective-permute-done.7.refs_5_), channel_id=1, source_target_pairs={{0,1},{1,0},{2,3},{3,2},{4,5},{5,4},{6,7},{7,6},{8,9},{9,8},{10,11... | collective-permute-start | bytes 221192 | tf_op jit(solution)/shard_map/ppermute | solution.py:40
  92.5 2.6 %collective-permute-start.12 = (bf16[144,256]{1,0:T(8,128)(2,1)}, bf16[144,256]{1,0:T(8,128)(2,1)S(1)}, u32[]{:S(2)}, u32[]{:S(2)}) collective-permute-start(bf16[144,256]{1,0:T(8,128)(2,1)} %collective-permute-done.8.refs_6_), channel_id=1, source_target_pairs={{0,1},{1,0},{2,3},{3,2},{4,5},{5,4},{6,7},{7,6},{8,9},{9,8},{10,11... | collective-permute-start | bytes 221192 | tf_op jit(solution)/shard_map/ppermute | solution.py:40
  93.2 0.6 copy-start.6
  93.9 0.6 copy-start.8
  94.5 0.6 copy-start.10
  95.1 0.6 copy-start.12
  95.8 1.2 copy-start.3
  97.0 0.9 copy-start.7
  97.9 0.9 copy-start.9
  98.8 0.9 copy-start.11
  99.6 0.9 copy-start.13
  100.5 0.8 copy-start.20
  101.4 0.7 copy-start.22
  106.3 62.8 %copy-start.28 = (s32[1,32]{1,0:T(1,128)S(1)}, s32[1,32]{1,0:T(1,128)}, u32[]{:S(2)}) copy-start(s32[1,32]{1,0:T(1,128)} %refs_3_.3) | copy-start | bytes 388
  134.5 5.5 %collective-permute-start.13 = (bf16[240,256]{1,0:T(8,128)(2,1)S(1)}, bf16[240,256]{1,0:T(8,128)(2,1)S(1)}, u32[]{:S(2)}, u32[]{:S(2)}) collective-permute-start(bf16[240,256]{1,0:T(8,128)(2,1)S(1)} %shard_map.146.refs_0_), channel_id=1, source_target_pairs={{0,64},{64,128},{128,192},{192,0},{1,65},{65,129},{129,193},{193,1... | collective-permute-start | bytes 368648 | tf_op jit(solution)/shard_map/ppermute | solution.py:447
  135.9 6.6 %collective-permute-start.14 = (bf16[240,256]{1,0:T(8,128)(2,1)S(1)}, bf16[240,256]{1,0:T(8,128)(2,1)S(1)}, u32[]{:S(2)}, u32[]{:S(2)}) collective-permute-start(bf16[240,256]{1,0:T(8,128)(2,1)S(1)} %shard_map.146.refs_0_), channel_id=1, source_target_pairs={{0,128},{64,192},{128,0},{192,64},{1,129},{65,193},{129,1},{193,65... | collective-permute-start | bytes 368648 | tf_op jit(solution)/shard_map/ppermute | solution.py:447
  138.9 4.0 %collective-permute-start.15 = (bf16[240,256]{1,0:T(8,128)(2,1)S(1)}, bf16[240,256]{1,0:T(8,128)(2,1)S(1)}, u32[]{:S(2)}, u32[]{:S(2)}) collective-permute-start(bf16[240,256]{1,0:T(8,128)(2,1)S(1)} %shard_map.146.refs_0_), channel_id=1, source_target_pairs={{0,192},{64,0},{128,64},{192,128},{1,193},{65,1},{129,65},{193,129... | collective-permute-start | bytes 368648 | tf_op jit(solution)/shard_map/ppermute | solution.py:447
  143.6 9.8 %collective-permute-start.16 = (bf16[128,256]{1,0:T(8,128)(2,1)S(1)}, bf16[128,256]{1,0:T(8,128)(2,1)S(1)}, u32[]{:S(2)}, u32[]{:S(2)}) collective-permute-start(bf16[128,256]{1,0:T(8,128)(2,1)S(1)} %get-tuple-element.46.refs_1_), channel_id=1, source_target_pairs={{0,16},{1,17},{2,18},{3,19},{4,20},{5,21},{6,22},{7,23},{8,24},{9,... | collective-permute-start | bytes 196616 | tf_op jit(solution)/shard_map/ppermute | solution.py:35
  148.5 6.2 %collective-permute-start.17 = (bf16[128,256]{1,0:T(8,128)(2,1)S(1)}, bf16[128,256]{1,0:T(8,128)(2,1)S(1)}, u32[]{:S(2)}, u32[]{:S(2)}) collective-permute-start(bf16[128,256]{1,0:T(8,128)(2,1)S(1)} %get-tuple-element.46.refs_1_), channel_id=1, source_target_pairs={{0,32},{1,33},{2,34},{3,35},{4,36},{5,37},{6,38},{7,39},{8,40},{9,... | collective-permute-start | bytes 196616 | tf_op jit(solution)/shard_map/ppermute | solution.py:35
  151.3 4.8 %collective-permute-start.18 = (bf16[128,256]{1,0:T(8,128)(2,1)S(1)}, bf16[128,256]{1,0:T(8,128)(2,1)S(1)}, u32[]{:S(2)}, u32[]{:S(2)}) collective-permute-start(bf16[128,256]{1,0:T(8,128)(2,1)S(1)} %get-tuple-element.46.refs_1_), channel_id=1, source_target_pairs={{0,48},{1,49},{2,50},{3,51},{4,52},{5,53},{6,54},{7,55},{8,56},{9,... | collective-permute-start | bytes 196616 | tf_op jit(solution)/shard_map/ppermute | solution.py:35
  151.3 18.6 %collective-permute-start.19 = (bf16[128,256]{1,0:T(8,128)(2,1)S(1)}, bf16[128,256]{1,0:T(8,128)(2,1)S(1)}, u32[]{:S(2)}, u32[]{:S(2)}) collective-permute-start(bf16[128,256]{1,0:T(8,128)(2,1)S(1)} %get-tuple-element.46.refs_1_), channel_id=1, source_target_pairs={{0,1},{1,0},{2,3},{3,2},{4,5},{5,4},{6,7},{7,6},{8,9},{9,8},{10,11... | collective-permute-start | bytes 196616 | tf_op jit(solution)/shard_map/ppermute | solution.py:40
  153.4 16.6 %collective-permute-start.20 = (bf16[128,256]{1,0:T(8,128)(2,1)S(1)}, bf16[128,256]{1,0:T(8,128)(2,1)S(1)}, u32[]{:S(2)}, u32[]{:S(2)}) collective-permute-start(bf16[128,256]{1,0:T(8,128)(2,1)S(1)} %collective-permute-done.16.refs_2_), channel_id=1, source_target_pairs={{0,1},{1,0},{2,3},{3,2},{4,5},{5,4},{6,7},{7,6},{8,9},{9,8},{10,11... | collective-permute-start | bytes 196616 | tf_op jit(solution)/shard_map/ppermute | solution.py:40
  154.7 15.3 %collective-permute-start.21 = (bf16[128,256]{1,0:T(8,128)(2,1)S(1)}, bf16[128,256]{1,0:T(8,128)(2,1)S(1)}, u32[]{:S(2)}, u32[]{:S(2)}) collective-permute-start(bf16[128,256]{1,0:T(8,128)(2,1)S(1)} %collective-permute-done.17.refs_3_), channel_id=1, source_target_pairs={{0,1},{1,0},{2,3},{3,2},{4,5},{5,4},{6,7},{7,6},{8,9},{9,8},{10,11... | collective-permute-start | bytes 196616 | tf_op jit(solution)/shard_map/ppermute | solution.py:40
  156.1 13.8 %collective-permute-start.22 = (bf16[128,256]{1,0:T(8,128)(2,1)S(1)}, bf16[128,256]{1,0:T(8,128)(2,1)S(1)}, u32[]{:S(2)}, u32[]{:S(2)}) collective-permute-start(bf16[128,256]{1,0:T(8,128)(2,1)S(1)} %collective-permute-done.18.refs_4_), channel_id=1, source_target_pairs={{0,1},{1,0},{2,3},{3,2},{4,5},{5,4},{6,7},{7,6},{8,9},{9,8},{10,11... | collective-permute-start | bytes 196616 | tf_op jit(solution)/shard_map/ppermute | solution.py:40
  161.0 3.1 %collective-permute-start.4 = (bf16[16,256]{1,0:T(8,128)(2,1)S(1)}, bf16[16,256]{1,0:T(8,128)(2,1)S(1)}, u32[]{:S(2)}, u32[]{:S(2)}) collective-permute-start(bf16[16,256]{1,0:T(8,128)(2,1)S(1)} %get-tuple-element.42), channel_id=1, source_target_pairs={{0,1},{1,2},{2,3},{3,4},{4,5},{5,6},{6,7},{7,8},{8,9},{9,10},{10,1... | collective-permute-start | bytes 24584 | tf_op jit(solution)/shard_map/ppermute | solution.py:428
  164.0 5.1 %collective-permute-start.5 = (bf16[16,256]{1,0:T(8,128)(2,1)S(1)}, bf16[16,256]{1,0:T(8,128)(2,1)S(1)}, u32[]{:S(2)}, u32[]{:S(2)}) collective-permute-start(bf16[16,256]{1,0:T(8,128)(2,1)S(1)} %get-tuple-element.43), channel_id=1, source_target_pairs={{1,0},{2,1},{3,2},{4,3},{5,4},{6,5},{7,6},{8,7},{9,8},{10,9},{11,1... | collective-permute-start | bytes 24584 | tf_op jit(solution)/shard_map/ppermute | solution.py:427
Sparse Core Ops, SparseCore 0:
  21.3 29.5 all-gather.2
  62.1 28.8 reduce-scatter.1

commit v3 on v2

v3 whole, which is shorter than its diff:
```python
import math

import jax
import jax.numpy as jnp
from jax import lax
from jax.experimental import pallas as pl
from jax.experimental.pallas import tpu as pltpu
from jax.sharding import PartitionSpec as P

HEADS = 16
NORM_EPS = 1e-05
BF = jnp.bfloat16
F32 = jnp.float32
I32 = jnp.int32

PTS = 128
FEAT = 256
OFFS = 27
RIM = 16
EXT = PTS + 2 * RIM
SLOTS = 512
PAY = 256
MIB = 1024 * 1024

NX, NZ, NC = 4, 8, 2
Z_GROUPS = [[x * 16 + z * 2 + c for z in range(NZ)] for x in range(NX) for c in range(NC)]
XC_GROUPS = [[x * 16 + z * 2 + c for x in range(NX) for c in range(NC)] for z in range(NZ)]
XZ_GROUPS = [[x * 16 + z * 2 + c for x in range(NX) for z in range(NZ)] for c in range(NC)]
SWAP = [(i, i ^ 1) for i in range(NX * NZ * NC)]
UP = [(i, i + 1) for i in range(NX * NZ * NC - 1)]
DOWN = [(i + 1, i) for i in range(NX * NZ * NC - 1)]


def along_x(value, d):
    n = NX * NZ * NC
    return lax.ppermute(value, "gz", [(i, (i + 16 * d) % n) for i in range(n)])


def over_chips(value):
    near = [value] + [along_x(value, d) for d in range(1, NX)]
    return near + [lax.ppermute(v, "gz", SWAP) for v in near]


def over_groups(value):
    n = lax.axis_size("grp")
    return [value] + [lax.ppermute(value, "grp", [(i, (i + d) % n) for i in range(n)]) for d in range(1, n)]


def mm(a, b):
    return jnp.dot(a, b, preferred_element_type=F32)


def mm_t(a, b):
    return lax.dot_general(a, b, (((1,), (1,)), ((), ())), preferred_element_type=F32)


def t_mm(a, b):
    return lax.dot_general(a, b, (((0,), (0,)), ((), ())), preferred_element_type=F32)


def one_hot(cond):
    return jnp.where(cond, 1.0, 0.0).astype(BF)


def iota(shape, dim):
    return lax.broadcasted_iota(I32, shape, dim)


def call(body, out_shape, *args, scratch=(), flops=1 << 26, nbytes=1 << 20, smem=0, fetched=(), late=(), idle=(), limit=16):
    fetched = tuple(fetched) + tuple(late)
    specs = []
    for i in range(len(args)):
        space = pltpu.SMEM if i < smem else pltpu.HBM if i in fetched else pl.ANY if i in idle else pltpu.VMEM
        specs.append(pl.BlockSpec(memory_space=space))
    single = not isinstance(out_shape, (list, tuple))
    outs = [out_shape] if single else list(out_shape)
    held = [pltpu.VMEM(args[i].shape, args[i].dtype) for i in fetched]
    held += [pltpu.SemaphoreType.DMA] * len(fetched)

    def outer(*refs):
        base = len(args) + len(outs) + len(scratch)
        views = list(refs[: len(args)])
        copies = {}
        for n, i in enumerate(fetched):
            copies[i] = pltpu.make_async_copy(refs[i], refs[base + n], refs[base + len(fetched) + n])
            copies[i].start()
            views[i] = refs[base + n]
        for i in fetched:
            if i in late:
                views[i] = (views[i], copies[i].wait)
            else:
                copies[i].wait()
        body(*[v for i, v in enumerate(views) if i not in idle], *refs[len(args) : base])

    got = pl.pallas_call(
        outer,
        out_shape=outs,
        in_specs=specs,
        out_specs=[pl.BlockSpec(memory_space=pltpu.VMEM)] * len(outs),
        scratch_shapes=list(scratch) + held,
        compiler_params=pltpu.CompilerParams(vmem_limit_bytes=limit * MIB),
        cost_estimate=pl.CostEstimate(flops=flops, bytes_accessed=nbytes, transcendentals=0),
    )(*args)
    return got[0] if single else got


def sds(shape, dtype=BF):
    return jax.ShapeDtypeStruct(shape, dtype)


def position():
    me = lax.axis_index("gz")
    return lax.shift_right_logical(me, 4), me & 1


def pick_body(pick_ref, feat_ref, down_ref, up_ref):
    rows = jnp.broadcast_to(pick_ref[...], (PTS, 2 * RIM))
    hit = one_hot(rows == iota((PTS, 2 * RIM), 0))
    got = t_mm(hit, feat_ref[...]).astype(BF)
    down_ref[...] = got[:RIM]
    up_ref[...] = got[RIM:]


def slot_hits(rank_row):
    owner = lax.shift_right_logical(rank_row, 7)
    wide = jnp.broadcast_to(owner, (PTS, PTS))
    tall = jnp.transpose(wide)
    earlier = (wide == tall) & (iota((PTS, PTS), 0) < iota((PTS, PTS), 1))
    slot = jnp.sum(jnp.where(earlier, 1, 0), axis=0, keepdims=True)
    target = owner * 8 + slot
    rows = iota((SLOTS, PTS), 0)
    return one_hot(rows == target), one_hot(rows == target + 4)


def conv_body(feat_ref, prev_ref, next_ref, nbr_ref, rank_ref, cot_ref, weight, send_ref, ext, tab, wide):
    weight_ref, weight_here = weight
    ext[:PTS] = feat_ref[...]
    ext[PTS : PTS + RIM] = prev_ref[...]
    ext[PTS + RIM : EXT] = next_ref[...]
    ext[EXT:] = jnp.zeros((FEAT - EXT, FEAT), BF)
    rows = ext[...]
    tab[:OFFS] = nbr_ref[...].astype(F32)
    tab[OFFS:] = jnp.zeros((PTS - OFFS, PTS), F32)
    table = jnp.transpose(tab[...])
    lanes = iota((PTS, FEAT), 1).astype(F32)
    for k in range(OFFS):
        hit = one_hot(table[:, k : k + 1] == lanes)
        wide[:, k * FEAT : (k + 1) * FEAT] = mm(hit, rows).astype(BF)
    weight_here()
    mixed = (feat_ref[...].astype(F32) + mm(wide[...], weight_ref[...])).astype(BF)
    rank_row = rank_ref[...]
    first, second = slot_hits(rank_row)
    place = jnp.transpose(jnp.broadcast_to(rank_row & (PTS - 1), (PTS, PTS))).astype(F32)
    send_ref[:, :FEAT] = (mm(first, mixed) + mm(second, cot_ref[...])).astype(BF)
    marks = mm(first, (place + 1.0).astype(BF)) + mm(second, (place + (PTS + 1.0)).astype(BF))
    send_ref[:, FEAT:] = marks.astype(BF)


def patch_hits(marks):
    upper = lax.shift_right_logical(iota((SLOTS, PTS), 0), 3) & 1
    marks = marks.astype(F32) + jnp.where(upper == 1, 512.0, 0.0)
    lanes = iota((SLOTS, PTS), 1).astype(F32)
    return jnp.concatenate([one_hot(marks == lanes + (b + 1.0)) for b in (0, 512, 128, 640)], 1)


def layer_norm(hidden):
    centred = hidden - jnp.mean(hidden, -1, keepdims=True)
    inverse = lax.rsqrt(jnp.mean(centred * centred, -1, keepdims=True) + NORM_EPS)
    return centred * inverse, inverse


def patch_body(
    a_ref, b_ref, qkv_ref, proj_ref, gain_ref,
    back_ref, d0_ref, d1_ref, d2_ref, d3_ref, gg_ref,
    hits, qm, am, pr, ds, sc, gs, dense,
):
    x, core = position()
    whole = 2 * PTS
    head_dim = FEAT // HEADS
    scale = head_dim ** (-0.5)
    hits[...] = patch_hits(a_ref[:, FEAT:])
    rows = t_mm(hits[...], a_ref[:, :FEAT]) + t_mm(patch_hits(b_ref[:, FEAT:]), b_ref[:, :FEAT])
    hidden = rows[:whole]
    cot = rows[whole:].astype(BF)
    gain = gain_ref[...]
    normed, inverse = layer_norm(hidden)
    scaled = (normed * gain).astype(BF)
    projected = mm(scaled, qkv_ref[...]).astype(BF)
    query, keys, values = (projected[:, i * FEAT : (i + 1) * FEAT] for i in range(3))
    grad_att = mm_t(cot, proj_ref[...]).astype(BF)
    head_of = iota((PTS, FEAT), 1) // head_dim
    zero = jnp.zeros((PTS, FEAT), BF)
    halves = [slice(0, PTS), slice(PTS, whole)]
    spans = [[slice((s * HEADS + h) * PTS, (s * HEADS + h + 1) * PTS) for h in range(HEADS)] for s in range(2)]
    for s in range(2):
        for h in range(HEADS):
            qm[spans[s][h]] = jnp.where(head_of == h, query[halves[s]], zero)
            am[spans[s][h]] = jnp.where(head_of == h, grad_att[halves[s]], zero)
    sc[...] = mm_t(qm[...], keys)
    gs[...] = mm_t(am[...], values)
    for span in spans[0] + spans[1]:
        e = jnp.exp(sc[span] * scale)
        probs = (e * (1.0 / jnp.sum(e, -1, keepdims=True))).astype(BF)
        pr[span] = probs
        wide = probs.astype(F32)
        grad_probs = gs[span]
        delta = jnp.sum(wide * grad_probs, -1, keepdims=True)
        ds[span] = (wide * (grad_probs - delta) * scale).astype(BF)
    sc[...] = mm(pr[...], values)
    gs[...] = mm(ds[...], keys)
    att_parts, gq_parts, parts = [], [], []
    for s in range(2):
        att, gq = sc[spans[s][0]], gs[spans[s][0]]
        for h in range(1, HEADS):
            att = jnp.where(head_of == h, sc[spans[s][h]], att)
            gq = jnp.where(head_of == h, gs[spans[s][h]], gq)
        att_parts.append(att.astype(BF))
        gq_parts.append(gq.astype(BF))
        half = slice(s * HEADS * PTS, (s + 1) * HEADS * PTS)
        parts.append((t_mm(ds[half], qm[half]).astype(BF), t_mm(pr[half], am[half]).astype(BF)))
    attended = jnp.concatenate(att_parts, 0)
    gq = jnp.concatenate(gq_parts, 0)
    out = (hidden + mm(attended, proj_ref[...])).astype(BF)
    w_query, w_key, w_value = (qkv_ref[:, i * FEAT : (i + 1) * FEAT] for i in range(3))
    grad_scaled = mm_t(gq, w_query)
    for grad_key, grad_value in parts:
        grad_scaled += mm_t(grad_key, w_key) + mm_t(grad_value, w_value)

    @pl.when(core == 0)
    def _():
        dense[:FEAT] = t_mm(scaled, gq).astype(BF)
        dense[FEAT:] = (t_mm(scaled, parts[0][0]) + t_mm(scaled, parts[1][0])).astype(BF)

    @pl.when(core == 1)
    def _():
        dense[:FEAT] = (t_mm(scaled, parts[0][1]) + t_mm(scaled, parts[1][1])).astype(BF)
        dense[FEAT:] = t_mm(attended, cot).astype(BF)

    for d, ref in enumerate((d0_ref, d1_ref, d2_ref, d3_ref)):
        ref[...] = dense[pl.ds(pl.multiple_of(((x + d) & (NX - 1)) * PTS, PTS), PTS), :]
    gain_terms = grad_scaled * normed
    gg_ref[...] = jnp.sum(jnp.where(core == 0, gain_terms[:PTS], gain_terms[PTS:]), 0, keepdims=True)
    grad_normed = grad_scaled * gain
    grad_hidden = (
        grad_normed
        - jnp.mean(grad_normed, -1, keepdims=True)
        - normed * jnp.mean(grad_normed * normed, -1, keepdims=True)
    ) * inverse
    grad_local = (cot.astype(F32) + grad_hidden).astype(BF)
    back_ref[...] = mm(hits[...], jnp.concatenate([out, grad_local], 0)).astype(BF)


def table_body(feat_ref, prev_ref, next_ref, nbr_ref, pay_ref):
    pay_ref[:PTS] = feat_ref[...]
    pay_ref[PTS : PTS + RIM] = prev_ref[...]
    pay_ref[PTS + RIM : EXT] = next_ref[...]
    table = nbr_ref[...].astype(F32)
    pay_ref[EXT : EXT + 16, :PTS] = table[:16].astype(BF)
    pay_ref[EXT : EXT + 16, PTS:] = jnp.concatenate([table[16:], jnp.zeros((5, PTS), F32)], 0).astype(BF)
    pay_ref[EXT + 16 :] = jnp.zeros((PAY - EXT - 16, FEAT), BF)


def unpack_body(back_ref, rank_ref, gg_ref, d0_ref, d1_ref, d2_ref, d3_ref, block_ref, grad_ref, dense_ref):
    first, second = slot_hits(rank_ref[...])
    rows = back_ref[...]
    grad_ref[:PTS] = t_mm(second, rows).astype(BF)
    grad_ref[PTS:] = jnp.broadcast_to(gg_ref[...], (16, FEAT)).astype(BF)
    dense = d0_ref[...].astype(F32) + d1_ref[...].astype(F32) + d2_ref[...].astype(F32) + d3_ref[...].astype(F32)
    dense_ref[...] = dense.astype(BF)
    block_ref[...] = t_mm(first, rows).astype(BF)


def spread_body(grad_ref, nbr_ref, weight_ref, own_ref, down_ref, up_ref, acc):
    grad = grad_ref[:PTS]
    table = nbr_ref[...].astype(F32)
    points = iota((EXT, PTS), 0).astype(F32)
    acc[...] = jnp.zeros((EXT, FEAT), F32)
    for k in range(OFFS):
        hit = one_hot(points == table[k : k + 1])
        term = mm(hit, grad).astype(BF)
        acc[...] += mm_t(term, weight_ref[k * FEAT : (k + 1) * FEAT])
    own_ref[...] = acc[:PTS] + grad.astype(F32)
    down_ref[...] = acc[PTS : PTS + RIM].astype(BF)
    up_ref[...] = acc[PTS + RIM :].astype(BF)


def rim_body(own_ref, down_ref, up_ref, pick_ref, out_ref):
    rows = jnp.broadcast_to(pick_ref[...], (PTS, 2 * RIM))
    hit = one_hot(rows == iota((PTS, 2 * RIM), 0))
    rims = jnp.concatenate([down_ref[...], up_ref[...]], 0)
    out_ref[...] = (own_ref[...] + mm(hit, rims)).astype(BF)


def kernel_grad_body(all_ref, p0_ref, p1_ref, p2_ref, p3_ref, *refs):
    grads, (out_ref, tab, exts, terms, total) = refs[: NX * NC], refs[NX * NC :]
    x, core = position()
    base = x * 1728 + core * 108
    first_offset = jnp.minimum(lax.shift_right_logical(base, 8), OFFS - 8)
    first_row = base - first_offset * FEAT - core * 4
    dense = p0_ref[...].astype(F32) + p1_ref[...].astype(F32) + p2_ref[...].astype(F32) + p3_ref[...].astype(F32)
    dense = dense.astype(BF)
    gain = jnp.zeros((1, FEAT), F32)
    for s in range(NX * NC):
        source = ((x + NX - s % NX) & (NX - 1)) * NC + (core if s < NX else 1 - core)
        rows = all_ref[source, EXT : EXT + 16].astype(F32)
        tab[s * 32 : s * 32 + 16] = rows[:, :PTS]
        tab[s * 32 + 16 : s * 32 + 32] = rows[:, PTS:]
        exts[s * EXT : (s + 1) * EXT] = all_ref[source, :EXT]
        gain += grads[s][PTS : PTS + 1].astype(F32)
    ext_t = jnp.transpose(exts[...])
    points = iota((EXT, PTS), 0).astype(F32)
    for k in range(8):
        for s in range(NX * NC):
            hit = one_hot(points == tab[pl.ds(first_offset + (s * 32 + k), 1), :])
            terms[s * EXT : (s + 1) * EXT] = mm(hit, grads[s][:PTS]).astype(BF)
        total[k * FEAT : (k + 1) * FEAT] = mm(ext_t, terms[...])
    total[8 * FEAT :] = jnp.zeros((16, FEAT), F32)
    at = iota((112, FEAT), 0)
    for z in range(NZ):
        wide = total[pl.ds(pl.multiple_of(first_row + z * 216, 8), 120), :]
        rows = jnp.where(core == 1, wide[4:116], wide[:112])
        rows = jnp.where(at < 108, rows, jnp.where(at == 108, gain, 0.0))
        out_ref[z, :112] = rows.astype(BF)
        out_ref[z, 112:] = dense


def sum_body(got_ref, conv_ref, dense_ref):
    total = got_ref[0].astype(F32)
    for i in range(1, NZ):
        total += got_ref[i].astype(F32)
    conv_ref[...] = total[:112].astype(BF)
    dense_ref[...] = total[112:].astype(BF)


def last_body(factor, *refs):
    groups, parts = refs[:4], refs[4 : 4 + NX * NC]
    conv_ref, gain_ref, qkv_ref, proj_ref, rows = refs[4 + NX * NC :]
    total = groups[0][...].astype(F32)
    for group in groups[1:]:
        total += group[...].astype(F32)
    conv_ref[...] = total[:108] * factor
    gain_ref[...] = total[108:109] * factor
    x, core = position()
    for s in range(NX * NC):
        source = ((x + NX - s % NX) & (NX - 1)) + NX * (core if s < NX else 1 - core)
        rows[source] = parts[s][...].astype(F32) * factor
    for b in range(NX * NC):
        part, at = b // 2, b % 2 * PTS
        if part < 3:
            qkv_ref[at : at + PTS, part * FEAT : (part + 1) * FEAT] = rows[b]
        else:
            proj_ref[at : at + PTS] = rows[b]


def shards(
    features,
    hilbert_rank,
    neighbours,
    halo_rows,
    cotangent,
    conv_weight,
    qkv_weight,
    proj_weight,
    norm_gain,
):
    factor = 1.0 / math.sqrt(PTS * NX * NZ * NC * lax.axis_size("grp"))
    rank_row = hilbert_rank.reshape(1, PTS)
    gain_row = norm_gain.reshape(1, FEAT)
    table = neighbours.T
    to_prev, to_next = call(
        pick_body, [sds((RIM, FEAT))] * 2, halo_rows, features, fetched=(0, 1), limit=8
    )
    from_prev = lax.ppermute(to_next, "gz", UP)
    from_next = lax.ppermute(to_prev, "gz", DOWN)
    payload = call(
        table_body, sds((PAY, FEAT)), features, from_prev, from_next, table, fetched=(0, 3), limit=8
    )
    everyone = lax.all_gather(payload, "gz", axis_index_groups=XC_GROUPS)
    send = call(
        conv_body,
        sds((SLOTS, FEAT + PTS)),
        features, from_prev, from_next, table, rank_row, cotangent, conv_weight, payload,
        scratch=[pltpu.VMEM((FEAT, FEAT), BF), pltpu.VMEM((PTS, PTS), F32), pltpu.VMEM((PTS, OFFS * FEAT), BF)],
        fetched=(0, 3, 4, 5), late=(6,), idle=(7,), limit=16,
    )
    got = lax.all_to_all(
        send.reshape(32, 16, FEAT + PTS), "gz", split_axis=0, concat_axis=0,
        axis_index_groups=XZ_GROUPS, tiled=True,
    ).reshape(SLOTS, FEAT + PTS)
    other = lax.ppermute(got, "gz", SWAP)
    rows = 2 * HEADS * PTS
    back, d0, d1, d2, d3, grad_gain = call(
        patch_body,
        [sds((SLOTS, FEAT))] + [sds((PTS, FEAT))] * 4 + [sds((1, FEAT), F32)],
        got, other, qkv_weight, proj_weight, gain_row,
        scratch=[pltpu.VMEM((SLOTS, SLOTS), BF)]
        + [pltpu.VMEM((rows, FEAT), BF)] * 4
        + [pltpu.VMEM((rows, FEAT), F32)] * 2
        + [pltpu.VMEM((2 * FEAT, FEAT), BF)],
        limit=32,
    )
    dense_parts = [d0] + [along_x(v, d) for d, v in ((1, d1), (2, d2), (3, d3))]
    returned = lax.all_to_all(
        back.reshape(32, 16, FEAT), "gz", split_axis=0, concat_axis=0,
        axis_index_groups=XZ_GROUPS, tiled=True,
    ).reshape(SLOTS, FEAT)
    block_out, grad, dense = call(
        unpack_body,
        [sds((PTS, FEAT)), sds((PTS + 16, FEAT)), sds((PTS, FEAT))],
        returned, rank_row, grad_gain, *dense_parts,
        fetched=(1,), limit=8,
    )
    grads = over_chips(grad)
    dense_groups = over_groups(dense)
    own_part, rim_down, rim_up = call(
        spread_body,
        [sds((PTS, FEAT), F32), sds((RIM, FEAT)), sds((RIM, FEAT))],
        grad, table, conv_weight,
        scratch=[pltpu.VMEM((EXT, FEAT), F32)],
        limit=8,
    )
    got_down = lax.ppermute(rim_down, "gz", DOWN)
    got_up = lax.ppermute(rim_up, "gz", UP)
    parts = call(
        kernel_grad_body,
        sds((NZ, 240, FEAT)),
        everyone, *dense_groups, *grads, own_part,
        scratch=[
            pltpu.VMEM((NX * NC * 32, PTS), F32),
            pltpu.VMEM((NX * NC * EXT, FEAT), BF),
            pltpu.VMEM((NX * NC * EXT, FEAT), BF),
            pltpu.VMEM((8 * FEAT + 16, FEAT), F32),
        ],
        idle=(13,),
    )
    grad_features = call(rim_body, sds((PTS, FEAT)), own_part, got_up, got_down, halo_rows, limit=8)
    z_parts = lax.all_to_all(
        parts, "gz", split_axis=0, concat_axis=0, axis_index_groups=Z_GROUPS, tiled=True
    )
    conv_part, dense_sum = call(
        sum_body, [sds((112, FEAT)), sds((PTS, FEAT))], z_parts, grad_features, idle=(1,), limit=8
    )
    grad_conv, gain_sum, grad_qkv, grad_proj = call(
        lambda *refs: last_body(factor, *refs),
        [sds((108, FEAT), F32), sds((1, FEAT), F32), sds((FEAT, 3 * FEAT), F32), sds((FEAT, FEAT), F32)],
        *over_groups(conv_part), *over_chips(dense_sum),
        scratch=[pltpu.VMEM((NX * NC, PTS, FEAT), F32)],
        limit=8,
    )
    return (block_out, grad_features, grad_conv, grad_qkv, grad_proj, gain_sum.reshape(FEAT))


def solution(mesh):
    return jax.shard_map(
        shards,
        mesh=mesh,
        in_specs=(
            P(("grp", "gz"), None),
            P(("grp", "gz")),
            P(("grp", "gz"), None),
            P(("grp", "gz"), None),
            P(("grp", "gz"), None),
            P(),
            P(),
            P(),
            P(),
        ),
        out_specs=(P(("grp", "gz"), None), P(("grp", "gz"), None), P("gz", None), P(), P(), P()),
        check_vma=False,
    )
```

time: 179 us -> 191 us (1.067); the launches traced: 178 us -> 187 us
  blocking collectives: 72.3 us -> 23.4 us
  local copies, waits for them, and re-layouts: 18.2 us -> 41.3 us
  starting transfers between devices: 39.6 us -> 59.7 us
  waiting for transfers between devices: 12.9 us -> 27.1 us
    all_to_all x3 -> x1, blocking collectives: 72.3 us -> 23.4 us  [shards(): lax.all_to_all(send.reshape(32, 16, FEAT + PTS), 'gz', split_axis=0, conc...]
    unnamed x58 -> x134, local copies, waits for them, and re-layouts: 18.2 us -> 41.3 us
    all_to_all x0 -> x2, starting transfers between devices: none -> 9.81 us  [the longest x1 5.32 us: shards(): lax.all_to_all(back.reshape(32, 16, FEAT), 'gz', split_axis=0, concat_axi...]
    ppermute x5 -> x7, starting transfers between devices: 6.43 us -> 13.4 us  [the longest x6 11 us: over_groups(): lax.ppermute(value, 'grp', [(i, (i + d) % n) for i in range(n)])]
    ppermute x1, waiting for transfers between devices: 1.14 us -> 7.7 us  [shards(): got_up = lax.ppermute(rim_up, 'gz', UP)]
    ppermute x1, starting transfers between devices: 1.92 us -> 6.71 us  [shards(): got_up = lax.ppermute(rim_up, 'gz', UP)]
    ppermute x1, waiting for transfers between devices: 3.07 us -> 6.62 us  [shards(): got_down = lax.ppermute(rim_down, 'gz', DOWN)]
    ppermute x6 -> x9, waiting for transfers between devices: 0.73 us -> 3.48 us  [along_x(): return lax.ppermute(value, 'gz', [(i, (i + 16 * d) % n) for i in range(n)])]
  transfers between devices with their start and end apart: 25 -> 31, of which waited for: 8 -> 9; matrix products, arithmetic and copies ran while one was open for 0% -> 0% of each run, Pallas kernels for 7% -> 8%
where the time goes in v3:
time: 191 us; the launch traced here: 187 us
  starting transfers between devices  59.7 us (31%)
  local copies, waits for them, and re-layouts  41.3 us (22%)
  waiting for transfers between devices  27.1 us (14%)
  blocking collectives  23.4 us (12%)
  Pallas kernels  21 us (11%)
  between operations  14.3 us (7%)
    unnamed x134, local copies, waits for them, and re-layouts  41.3 us
    all_to_all x1, blocking collectives, shards(): lax.all_to_all(send.reshape(32, 16, FEAT + PTS), 'gz', split_axis=0, conc...  23.4 us
    pallas_call x10, Pallas kernels, call(): pl.pallas_call(outer, out_shape=outs, in_specs=specs, out_specs=[pl.Block...  21 us
    ppermute x9, starting transfers between devices, along_x(): return lax.ppermute(value, 'gz', [(i, (i + 16 * d) % n) for i in range(n)])  12.7 us
    ppermute x6, starting transfers between devices, over_groups(): lax.ppermute(value, 'grp', [(i, (i + d) % n) for i in range(n)])  11 us
    ppermute x8, starting transfers between devices, over_chips(): return near + [lax.ppermute(v, 'gz', SWAP) for v in near]  8.04 us
    ppermute x1, waiting for transfers between devices, shards(): got_up = lax.ppermute(rim_up, 'gz', UP)  7.7 us
    ppermute x1, starting transfers between devices, shards(): got_up = lax.ppermute(rim_up, 'gz', UP)  6.71 us
  transfers between devices with their start and end apart: 31, of which 9 were waited for; matrix products, arithmetic and copies ran while one was open for 0% of the time, Pallas kernels for 8%

profile of v3, /device:TPU:1, one launch (start us, length us, event | category | flops | bytes accessed | tf_op | source)
XLA Modules:
  0.0 186.9 jit_solution(1165313278526759379)
XLA Ops:
  7.2 0.8 copy-done.25
  9.0 4.9 %collective-permute-start = (bf16[16,256]{1,0:T(8,128)(2,1)S(1)}, bf16[16,256]{1,0:T(8,128)(2,1)S(1)}, u32[]{:S(2)}, u32[]{:S(2)}) collective-permute-start(bf16[16,256]{1,0:T(8,128)(2,1)S(1)} %get-tuple-element.26), channel_id=1, source_target_pairs={{0,1},{1,2},{2,3},{3,4},{4,5},{5,6},{6,7},{7,8},{8,9},{9,10},{10,1... | collective-permute-start | bytes 24584 | tf_op jit(solution)/shard_map/ppermute | solution.py:373
  13.9 1.9 %collective-permute-start.1 = (bf16[16,256]{1,0:T(8,128)(2,1)S(1)}, bf16[16,256]{1,0:T(8,128)(2,1)S(1)}, u32[]{:S(2)}, u32[]{:S(2)}) collective-permute-start(bf16[16,256]{1,0:T(8,128)(2,1)S(1)} %get-tuple-element.27), channel_id=1, source_target_pairs={{1,0},{2,1},{3,2},{4,3},{5,4},{6,5},{7,6},{8,7},{9,8},{10,9},{11,1... | collective-permute-start | bytes 24584 | tf_op jit(solution)/shard_map/ppermute | solution.py:374
  15.9 3.0 %collective-permute-done.1.refs_2_ = bf16[16,256]{1,0:T(8,128)(2,1)S(1)} collective-permute-done((bf16[16,256]{1,0:T(8,128)(2,1)S(1)}, bf16[16,256]{1,0:T(8,128)(2,1)S(1)}, u32[]{:S(2)}, u32[]{:S(2)}) %collective-permute-start.1) | collective-permute-done | bytes 8224 | tf_op jit(solution)/shard_map/ppermute | solution.py:374
  18.9 0.8 copy-done.26
  19.7 0.7 copy-done.29
  20.4 0.8 shard_map.137.refs_7_
  22.5 2.0 %copy-done = bf16[6912,256]{1,0:T(8,128)(2,1)S(1)} copy-done((bf16[6912,256]{1,0:T(8,128)(2,1)S(1)}, bf16[6912,256]{1,0:T(8,128)(2,1)}, u32[]{:S(2)}) %copy-start) | copy-done | bytes 3538968
  24.5 0.8 copy-done.27
  25.3 0.8 copy-done.28
  26.1 0.7 copy-done.30
  26.9 0.7 copy-done.50
  27.6 0.7 copy-done.52
  28.9 3.1 %shard_map.138 = bf16[512,384]{1,0:T(8,128)(2,1)S(1)} custom-call(bf16[128,256]{1,0:T(8,128)(2,1)S(1)} %copy-done.27, bf16[16,256]{1,0:T(8,128)(2,1)S(1)} %copy-done.50, bf16[16,256]{1,0:T(8,128)(2,1)S(1)} %copy-done.52, s32[27,128]{1,0:T(8,128)S(1)} %bitcast.15, s32[1,128]{1,0:T(1,128)S(1)} %bitcast.17, bf16[128,256]{1,0:T(8,128)(2,1)S(1)} %copy-done.28, ...), custom_call_target="tpu_custom_call" | custom-call | flops 67108864 | bytes 1048576 | tf_op jit(solution)/shard_map/pallas_call | solution.py:95
  32.0 23.4 %all_to_all.15 = bf16[32,16,384]{2,1,0:T(8,128)(2,1)S(1)} all-to-all(bf16[32,16,384]{2,1,0:T(8,128)(2,1)S(1)} %bitcast.9), channel_id=1, replica_groups={{0,2,4,6,8,10,12,14,16,18,20,22,24,26,28,30,32,34,36,38,40,42,44,46,48,..., dimensions={0} | all-to-all | bytes 786432 | tf_op jit(solution)/shard_map/all_to_all | solution.py:386
  55.4 2.4 %collective-permute-start.2 = (bf16[512,384]{1,0:T(8,128)(2,1)S(1)}, bf16[512,384]{1,0:T(8,128)(2,1)S(1)}, u32[]{:S(2)}, u32[]{:S(2)}) collective-permute-start(bf16[512,384]{1,0:T(8,128)(2,1)S(1)} %bitcast.10), channel_id=1, source_target_pairs={{0,1},{1,0},{2,3},{3,2},{4,5},{5,4},{6,7},{7,6},{8,9},{9,8},{10,11... | collective-permute-start | bytes 1179656 | tf_op jit(solution)/shard_map/ppermute | solution.py:390
  57.8 1.3 collective-permute-done.2.refs_1_
  59.2 6.0 %shard_map.139 = (bf16[512,256]{1,0:T(8,128)(2,1)S(1)}, bf16[128,256]{1,0:T(8,128)(2,1)S(1)}, bf16[128,256]{1,0:T(8,128)(2,1)S(1)}, bf16[128,256]{1,0:T(8,128)(2...) custom-call(bf16[512,384]{1,0:T(8,128)(2,1)S(1)} %bitcast.11, ...), custom_call_target="tpu_custom_call" | custom-call | flops 67108864 | bytes 1048576 | tf_op jit(solution)/shard_map/pallas_call | solution.py:95
  69.0 5.3 %all-to-all-start.1 = ((bf16[32,16,256]{2,1,0:T(8,128)(2,1)}), bf16[32,16,256]{2,1,0:T(8,128)(2,1)}, u32[]{:S(2)}, u32[]{:S(2)}) async-start(bf16[32,16,256]{2,1,0:T(8,128)(2,1)} %bitcast.13), calls=%async_computation.1 | async-start | bytes 524288 | tf_op jit(solution)/shard_map/all_to_all | solution.py:403
  74.3 1.2 collective-permute-start.3
  75.5 2.4 %collective-permute-start.4 = (bf16[128,256]{1,0:T(8,128)(2,1)}, bf16[128,256]{1,0:T(8,128)(2,1)S(1)}, u32[]{:S(2)}, u32[]{:S(2)}) collective-permute-start(bf16[128,256]{1,0:T(8,128)(2,1)} %copy-done.59), channel_id=1, source_target_pairs={{0,32},{1,33},{2,34},{3,35},{4,36},{5,37},{6,38},{7,39},{8,40},{9,... | collective-permute-start | bytes 196616 | tf_op jit(solution)/shard_map/ppermute | solution.py:36
  78.0 1.1 collective-permute-start.5
  79.7 3.0 %collective-permute-done.4.refs_5_ = bf16[128,256]{1,0:T(8,128)(2,1)S(1)} collective-permute-done((bf16[128,256]{1,0:T(8,128)(2,1)}, bf16[128,256]{1,0:T(8,128)(2,1)S(1)}, u32[]{:S(2)}, u32[]{:S(2)}) %collective-permute-start.4) | collective-permute-done | bytes 65568 | tf_op jit(solution)/shard_map/ppermute | solution.py:36
  84.5 0.8 copy-done.40
  85.3 0.8 copy-done.44
  86.1 0.8 copy-done.46
  87.0 0.8 copy-done.48
  89.1 2.0 %shard_map.140 = (bf16[128,256]{1,0:T(8,128)(2,1)}, bf16[144,256]{1,0:T(8,128)(2,1)S(1)}, bf16[128,256]{1,0:T(8,128)(2,1)S(1)}) custom-call(bf16[512,256]{1,0:T(8,128)(2,1)} %bitcast.6.refs_0_, s32[1,128]{1,0:T(1,128)S(1)} %bitcast.18, f32[1,256]{1,0:T(1,128)S(1)} %copy-done.56, bf16[128,256]{1,0:T(8,128)(2,1)S(1)} %copy-done.40, ...), custom_call_target="tpu_custom_call" | custom-call | flops 67108864 | bytes 1048576 | tf_op jit(solution)/shard_map/pallas_call | solution.py:95
  91.2 2.3 %collective-permute-start.13 = (bf16[144,256]{1,0:T(8,128)(2,1)S(1)}, bf16[144,256]{1,0:T(8,128)(2,1)S(1)}, u32[]{:S(2)}, u32[]{:S(2)}) collective-permute-start(bf16[144,256]{1,0:T(8,128)(2,1)S(1)} %get-tuple-element.35.refs_0_.refs_5_), channel_id=1, source_target_pairs={{0,48},{1,49},{2,50},{3,51},{4,52},{5,53},{6,54},{7,55},{8,56},{9,... | collective-permute-start | bytes 221192 | tf_op jit(solution)/shard_map/ppermute | solution.py:36
  94.2 2.7 %collective-permute-start.10 = (bf16[128,256]{1,0:T(8,128)(2,1)S(1)}, bf16[128,256]{1,0:T(8,128)(2,1)S(1)}, u32[]{:S(2)}, u32[]{:S(2)}) collective-permute-start(bf16[128,256]{1,0:T(8,128)(2,1)S(1)} %get-tuple-element.39.refs_1_), channel_id=1, source_target_pairs={{0,192},{64,0},{128,64},{192,128},{1,193},{65,1},{129,65},{193,129... | collective-permute-start | bytes 196616 | tf_op jit(solution)/shard_map/ppermute | solution.py:46
  97.3 1.0 collective-permute-done.10.refs_4_
  98.9 4.1 %collective-permute-start.14 = (bf16[144,256]{1,0:T(8,128)(2,1)S(1)}, bf16[144,256]{1,0:T(8,128)(2,1)S(1)}, u32[]{:S(2)}, u32[]{:S(2)}) collective-permute-start(bf16[144,256]{1,0:T(8,128)(2,1)S(1)} %get-tuple-element.35.refs_0_.refs_5_), channel_id=1, source_target_pairs={{0,1},{1,0},{2,3},{3,2},{4,5},{5,4},{6,7},{7,6},{8,9},{9,8},{10,11... | collective-permute-start | bytes 221192 | tf_op jit(solution)/shard_map/ppermute | solution.py:41
  104.9 2.6 %shard_map.141 = (f32[128,256]{1,0:T(8,128)S(1)}, bf16[16,256]{1,0:T(8,128)(2,1)S(1)}, bf16[16,256]{1,0:T(8,128)(2,1)S(1)}) custom-call(bf16[144,256]{1,0:T(8,128)(2,1)S(1)} %get-tuple-element.35.refs_0_.refs_5_, s32[27,128]{1,0:T(8,128)S(1)} %bitcast.16, bf16[6912,256]{1,0:T(8,128)(2,1)S(1)} %copy-done.1), custom_call_target="tpu_custom_call" | custom-call | flops 67108864 | bytes 1048576 | tf_op jit(solution)/shard_map/pallas_call | solution.py:95
  112.5 1.2 copy-done.2
  113.8 0.9 copy-done.5
  114.6 0.9 copy-done.9
  115.5 0.9 copy-done.12
  116.4 0.9 copy-done.14
  117.3 0.9 copy-done.16
  118.2 0.9 copy-done.18
  119.1 0.9 copy-done.20
  120.0 0.9 copy-done.22
  120.9 0.9 copy-done.24
  121.7 0.8 copy-done.34
  122.6 0.8 copy-done.36
  123.4 0.8 copy-done.38
  124.3 0.8 copy-done.42
  125.1 4.3 %shard_map.143 = bf16[8,240,256]{2,1,0:T(8,128)(2,1)} custom-call(bf16[8,256,256]{2,1,0:T(8,128)(2,1)S(1)} %bitcast.12, bf16[128,256]{1,0:T(8,128)(2,1)S(1)} %copy-done.34, bf16[128,256]{1,0:T(8,128)(2,1)S(1)} %copy-done.42, bf16[128,256]{1,0:T(8,128)(2,1)S(1)} %copy-done.38, bf16[128,256]{1,0:T(8,128)(2,1)S(1)} %copy-done.36, ...), custom_call_target="tpu_custom_call" | custom-call | flops 67108864 | bytes 1048576 | tf_op jit(solution)/shard_map/pallas_call | solution.py:95
  129.4 4.5 %all-to-all-start.2 = ((bf16[8,240,256]{2,1,0:T(8,128)(2,1)}), bf16[8,240,256]{2,1,0:T(8,128)(2,1)S(1)}, u32[]{:S(2)}, u32[]{:S(2)}) async-start(bf16[8,240,256]{2,1,0:T(8,128)(2,1)} %shard_map.143), calls=%async_computation.2 | async-start | bytes 1966080 | tf_op jit(solution)/shard_map/all_to_all | solution.py:437
  133.9 6.7 %collective-permute-start.6 = (bf16[16,256]{1,0:T(8,128)(2,1)S(1)}, bf16[16,256]{1,0:T(8,128)(2,1)S(1)}, u32[]{:S(2)}, u32[]{:S(2)}) collective-permute-start(bf16[16,256]{1,0:T(8,128)(2,1)S(1)} %copy-done.64), channel_id=1, source_target_pairs={{0,1},{1,2},{2,3},{3,4},{4,5},{5,6},{6,7},{7,8},{8,9},{9,10},{10,1... | collective-permute-start | bytes 24584 | tf_op jit(solution)/shard_map/ppermute | solution.py:423
  140.6 2.1 %collective-permute-start.7 = (bf16[16,256]{1,0:T(8,128)(2,1)S(1)}, bf16[16,256]{1,0:T(8,128)(2,1)S(1)}, u32[]{:S(2)}, u32[]{:S(2)}) collective-permute-start(bf16[16,256]{1,0:T(8,128)(2,1)S(1)} %copy-done.62), channel_id=1, source_target_pairs={{1,0},{2,1},{3,2},{4,3},{5,4},{6,5},{7,6},{8,7},{9,8},{10,9},{11,1... | collective-permute-start | bytes 24584 | tf_op jit(solution)/shard_map/ppermute | solution.py:422
  142.7 7.7 %collective-permute-done.6.refs_1_ = bf16[16,256]{1,0:T(8,128)(2,1)S(1)} collective-permute-done((bf16[16,256]{1,0:T(8,128)(2,1)S(1)}, bf16[16,256]{1,0:T(8,128)(2,1)S(1)}, u32[]{:S(2)}, u32[]{:S(2)}) %collective-permute-start.6) | collective-permute-done | bytes 8224 | tf_op jit(solution)/shard_map/ppermute | solution.py:423
  150.4 6.6 %collective-permute-done.7.refs_2_ = bf16[16,256]{1,0:T(8,128)(2,1)S(1)} collective-permute-done((bf16[16,256]{1,0:T(8,128)(2,1)S(1)}, bf16[16,256]{1,0:T(8,128)(2,1)S(1)}, u32[]{:S(2)}, u32[]{:S(2)}) %collective-permute-start.7) | collective-permute-done | bytes 8224 | tf_op jit(solution)/shard_map/ppermute | solution.py:422
  157.7 0.8 shard_map.142.refs_1_
  158.9 0.8 copy-done.32
  159.8 2.9 %collective-permute-start.23 = (bf16[128,256]{1,0:T(8,128)(2,1)S(1)}, bf16[128,256]{1,0:T(8,128)(2,1)S(1)}, u32[]{:S(2)}, u32[]{:S(2)}) collective-permute-start(bf16[128,256]{1,0:T(8,128)(2,1)S(1)} %get-tuple-element.41.refs_4_), channel_id=1, source_target_pairs={{0,48},{1,49},{2,50},{3,51},{4,52},{5,53},{6,54},{7,55},{8,56},{9,... | collective-permute-start | bytes 196616 | tf_op jit(solution)/shard_map/ppermute | solution.py:36
  162.7 1.2 collective-permute-start.22
  164.0 0.8 collective-permute-start.21
  164.7 2.7 %collective-permute-start.20 = (bf16[112,256]{1,0:T(8,128)(2,1)S(1)}, bf16[112,256]{1,0:T(8,128)(2,1)S(1)}, u32[]{:S(2)}, u32[]{:S(2)}) collective-permute-start(bf16[112,256]{1,0:T(8,128)(2,1)S(1)} %get-tuple-element.40.refs_0_), channel_id=1, source_target_pairs={{0,192},{64,0},{128,64},{192,128},{1,193},{65,1},{129,65},{193,129... | collective-permute-start | bytes 172040 | tf_op jit(solution)/shard_map/ppermute | solution.py:46
  167.4 3.1 %collective-permute-start.19 = (bf16[112,256]{1,0:T(8,128)(2,1)S(1)}, bf16[112,256]{1,0:T(8,128)(2,1)S(1)}, u32[]{:S(2)}, u32[]{:S(2)}) collective-permute-start(bf16[112,256]{1,0:T(8,128)(2,1)S(1)} %get-tuple-element.40.refs_0_), channel_id=1, source_target_pairs={{0,128},{64,192},{128,0},{192,64},{1,129},{65,193},{129,1},{193,65... | collective-permute-start | bytes 172040 | tf_op jit(solution)/shard_map/ppermute | solution.py:46
  170.6 2.7 %collective-permute-start.24 = (bf16[128,256]{1,0:T(8,128)(2,1)S(1)}, bf16[128,256]{1,0:T(8,128)(2,1)S(1)}, u32[]{:S(2)}, u32[]{:S(2)}) collective-permute-start(bf16[128,256]{1,0:T(8,128)(2,1)S(1)} %get-tuple-element.41.refs_4_), channel_id=1, source_target_pairs={{0,1},{1,0},{2,3},{3,2},{4,5},{5,4},{6,7},{7,6},{8,9},{9,8},{10,11... | collective-permute-start | bytes 196616 | tf_op jit(solution)/shard_map/ppermute | solution.py:41
  173.9 1.4 collective-permute-start.18
  175.3 3.5 %collective-permute-done.18.refs_1_ = bf16[112,256]{1,0:T(8,128)(2,1)S(1)} collective-permute-done((bf16[112,256]{1,0:T(8,128)(2,1)S(1)}, bf16[112,256]{1,0:T(8,128)(2,1)S(1)}, u32[]{:S(2)}, u32[]{:S(2)}) %collective-permute-start.18) | collective-permute-done | bytes 57376 | tf_op jit(solution)/shard_map/ppermute | solution.py:46
  178.9 1.1 shard_map.145
  (144 shorter events, 20.7 us)
Async XLA Ops:
  7.2 105.4 %all-gather.3.cloned.1.call-start = ((), (), s32[]{:S(2)}) async-start(), calls=%async_computation.3 | async-start | bytes 1179648 | tf_op jit(solution)/shard_map/all_gather | solution.py:378
  7.2 0.8 copy-start.25
  9.0 6.9 %collective-permute-start = (bf16[16,256]{1,0:T(8,128)(2,1)S(1)}, bf16[16,256]{1,0:T(8,128)(2,1)S(1)}, u32[]{:S(2)}, u32[]{:S(2)}) collective-permute-start(bf16[16,256]{1,0:T(8,128)(2,1)S(1)} %get-tuple-element.26), channel_id=1, source_target_pairs={{0,1},{1,2},{2,3},{3,4},{4,5},{5,6},{6,7},{7,8},{8,9},{9,10},{10,1... | collective-permute-start | bytes 24584 | tf_op jit(solution)/shard_map/ppermute | solution.py:373
  13.9 5.0 %collective-permute-start.1 = (bf16[16,256]{1,0:T(8,128)(2,1)S(1)}, bf16[16,256]{1,0:T(8,128)(2,1)S(1)}, u32[]{:S(2)}, u32[]{:S(2)}) collective-permute-start(bf16[16,256]{1,0:T(8,128)(2,1)S(1)} %get-tuple-element.27), channel_id=1, source_target_pairs={{1,0},{2,1},{3,2},{4,3},{5,4},{6,5},{7,6},{8,7},{9,8},{10,9},{11,1... | collective-permute-start | bytes 24584 | tf_op jit(solution)/shard_map/ppermute | solution.py:374
  18.9 0.8 copy-start.26
  22.4 36.8 %copy-start.57 = (f32[256]{0:T(256)S(1)}, f32[256]{0:T(256)}, u32[]{:S(2)}) copy-start(f32[256]{0:T(256)} %param.17) | copy-start | bytes 3076
  22.4 2.0 %copy-start = (bf16[6912,256]{1,0:T(8,128)(2,1)S(1)}, bf16[6912,256]{1,0:T(8,128)(2,1)}, u32[]{:S(2)}) copy-start(bf16[6912,256]{1,0:T(8,128)(2,1)} %refs_2_.3) | copy-start | bytes 10616836
  24.5 0.8 copy-start.27
  25.3 0.8 copy-start.28
  28.9 30.3 %copy-start.3 = (bf16[256,768]{1,0:T(8,128)(2,1)S(1)}, bf16[256,768]{1,0:T(8,128)(2,1)}, u32[]{:S(2)}) copy-start(bf16[256,768]{1,0:T(8,128)(2,1)} %refs_2_.2) | copy-start | bytes 1179652
  28.9 30.3 %copy-start.7 = (bf16[256,256]{1,0:T(8,128)(2,1)S(1)}, bf16[256,256]{1,0:T(8,128)(2,1)}, u32[]{:S(2)}) copy-start(bf16[256,256]{1,0:T(8,128)(2,1)} %refs_3_.2) | copy-start | bytes 393220
  28.9 76.0 %copy-start.1 = (bf16[6912,256]{1,0:T(8,128)(2,1)S(1)}, bf16[6912,256]{1,0:T(8,128)(2,1)}, u32[]{:S(2)}) copy-start(bf16[6912,256]{1,0:T(8,128)(2,1)} %refs_2_.3) | copy-start | bytes 10616836
  28.9 76.0 %copy-start.31 = (s32[128,27]{0,1:T(8,128)S(1)}, s32[128,27]{0,1:T(8,128)}, u32[]{:S(2)}) copy-start(s32[128,27]{0,1:T(8,128)} %param.11) | copy-start | bytes 41476
  55.4 3.8 %collective-permute-start.2 = (bf16[512,384]{1,0:T(8,128)(2,1)S(1)}, bf16[512,384]{1,0:T(8,128)(2,1)S(1)}, u32[]{:S(2)}, u32[]{:S(2)}) collective-permute-start(bf16[512,384]{1,0:T(8,128)(2,1)S(1)} %bitcast.10), channel_id=1, source_target_pairs={{0,1},{1,0},{2,3},{3,2},{4,5},{5,4},{6,7},{7,6},{8,9},{9,8},{10,11... | collective-permute-start | bytes 1179656 | tf_op jit(solution)/shard_map/ppermute | solution.py:390
  69.0 15.5 %all-to-all-start.1 = ((bf16[32,16,256]{2,1,0:T(8,128)(2,1)}), bf16[32,16,256]{2,1,0:T(8,128)(2,1)}, u32[]{:S(2)}, u32[]{:S(2)}) async-start(bf16[32,16,256]{2,1,0:T(8,128)(2,1)} %bitcast.13), calls=%async_computation.1 | async-start | bytes 524288 | tf_op jit(solution)/shard_map/all_to_all | solution.py:403
  74.3 4.8 %collective-permute-start.3 = (bf16[128,256]{1,0:T(8,128)(2,1)}, bf16[128,256]{1,0:T(8,128)(2,1)S(1)}, u32[]{:S(2)}, u32[]{:S(2)}) collective-permute-start(bf16[128,256]{1,0:T(8,128)(2,1)} %copy-done.60), channel_id=1, source_target_pairs={{0,16},{1,17},{2,18},{3,19},{4,20},{5,21},{6,22},{7,23},{8,24},{9,... | collective-permute-start | bytes 196616 | tf_op jit(solution)/shard_map/ppermute | solution.py:36
  75.5 7.2 %collective-permute-start.4 = (bf16[128,256]{1,0:T(8,128)(2,1)}, bf16[128,256]{1,0:T(8,128)(2,1)S(1)}, u32[]{:S(2)}, u32[]{:S(2)}) collective-permute-start(bf16[128,256]{1,0:T(8,128)(2,1)} %copy-done.59), channel_id=1, source_target_pairs={{0,32},{1,33},{2,34},{3,35},{4,36},{5,37},{6,38},{7,39},{8,40},{9,... | collective-permute-start | bytes 196616 | tf_op jit(solution)/shard_map/ppermute | solution.py:36
  78.0 5.9 %collective-permute-start.5 = (bf16[128,256]{1,0:T(8,128)(2,1)}, bf16[128,256]{1,0:T(8,128)(2,1)S(1)}, u32[]{:S(2)}, u32[]{:S(2)}) collective-permute-start(bf16[128,256]{1,0:T(8,128)(2,1)} %copy-done.58), channel_id=1, source_target_pairs={{0,48},{1,49},{2,50},{3,51},{4,52},{5,53},{6,54},{7,55},{8,56},{9,... | collective-permute-start | bytes 196616 | tf_op jit(solution)/shard_map/ppermute | solution.py:36
  84.5 0.8 copy-start.40
  91.2 16.3 %copy-start.4 = (bf16[144,256]{1,0:T(8,128)(2,1)}, bf16[144,256]{1,0:T(8,128)(2,1)S(1)}, u32[]{:S(2)}) copy-start(bf16[144,256]{1,0:T(8,128)(2,1)S(1)} %get-tuple-element.35.refs_0_.refs_5_) | copy-start | bytes 221188
  91.2 20.1 %copy-start.33 = (bf16[128,256]{1,0:T(8,128)(2,1)}, bf16[128,256]{1,0:T(8,128)(2,1)S(1)}, u32[]{:S(2)}) copy-start(bf16[128,256]{1,0:T(8,128)(2,1)S(1)} %get-tuple-element.39.refs_1_) | copy-start | bytes 196612
  91.2 11.8 %collective-permute-start.13 = (bf16[144,256]{1,0:T(8,128)(2,1)S(1)}, bf16[144,256]{1,0:T(8,128)(2,1)S(1)}, u32[]{:S(2)}, u32[]{:S(2)}) collective-permute-start(bf16[144,256]{1,0:T(8,128)(2,1)S(1)} %get-tuple-element.35.refs_0_.refs_5_), channel_id=1, source_target_pairs={{0,48},{1,49},{2,50},{3,51},{4,52},{5,53},{6,54},{7,55},{8,56},{9,... | collective-permute-start | bytes 221192 | tf_op jit(solution)/shard_map/ppermute | solution.py:36
  93.5 9.6 %collective-permute-start.12 = (bf16[144,256]{1,0:T(8,128)(2,1)S(1)}, bf16[144,256]{1,0:T(8,128)(2,1)S(1)}, u32[]{:S(2)}, u32[]{:S(2)}) collective-permute-start(bf16[144,256]{1,0:T(8,128)(2,1)S(1)} %get-tuple-element.35.refs_0_.refs_5_), channel_id=1, source_target_pairs={{0,32},{1,33},{2,34},{3,35},{4,36},{5,37},{6,38},{7,39},{8,40},{9,... | collective-permute-start | bytes 221192 | tf_op jit(solution)/shard_map/ppermute | solution.py:36
  93.5 10.0 %collective-permute-start.11 = (bf16[144,256]{1,0:T(8,128)(2,1)S(1)}, bf16[144,256]{1,0:T(8,128)(2,1)S(1)}, u32[]{:S(2)}, u32[]{:S(2)}) collective-permute-start(bf16[144,256]{1,0:T(8,128)(2,1)S(1)} %get-tuple-element.35.refs_0_.refs_5_), channel_id=1, source_target_pairs={{0,16},{1,17},{2,18},{3,19},{4,20},{5,21},{6,22},{7,23},{8,24},{9,... | collective-permute-start | bytes 221192 | tf_op jit(solution)/shard_map/ppermute | solution.py:36
  94.2 4.1 %collective-permute-start.10 = (bf16[128,256]{1,0:T(8,128)(2,1)S(1)}, bf16[128,256]{1,0:T(8,128)(2,1)S(1)}, u32[]{:S(2)}, u32[]{:S(2)}) collective-permute-start(bf16[128,256]{1,0:T(8,128)(2,1)S(1)} %get-tuple-element.39.refs_1_), channel_id=1, source_target_pairs={{0,192},{64,0},{128,64},{192,128},{1,193},{65,1},{129,65},{193,129... | collective-permute-start | bytes 196616 | tf_op jit(solution)/shard_map/ppermute | solution.py:46
  96.9 6.7 %collective-permute-start.9 = (bf16[128,256]{1,0:T(8,128)(2,1)S(1)}, bf16[128,256]{1,0:T(8,128)(2,1)S(1)}, u32[]{:S(2)}, u32[]{:S(2)}) collective-permute-start(bf16[128,256]{1,0:T(8,128)(2,1)S(1)} %get-tuple-element.39.refs_1_), channel_id=1, source_target_pairs={{0,128},{64,192},{128,0},{192,64},{1,129},{65,193},{129,1},{193,65... | collective-permute-start | bytes 196616 | tf_op jit(solution)/shard_map/ppermute | solution.py:46
  98.9 11.1 %collective-permute-start.14 = (bf16[144,256]{1,0:T(8,128)(2,1)S(1)}, bf16[144,256]{1,0:T(8,128)(2,1)S(1)}, u32[]{:S(2)}, u32[]{:S(2)}) collective-permute-start(bf16[144,256]{1,0:T(8,128)(2,1)S(1)} %get-tuple-element.35.refs_0_.refs_5_), channel_id=1, source_target_pairs={{0,1},{1,0},{2,3},{3,2},{4,5},{5,4},{6,7},{7,6},{8,9},{9,8},{10,11... | collective-permute-start | bytes 221192 | tf_op jit(solution)/shard_map/ppermute | solution.py:41
  103.0 7.0 %copy-start.11 = (bf16[144,256]{1,0:T(8,128)(2,1)}, bf16[144,256]{1,0:T(8,128)(2,1)S(1)}, u32[]{:S(2)}) copy-start(bf16[144,256]{1,0:T(8,128)(2,1)S(1)} %collective-permute-done.13.refs_8_) | copy-start | bytes 221188
  103.0 7.7 %collective-permute-start.17 = (bf16[144,256]{1,0:T(8,128)(2,1)S(1)}, bf16[144,256]{1,0:T(8,128)(2,1)S(1)}, u32[]{:S(2)}, u32[]{:S(2)}) collective-permute-start(bf16[144,256]{1,0:T(8,128)(2,1)S(1)} %collective-permute-done.13.refs_8_), channel_id=1, source_target_pairs={{0,1},{1,0},{2,3},{3,2},{4,5},{5,4},{6,7},{7,6},{8,9},{9,8},{10,11... | collective-permute-start | bytes 221192 | tf_op jit(solution)/shard_map/ppermute | solution.py:41
  103.1 7.6 %copy-start.13 = (bf16[144,256]{1,0:T(8,128)(2,1)}, bf16[144,256]{1,0:T(8,128)(2,1)S(1)}, u32[]{:S(2)}) copy-start(bf16[144,256]{1,0:T(8,128)(2,1)S(1)} %collective-permute-done.12.refs_7_) | copy-start | bytes 221188
  103.1 8.2 %collective-permute-start.16 = (bf16[144,256]{1,0:T(8,128)(2,1)S(1)}, bf16[144,256]{1,0:T(8,128)(2,1)S(1)}, u32[]{:S(2)}, u32[]{:S(2)}) collective-permute-start(bf16[144,256]{1,0:T(8,128)(2,1)S(1)} %collective-permute-done.12.refs_7_), channel_id=1, source_target_pairs={{0,1},{1,0},{2,3},{3,2},{4,5},{5,4},{6,7},{7,6},{8,9},{9,8},{10,11... | collective-permute-start | bytes 221192 | tf_op jit(solution)/shard_map/ppermute | solution.py:41
  103.5 7.8 %copy-start.15 = (bf16[144,256]{1,0:T(8,128)(2,1)}, bf16[144,256]{1,0:T(8,128)(2,1)S(1)}, u32[]{:S(2)}) copy-start(bf16[144,256]{1,0:T(8,128)(2,1)S(1)} %collective-permute-done.11.refs_6_) | copy-start | bytes 221188
  103.5 8.4 %collective-permute-start.15 = (bf16[144,256]{1,0:T(8,128)(2,1)S(1)}, bf16[144,256]{1,0:T(8,128)(2,1)S(1)}, u32[]{:S(2)}, u32[]{:S(2)}) collective-permute-start(bf16[144,256]{1,0:T(8,128)(2,1)S(1)} %collective-permute-done.11.refs_6_), channel_id=1, source_target_pairs={{0,1},{1,0},{2,3},{3,2},{4,5},{5,4},{6,7},{7,6},{8,9},{9,8},{10,11... | collective-permute-start | bytes 221192 | tf_op jit(solution)/shard_map/ppermute | solution.py:41
  104.2 5.1 %collective-permute-start.8 = (bf16[128,256]{1,0:T(8,128)(2,1)S(1)}, bf16[128,256]{1,0:T(8,128)(2,1)S(1)}, u32[]{:S(2)}, u32[]{:S(2)}) collective-permute-start(bf16[128,256]{1,0:T(8,128)(2,1)S(1)} %get-tuple-element.39.refs_1_), channel_id=1, source_target_pairs={{0,64},{64,128},{128,192},{192,0},{1,65},{65,129},{129,193},{193,1... | collective-permute-start | bytes 196616 | tf_op jit(solution)/shard_map/ppermute | solution.py:46
  112.5 1.2 copy-start.2
  113.8 0.9 copy-start.5
  114.6 0.9 copy-start.9
  115.5 0.9 copy-start.12
  116.4 0.9 copy-start.14
  117.3 0.9 copy-start.16
  118.2 0.9 copy-start.18
  119.1 0.9 copy-start.20
  120.0 0.9 copy-start.22
  120.8 0.9 copy-start.24
  121.7 0.8 copy-start.34
  122.6 0.8 copy-start.36
  123.4 0.8 copy-start.38
  125.1 8.8 %copy-start.64 = (bf16[16,256]{1,0:T(8,128)(2,1)S(1)}, bf16[16,256]{1,0:T(8,128)(2,1)}, u32[]{:S(2)}) copy-start(bf16[16,256]{1,0:T(8,128)(2,1)} %copy-done.63) | copy-start | bytes 24580
  125.1 15.5 %copy-start.62 = (bf16[16,256]{1,0:T(8,128)(2,1)S(1)}, bf16[16,256]{1,0:T(8,128)(2,1)}, u32[]{:S(2)}) copy-start(bf16[16,256]{1,0:T(8,128)(2,1)} %copy-done.61) | copy-start | bytes 24580
  125.1 32.0 %copy-start.10 = (f32[128,256]{1,0:T(8,128)S(1)}, f32[128,256]{1,0:T(8,128)}, u32[]{:S(2)}) copy-start(f32[128,256]{1,0:T(8,128)} %copy-done.8) | copy-start | bytes 393220
  129.4 29.5 %all-to-all-start.2 = ((bf16[8,240,256]{2,1,0:T(8,128)(2,1)}), bf16[8,240,256]{2,1,0:T(8,128)(2,1)S(1)}, u32[]{:S(2)}, u32[]{:S(2)}) async-start(bf16[8,240,256]{2,1,0:T(8,128)(2,1)} %shard_map.143), calls=%async_computation.2 | async-start | bytes 1966080 | tf_op jit(solution)/shard_map/all_to_all | solution.py:437
  133.9 16.6 %collective-permute-start.6 = (bf16[16,256]{1,0:T(8,128)(2,1)S(1)}, bf16[16,256]{1,0:T(8,128)(2,1)S(1)}, u32[]{:S(2)}, u32[]{:S(2)}) collective-permute-start(bf16[16,256]{1,0:T(8,128)(2,1)S(1)} %copy-done.64), channel_id=1, source_target_pairs={{0,1},{1,2},{2,3},{3,4},{4,5},{5,6},{6,7},{7,8},{8,9},{9,10},{10,1... | collective-permute-start | bytes 24584 | tf_op jit(solution)/shard_map/ppermute | solution.py:423
  140.6 16.5 %collective-permute-start.7 = (bf16[16,256]{1,0:T(8,128)(2,1)S(1)}, bf16[16,256]{1,0:T(8,128)(2,1)S(1)}, u32[]{:S(2)}, u32[]{:S(2)}) collective-permute-start(bf16[16,256]{1,0:T(8,128)(2,1)S(1)} %copy-done.62), channel_id=1, source_target_pairs={{1,0},{2,1},{3,2},{4,3},{5,4},{6,5},{7,6},{8,7},{9,8},{10,9},{11,1... | collective-permute-start | bytes 24584 | tf_op jit(solution)/shard_map/ppermute | solution.py:422
  158.9 0.8 copy-start.32
  159.8 13.5 %collective-permute-start.23 = (bf16[128,256]{1,0:T(8,128)(2,1)S(1)}, bf16[128,256]{1,0:T(8,128)(2,1)S(1)}, u32[]{:S(2)}, u32[]{:S(2)}) collective-permute-start(bf16[128,256]{1,0:T(8,128)(2,1)S(1)} %get-tuple-element.41.refs_4_), channel_id=1, source_target_pairs={{0,48},{1,49},{2,50},{3,51},{4,52},{5,53},{6,54},{7,55},{8,56},{9,... | collective-permute-start | bytes 196616 | tf_op jit(solution)/shard_map/ppermute | solution.py:36
  162.7 10.6 %collective-permute-start.22 = (bf16[128,256]{1,0:T(8,128)(2,1)S(1)}, bf16[128,256]{1,0:T(8,128)(2,1)S(1)}, u32[]{:S(2)}, u32[]{:S(2)}) collective-permute-start(bf16[128,256]{1,0:T(8,128)(2,1)S(1)} %get-tuple-element.41.refs_4_), channel_id=1, source_target_pairs={{0,32},{1,33},{2,34},{3,35},{4,36},{5,37},{6,38},{7,39},{8,40},{9,... | collective-permute-start | bytes 196616 | tf_op jit(solution)/shard_map/ppermute | solution.py:36
  164.0 9.9 %collective-permute-start.21 = (bf16[128,256]{1,0:T(8,128)(2,1)S(1)}, bf16[128,256]{1,0:T(8,128)(2,1)S(1)}, u32[]{:S(2)}, u32[]{:S(2)}) collective-permute-start(bf16[128,256]{1,0:T(8,128)(2,1)S(1)} %get-tuple-element.41.refs_4_), channel_id=1, source_target_pairs={{0,16},{1,17},{2,18},{3,19},{4,20},{5,21},{6,22},{7,23},{8,24},{9,... | collective-permute-start | bytes 196616 | tf_op jit(solution)/shard_map/ppermute | solution.py:36
  164.7 5.8 %collective-permute-start.20 = (bf16[112,256]{1,0:T(8,128)(2,1)S(1)}, bf16[112,256]{1,0:T(8,128)(2,1)S(1)}, u32[]{:S(2)}, u32[]{:S(2)}) collective-permute-start(bf16[112,256]{1,0:T(8,128)(2,1)S(1)} %get-tuple-element.40.refs_0_), channel_id=1, source_target_pairs={{0,192},{64,0},{128,64},{192,128},{1,193},{65,1},{129,65},{193,129... | collective-permute-start | bytes 172040 | tf_op jit(solution)/shard_map/ppermute | solution.py:46
  167.4 6.5 %collective-permute-start.19 = (bf16[112,256]{1,0:T(8,128)(2,1)S(1)}, bf16[112,256]{1,0:T(8,128)(2,1)S(1)}, u32[]{:S(2)}, u32[]{:S(2)}) collective-permute-start(bf16[112,256]{1,0:T(8,128)(2,1)S(1)} %get-tuple-element.40.refs_0_), channel_id=1, source_target_pairs={{0,128},{64,192},{128,0},{192,64},{1,129},{65,193},{129,1},{193,65... | collective-permute-start | bytes 172040 | tf_op jit(solution)/shard_map/ppermute | solution.py:46
  170.6 8.3 %collective-permute-start.24 = (bf16[128,256]{1,0:T(8,128)(2,1)S(1)}, bf16[128,256]{1,0:T(8,128)(2,1)S(1)}, u32[]{:S(2)}, u32[]{:S(2)}) collective-permute-start(bf16[128,256]{1,0:T(8,128)(2,1)S(1)} %get-tuple-element.41.refs_4_), channel_id=1, source_target_pairs={{0,1},{1,0},{2,3},{3,2},{4,5},{5,4},{6,7},{7,6},{8,9},{9,8},{10,11... | collective-permute-start | bytes 196616 | tf_op jit(solution)/shard_map/ppermute | solution.py:41
  173.3 5.6 %collective-permute-start.27 = (bf16[128,256]{1,0:T(8,128)(2,1)S(1)}, bf16[128,256]{1,0:T(8,128)(2,1)S(1)}, u32[]{:S(2)}, u32[]{:S(2)}) collective-permute-start(bf16[128,256]{1,0:T(8,128)(2,1)S(1)} %collective-permute-done.23.refs_7_), channel_id=1, source_target_pairs={{0,1},{1,0},{2,3},{3,2},{4,5},{5,4},{6,7},{7,6},{8,9},{9,8},{10,11... | collective-permute-start | bytes 196616 | tf_op jit(solution)/shard_map/ppermute | solution.py:41
  173.3 5.6 %collective-permute-start.26 = (bf16[128,256]{1,0:T(8,128)(2,1)S(1)}, bf16[128,256]{1,0:T(8,128)(2,1)S(1)}, u32[]{:S(2)}, u32[]{:S(2)}) collective-permute-start(bf16[128,256]{1,0:T(8,128)(2,1)S(1)} %collective-permute-done.22.refs_6_), channel_id=1, source_target_pairs={{0,1},{1,0},{2,3},{3,2},{4,5},{5,4},{6,7},{7,6},{8,9},{9,8},{10,11... | collective-permute-start | bytes 196616 | tf_op jit(solution)/shard_map/ppermute | solution.py:41
  173.8 5.1 %collective-permute-start.25 = (bf16[128,256]{1,0:T(8,128)(2,1)S(1)}, bf16[128,256]{1,0:T(8,128)(2,1)S(1)}, u32[]{:S(2)}, u32[]{:S(2)}) collective-permute-start(bf16[128,256]{1,0:T(8,128)(2,1)S(1)} %collective-permute-done.21.refs_5_), channel_id=1, source_target_pairs={{0,1},{1,0},{2,3},{3,2},{4,5},{5,4},{6,7},{7,6},{8,9},{9,8},{10,11... | collective-permute-start | bytes 196616 | tf_op jit(solution)/shard_map/ppermute | solution.py:41
  173.9 4.9 %collective-permute-start.18 = (bf16[112,256]{1,0:T(8,128)(2,1)S(1)}, bf16[112,256]{1,0:T(8,128)(2,1)S(1)}, u32[]{:S(2)}, u32[]{:S(2)}) collective-permute-start(bf16[112,256]{1,0:T(8,128)(2,1)S(1)} %get-tuple-element.40.refs_0_), channel_id=1, source_target_pairs={{0,64},{64,128},{128,192},{192,0},{1,65},{65,129},{129,193},{193,1... | collective-permute-start | bytes 172040 | tf_op jit(solution)/shard_map/ppermute | solution.py:46
  (34 other events, 22.6 us)
Sparse Core Ops, SparseCore 0:
  22.6 29.0 all-gather.2

commit v4 on v3

--- a/solution.py
+++ b/solution.py
@@ -66,40 +66,57 @@
     return lax.broadcasted_iota(I32, shape, dim)
 
 
-def call(body, out_shape, *args, scratch=(), flops=1 << 26, nbytes=1 << 20, smem=0, fetched=(), late=(), idle=(), limit=16):
+def call(body, out_shape, *args, scratch=(), us=1.0, fetched=(), late=(), idle=(), pinned=(), limit=16):
     fetched = tuple(fetched) + tuple(late)
+    args = [pltpu.with_memory_space_constraint(a, pltpu.HBM) if i in fetched else a for i, a in enumerate(args)]
     specs = []
     for i in range(len(args)):
-        space = pltpu.SMEM if i < smem else pltpu.HBM if i in fetched else pl.ANY if i in idle else pltpu.VMEM
+        space = pltpu.HBM if i in fetched else pl.ANY if i in idle else pltpu.VMEM
         specs.append(pl.BlockSpec(memory_space=space))
     single = not isinstance(out_shape, (list, tuple))
     outs = [out_shape] if single else list(out_shape)
     held = [pltpu.VMEM(args[i].shape, args[i].dtype) for i in fetched]
-    held += [pltpu.SemaphoreType.DMA] * len(fetched)
+    held += [pltpu.VMEM(outs[i].shape, outs[i].dtype) for i in pinned]
+    held += [pltpu.SemaphoreType.DMA] * (len(fetched) + len(pinned))
+    shapes = [pltpu.HBM(o.shape, o.dtype) if i in pinned else o for i, o in enumerate(outs)]
 
     def outer(*refs):
-        base = len(args) + len(outs) + len(scratch)
-        views = list(refs[: len(args)])
+        ins = list(refs[: len(args)])
+        results = list(refs[len(args) : len(args) + len(outs)])
+        first = len(args) + len(outs)
+        extra = refs[first : first + len(scratch)]
+        rest = refs[first + len(scratch) :]
+        moved = len(fetched) + len(pinned)
+        buffers, sems = rest[:moved], rest[moved:]
         copies = {}
         for n, i in enumerate(fetched):
-            copies[i] = pltpu.make_async_copy(refs[i], refs[base + n], refs[base + len(fetched) + n])
+            copies[i] = pltpu.make_async_copy(ins[i], buffers[n], sems[n])
             copies[i].start()
-            views[i] = refs[base + n]
+            ins[i] = buffers[n]
         for i in fetched:
             if i in late:
-                views[i] = (views[i], copies[i].wait)
+                ins[i] = (ins[i], copies[i].wait)
             else:
                 copies[i].wait()
-        body(*[v for i, v in enumerate(views) if i not in idle], *refs[len(args) : base])
+        leaving = []
+        for n, i in enumerate(pinned):
+            n += len(fetched)
+            leaving.append(pltpu.make_async_copy(buffers[n], results[i], sems[n]))
+            results[i] = buffers[n]
+        body(*[v for i, v in enumerate(ins) if i not in idle], *results, *extra)
+        for copy in leaving:
+            copy.start()
+        for copy in leaving:
+            copy.wait()
 
     got = pl.pallas_call(
         outer,
-        out_shape=outs,
+        out_shape=shapes,
         in_specs=specs,
-        out_specs=[pl.BlockSpec(memory_space=pltpu.VMEM)] * len(outs),
+        out_specs=[pl.BlockSpec(memory_space=pltpu.HBM if i in pinned else pltpu.VMEM) for i in range(len(outs))],
         scratch_shapes=list(scratch) + held,
         compiler_params=pltpu.CompilerParams(vmem_limit_bytes=limit * MIB),
-        cost_estimate=pl.CostEstimate(flops=flops, bytes_accessed=nbytes, transcendentals=0),
+        cost_estimate=pl.CostEstimate(flops=int(us * 1.1e9), bytes_accessed=1 << 18, transcendentals=0),
     )(*args)
     return got[0] if single else got
 
@@ -132,7 +149,7 @@
     return one_hot(rows == target), one_hot(rows == target + 4)
 
 
-def conv_body(feat_ref, prev_ref, next_ref, nbr_ref, rank_ref, cot_ref, weight, send_ref, ext, tab, wide):
+def conv_body(feat_ref, prev_ref, next_ref, nbr_ref, rank_ref, cot_ref, weight, send_ref, pay_ref, ext, tab, wide):
     weight_ref, weight_here = weight
     ext[:PTS] = feat_ref[...]
     ext[PTS : PTS + RIM] = prev_ref[...]
@@ -141,6 +158,10 @@
     rows = ext[...]
     tab[:OFFS] = nbr_ref[...].astype(F32)
     tab[OFFS:] = jnp.zeros((PTS - OFFS, PTS), F32)
+    pay_ref[:EXT] = rows[:EXT]
+    pay_ref[EXT : EXT + 16, :PTS] = tab[:16].astype(BF)
+    pay_ref[EXT : EXT + 16, PTS:] = tab[16:32].astype(BF)
+    pay_ref[EXT + 16 :] = jnp.zeros((PAY - EXT - 16, FEAT), BF)
     table = jnp.transpose(tab[...])
     lanes = iota((PTS, FEAT), 1).astype(F32)
     for k in range(OFFS):
@@ -171,7 +192,7 @@
 
 def patch_body(
     a_ref, b_ref, qkv_ref, proj_ref, gain_ref,
-    back_ref, d0_ref, d1_ref, d2_ref, d3_ref, gg_ref,
+    back_ref, gg_ref,
     hits, qm, am, pr, ds, sc, gs, dense,
 ):
     x, core = position()
@@ -236,8 +257,7 @@
         dense[:FEAT] = (t_mm(scaled, parts[0][1]) + t_mm(scaled, parts[1][1])).astype(BF)
         dense[FEAT:] = t_mm(attended, cot).astype(BF)
 
-    for d, ref in enumerate((d0_ref, d1_ref, d2_ref, d3_ref)):
-        ref[...] = dense[pl.ds(pl.multiple_of(((x + d) & (NX - 1)) * PTS, PTS), PTS), :]
+    back_ref[:, 16:] = dense[...].reshape(32, 16, FEAT)
     gain_terms = grad_scaled * normed
     gg_ref[...] = jnp.sum(jnp.where(core == 0, gain_terms[:PTS], gain_terms[PTS:]), 0, keepdims=True)
     grad_normed = grad_scaled * gain
@@ -247,38 +267,31 @@
         - normed * jnp.mean(grad_normed * normed, -1, keepdims=True)
     ) * inverse
     grad_local = (cot.astype(F32) + grad_hidden).astype(BF)
-    back_ref[...] = mm(hits[...], jnp.concatenate([out, grad_local], 0)).astype(BF)
-
-
-def table_body(feat_ref, prev_ref, next_ref, nbr_ref, pay_ref):
-    pay_ref[:PTS] = feat_ref[...]
-    pay_ref[PTS : PTS + RIM] = prev_ref[...]
-    pay_ref[PTS + RIM : EXT] = next_ref[...]
-    table = nbr_ref[...].astype(F32)
-    pay_ref[EXT : EXT + 16, :PTS] = table[:16].astype(BF)
-    pay_ref[EXT : EXT + 16, PTS:] = jnp.concatenate([table[16:], jnp.zeros((5, PTS), F32)], 0).astype(BF)
-    pay_ref[EXT + 16 :] = jnp.zeros((PAY - EXT - 16, FEAT), BF)
-
-
-def unpack_body(back_ref, rank_ref, gg_ref, d0_ref, d1_ref, d2_ref, d3_ref, block_ref, grad_ref, dense_ref):
+    back = mm(hits[...], jnp.concatenate([out, grad_local], 0)).astype(BF)
+    back_ref[:, :16] = back.reshape(32, 16, FEAT)
+
+
+def unpack_body(back_ref, rank_ref, gg_ref, block_ref, grad_ref, dense_ref):
     first, second = slot_hits(rank_ref[...])
-    rows = back_ref[...]
+    rows = back_ref[:, :16].reshape(SLOTS, FEAT)
     grad_ref[:PTS] = t_mm(second, rows).astype(BF)
     grad_ref[PTS:] = jnp.broadcast_to(gg_ref[...], (16, FEAT)).astype(BF)
-    dense = d0_ref[...].astype(F32) + d1_ref[...].astype(F32) + d2_ref[...].astype(F32) + d3_ref[...].astype(F32)
-    dense_ref[...] = dense.astype(BF)
+    dense_ref[...] = jnp.sum(back_ref[:, 16:].astype(F32), 0).astype(BF)
     block_ref[...] = t_mm(first, rows).astype(BF)
 
 
-def spread_body(grad_ref, nbr_ref, weight_ref, own_ref, down_ref, up_ref, acc):
+def spread_body(grad_ref, nbr_ref, weight, own_ref, down_ref, up_ref, terms, acc):
+    weight_ref, weight_here = weight
     grad = grad_ref[:PTS]
     table = nbr_ref[...].astype(F32)
     points = iota((EXT, PTS), 0).astype(F32)
+    for k in range(OFFS):
+        hit = one_hot(points == table[k : k + 1])
+        terms[k * EXT : (k + 1) * EXT] = mm(hit, grad).astype(BF)
+    weight_here()
     acc[...] = jnp.zeros((EXT, FEAT), F32)
     for k in range(OFFS):
-        hit = one_hot(points == table[k : k + 1])
-        term = mm(hit, grad).astype(BF)
-        acc[...] += mm_t(term, weight_ref[k * FEAT : (k + 1) * FEAT])
+        acc[...] += mm_t(terms[k * EXT : (k + 1) * EXT], weight_ref[k * FEAT : (k + 1) * FEAT])
     own_ref[...] = acc[:PTS] + grad.astype(F32)
     down_ref[...] = acc[PTS : PTS + RIM].astype(BF)
     up_ref[...] = acc[PTS + RIM :].astype(BF)
@@ -329,7 +342,8 @@
     for i in range(1, NZ):
         total += got_ref[i].astype(F32)
     conv_ref[...] = total[:112].astype(BF)
-    dense_ref[...] = total[112:].astype(BF)
+    for i in range(NZ):
+        dense_ref[i * 16 : (i + 1) * 16] = got_ref[i, 112:]
 
 
 def last_body(factor, *refs):
@@ -368,47 +382,42 @@
     gain_row = norm_gain.reshape(1, FEAT)
     table = neighbours.T
     to_prev, to_next = call(
-        pick_body, [sds((RIM, FEAT))] * 2, halo_rows, features, fetched=(0, 1), limit=8
+        pick_body, [sds((RIM, FEAT))] * 2, halo_rows, features, fetched=(0, 1), us=0.5, limit=8
     )
     from_prev = lax.ppermute(to_next, "gz", UP)
     from_next = lax.ppermute(to_prev, "gz", DOWN)
-    payload = call(
-        table_body, sds((PAY, FEAT)), features, from_prev, from_next, table, fetched=(0, 3), limit=8
+    send, payload = call(
+        conv_body,
+        [sds((SLOTS, FEAT + PTS)), sds((PAY, FEAT))],
+        features, from_prev, from_next, table, rank_row, cotangent, conv_weight,
+        scratch=[pltpu.VMEM((FEAT, FEAT), BF), pltpu.VMEM((PTS, PTS), F32), pltpu.VMEM((PTS, OFFS * FEAT), BF)],
+        fetched=(0, 3, 4, 5), late=(6,), pinned=(0, 1), us=3.0,
     )
     everyone = lax.all_gather(payload, "gz", axis_index_groups=XC_GROUPS)
-    send = call(
-        conv_body,
-        sds((SLOTS, FEAT + PTS)),
-        features, from_prev, from_next, table, rank_row, cotangent, conv_weight, payload,
-        scratch=[pltpu.VMEM((FEAT, FEAT), BF), pltpu.VMEM((PTS, PTS), F32), pltpu.VMEM((PTS, OFFS * FEAT), BF)],
-        fetched=(0, 3, 4, 5), late=(6,), idle=(7,), limit=16,
-    )
     got = lax.all_to_all(
         send.reshape(32, 16, FEAT + PTS), "gz", split_axis=0, concat_axis=0,
         axis_index_groups=XZ_GROUPS, tiled=True,
     ).reshape(SLOTS, FEAT + PTS)
     other = lax.ppermute(got, "gz", SWAP)
     rows = 2 * HEADS * PTS
-    back, d0, d1, d2, d3, grad_gain = call(
+    back, grad_gain = call(
         patch_body,
-        [sds((SLOTS, FEAT))] + [sds((PTS, FEAT))] * 4 + [sds((1, FEAT), F32)],
+        [sds((32, 32, FEAT)), sds((1, FEAT), F32)],
         got, other, qkv_weight, proj_weight, gain_row,
         scratch=[pltpu.VMEM((SLOTS, SLOTS), BF)]
         + [pltpu.VMEM((rows, FEAT), BF)] * 4
         + [pltpu.VMEM((rows, FEAT), F32)] * 2
         + [pltpu.VMEM((2 * FEAT, FEAT), BF)],
-        limit=32,
-    )
-    dense_parts = [d0] + [along_x(v, d) for d, v in ((1, d1), (2, d2), (3, d3))]
+        pinned=(0, 1), us=6.0, limit=32,
+    )
     returned = lax.all_to_all(
-        back.reshape(32, 16, FEAT), "gz", split_axis=0, concat_axis=0,
-        axis_index_groups=XZ_GROUPS, tiled=True,
-    ).reshape(SLOTS, FEAT)
+        back, "gz", split_axis=0, concat_axis=0, axis_index_groups=XZ_GROUPS, tiled=True
+    )
     block_out, grad, dense = call(
         unpack_body,
-        [sds((PTS, FEAT)), sds((PTS + 16, FEAT)), sds((PTS, FEAT))],
-        returned, rank_row, grad_gain, *dense_parts,
-        fetched=(1,), limit=8,
+        [sds((PTS, FEAT)), sds((PTS + 16, FEAT)), sds((16, FEAT))],
+        returned, rank_row, grad_gain,
+        fetched=(0, 1, 2), pinned=(1, 2), us=1.5, limit=8,
     )
     grads = over_chips(grad)
     dense_groups = over_groups(dense)
@@ -416,14 +425,14 @@
         spread_body,
         [sds((PTS, FEAT), F32), sds((RIM, FEAT)), sds((RIM, FEAT))],
         grad, table, conv_weight,
-        scratch=[pltpu.VMEM((EXT, FEAT), F32)],
-        limit=8,
+        scratch=[pltpu.VMEM((OFFS * EXT, FEAT), BF), pltpu.VMEM((EXT, FEAT), F32)],
+        fetched=(0, 1), late=(2,), pinned=(0, 1, 2), us=4.0,
     )
     got_down = lax.ppermute(rim_down, "gz", DOWN)
     got_up = lax.ppermute(rim_up, "gz", UP)
     parts = call(
         kernel_grad_body,
-        sds((NZ, 240, FEAT)),
+        sds((NZ, 128, FEAT)),
         everyone, *dense_groups, *grads, own_part,
         scratch=[
             pltpu.VMEM((NX * NC * 32, PTS), F32),
@@ -431,14 +440,18 @@
             pltpu.VMEM((NX * NC * EXT, FEAT), BF),
             pltpu.VMEM((8 * FEAT + 16, FEAT), F32),
         ],
-        idle=(13,),
-    )
-    grad_features = call(rim_body, sds((PTS, FEAT)), own_part, got_up, got_down, halo_rows, limit=8)
+        fetched=tuple(range(13)), idle=(13,), pinned=(0,), us=5.0,
+    )
+    grad_features = call(
+        rim_body, sds((PTS, FEAT)), own_part, got_up, got_down, halo_rows,
+        fetched=(0, 1, 2, 3), us=1.0, limit=8,
+    )
     z_parts = lax.all_to_all(
         parts, "gz", split_axis=0, concat_axis=0, axis_index_groups=Z_GROUPS, tiled=True
     )
     conv_part, dense_sum = call(
-        sum_body, [sds((112, FEAT)), sds((PTS, FEAT))], z_parts, grad_features, idle=(1,), limit=8
+        sum_body, [sds((112, FEAT)), sds((PTS, FEAT))], z_parts, grad_features,
+        fetched=(0,), idle=(1,), us=1.0, limit=8,
     )
     grad_conv, gain_sum, grad_qkv, grad_proj = call(
         lambda *refs: last_body(factor, *refs),

time: 191 us -> 156 us (0.82)
  local copies, waits for them, and re-layouts: 41.3 us -> 3.8 us
  starting transfers between devices: 59.7 us -> 39.4 us
  blocking collectives: 23.4 us -> 43.1 us
  Pallas kernels: 21 us -> 28.7 us
  waiting for transfers between devices: 27.1 us -> 24.2 us
    unnamed x134 -> x40, local copies, waits for them, and re-layouts: 41.3 us -> 3.8 us
    all_to_all x0 -> x1, blocking collectives: none -> 19.4 us  [shards(): lax.all_to_all(back, 'gz', split_axis=0, concat_axis=0, axis_index_groups...]
    pallas_call x10 -> x9, Pallas kernels: 21 us -> 28.7 us  [call(): pl.pallas_call(outer, out_shape=shapes, in_specs=specs, out_specs=[pl.Blo...]
    ppermute x6, starting transfers between devices: 11 us -> 4.24 us  [over_groups(): lax.ppermute(value, 'grp', [(i, (i + d) % n) for i in range(n)])]
    ppermute x9 -> x6, starting transfers between devices: 12.7 us -> 6.95 us  [along_x(): return lax.ppermute(value, 'gz', [(i, (i + 16 * d) % n) for i in range(n)])]
    ppermute x6, waiting for transfers between devices: 4.53 us -> 10.3 us  [over_groups(): lax.ppermute(value, 'grp', [(i, (i + d) % n) for i in range(n)])]
    all_to_all x1 -> x0, starting transfers between devices: 5.32 us -> none  [shards(): lax.all_to_all(back.reshape(32, 16, FEAT), 'gz', split_axis=0, concat_axi...]
    ppermute x1, waiting for transfers between devices: 7.7 us -> 2.56 us  [shards(): got_up = lax.ppermute(rim_up, 'gz', UP)]
  transfers between devices with their start and end apart: 31 -> 27, of which waited for: 9 -> 9; matrix products, arithmetic and copies ran while one was open for 0% -> 0% of each run, Pallas kernels for 8% -> 10%
where the time goes in v4:
time: 156 us; the launch traced here: 153 us
  blocking collectives  43.1 us (28%)
  starting transfers between devices  39.4 us (25%)
  Pallas kernels  28.7 us (18%)
  waiting for transfers between devices  24.2 us (16%)
  between operations  14.3 us (9%)
  local copies, waits for them, and re-layouts  3.8 us (2%)
    pallas_call x9, Pallas kernels, call(): pl.pallas_call(outer, out_shape=shapes, in_specs=specs, out_specs=[pl.Blo...  28.7 us
    all_to_all x1, blocking collectives, shards(): lax.all_to_all(send.reshape(32, 16, FEAT + PTS), 'gz', split_axis=0, conc...  23.6 us
    all_to_all x1, blocking collectives, shards(): lax.all_to_all(back, 'gz', split_axis=0, concat_axis=0, axis_index_groups...  19.4 us
    ppermute x6, waiting for transfers between devices, over_groups(): lax.ppermute(value, 'grp', [(i, (i + d) % n) for i in range(n)])  10.3 us
    ppermute x8, starting transfers between devices, over_chips(): return near + [lax.ppermute(v, 'gz', SWAP) for v in near]  8.93 us
    ppermute x6, starting transfers between devices, along_x(): return lax.ppermute(value, 'gz', [(i, (i + 16 * d) % n) for i in range(n)])  6.95 us
    ppermute x1, waiting for transfers between devices, shards(): got_down = lax.ppermute(rim_down, 'gz', DOWN)  5.3 us
    ppermute x1, starting transfers between devices, shards(): from_prev = lax.ppermute(to_next, 'gz', UP)  4.94 us
  transfers between devices with their start and end apart: 27, of which 9 were waited for; matrix products, arithmetic and copies ran while one was open for 0% of the time, Pallas kernels for 10%

profile of v4, /device:TPU:1, one launch (start us, length us, event | category | flops | bytes accessed | tf_op | source)
XLA Modules:
  0.0 153.5 jit_solution(9789076140592246485)
XLA Ops:
  7.2 0.0 all-gather.3.cloned.1.call-start
  7.2 1.1 shard_map.136
  8.3 4.9 %collective-permute-start = (bf16[16,256]{1,0:T(8,128)(2,1)S(1)}, bf16[16,256]{1,0:T(8,128)(2,1)S(1)}, u32[]{:S(2)}, u32[]{:S(2)}) collective-permute-start(bf16[16,256]{1,0:T(8,128)(2,1)S(1)} %get-tuple-element.24), channel_id=1, source_target_pairs={{0,1},{1,2},{2,3},{3,4},{4,5},{5,6},{6,7},{7,8},{8,9},{9,10},{10,1... | collective-permute-start | bytes 24584 | tf_op jit(solution)/shard_map/ppermute | solution.py:387
  13.2 1.9 %collective-permute-start.1 = (bf16[16,256]{1,0:T(8,128)(2,1)S(1)}, bf16[16,256]{1,0:T(8,128)(2,1)S(1)}, u32[]{:S(2)}, u32[]{:S(2)}) collective-permute-start(bf16[16,256]{1,0:T(8,128)(2,1)S(1)} %get-tuple-element.25), channel_id=1, source_target_pairs={{1,0},{2,1},{3,2},{4,3},{5,4},{6,5},{7,6},{8,7},{9,8},{10,9},{11,1... | collective-permute-start | bytes 24584 | tf_op jit(solution)/shard_map/ppermute | solution.py:388
  15.2 3.0 %collective-permute-done.1.refs_2_ = bf16[16,256]{1,0:T(8,128)(2,1)S(1)} collective-permute-done((bf16[16,256]{1,0:T(8,128)(2,1)S(1)}, bf16[16,256]{1,0:T(8,128)(2,1)S(1)}, u32[]{:S(2)}, u32[]{:S(2)}) %collective-permute-start.1) | collective-permute-done | bytes 8224 | tf_op jit(solution)/shard_map/ppermute | solution.py:388
  18.2 4.4 %shard_map.137 = (bf16[512,384]{1,0:T(8,128)(2,1)}, bf16[256,256]{1,0:T(8,128)(2,1)}) custom-call(bf16[128,256]{1,0:T(8,128)(2,1)} %refs_0_.3, bf16[16,256]{1,0:T(8,128)(2,1)S(1)} %collective-permute-done.refs_1_, bf16[16,256]{1,0:T(8,128)(2,1)S(1)} %collective-permute-done.1.refs_2_, s32[27,128]{1,0:T(8,128)} %bitcast.12, s32[1,128]{1,0:T(1,128)} %bitcast.14, ...), custom_call_target="tpu_custom_call" | custom-call | flops 3300000000 | bytes 262144 | tf_op jit(solution)/shard_map/pallas_call | solution.py:112
  22.6 23.6 %all_to_all.15 = bf16[32,16,384]{2,1,0:T(8,128)(2,1)S(1)} all-to-all(bf16[32,16,384]{2,1,0:T(8,128)(2,1)} %bitcast.10), channel_id=1, replica_groups={{0,2,4,6,8,10,12,14,16,18,20,22,24,26,28,30,32,34,36,38,40,42,44,46,48,..., dimensions={0} | all-to-all | bytes 786432 | tf_op jit(solution)/shard_map/all_to_all | solution.py:397
  46.2 2.4 %collective-permute-start.2 = (bf16[512,384]{1,0:T(8,128)(2,1)S(1)}, bf16[512,384]{1,0:T(8,128)(2,1)S(1)}, u32[]{:S(2)}, u32[]{:S(2)}) collective-permute-start(bf16[512,384]{1,0:T(8,128)(2,1)S(1)} %bitcast.7), channel_id=1, source_target_pairs={{0,1},{1,0},{2,3},{3,2},{4,5},{5,4},{6,7},{7,6},{8,9},{9,8},{10,11... | collective-permute-start | bytes 1179656 | tf_op jit(solution)/shard_map/ppermute | solution.py:401
  48.7 0.0 all-gather.3.cloned.1.call-update
  48.7 1.3 collective-permute-done.2.refs_1_
  50.0 6.8 %shard_map.138 = (bf16[32,32,256]{2,1,0:T(8,128)(2,1)}, f32[1,256]{1,0:T(1,128)}) custom-call(bf16[512,384]{1,0:T(8,128)(2,1)S(1)} %bitcast.8, bf16[512,384]{1,0:T(8,128)(2,1)S(1)} %collective-permute-done.2.refs_1_, bf16[256,768]{1,0:T(8,128)(2,1)S(1)} %copy-done, bf16[256,256]{1,0:T(8,128)(2,1)S(1)} %copy-done.1, f32[1,256]{1,0:T(1,128)S(1)} %bitcast.9), custom_call_target="tpu_custom_call" | custom-call | flops 6600000000 | bytes 262144 | tf_op jit(solution)/shard_map/pallas_call | solution.py:112
  56.8 19.4 %all_to_all.16.refs_0_ = bf16[32,32,256]{2,1,0:T(8,128)(2,1)} all-to-all(bf16[32,32,256]{2,1,0:T(8,128)(2,1)} %get-tuple-element.27), channel_id=1, replica_groups={{0,2,4,6,8,10,12,14,16,18,20,22,24,26,28,30,32,34,36,38,40,42,44,46,48,..., dimensions={0} | all-to-all | bytes 1048576 | tf_op jit(solution)/shard_map/all_to_all | solution.py:413
  76.3 2.7 %shard_map.139 = (bf16[128,256]{1,0:T(8,128)(2,1)}, bf16[144,256]{1,0:T(8,128)(2,1)}, bf16[16,256]{1,0:T(8,128)(2,1)}) custom-call(bf16[32,32,256]{2,1,0:T(8,128)(2,1)} %all_to_all.16.refs_0_, s32[1,128]{1,0:T(1,128)} %bitcast.15, f32[1,256]{1,0:T(1,128)} %get-tuple-element.28.refs_2_), custom_call_target="tpu_custom_call" | custom-call | flops 1650000000 | bytes 262144 | tf_op jit(solution)/shard_map/pallas_call | solution.py:112
  79.0 2.0 %collective-permute-start.10 = (bf16[144,256]{1,0:T(8,128)(2,1)}, bf16[144,256]{1,0:T(8,128)(2,1)S(1)}, u32[]{:S(2)}, u32[]{:S(2)}) collective-permute-start(bf16[144,256]{1,0:T(8,128)(2,1)} %get-tuple-element.30.refs_0_.refs_5_), channel_id=1, source_target_pairs={{0,48},{1,49},{2,50},{3,51},{4,52},{5,53},{6,54},{7,55},{8,56},{9,... | collective-permute-start | bytes 221192 | tf_op jit(solution)/shard_map/ppermute | solution.py:36
  81.0 0.2 collective-permute-start.9
  81.3 0.7 collective-permute-start.8
  81.9 2.7 %collective-permute-start.7 = (bf16[16,256]{1,0:T(8,128)(2,1)}, bf16[16,256]{1,0:T(8,128)(2,1)S(1)}, u32[]{:S(2)}, u32[]{:S(2)}) collective-permute-start(bf16[16,256]{1,0:T(8,128)(2,1)} %get-tuple-element.35.refs_1_), channel_id=1, source_target_pairs={{0,192},{64,0},{128,64},{192,128},{1,193},{65,1},{129,65},{193,129... | collective-permute-start | bytes 24584 | tf_op jit(solution)/shard_map/ppermute | solution.py:46
  84.7 0.4 collective-permute-start.6
  85.0 0.7 collective-permute-done.7.refs_4_
  85.7 0.3 collective-permute-start.5
  85.9 3.2 %collective-permute-done.6.refs_3_ = bf16[16,256]{1,0:T(8,128)(2,1)S(1)} collective-permute-done((bf16[16,256]{1,0:T(8,128)(2,1)}, bf16[16,256]{1,0:T(8,128)(2,1)S(1)}, u32[]{:S(2)}, u32[]{:S(2)}) %collective-permute-start.6) | collective-permute-done | bytes 8224 | tf_op jit(solution)/shard_map/ppermute | solution.py:46
  89.2 5.1 %collective-permute-start.11 = (bf16[144,256]{1,0:T(8,128)(2,1)}, bf16[144,256]{1,0:T(8,128)(2,1)S(1)}, u32[]{:S(2)}, u32[]{:S(2)}) collective-permute-start(bf16[144,256]{1,0:T(8,128)(2,1)} %get-tuple-element.30.refs_0_.refs_5_), channel_id=1, source_target_pairs={{0,1},{1,0},{2,3},{3,2},{4,5},{5,4},{6,7},{7,6},{8,9},{9,8},{10,11... | collective-permute-start | bytes 221192 | tf_op jit(solution)/shard_map/ppermute | solution.py:41
  94.2 0.0 collective-permute-done.10.refs_8_
  94.2 0.1 collective-permute-start.14
  94.3 0.4 collective-permute-start.13
  94.7 0.0 collective-permute-done.8.refs_6_
  94.8 0.1 collective-permute-start.12
  94.9 4.1 %shard_map.140 = (f32[128,256]{1,0:T(8,128)}, bf16[16,256]{1,0:T(8,128)(2,1)}, bf16[16,256]{1,0:T(8,128)(2,1)}) custom-call(bf16[144,256]{1,0:T(8,128)(2,1)} %get-tuple-element.30.refs_0_.refs_5_, s32[27,128]{1,0:T(8,128)} %bitcast.13, bf16[6912,256]{1,0:T(8,128)(2,1)} %refs_2_.3), custom_call_target="tpu_custom_call" | custom-call | flops 4400000000 | bytes 262144 | tf_op jit(solution)/shard_map/pallas_call | solution.py:112
  99.0 0.0 all-gather.3.cloned.1.call-done
  99.1 0.0 collective-permute-done.5.refs_2_
  99.1 0.0 collective-permute-done.11.refs_9_
  99.1 0.0 copy-start.9
  99.1 0.0 collective-permute-done.14.refs_12_
  99.1 0.0 collective-permute-done.13.refs_11_
  99.2 0.5 copy-done.15
  99.7 0.1 copy-done.9
  99.7 0.0 copy-done.10
  99.8 0.0 copy-done.11
  99.8 0.0 copy-done.12
  99.8 0.9 copy-done.4
  100.7 5.6 %shard_map.142 = bf16[8,128,256]{2,1,0:T(8,128)(2,1)} custom-call(bf16[8,256,256]{2,1,0:T(8,128)(2,1)} %bitcast.11, bf16[16,256]{1,0:T(8,128)(2,1)} %get-tuple-element.35.refs_1_, bf16[16,256]{1,0:T(8,128)(2,1)} %copy-done.15, bf16[16,256]{1,0:T(8,128)(2,1)} %copy-done.14, bf16[16,256]{1,0:T(8,128)(2,1)} %copy-done.13, ...), custom_call_target="tpu_custom_call" | custom-call | flops 5500000256 | bytes 262144 | tf_op jit(solution)/shard_map/pallas_call | solution.py:112
  106.3 3.9 %all-to-all-start.2 = ((bf16[8,128,256]{2,1,0:T(8,128)(2,1)}), bf16[8,128,256]{2,1,0:T(8,128)(2,1)S(1)}, u32[]{:S(2)}, u32[]{:S(2)}) async-start(bf16[8,128,256]{2,1,0:T(8,128)(2,1)} %shard_map.142), calls=%async_computation.2 | async-start | bytes 1048576 | tf_op jit(solution)/shard_map/all_to_all | solution.py:449
  110.2 4.2 %collective-permute-start.3 = (bf16[16,256]{1,0:T(8,128)(2,1)S(1)}, bf16[16,256]{1,0:T(8,128)(2,1)S(1)}, u32[]{:S(2)}, u32[]{:S(2)}) collective-permute-start(bf16[16,256]{1,0:T(8,128)(2,1)S(1)} %copy-done.17), channel_id=1, source_target_pairs={{0,1},{1,2},{2,3},{3,4},{4,5},{5,6},{6,7},{7,8},{8,9},{9,10},{10,1... | collective-permute-start | bytes 24584 | tf_op jit(solution)/shard_map/ppermute | solution.py:432
  114.4 1.9 %collective-permute-start.4 = (bf16[16,256]{1,0:T(8,128)(2,1)S(1)}, bf16[16,256]{1,0:T(8,128)(2,1)S(1)}, u32[]{:S(2)}, u32[]{:S(2)}) collective-permute-start(bf16[16,256]{1,0:T(8,128)(2,1)S(1)} %copy-done.16), channel_id=1, source_target_pairs={{1,0},{2,1},{3,2},{4,3},{5,4},{6,5},{7,6},{8,7},{9,8},{10,9},{11,1... | collective-permute-start | bytes 24584 | tf_op jit(solution)/shard_map/ppermute | solution.py:431
  116.4 2.6 %collective-permute-done.3.refs_1_ = bf16[16,256]{1,0:T(8,128)(2,1)S(1)} collective-permute-done((bf16[16,256]{1,0:T(8,128)(2,1)S(1)}, bf16[16,256]{1,0:T(8,128)(2,1)S(1)}, u32[]{:S(2)}, u32[]{:S(2)}) %collective-permute-start.3) | collective-permute-done | bytes 8224 | tf_op jit(solution)/shard_map/ppermute | solution.py:432
  118.9 5.3 %collective-permute-done.4.refs_2_ = bf16[16,256]{1,0:T(8,128)(2,1)S(1)} collective-permute-done((bf16[16,256]{1,0:T(8,128)(2,1)S(1)}, bf16[16,256]{1,0:T(8,128)(2,1)S(1)}, u32[]{:S(2)}, u32[]{:S(2)}) %collective-permute-start.4) | collective-permute-done | bytes 8224 | tf_op jit(solution)/shard_map/ppermute | solution.py:431
  124.2 0.6 copy-done.19
  124.8 1.7 %shard_map.141.refs_1_ = bf16[128,256]{1,0:T(8,128)(2,1)} custom-call(f32[128,256]{1,0:T(8,128)} %get-tuple-element.31.refs_0_.refs_13_, bf16[16,256]{1,0:T(8,128)(2,1)} %copy-done.18, bf16[16,256]{1,0:T(8,128)(2,1)} %copy-done.19, s32[1,32]{1,0:T(1,128)} %refs_3_.3), custom_call_target="tpu_custom_call" | custom-call | flops 1100000000 | bytes 262144 | tf_op jit(solution)/shard_map/pallas_call | solution.py:112
  126.5 1.6 %all-to-all-done.2.refs_0_ = bf16[8,128,256]{2,1,0:T(8,128)(2,1)S(1)} async-done(((bf16[8,128,256]{2,1,0:T(8,128)(2,1)}), bf16[8,128,256]{2,1,0:T(8,128)(2,1)S(1)}, u32[]{:S(2)}, u32[]{:S(2)}) %all-to-all-start.2) | async-done | bytes 524320 | tf_op jit(solution)/shard_map/all_to_all | solution.py:449
  128.2 0.8 copy-done.5
  129.0 0.8 copy-done.3
  129.8 1.1 shard_map.143
  130.9 2.9 %collective-permute-start.20 = (bf16[128,256]{1,0:T(8,128)(2,1)S(1)}, bf16[128,256]{1,0:T(8,128)(2,1)S(1)}, u32[]{:S(2)}, u32[]{:S(2)}) collective-permute-start(bf16[128,256]{1,0:T(8,128)(2,1)S(1)} %get-tuple-element.37.refs_4_), channel_id=1, source_target_pairs={{0,48},{1,49},{2,50},{3,51},{4,52},{5,53},{6,54},{7,55},{8,56},{9,... | collective-permute-start | bytes 196616 | tf_op jit(solution)/shard_map/ppermute | solution.py:36
  133.8 0.5 collective-permute-start.19
  134.3 0.6 collective-permute-start.18
  134.9 0.5 collective-permute-start.17
  135.4 0.4 collective-permute-start.16
  135.8 2.1 %collective-permute-done.17.refs_3_ = bf16[112,256]{1,0:T(8,128)(2,1)S(1)} collective-permute-done((bf16[112,256]{1,0:T(8,128)(2,1)S(1)}, bf16[112,256]{1,0:T(8,128)(2,1)S(1)}, u32[]{:S(2)}, u32[]{:S(2)}) %collective-permute-start.17) | collective-permute-done | bytes 57376 | tf_op jit(solution)/shard_map/ppermute | solution.py:46
  138.0 2.6 %collective-permute-start.21 = (bf16[128,256]{1,0:T(8,128)(2,1)S(1)}, bf16[128,256]{1,0:T(8,128)(2,1)S(1)}, u32[]{:S(2)}, u32[]{:S(2)}) collective-permute-start(bf16[128,256]{1,0:T(8,128)(2,1)S(1)} %get-tuple-element.37.refs_4_), channel_id=1, source_target_pairs={{0,1},{1,0},{2,3},{3,2},{4,5},{5,4},{6,7},{7,6},{8,9},{9,8},{10,11... | collective-permute-start | bytes 196616 | tf_op jit(solution)/shard_map/ppermute | solution.py:41
  140.5 0.0 collective-permute-start.24
  140.5 0.5 collective-permute-start.23
  141.1 0.2 collective-permute-start.22
  141.2 4.2 %collective-permute-done.15.refs_1_ = bf16[112,256]{1,0:T(8,128)(2,1)S(1)} collective-permute-done((bf16[112,256]{1,0:T(8,128)(2,1)S(1)}, bf16[112,256]{1,0:T(8,128)(2,1)S(1)}, u32[]{:S(2)}, u32[]{:S(2)}) %collective-permute-start.15) | collective-permute-done | bytes 57376 | tf_op jit(solution)/shard_map/ppermute | solution.py:46
  145.5 1.1 shard_map.144
  (42 shorter events, 0.1 us)
Async XLA Ops:
  7.2 91.9 %all-gather.3.cloned.1.call-start = ((), (), s32[]{:S(2)}) async-start(), calls=%async_computation.3 | async-start | bytes 1179648 | tf_op jit(solution)/shard_map/all_gather | solution.py:396
  8.3 6.9 %collective-permute-start = (bf16[16,256]{1,0:T(8,128)(2,1)S(1)}, bf16[16,256]{1,0:T(8,128)(2,1)S(1)}, u32[]{:S(2)}, u32[]{:S(2)}) collective-permute-start(bf16[16,256]{1,0:T(8,128)(2,1)S(1)} %get-tuple-element.24), channel_id=1, source_target_pairs={{0,1},{1,2},{2,3},{3,4},{4,5},{5,6},{6,7},{7,8},{8,9},{9,10},{10,1... | collective-permute-start | bytes 24584 | tf_op jit(solution)/shard_map/ppermute | solution.py:387
  13.2 5.0 %collective-permute-start.1 = (bf16[16,256]{1,0:T(8,128)(2,1)S(1)}, bf16[16,256]{1,0:T(8,128)(2,1)S(1)}, u32[]{:S(2)}, u32[]{:S(2)}) collective-permute-start(bf16[16,256]{1,0:T(8,128)(2,1)S(1)} %get-tuple-element.25), channel_id=1, source_target_pairs={{1,0},{2,1},{3,2},{4,3},{5,4},{6,5},{7,6},{8,7},{9,8},{10,9},{11,1... | collective-permute-start | bytes 24584 | tf_op jit(solution)/shard_map/ppermute | solution.py:388
  18.2 31.8 %copy-start = (bf16[256,768]{1,0:T(8,128)(2,1)S(1)}, bf16[256,768]{1,0:T(8,128)(2,1)}, u32[]{:S(2)}) copy-start(bf16[256,768]{1,0:T(8,128)(2,1)} %refs_2_.2) | copy-start | bytes 1179652
  18.2 31.8 %copy-start.1 = (bf16[256,256]{1,0:T(8,128)(2,1)S(1)}, bf16[256,256]{1,0:T(8,128)(2,1)}, u32[]{:S(2)}) copy-start(bf16[256,256]{1,0:T(8,128)(2,1)} %refs_3_.2) | copy-start | bytes 393220
  18.2 31.8 %copy-start.2 = (f32[256]{0:T(256)S(1)}, f32[256]{0:T(256)}, u32[]{:S(2)}) copy-start(f32[256]{0:T(256)} %param.17) | copy-start | bytes 3076
  46.2 3.8 %collective-permute-start.2 = (bf16[512,384]{1,0:T(8,128)(2,1)S(1)}, bf16[512,384]{1,0:T(8,128)(2,1)S(1)}, u32[]{:S(2)}, u32[]{:S(2)}) collective-permute-start(bf16[512,384]{1,0:T(8,128)(2,1)S(1)} %bitcast.7), channel_id=1, source_target_pairs={{0,1},{1,0},{2,3},{3,2},{4,5},{5,4},{6,7},{7,6},{8,9},{9,8},{10,11... | collective-permute-start | bytes 1179656 | tf_op jit(solution)/shard_map/ppermute | solution.py:401
  79.0 15.2 %collective-permute-start.10 = (bf16[144,256]{1,0:T(8,128)(2,1)}, bf16[144,256]{1,0:T(8,128)(2,1)S(1)}, u32[]{:S(2)}, u32[]{:S(2)}) collective-permute-start(bf16[144,256]{1,0:T(8,128)(2,1)} %get-tuple-element.30.refs_0_.refs_5_), channel_id=1, source_target_pairs={{0,48},{1,49},{2,50},{3,51},{4,52},{5,53},{6,54},{7,55},{8,56},{9,... | collective-permute-start | bytes 221192 | tf_op jit(solution)/shard_map/ppermute | solution.py:36
  81.0 13.3 %collective-permute-start.9 = (bf16[144,256]{1,0:T(8,128)(2,1)}, bf16[144,256]{1,0:T(8,128)(2,1)S(1)}, u32[]{:S(2)}, u32[]{:S(2)}) collective-permute-start(bf16[144,256]{1,0:T(8,128)(2,1)} %get-tuple-element.30.refs_0_.refs_5_), channel_id=1, source_target_pairs={{0,32},{1,33},{2,34},{3,35},{4,36},{5,37},{6,38},{7,39},{8,40},{9,... | collective-permute-start | bytes 221192 | tf_op jit(solution)/shard_map/ppermute | solution.py:36
  81.3 13.5 %collective-permute-start.8 = (bf16[144,256]{1,0:T(8,128)(2,1)}, bf16[144,256]{1,0:T(8,128)(2,1)S(1)}, u32[]{:S(2)}, u32[]{:S(2)}) collective-permute-start(bf16[144,256]{1,0:T(8,128)(2,1)} %get-tuple-element.30.refs_0_.refs_5_), channel_id=1, source_target_pairs={{0,16},{1,17},{2,18},{3,19},{4,20},{5,21},{6,22},{7,23},{8,24},{9,... | collective-permute-start | bytes 221192 | tf_op jit(solution)/shard_map/ppermute | solution.py:36
  81.9 3.7 %collective-permute-start.7 = (bf16[16,256]{1,0:T(8,128)(2,1)}, bf16[16,256]{1,0:T(8,128)(2,1)S(1)}, u32[]{:S(2)}, u32[]{:S(2)}) collective-permute-start(bf16[16,256]{1,0:T(8,128)(2,1)} %get-tuple-element.35.refs_1_), channel_id=1, source_target_pairs={{0,192},{64,0},{128,64},{192,128},{1,193},{65,1},{129,65},{193,129... | collective-permute-start | bytes 24584 | tf_op jit(solution)/shard_map/ppermute | solution.py:46
  84.7 4.5 %collective-permute-start.6 = (bf16[16,256]{1,0:T(8,128)(2,1)}, bf16[16,256]{1,0:T(8,128)(2,1)S(1)}, u32[]{:S(2)}, u32[]{:S(2)}) collective-permute-start(bf16[16,256]{1,0:T(8,128)(2,1)} %get-tuple-element.35.refs_1_), channel_id=1, source_target_pairs={{0,128},{64,192},{128,0},{192,64},{1,129},{65,193},{129,1},{193,65... | collective-permute-start | bytes 24584 | tf_op jit(solution)/shard_map/ppermute | solution.py:46
  85.7 13.3 %copy-start.13 = (bf16[16,256]{1,0:T(8,128)(2,1)}, bf16[16,256]{1,0:T(8,128)(2,1)S(1)}, u32[]{:S(2)}) copy-start(bf16[16,256]{1,0:T(8,128)(2,1)S(1)} %collective-permute-done.7.refs_4_) | copy-start | bytes 24580
  85.7 13.4 %collective-permute-start.5 = (bf16[16,256]{1,0:T(8,128)(2,1)}, bf16[16,256]{1,0:T(8,128)(2,1)S(1)}, u32[]{:S(2)}, u32[]{:S(2)}) collective-permute-start(bf16[16,256]{1,0:T(8,128)(2,1)} %get-tuple-element.35.refs_1_), channel_id=1, source_target_pairs={{0,64},{64,128},{128,192},{192,0},{1,65},{65,129},{129,193},{193,1... | collective-permute-start | bytes 24584 | tf_op jit(solution)/shard_map/ppermute | solution.py:46
  89.2 9.8 %copy-start.14 = (bf16[16,256]{1,0:T(8,128)(2,1)}, bf16[16,256]{1,0:T(8,128)(2,1)S(1)}, u32[]{:S(2)}) copy-start(bf16[16,256]{1,0:T(8,128)(2,1)S(1)} %collective-permute-done.6.refs_3_) | copy-start | bytes 24580
  89.2 9.9 %collective-permute-start.11 = (bf16[144,256]{1,0:T(8,128)(2,1)}, bf16[144,256]{1,0:T(8,128)(2,1)S(1)}, u32[]{:S(2)}, u32[]{:S(2)}) collective-permute-start(bf16[144,256]{1,0:T(8,128)(2,1)} %get-tuple-element.30.refs_0_.refs_5_), channel_id=1, source_target_pairs={{0,1},{1,0},{2,3},{3,2},{4,5},{5,4},{6,7},{7,6},{8,9},{9,8},{10,11... | collective-permute-start | bytes 221192 | tf_op jit(solution)/shard_map/ppermute | solution.py:41
  94.2 4.8 %copy-start.6 = (bf16[144,256]{1,0:T(8,128)(2,1)}, bf16[144,256]{1,0:T(8,128)(2,1)S(1)}, u32[]{:S(2)}) copy-start(bf16[144,256]{1,0:T(8,128)(2,1)S(1)} %collective-permute-done.10.refs_8_) | copy-start | bytes 221188
  94.2 4.9 %collective-permute-start.14 = (bf16[144,256]{1,0:T(8,128)(2,1)S(1)}, bf16[144,256]{1,0:T(8,128)(2,1)S(1)}, u32[]{:S(2)}, u32[]{:S(2)}) collective-permute-start(bf16[144,256]{1,0:T(8,128)(2,1)S(1)} %collective-permute-done.10.refs_8_), channel_id=1, source_target_pairs={{0,1},{1,0},{2,3},{3,2},{4,5},{5,4},{6,7},{7,6},{8,9},{9,8},{10,11... | collective-permute-start | bytes 221192 | tf_op jit(solution)/shard_map/ppermute | solution.py:41
  94.3 4.7 %copy-start.7 = (bf16[144,256]{1,0:T(8,128)(2,1)}, bf16[144,256]{1,0:T(8,128)(2,1)S(1)}, u32[]{:S(2)}) copy-start(bf16[144,256]{1,0:T(8,128)(2,1)S(1)} %collective-permute-done.9.refs_7_) | copy-start | bytes 221188
  94.3 4.8 %collective-permute-start.13 = (bf16[144,256]{1,0:T(8,128)(2,1)S(1)}, bf16[144,256]{1,0:T(8,128)(2,1)S(1)}, u32[]{:S(2)}, u32[]{:S(2)}) collective-permute-start(bf16[144,256]{1,0:T(8,128)(2,1)S(1)} %collective-permute-done.9.refs_7_), channel_id=1, source_target_pairs={{0,1},{1,0},{2,3},{3,2},{4,5},{5,4},{6,7},{7,6},{8,9},{9,8},{10,11... | collective-permute-start | bytes 221192 | tf_op jit(solution)/shard_map/ppermute | solution.py:41
  94.8 4.3 %copy-start.8 = (bf16[144,256]{1,0:T(8,128)(2,1)}, bf16[144,256]{1,0:T(8,128)(2,1)S(1)}, u32[]{:S(2)}) copy-start(bf16[144,256]{1,0:T(8,128)(2,1)S(1)} %collective-permute-done.8.refs_6_) | copy-start | bytes 221188
  94.8 4.4 %collective-permute-start.12 = (bf16[144,256]{1,0:T(8,128)(2,1)S(1)}, bf16[144,256]{1,0:T(8,128)(2,1)S(1)}, u32[]{:S(2)}, u32[]{:S(2)}) collective-permute-start(bf16[144,256]{1,0:T(8,128)(2,1)S(1)} %collective-permute-done.8.refs_6_), channel_id=1, source_target_pairs={{0,1},{1,0},{2,3},{3,2},{4,5},{5,4},{6,7},{7,6},{8,9},{9,8},{10,11... | collective-permute-start | bytes 221192 | tf_op jit(solution)/shard_map/ppermute | solution.py:41
  99.1 0.6 copy-start.15
  99.1 0.6 copy-start.9
  99.1 0.6 copy-start.10
  99.1 0.6 copy-start.11
  99.2 0.6 copy-start.12
  99.8 0.9 copy-start.4
  100.7 9.5 %copy-start.17 = (bf16[16,256]{1,0:T(8,128)(2,1)S(1)}, bf16[16,256]{1,0:T(8,128)(2,1)}, u32[]{:S(2)}) copy-start(bf16[16,256]{1,0:T(8,128)(2,1)} %get-tuple-element.32) | copy-start | bytes 24580
  100.7 13.7 %copy-start.16 = (bf16[16,256]{1,0:T(8,128)(2,1)S(1)}, bf16[16,256]{1,0:T(8,128)(2,1)}, u32[]{:S(2)}) copy-start(bf16[16,256]{1,0:T(8,128)(2,1)} %get-tuple-element.33) | copy-start | bytes 24580
  106.3 21.8 %all-to-all-start.2 = ((bf16[8,128,256]{2,1,0:T(8,128)(2,1)}), bf16[8,128,256]{2,1,0:T(8,128)(2,1)S(1)}, u32[]{:S(2)}, u32[]{:S(2)}) async-start(bf16[8,128,256]{2,1,0:T(8,128)(2,1)} %shard_map.142), calls=%async_computation.2 | async-start | bytes 1048576 | tf_op jit(solution)/shard_map/all_to_all | solution.py:449
  110.2 8.7 %collective-permute-start.3 = (bf16[16,256]{1,0:T(8,128)(2,1)S(1)}, bf16[16,256]{1,0:T(8,128)(2,1)S(1)}, u32[]{:S(2)}, u32[]{:S(2)}) collective-permute-start(bf16[16,256]{1,0:T(8,128)(2,1)S(1)} %copy-done.17), channel_id=1, source_target_pairs={{0,1},{1,2},{2,3},{3,4},{4,5},{5,6},{6,7},{7,8},{8,9},{9,10},{10,1... | collective-permute-start | bytes 24584 | tf_op jit(solution)/shard_map/ppermute | solution.py:432
  114.4 9.8 %collective-permute-start.4 = (bf16[16,256]{1,0:T(8,128)(2,1)S(1)}, bf16[16,256]{1,0:T(8,128)(2,1)S(1)}, u32[]{:S(2)}, u32[]{:S(2)}) collective-permute-start(bf16[16,256]{1,0:T(8,128)(2,1)S(1)} %copy-done.16), channel_id=1, source_target_pairs={{1,0},{2,1},{3,2},{4,3},{5,4},{6,5},{7,6},{8,7},{9,8},{10,9},{11,1... | collective-permute-start | bytes 24584 | tf_op jit(solution)/shard_map/ppermute | solution.py:431
  118.9 5.3 %copy-start.18 = (bf16[16,256]{1,0:T(8,128)(2,1)}, bf16[16,256]{1,0:T(8,128)(2,1)S(1)}, u32[]{:S(2)}) copy-start(bf16[16,256]{1,0:T(8,128)(2,1)S(1)} %collective-permute-done.3.refs_1_) | copy-start | bytes 24580
  124.2 0.6 copy-start.19
  128.2 0.8 copy-start.5
  128.9 0.8 copy-start.3
  130.9 9.6 %collective-permute-start.20 = (bf16[128,256]{1,0:T(8,128)(2,1)S(1)}, bf16[128,256]{1,0:T(8,128)(2,1)S(1)}, u32[]{:S(2)}, u32[]{:S(2)}) collective-permute-start(bf16[128,256]{1,0:T(8,128)(2,1)S(1)} %get-tuple-element.37.refs_4_), channel_id=1, source_target_pairs={{0,48},{1,49},{2,50},{3,51},{4,52},{5,53},{6,54},{7,55},{8,56},{9,... | collective-permute-start | bytes 196616 | tf_op jit(solution)/shard_map/ppermute | solution.py:36
  133.8 6.7 %collective-permute-start.19 = (bf16[128,256]{1,0:T(8,128)(2,1)S(1)}, bf16[128,256]{1,0:T(8,128)(2,1)S(1)}, u32[]{:S(2)}, u32[]{:S(2)}) collective-permute-start(bf16[128,256]{1,0:T(8,128)(2,1)S(1)} %get-tuple-element.37.refs_4_), channel_id=1, source_target_pairs={{0,32},{1,33},{2,34},{3,35},{4,36},{5,37},{6,38},{7,39},{8,40},{9,... | collective-permute-start | bytes 196616 | tf_op jit(solution)/shard_map/ppermute | solution.py:36
  134.3 6.7 %collective-permute-start.18 = (bf16[128,256]{1,0:T(8,128)(2,1)S(1)}, bf16[128,256]{1,0:T(8,128)(2,1)S(1)}, u32[]{:S(2)}, u32[]{:S(2)}) collective-permute-start(bf16[128,256]{1,0:T(8,128)(2,1)S(1)} %get-tuple-element.37.refs_4_), channel_id=1, source_target_pairs={{0,16},{1,17},{2,18},{3,19},{4,20},{5,21},{6,22},{7,23},{8,24},{9,... | collective-permute-start | bytes 196616 | tf_op jit(solution)/shard_map/ppermute | solution.py:36
  134.9 3.0 %collective-permute-start.17 = (bf16[112,256]{1,0:T(8,128)(2,1)S(1)}, bf16[112,256]{1,0:T(8,128)(2,1)S(1)}, u32[]{:S(2)}, u32[]{:S(2)}) collective-permute-start(bf16[112,256]{1,0:T(8,128)(2,1)S(1)} %get-tuple-element.36.refs_0_), channel_id=1, source_target_pairs={{0,192},{64,0},{128,64},{192,128},{1,193},{65,1},{129,65},{193,129... | collective-permute-start | bytes 172040 | tf_op jit(solution)/shard_map/ppermute | solution.py:46
  135.4 5.8 %collective-permute-start.16 = (bf16[112,256]{1,0:T(8,128)(2,1)S(1)}, bf16[112,256]{1,0:T(8,128)(2,1)S(1)}, u32[]{:S(2)}, u32[]{:S(2)}) collective-permute-start(bf16[112,256]{1,0:T(8,128)(2,1)S(1)} %get-tuple-element.36.refs_0_), channel_id=1, source_target_pairs={{0,128},{64,192},{128,0},{192,64},{1,129},{65,193},{129,1},{193,65... | collective-permute-start | bytes 172040 | tf_op jit(solution)/shard_map/ppermute | solution.py:46
  138.0 7.5 %collective-permute-start.21 = (bf16[128,256]{1,0:T(8,128)(2,1)S(1)}, bf16[128,256]{1,0:T(8,128)(2,1)S(1)}, u32[]{:S(2)}, u32[]{:S(2)}) collective-permute-start(bf16[128,256]{1,0:T(8,128)(2,1)S(1)} %get-tuple-element.37.refs_4_), channel_id=1, source_target_pairs={{0,1},{1,0},{2,3},{3,2},{4,5},{5,4},{6,7},{7,6},{8,9},{9,8},{10,11... | collective-permute-start | bytes 196616 | tf_op jit(solution)/shard_map/ppermute | solution.py:41
  140.5 4.9 %collective-permute-start.24 = (bf16[128,256]{1,0:T(8,128)(2,1)S(1)}, bf16[128,256]{1,0:T(8,128)(2,1)S(1)}, u32[]{:S(2)}, u32[]{:S(2)}) collective-permute-start(bf16[128,256]{1,0:T(8,128)(2,1)S(1)} %collective-permute-done.20.refs_7_), channel_id=1, source_target_pairs={{0,1},{1,0},{2,3},{3,2},{4,5},{5,4},{6,7},{7,6},{8,9},{9,8},{10,11... | collective-permute-start | bytes 196616 | tf_op jit(solution)/shard_map/ppermute | solution.py:41
  140.5 4.9 %collective-permute-start.23 = (bf16[128,256]{1,0:T(8,128)(2,1)S(1)}, bf16[128,256]{1,0:T(8,128)(2,1)S(1)}, u32[]{:S(2)}, u32[]{:S(2)}) collective-permute-start(bf16[128,256]{1,0:T(8,128)(2,1)S(1)} %collective-permute-done.19.refs_6_), channel_id=1, source_target_pairs={{0,1},{1,0},{2,3},{3,2},{4,5},{5,4},{6,7},{7,6},{8,9},{9,8},{10,11... | collective-permute-start | bytes 196616 | tf_op jit(solution)/shard_map/ppermute | solution.py:41
  141.1 4.4 %collective-permute-start.22 = (bf16[128,256]{1,0:T(8,128)(2,1)S(1)}, bf16[128,256]{1,0:T(8,128)(2,1)S(1)}, u32[]{:S(2)}, u32[]{:S(2)}) collective-permute-start(bf16[128,256]{1,0:T(8,128)(2,1)S(1)} %collective-permute-done.18.refs_5_), channel_id=1, source_target_pairs={{0,1},{1,0},{2,3},{3,2},{4,5},{5,4},{6,7},{7,6},{8,9},{9,8},{10,11... | collective-permute-start | bytes 196616 | tf_op jit(solution)/shard_map/ppermute | solution.py:41
  141.2 4.2 %collective-permute-start.15 = (bf16[112,256]{1,0:T(8,128)(2,1)S(1)}, bf16[112,256]{1,0:T(8,128)(2,1)S(1)}, u32[]{:S(2)}, u32[]{:S(2)}) collective-permute-start(bf16[112,256]{1,0:T(8,128)(2,1)S(1)} %get-tuple-element.36.refs_0_), channel_id=1, source_target_pairs={{0,64},{64,128},{128,192},{192,0},{1,65},{65,129},{129,193},{193,1... | collective-permute-start | bytes 172040 | tf_op jit(solution)/shard_map/ppermute | solution.py:46
Sparse Core Ops, SparseCore 0:
  48.8 23.2 all-gather.2

commit v5 on v4

--- a/solution.py
+++ b/solution.py
@@ -19,18 +19,23 @@
 RIM = 16
 EXT = PTS + 2 * RIM
 SLOTS = 512
-PAY = 256
+AT_GAIN, AT_EXT, AT_TAB, PAY = 128, 144, 304, 320
 MIB = 1024 * 1024
 
 NX, NZ, NC = 4, 8, 2
 Z_GROUPS = [[x * 16 + z * 2 + c for z in range(NZ)] for x in range(NX) for c in range(NC)]
-XC_GROUPS = [[x * 16 + z * 2 + c for x in range(NX) for c in range(NC)] for z in range(NZ)]
+X_GROUPS = [[x * 16 + z * 2 + c for x in range(NX)] for z in range(NZ) for c in range(NC)]
 XZ_GROUPS = [[x * 16 + z * 2 + c for x in range(NX) for z in range(NZ)] for c in range(NC)]
 SWAP = [(i, i ^ 1) for i in range(NX * NZ * NC)]
 UP = [(i, i + 1) for i in range(NX * NZ * NC - 1)]
 DOWN = [(i + 1, i) for i in range(NX * NZ * NC - 1)]
 
 
+def by_chips(copies):
+    near = lax.all_to_all(copies, "gz", split_axis=0, concat_axis=0, axis_index_groups=X_GROUPS, tiled=True)
+    return near, lax.ppermute(near, "gz", SWAP)
+
+
 def along_x(value, d):
     n = NX * NZ * NC
     return lax.ppermute(value, "gz", [(i, (i + 16 * d) % n) for i in range(n)])
@@ -68,10 +73,10 @@
 
 def call(body, out_shape, *args, scratch=(), us=1.0, fetched=(), late=(), idle=(), pinned=(), limit=16):
     fetched = tuple(fetched) + tuple(late)
-    args = [pltpu.with_memory_space_constraint(a, pltpu.HBM) if i in fetched else a for i, a in enumerate(args)]
+    args = [pltpu.with_memory_space_constraint(a, pltpu.HBM) if i in fetched + tuple(idle) else a for i, a in enumerate(args)]
     specs = []
     for i in range(len(args)):
-        space = pltpu.HBM if i in fetched else pl.ANY if i in idle else pltpu.VMEM
+        space = pltpu.HBM if i in fetched + tuple(idle) else pltpu.VMEM
         specs.append(pl.BlockSpec(memory_space=space))
     single = not isinstance(out_shape, (list, tuple))
     outs = [out_shape] if single else list(out_shape)
@@ -149,7 +154,7 @@
     return one_hot(rows == target), one_hot(rows == target + 4)
 
 
-def conv_body(feat_ref, prev_ref, next_ref, nbr_ref, rank_ref, cot_ref, weight, send_ref, pay_ref, ext, tab, wide):
+def conv_body(feat_ref, prev_ref, next_ref, nbr_ref, rank_ref, cot_ref, weight, send_ref, ext, tab, wide):
     weight_ref, weight_here = weight
     ext[:PTS] = feat_ref[...]
     ext[PTS : PTS + RIM] = prev_ref[...]
@@ -158,10 +163,6 @@
     rows = ext[...]
     tab[:OFFS] = nbr_ref[...].astype(F32)
     tab[OFFS:] = jnp.zeros((PTS - OFFS, PTS), F32)
-    pay_ref[:EXT] = rows[:EXT]
-    pay_ref[EXT : EXT + 16, :PTS] = tab[:16].astype(BF)
-    pay_ref[EXT : EXT + 16, PTS:] = tab[16:32].astype(BF)
-    pay_ref[EXT + 16 :] = jnp.zeros((PAY - EXT - 16, FEAT), BF)
     table = jnp.transpose(tab[...])
     lanes = iota((PTS, FEAT), 1).astype(F32)
     for k in range(OFFS):
@@ -271,18 +272,32 @@
     back_ref[:, :16] = back.reshape(32, 16, FEAT)
 
 
-def unpack_body(back_ref, rank_ref, gg_ref, block_ref, grad_ref, dense_ref):
+def unpack_body(
+    back_ref, rank_ref, gg_ref, feat_ref, prev_ref, next_ref, nbr_ref,
+    block_ref, grad_ref, copies_ref, dense_ref,
+):
     first, second = slot_hits(rank_ref[...])
     rows = back_ref[:, :16].reshape(SLOTS, FEAT)
-    grad_ref[:PTS] = t_mm(second, rows).astype(BF)
-    grad_ref[PTS:] = jnp.broadcast_to(gg_ref[...], (16, FEAT)).astype(BF)
+    grad = t_mm(second, rows).astype(BF)
+    gain = jnp.broadcast_to(gg_ref[...], (16, FEAT)).astype(BF)
+    table = nbr_ref[...].astype(F32)
+    table = jnp.concatenate([table, jnp.zeros((32 - OFFS, PTS), F32)], 0).astype(BF)
+    grad_ref[...] = grad
+    for x in range(NX):
+        copies_ref[x, :AT_GAIN] = grad
+        copies_ref[x, AT_GAIN:AT_EXT] = gain
+        copies_ref[x, AT_EXT : AT_EXT + PTS] = feat_ref[...]
+        copies_ref[x, AT_EXT + PTS : AT_EXT + PTS + RIM] = prev_ref[...]
+        copies_ref[x, AT_EXT + PTS + RIM : AT_TAB] = next_ref[...]
+        copies_ref[x, AT_TAB:, :PTS] = table[:16]
+        copies_ref[x, AT_TAB:, PTS:] = table[16:]
     dense_ref[...] = jnp.sum(back_ref[:, 16:].astype(F32), 0).astype(BF)
     block_ref[...] = t_mm(first, rows).astype(BF)
 
 
 def spread_body(grad_ref, nbr_ref, weight, own_ref, down_ref, up_ref, terms, acc):
     weight_ref, weight_here = weight
-    grad = grad_ref[:PTS]
+    grad = grad_ref[...]
     table = nbr_ref[...].astype(F32)
     points = iota((EXT, PTS), 0).astype(F32)
     for k in range(OFFS):
@@ -304,8 +319,7 @@
     out_ref[...] = (own_ref[...] + mm(hit, rims)).astype(BF)
 
 
-def kernel_grad_body(all_ref, p0_ref, p1_ref, p2_ref, p3_ref, *refs):
-    grads, (out_ref, tab, exts, terms, total) = refs[: NX * NC], refs[NX * NC :]
+def kernel_grad_body(p0_ref, p1_ref, p2_ref, p3_ref, near_ref, far_ref, out_ref, tab, exts, terms, total):
     x, core = position()
     base = x * 1728 + core * 108
     first_offset = jnp.minimum(lax.shift_right_logical(base, 8), OFFS - 8)
@@ -313,20 +327,21 @@
     dense = p0_ref[...].astype(F32) + p1_ref[...].astype(F32) + p2_ref[...].astype(F32) + p3_ref[...].astype(F32)
     dense = dense.astype(BF)
     gain = jnp.zeros((1, FEAT), F32)
+    points = iota((EXT, PTS), 0).astype(F32)
     for s in range(NX * NC):
-        source = ((x + NX - s % NX) & (NX - 1)) * NC + (core if s < NX else 1 - core)
-        rows = all_ref[source, EXT : EXT + 16].astype(F32)
+        held = near_ref if s < NX else far_ref
+        rows = held[s % NX, AT_TAB:].astype(F32)
         tab[s * 32 : s * 32 + 16] = rows[:, :PTS]
         tab[s * 32 + 16 : s * 32 + 32] = rows[:, PTS:]
-        exts[s * EXT : (s + 1) * EXT] = all_ref[source, :EXT]
-        gain += grads[s][PTS : PTS + 1].astype(F32)
+        exts[s * EXT : (s + 1) * EXT] = held[s % NX, AT_EXT:AT_TAB]
+        gain += held[s % NX, AT_GAIN : AT_GAIN + 1].astype(F32)
+        hits = [one_hot(points == tab[pl.ds(first_offset + (s * 32 + k), 1), :]) for k in range(8)]
+        found = mm(jnp.concatenate(hits, 0), held[s % NX, :PTS]).astype(BF)
+        for k in range(8):
+            terms[k, s * EXT : (s + 1) * EXT] = found[k * EXT : (k + 1) * EXT]
     ext_t = jnp.transpose(exts[...])
-    points = iota((EXT, PTS), 0).astype(F32)
     for k in range(8):
-        for s in range(NX * NC):
-            hit = one_hot(points == tab[pl.ds(first_offset + (s * 32 + k), 1), :])
-            terms[s * EXT : (s + 1) * EXT] = mm(hit, grads[s][:PTS]).astype(BF)
-        total[k * FEAT : (k + 1) * FEAT] = mm(ext_t, terms[...])
+        total[k * FEAT : (k + 1) * FEAT] = mm(ext_t, terms[k])
     total[8 * FEAT :] = jnp.zeros((16, FEAT), F32)
     at = iota((112, FEAT), 0)
     for z in range(NZ):
@@ -386,14 +401,13 @@
     )
     from_prev = lax.ppermute(to_next, "gz", UP)
     from_next = lax.ppermute(to_prev, "gz", DOWN)
-    send, payload = call(
+    send = call(
         conv_body,
-        [sds((SLOTS, FEAT + PTS)), sds((PAY, FEAT))],
+        sds((SLOTS, FEAT + PTS)),
         features, from_prev, from_next, table, rank_row, cotangent, conv_weight,
         scratch=[pltpu.VMEM((FEAT, FEAT), BF), pltpu.VMEM((PTS, PTS), F32), pltpu.VMEM((PTS, OFFS * FEAT), BF)],
-        fetched=(0, 3, 4, 5), late=(6,), pinned=(0, 1), us=3.0,
-    )
-    everyone = lax.all_gather(payload, "gz", axis_index_groups=XC_GROUPS)
+        fetched=(0, 3, 4, 5), late=(6,), us=3.0,
+    )
     got = lax.all_to_all(
         send.reshape(32, 16, FEAT + PTS), "gz", split_axis=0, concat_axis=0,
         axis_index_groups=XZ_GROUPS, tiled=True,
@@ -408,18 +422,18 @@
         + [pltpu.VMEM((rows, FEAT), BF)] * 4
         + [pltpu.VMEM((rows, FEAT), F32)] * 2
         + [pltpu.VMEM((2 * FEAT, FEAT), BF)],
-        pinned=(0, 1), us=6.0, limit=32,
+        us=6.0, limit=32,
     )
     returned = lax.all_to_all(
         back, "gz", split_axis=0, concat_axis=0, axis_index_groups=XZ_GROUPS, tiled=True
     )
-    block_out, grad, dense = call(
+    block_out, grad, grad_copies, dense = call(
         unpack_body,
-        [sds((PTS, FEAT)), sds((PTS + 16, FEAT)), sds((16, FEAT))],
-        returned, rank_row, grad_gain,
-        fetched=(0, 1, 2), pinned=(1, 2), us=1.5, limit=8,
-    )
-    grads = over_chips(grad)
+        [sds((PTS, FEAT)), sds((PTS, FEAT)), sds((NX, PAY, FEAT)), sds((16, FEAT))],
+        returned, rank_row, grad_gain, features, from_prev, from_next, table,
+        fetched=(1, 3, 6), pinned=(1, 2, 3), us=1.5, limit=8,
+    )
+    near_grads, far_grads = by_chips(grad_copies)
     dense_groups = over_groups(dense)
     own_part, rim_down, rim_up = call(
         spread_body,
@@ -433,25 +447,25 @@
     parts = call(
         kernel_grad_body,
         sds((NZ, 128, FEAT)),
-        everyone, *dense_groups, *grads, own_part,
+        *dense_groups, near_grads, far_grads, own_part,
         scratch=[
             pltpu.VMEM((NX * NC * 32, PTS), F32),
             pltpu.VMEM((NX * NC * EXT, FEAT), BF),
-            pltpu.VMEM((NX * NC * EXT, FEAT), BF),
+            pltpu.VMEM((8, NX * NC * EXT, FEAT), BF),
             pltpu.VMEM((8 * FEAT + 16, FEAT), F32),
         ],
-        fetched=tuple(range(13)), idle=(13,), pinned=(0,), us=5.0,
+        fetched=(0,), idle=(6,), pinned=(0,), us=5.0, limit=24,
     )
     grad_features = call(
         rim_body, sds((PTS, FEAT)), own_part, got_up, got_down, halo_rows,
-        fetched=(0, 1, 2, 3), us=1.0, limit=8,
+        fetched=(0, 3), us=1.0, limit=8,
     )
     z_parts = lax.all_to_all(
         parts, "gz", split_axis=0, concat_axis=0, axis_index_groups=Z_GROUPS, tiled=True
     )
     conv_part, dense_sum = call(
         sum_body, [sds((112, FEAT)), sds((PTS, FEAT))], z_parts, grad_features,
-        fetched=(0,), idle=(1,), us=1.0, limit=8,
+        idle=(1,), us=1.0, limit=8,
     )
     grad_conv, gain_sum, grad_qkv, grad_proj = call(
         lambda *refs: last_body(factor, *refs),

time: 156 us -> 140 us (0.90); the launches traced: 153 us -> 140 us
  between operations: 14.3 us -> 0.82 us
  blocking collectives: 43.1 us -> 53.6 us
  waiting for transfers between devices: 24.2 us -> 18.9 us
  local copies, waits for them, and re-layouts: 3.8 us -> 0.02 us
  Pallas kernels: 28.7 us -> 25.1 us
  starting transfers between devices: 39.4 us -> 41.2 us
    all_to_all x0 -> x1, blocking collectives: none -> 11.1 us  [by_chips(): lax.all_to_all(copies, 'gz', split_axis=0, concat_axis=0, axis_index_grou...]
    ppermute x8 -> x4, starting transfers between devices: 8.93 us -> 3.79 us  [over_chips(): return near + [lax.ppermute(v, 'gz', SWAP) for v in near]]
    ppermute x0 -> x1, starting transfers between devices: none -> 4.71 us  [by_chips(): return (near, lax.ppermute(near, 'gz', SWAP))]
    ppermute x6, waiting for transfers between devices: 10.3 us -> 5.6 us  [over_groups(): lax.ppermute(value, 'grp', [(i, (i + d) % n) for i in range(n)])]
    ppermute x6 -> x3, starting transfers between devices: 6.95 us -> 2.86 us  [along_x(): return lax.ppermute(value, 'gz', [(i, (i + 16 * d) % n) for i in range(n)])]
    ppermute x6, starting transfers between devices: 4.24 us -> 8.17 us  [over_groups(): lax.ppermute(value, 'grp', [(i, (i + d) % n) for i in range(n)])]
    unnamed x40 -> x10, local copies, waits for them, and re-layouts: 3.8 us -> 0.02 us
    pallas_call x9, Pallas kernels: 28.7 us -> 25.1 us  [call(): pl.pallas_call(outer, out_shape=shapes, in_specs=specs, out_specs=[pl.Blo...]
  transfers between devices with their start and end apart: 27 -> 20, of which waited for: 9 -> 7; matrix products, arithmetic and copies ran while one was open for 0% -> 0% of each run, Pallas kernels for 10% -> 4%
where the time goes in v5:
time: 140 us
  blocking collectives  53.6 us (38%)
  starting transfers between devices  41.2 us (29%)
  Pallas kernels  25.1 us (18%)
  waiting for transfers between devices  18.9 us (13%)
    pallas_call x9, Pallas kernels, call(): pl.pallas_call(outer, out_shape=shapes, in_specs=specs, out_specs=[pl.Blo...  25.1 us
    all_to_all x1, blocking collectives, shards(): lax.all_to_all(send.reshape(32, 16, FEAT + PTS), 'gz', split_axis=0, conc...  23.4 us
    all_to_all x1, blocking collectives, shards(): lax.all_to_all(back, 'gz', split_axis=0, concat_axis=0, axis_index_groups...  19.1 us
    all_to_all x1, blocking collectives, by_chips(): lax.all_to_all(copies, 'gz', split_axis=0, concat_axis=0, axis_index_grou...  11.1 us
    ppermute x6, starting transfers between devices, over_groups(): lax.ppermute(value, 'grp', [(i, (i + d) % n) for i in range(n)])  8.17 us
    ppermute x1, waiting for transfers between devices, shards(): got_down = lax.ppermute(rim_down, 'gz', DOWN)  6.04 us
    all_to_all x1, starting transfers between devices, shards(): lax.all_to_all(parts, 'gz', split_axis=0, concat_axis=0, axis_index_group...  5.84 us
    ppermute x6, waiting for transfers between devices, over_groups(): lax.ppermute(value, 'grp', [(i, (i + d) % n) for i in range(n)])  5.6 us
  transfers between devices with their start and end apart: 20, of which 7 were waited for; matrix products, arithmetic and copies ran while one was open for 0% of the time, Pallas kernels for 4%

profile of v5, /device:TPU:1, one launch (start us, length us, event | category | flops | bytes accessed | tf_op | source)
XLA Modules:
  0.0 139.6 jit_solution(5356417952492788717)
XLA Ops:
  0.6 1.1 shard_map.136
  1.7 4.9 %collective-permute-start = (bf16[16,256]{1,0:T(8,128)(2,1)S(1)}, bf16[16,256]{1,0:T(8,128)(2,1)S(1)}, u32[]{:S(2)}, u32[]{:S(2)}) collective-permute-start(bf16[16,256]{1,0:T(8,128)(2,1)S(1)} %get-tuple-element.23), channel_id=1, source_target_pairs={{0,1},{1,2},{2,3},{3,4},{4,5},{5,6},{6,7},{7,8},{8,9},{9,10},{10,1... | collective-permute-start | bytes 24584 | tf_op jit(solution)/shard_map/ppermute | solution.py:402
  6.6 1.9 %collective-permute-start.1 = (bf16[16,256]{1,0:T(8,128)(2,1)S(1)}, bf16[16,256]{1,0:T(8,128)(2,1)S(1)}, u32[]{:S(2)}, u32[]{:S(2)}) collective-permute-start(bf16[16,256]{1,0:T(8,128)(2,1)S(1)} %get-tuple-element.24), channel_id=1, source_target_pairs={{1,0},{2,1},{3,2},{4,3},{5,4},{6,5},{7,6},{8,7},{9,8},{10,9},{11,1... | collective-permute-start | bytes 24584 | tf_op jit(solution)/shard_map/ppermute | solution.py:403
  8.6 0.0 collective-permute-done.refs_1_.refs_4_
  8.6 3.0 %collective-permute-done.1.refs_2_.refs_5_ = bf16[16,256]{1,0:T(8,128)(2,1)S(1)} collective-permute-done((bf16[16,256]{1,0:T(8,128)(2,1)S(1)}, bf16[16,256]{1,0:T(8,128)(2,1)S(1)}, u32[]{:S(2)}, u32[]{:S(2)}) %collective-permute-start.1) | collective-permute-done | bytes 8224 | tf_op jit(solution)/shard_map/ppermute | solution.py:403
  11.6 0.0 copy-start
  11.6 0.0 copy-start.1
  11.6 0.0 copy-start.2
  11.6 3.7 %shard_map.137 = bf16[512,384]{1,0:T(8,128)(2,1)S(1)} custom-call(bf16[128,256]{1,0:T(8,128)(2,1)} %refs_3_.4, bf16[16,256]{1,0:T(8,128)(2,1)S(1)} %collective-permute-done.refs_1_.refs_4_, bf16[16,256]{1,0:T(8,128)(2,1)S(1)} %collective-permute-done.1.refs_2_.refs_5_, s32[27,128]{1,0:T(8,128)} %bitcast.10, s32[1,128]{1,0:T(1,128)} %bitcast.13, ...), custom_call_target="tpu_custom_call" | custom-call | flops 3300000000 | bytes 262144 | tf_op jit(solution)/shard_map/pallas_call | solution.py:117
  15.3 23.4 %all_to_all.20 = bf16[32,16,384]{2,1,0:T(8,128)(2,1)S(1)} all-to-all(bf16[32,16,384]{2,1,0:T(8,128)(2,1)S(1)} %bitcast.8), channel_id=1, replica_groups={{0,2,4,6,8,10,12,14,16,18,20,22,24,26,28,30,32,34,36,38,40,42,44,46,48,..., dimensions={0} | all-to-all | bytes 786432 | tf_op jit(solution)/shard_map/all_to_all | solution.py:411
  38.7 2.4 %collective-permute-start.2 = (bf16[512,384]{1,0:T(8,128)(2,1)S(1)}, bf16[512,384]{1,0:T(8,128)(2,1)S(1)}, u32[]{:S(2)}, u32[]{:S(2)}) collective-permute-start(bf16[512,384]{1,0:T(8,128)(2,1)S(1)} %bitcast.6), channel_id=1, source_target_pairs={{0,1},{1,0},{2,3},{3,2},{4,5},{5,4},{6,7},{7,6},{8,9},{9,8},{10,11... | collective-permute-start | bytes 1179656 | tf_op jit(solution)/shard_map/ppermute | solution.py:415
  41.1 1.3 collective-permute-done.2.refs_1_
  42.5 0.0 copy-done
  42.5 0.0 copy-done.1
  42.5 0.0 copy-done.2
  42.5 6.0 %shard_map.138 = (bf16[32,32,256]{2,1,0:T(8,128)(2,1)S(1)}, f32[1,256]{1,0:T(1,128)S(1)}) custom-call(bf16[512,384]{1,0:T(8,128)(2,1)S(1)} %bitcast.7, bf16[512,384]{1,0:T(8,128)(2,1)S(1)} %collective-permute-done.2.refs_1_, bf16[256,768]{1,0:T(8,128)(2,1)S(1)} %copy-done, bf16[256,256]{1,0:T(8,128)(2,1)S(1)} %copy-done.1, f32[1,256]{1,0:T(1,128)S(1)} %bitcast.9), custom_call_target="tpu_custom_call" | custom-call | flops 6600000000 | bytes 262144 | tf_op jit(solution)/shard_map/pallas_call | solution.py:117
  48.5 19.1 %all_to_all.21.refs_0_ = bf16[32,32,256]{2,1,0:T(8,128)(2,1)S(1)} all-to-all(bf16[32,32,256]{2,1,0:T(8,128)(2,1)S(1)} %get-tuple-element.25), channel_id=1, replica_groups={{0,2,4,6,8,10,12,14,16,18,20,22,24,26,28,30,32,34,36,38,40,42,44,46,48,..., dimensions={0} | all-to-all | bytes 1048576 | tf_op jit(solution)/shard_map/all_to_all | solution.py:427
  67.6 2.8 %shard_map.139 = (bf16[128,256]{1,0:T(8,128)(2,1)}, bf16[128,256]{1,0:T(8,128)(2,1)}, bf16[4,320,256]{2,1,0:T(8,128)(2,1)}, bf16[16,256]{1,0:T(8,128)(2,1)}) custom-call(bf16[32,32,256]{2,1,0:T(8,128)(2,1)S(1)} %all_to_all.21.refs_0_, s32[1,128]{1,0:T(1,128)} %bitcast.14, f32[1,256]{1,0:T(1,128)S(1)} %get-tuple-element.26.refs_2_, bf16[128,256]{1,0:T(8,128)(2,1)} %refs_3_.4, ...), custom_call_target="tpu_custom_call" | custom-call | flops 1650000000 | bytes 262144 | tf_op jit(solution)/shard_map/pallas_call | solution.py:117
  70.4 11.1 %all_to_all.22.refs_4_ = bf16[4,320,256]{2,1,0:T(8,128)(2,1)S(1)} all-to-all(bf16[4,320,256]{2,1,0:T(8,128)(2,1)} %get-tuple-element.33), channel_id=1, replica_groups={{0,16,32,48},{1,17,33,49},{2,18,34,50},{3,19,35,51},{4,20,36,52},{5,21,..., dimensions={0} | all-to-all | bytes 1310720 | tf_op jit(solution)/shard_map/all_to_all | solution.py:35
  81.5 4.7 %collective-permute-start.8 = (bf16[4,320,256]{2,1,0:T(8,128)(2,1)S(1)}, bf16[4,320,256]{2,1,0:T(8,128)(2,1)S(1)}, u32[]{:S(2)}, u32[]{:S(2)}) collective-permute-start(bf16[4,320,256]{2,1,0:T(8,128)(2,1)S(1)} %all_to_all.22.refs_4_), channel_id=1, source_target_pairs={{0,1},{1,0},{2,3},{3,2},{4,5},{5,4},{6,7},{7,6},{8,9},{9,8},{10,11... | collective-permute-start | bytes 1966088 | tf_op jit(solution)/shard_map/ppermute | solution.py:36
  86.2 1.3 collective-permute-start.5
  87.5 2.6 %collective-permute-start.6 = (bf16[16,256]{1,0:T(8,128)(2,1)}, bf16[16,256]{1,0:T(8,128)(2,1)S(1)}, u32[]{:S(2)}, u32[]{:S(2)}) collective-permute-start(bf16[16,256]{1,0:T(8,128)(2,1)} %get-tuple-element.32.refs_0_), channel_id=1, source_target_pairs={{0,128},{64,192},{128,0},{192,64},{1,129},{65,193},{129,1},{193,65... | collective-permute-start | bytes 24584 | tf_op jit(solution)/shard_map/ppermute | solution.py:51
  90.1 1.1 collective-permute-start.7
  91.2 4.1 %shard_map.140 = (f32[128,256]{1,0:T(8,128)}, bf16[16,256]{1,0:T(8,128)(2,1)}, bf16[16,256]{1,0:T(8,128)(2,1)}) custom-call(bf16[128,256]{1,0:T(8,128)(2,1)} %get-tuple-element.28.refs_0_, s32[27,128]{1,0:T(8,128)} %bitcast.12, bf16[6912,256]{1,0:T(8,128)(2,1)} %refs_2_.3), custom_call_target="tpu_custom_call" | custom-call | flops 4400000000 | bytes 262144 | tf_op jit(solution)/shard_map/pallas_call | solution.py:117
  95.3 0.0 collective-permute-done.5.refs_1_
  95.3 0.0 collective-permute-done.6.refs_2_
  95.3 0.0 collective-permute-done.7.refs_3_
  95.3 0.0 collective-permute-done.8.refs_5_
  95.3 0.0 copy-start.4
  95.3 0.0 copy-start.3
  95.3 4.6 %shard_map.142 = bf16[8,128,256]{2,1,0:T(8,128)(2,1)} custom-call(bf16[16,256]{1,0:T(8,128)(2,1)} %get-tuple-element.32.refs_0_, bf16[16,256]{1,0:T(8,128)(2,1)S(1)} %collective-permute-done.5.refs_1_, bf16[16,256]{1,0:T(8,128)(2,1)S(1)} %collective-permute-done.6.refs_2_, bf16[16,256]{1,0:T(8,128)(2,1)S(1)} %collective-permute-done.7.refs_3_, ...), custom_call_target="tpu_custom_call" | custom-call | flops 5500000256 | bytes 262144 | tf_op jit(solution)/shard_map/pallas_call | solution.py:117
  99.9 5.8 %all-to-all-start.3 = ((bf16[8,128,256]{2,1,0:T(8,128)(2,1)}), bf16[8,128,256]{2,1,0:T(8,128)(2,1)S(1)}, u32[]{:S(2)}, u32[]{:S(2)}) async-start(bf16[8,128,256]{2,1,0:T(8,128)(2,1)} %shard_map.142), calls=%async_computation.3 | async-start | bytes 1048576 | tf_op jit(solution)/shard_map/all_to_all | solution.py:463
  105.8 0.0 copy-done.4
  105.8 4.6 %collective-permute-start.3 = (bf16[16,256]{1,0:T(8,128)(2,1)S(1)}, bf16[16,256]{1,0:T(8,128)(2,1)S(1)}, u32[]{:S(2)}, u32[]{:S(2)}) collective-permute-start(bf16[16,256]{1,0:T(8,128)(2,1)S(1)} %copy-done.4), channel_id=1, source_target_pairs={{0,1},{1,2},{2,3},{3,4},{4,5},{5,6},{6,7},{7,8},{8,9},{9,10},{10,1... | collective-permute-start | bytes 24584 | tf_op jit(solution)/shard_map/ppermute | solution.py:446
  110.4 0.0 copy-done.3
  110.4 1.9 %collective-permute-start.4 = (bf16[16,256]{1,0:T(8,128)(2,1)S(1)}, bf16[16,256]{1,0:T(8,128)(2,1)S(1)}, u32[]{:S(2)}, u32[]{:S(2)}) collective-permute-start(bf16[16,256]{1,0:T(8,128)(2,1)S(1)} %copy-done.3), channel_id=1, source_target_pairs={{1,0},{2,1},{3,2},{4,3},{5,4},{6,5},{7,6},{8,7},{9,8},{10,9},{11,1... | collective-permute-start | bytes 24584 | tf_op jit(solution)/shard_map/ppermute | solution.py:445
  112.3 1.3 collective-permute-done.3.refs_1_
  113.7 6.0 %collective-permute-done.4.refs_2_ = bf16[16,256]{1,0:T(8,128)(2,1)S(1)} collective-permute-done((bf16[16,256]{1,0:T(8,128)(2,1)S(1)}, bf16[16,256]{1,0:T(8,128)(2,1)S(1)}, u32[]{:S(2)}, u32[]{:S(2)}) %collective-permute-start.4) | collective-permute-done | bytes 8224 | tf_op jit(solution)/shard_map/ppermute | solution.py:445
  119.7 1.7 %shard_map.141.refs_1_ = bf16[128,256]{1,0:T(8,128)(2,1)} custom-call(f32[128,256]{1,0:T(8,128)} %get-tuple-element.29.refs_0_.refs_6_, bf16[16,256]{1,0:T(8,128)(2,1)S(1)} %collective-permute-done.3.refs_1_, bf16[16,256]{1,0:T(8,128)(2,1)S(1)} %collective-permute-done.4.refs_2_, s32[1,32]{1,0:T(1,128)} %refs_3_.5), custom_call_target="tpu_custom_call" | custom-call | flops 1100000000 | bytes 262144 | tf_op jit(solution)/shard_map/pallas_call | solution.py:117
  121.4 1.5 %all-to-all-done.3.refs_0_ = bf16[8,128,256]{2,1,0:T(8,128)(2,1)S(1)} async-done(((bf16[8,128,256]{2,1,0:T(8,128)(2,1)}), bf16[8,128,256]{2,1,0:T(8,128)(2,1)S(1)}, u32[]{:S(2)}, u32[]{:S(2)}) %all-to-all-start.3) | async-done | bytes 524320 | tf_op jit(solution)/shard_map/all_to_all | solution.py:463
  122.9 0.1 shard_map.143
  123.0 0.4 collective-permute-start.12
  123.4 1.8 %collective-permute-start.13 = (bf16[128,256]{1,0:T(8,128)(2,1)S(1)}, bf16[128,256]{1,0:T(8,128)(2,1)S(1)}, u32[]{:S(2)}, u32[]{:S(2)}) collective-permute-start(bf16[128,256]{1,0:T(8,128)(2,1)S(1)} %get-tuple-element.35.refs_4_), channel_id=1, source_target_pairs={{0,32},{1,33},{2,34},{3,35},{4,36},{5,37},{6,38},{7,39},{8,40},{9,... | collective-permute-start | bytes 196616 | tf_op jit(solution)/shard_map/ppermute | solution.py:41
  125.1 0.7 collective-permute-start.14
  125.8 0.9 collective-permute-start.10
  126.7 1.9 %collective-permute-start.11 = (bf16[112,256]{1,0:T(8,128)(2,1)S(1)}, bf16[112,256]{1,0:T(8,128)(2,1)S(1)}, u32[]{:S(2)}, u32[]{:S(2)}) collective-permute-start(bf16[112,256]{1,0:T(8,128)(2,1)S(1)} %get-tuple-element.34.refs_0_), channel_id=1, source_target_pairs={{0,192},{64,0},{128,64},{192,128},{1,193},{65,1},{129,65},{193,129... | collective-permute-start | bytes 172040 | tf_op jit(solution)/shard_map/ppermute | solution.py:51
  128.6 1.7 %collective-permute-done.10.refs_2_ = bf16[112,256]{1,0:T(8,128)(2,1)S(1)} collective-permute-done((bf16[112,256]{1,0:T(8,128)(2,1)S(1)}, bf16[112,256]{1,0:T(8,128)(2,1)S(1)}, u32[]{:S(2)}, u32[]{:S(2)}) %collective-permute-start.10) | collective-permute-done | bytes 57376 | tf_op jit(solution)/shard_map/ppermute | solution.py:51
  130.4 3.2 %collective-permute-start.15 = (bf16[128,256]{1,0:T(8,128)(2,1)S(1)}, bf16[128,256]{1,0:T(8,128)(2,1)S(1)}, u32[]{:S(2)}, u32[]{:S(2)}) collective-permute-start(bf16[128,256]{1,0:T(8,128)(2,1)S(1)} %get-tuple-element.35.refs_4_), channel_id=1, source_target_pairs={{0,1},{1,0},{2,3},{3,2},{4,5},{5,4},{6,7},{7,6},{8,9},{9,8},{10,11... | collective-permute-start | bytes 196616 | tf_op jit(solution)/shard_map/ppermute | solution.py:46
  133.6 0.0 collective-permute-done.12.refs_5_
  133.6 0.0 collective-permute-start.16
  133.6 0.0 collective-permute-done.13.refs_6_
  133.6 0.5 collective-permute-start.17
  134.1 0.0 collective-permute-done.14.refs_7_
  134.1 0.1 collective-permute-start.18
  134.2 0.0 collective-permute-done.11.refs_3_
  134.2 0.4 collective-permute-start.9
  134.6 3.8 %collective-permute-done.9.refs_1_ = bf16[112,256]{1,0:T(8,128)(2,1)S(1)} collective-permute-done((bf16[112,256]{1,0:T(8,128)(2,1)S(1)}, bf16[112,256]{1,0:T(8,128)(2,1)S(1)}, u32[]{:S(2)}, u32[]{:S(2)}) %collective-permute-start.9) | collective-permute-done | bytes 57376 | tf_op jit(solution)/shard_map/ppermute | solution.py:51
  138.4 0.0 collective-permute-done.15.refs_8_
  138.4 0.0 collective-permute-done.16.refs_9_
  138.4 0.0 collective-permute-done.17.refs_10_
  138.4 0.0 collective-permute-done.18.refs_11_
  138.5 1.1 shard_map.144
Async XLA Ops:
  1.7 6.9 %collective-permute-start = (bf16[16,256]{1,0:T(8,128)(2,1)S(1)}, bf16[16,256]{1,0:T(8,128)(2,1)S(1)}, u32[]{:S(2)}, u32[]{:S(2)}) collective-permute-start(bf16[16,256]{1,0:T(8,128)(2,1)S(1)} %get-tuple-element.23), channel_id=1, source_target_pairs={{0,1},{1,2},{2,3},{3,4},{4,5},{5,6},{6,7},{7,8},{8,9},{9,10},{10,1... | collective-permute-start | bytes 24584 | tf_op jit(solution)/shard_map/ppermute | solution.py:402
  6.6 5.0 %collective-permute-start.1 = (bf16[16,256]{1,0:T(8,128)(2,1)S(1)}, bf16[16,256]{1,0:T(8,128)(2,1)S(1)}, u32[]{:S(2)}, u32[]{:S(2)}) collective-permute-start(bf16[16,256]{1,0:T(8,128)(2,1)S(1)} %get-tuple-element.24), channel_id=1, source_target_pairs={{1,0},{2,1},{3,2},{4,3},{5,4},{6,5},{7,6},{8,7},{9,8},{10,9},{11,1... | collective-permute-start | bytes 24584 | tf_op jit(solution)/shard_map/ppermute | solution.py:403
  11.6 30.9 %copy-start = (bf16[256,768]{1,0:T(8,128)(2,1)S(1)}, bf16[256,768]{1,0:T(8,128)(2,1)}, u32[]{:S(2)}) copy-start(bf16[256,768]{1,0:T(8,128)(2,1)} %refs_2_.2) | copy-start | bytes 1179652
  11.6 30.9 %copy-start.1 = (bf16[256,256]{1,0:T(8,128)(2,1)S(1)}, bf16[256,256]{1,0:T(8,128)(2,1)}, u32[]{:S(2)}) copy-start(bf16[256,256]{1,0:T(8,128)(2,1)} %refs_3_.3) | copy-start | bytes 393220
  11.6 30.9 %copy-start.2 = (f32[256]{0:T(256)S(1)}, f32[256]{0:T(256)}, u32[]{:S(2)}) copy-start(f32[256]{0:T(256)} %param.17) | copy-start | bytes 3076
  38.7 3.8 %collective-permute-start.2 = (bf16[512,384]{1,0:T(8,128)(2,1)S(1)}, bf16[512,384]{1,0:T(8,128)(2,1)S(1)}, u32[]{:S(2)}, u32[]{:S(2)}) collective-permute-start(bf16[512,384]{1,0:T(8,128)(2,1)S(1)} %bitcast.6), channel_id=1, source_target_pairs={{0,1},{1,0},{2,3},{3,2},{4,5},{5,4},{6,7},{7,6},{8,9},{9,8},{10,11... | collective-permute-start | bytes 1179656 | tf_op jit(solution)/shard_map/ppermute | solution.py:415
  81.5 13.8 %collective-permute-start.8 = (bf16[4,320,256]{2,1,0:T(8,128)(2,1)S(1)}, bf16[4,320,256]{2,1,0:T(8,128)(2,1)S(1)}, u32[]{:S(2)}, u32[]{:S(2)}) collective-permute-start(bf16[4,320,256]{2,1,0:T(8,128)(2,1)S(1)} %all_to_all.22.refs_4_), channel_id=1, source_target_pairs={{0,1},{1,0},{2,3},{3,2},{4,5},{5,4},{6,7},{7,6},{8,9},{9,8},{10,11... | collective-permute-start | bytes 1966088 | tf_op jit(solution)/shard_map/ppermute | solution.py:36
  86.2 9.1 %collective-permute-start.5 = (bf16[16,256]{1,0:T(8,128)(2,1)}, bf16[16,256]{1,0:T(8,128)(2,1)S(1)}, u32[]{:S(2)}, u32[]{:S(2)}) collective-permute-start(bf16[16,256]{1,0:T(8,128)(2,1)} %get-tuple-element.32.refs_0_), channel_id=1, source_target_pairs={{0,64},{64,128},{128,192},{192,0},{1,65},{65,129},{129,193},{193,1... | collective-permute-start | bytes 24584 | tf_op jit(solution)/shard_map/ppermute | solution.py:51
  87.5 7.8 %collective-permute-start.6 = (bf16[16,256]{1,0:T(8,128)(2,1)}, bf16[16,256]{1,0:T(8,128)(2,1)S(1)}, u32[]{:S(2)}, u32[]{:S(2)}) collective-permute-start(bf16[16,256]{1,0:T(8,128)(2,1)} %get-tuple-element.32.refs_0_), channel_id=1, source_target_pairs={{0,128},{64,192},{128,0},{192,64},{1,129},{65,193},{129,1},{193,65... | collective-permute-start | bytes 24584 | tf_op jit(solution)/shard_map/ppermute | solution.py:51
  90.1 5.2 %collective-permute-start.7 = (bf16[16,256]{1,0:T(8,128)(2,1)}, bf16[16,256]{1,0:T(8,128)(2,1)S(1)}, u32[]{:S(2)}, u32[]{:S(2)}) collective-permute-start(bf16[16,256]{1,0:T(8,128)(2,1)} %get-tuple-element.32.refs_0_), channel_id=1, source_target_pairs={{0,192},{64,0},{128,64},{192,128},{1,193},{65,1},{129,65},{193,129... | collective-permute-start | bytes 24584 | tf_op jit(solution)/shard_map/ppermute | solution.py:51
  95.3 10.4 %copy-start.4 = (bf16[16,256]{1,0:T(8,128)(2,1)S(1)}, bf16[16,256]{1,0:T(8,128)(2,1)}, u32[]{:S(2)}) copy-start(bf16[16,256]{1,0:T(8,128)(2,1)} %get-tuple-element.30) | copy-start | bytes 24580
  95.3 15.1 %copy-start.3 = (bf16[16,256]{1,0:T(8,128)(2,1)S(1)}, bf16[16,256]{1,0:T(8,128)(2,1)}, u32[]{:S(2)}) copy-start(bf16[16,256]{1,0:T(8,128)(2,1)} %get-tuple-element.31) | copy-start | bytes 24580
  99.9 23.0 %all-to-all-start.3 = ((bf16[8,128,256]{2,1,0:T(8,128)(2,1)}), bf16[8,128,256]{2,1,0:T(8,128)(2,1)S(1)}, u32[]{:S(2)}, u32[]{:S(2)}) async-start(bf16[8,128,256]{2,1,0:T(8,128)(2,1)} %shard_map.142), calls=%async_computation.3 | async-start | bytes 1048576 | tf_op jit(solution)/shard_map/all_to_all | solution.py:463
  105.8 7.9 %collective-permute-start.3 = (bf16[16,256]{1,0:T(8,128)(2,1)S(1)}, bf16[16,256]{1,0:T(8,128)(2,1)S(1)}, u32[]{:S(2)}, u32[]{:S(2)}) collective-permute-start(bf16[16,256]{1,0:T(8,128)(2,1)S(1)} %copy-done.4), channel_id=1, source_target_pairs={{0,1},{1,2},{2,3},{3,4},{4,5},{5,6},{6,7},{7,8},{8,9},{9,10},{10,1... | collective-permute-start | bytes 24584 | tf_op jit(solution)/shard_map/ppermute | solution.py:446
  110.4 9.3 %collective-permute-start.4 = (bf16[16,256]{1,0:T(8,128)(2,1)S(1)}, bf16[16,256]{1,0:T(8,128)(2,1)S(1)}, u32[]{:S(2)}, u32[]{:S(2)}) collective-permute-start(bf16[16,256]{1,0:T(8,128)(2,1)S(1)} %copy-done.3), channel_id=1, source_target_pairs={{1,0},{2,1},{3,2},{4,3},{5,4},{6,5},{7,6},{8,7},{9,8},{10,9},{11,1... | collective-permute-start | bytes 24584 | tf_op jit(solution)/shard_map/ppermute | solution.py:445
  123.0 10.6 %collective-permute-start.12 = (bf16[128,256]{1,0:T(8,128)(2,1)S(1)}, bf16[128,256]{1,0:T(8,128)(2,1)S(1)}, u32[]{:S(2)}, u32[]{:S(2)}) collective-permute-start(bf16[128,256]{1,0:T(8,128)(2,1)S(1)} %get-tuple-element.35.refs_4_), channel_id=1, source_target_pairs={{0,16},{1,17},{2,18},{3,19},{4,20},{5,21},{6,22},{7,23},{8,24},{9,... | collective-permute-start | bytes 196616 | tf_op jit(solution)/shard_map/ppermute | solution.py:41
  123.4 10.2 %collective-permute-start.13 = (bf16[128,256]{1,0:T(8,128)(2,1)S(1)}, bf16[128,256]{1,0:T(8,128)(2,1)S(1)}, u32[]{:S(2)}, u32[]{:S(2)}) collective-permute-start(bf16[128,256]{1,0:T(8,128)(2,1)S(1)} %get-tuple-element.35.refs_4_), channel_id=1, source_target_pairs={{0,32},{1,33},{2,34},{3,35},{4,36},{5,37},{6,38},{7,39},{8,40},{9,... | collective-permute-start | bytes 196616 | tf_op jit(solution)/shard_map/ppermute | solution.py:41
  125.1 9.0 %collective-permute-start.14 = (bf16[128,256]{1,0:T(8,128)(2,1)S(1)}, bf16[128,256]{1,0:T(8,128)(2,1)S(1)}, u32[]{:S(2)}, u32[]{:S(2)}) collective-permute-start(bf16[128,256]{1,0:T(8,128)(2,1)S(1)} %get-tuple-element.35.refs_4_), channel_id=1, source_target_pairs={{0,48},{1,49},{2,50},{3,51},{4,52},{5,53},{6,54},{7,55},{8,56},{9,... | collective-permute-start | bytes 196616 | tf_op jit(solution)/shard_map/ppermute | solution.py:41
  125.8 4.5 %collective-permute-start.10 = (bf16[112,256]{1,0:T(8,128)(2,1)S(1)}, bf16[112,256]{1,0:T(8,128)(2,1)S(1)}, u32[]{:S(2)}, u32[]{:S(2)}) collective-permute-start(bf16[112,256]{1,0:T(8,128)(2,1)S(1)} %get-tuple-element.34.refs_0_), channel_id=1, source_target_pairs={{0,128},{64,192},{128,0},{192,64},{1,129},{65,193},{129,1},{193,65... | collective-permute-start | bytes 172040 | tf_op jit(solution)/shard_map/ppermute | solution.py:51
  126.7 7.5 %collective-permute-start.11 = (bf16[112,256]{1,0:T(8,128)(2,1)S(1)}, bf16[112,256]{1,0:T(8,128)(2,1)S(1)}, u32[]{:S(2)}, u32[]{:S(2)}) collective-permute-start(bf16[112,256]{1,0:T(8,128)(2,1)S(1)} %get-tuple-element.34.refs_0_), channel_id=1, source_target_pairs={{0,192},{64,0},{128,64},{192,128},{1,193},{65,1},{129,65},{193,129... | collective-permute-start | bytes 172040 | tf_op jit(solution)/shard_map/ppermute | solution.py:51
  130.4 8.1 %collective-permute-start.15 = (bf16[128,256]{1,0:T(8,128)(2,1)S(1)}, bf16[128,256]{1,0:T(8,128)(2,1)S(1)}, u32[]{:S(2)}, u32[]{:S(2)}) collective-permute-start(bf16[128,256]{1,0:T(8,128)(2,1)S(1)} %get-tuple-element.35.refs_4_), channel_id=1, source_target_pairs={{0,1},{1,0},{2,3},{3,2},{4,5},{5,4},{6,7},{7,6},{8,9},{9,8},{10,11... | collective-permute-start | bytes 196616 | tf_op jit(solution)/shard_map/ppermute | solution.py:46
  133.6 4.9 %collective-permute-start.16 = (bf16[128,256]{1,0:T(8,128)(2,1)S(1)}, bf16[128,256]{1,0:T(8,128)(2,1)S(1)}, u32[]{:S(2)}, u32[]{:S(2)}) collective-permute-start(bf16[128,256]{1,0:T(8,128)(2,1)S(1)} %collective-permute-done.12.refs_5_), channel_id=1, source_target_pairs={{0,1},{1,0},{2,3},{3,2},{4,5},{5,4},{6,7},{7,6},{8,9},{9,8},{10,11... | collective-permute-start | bytes 196616 | tf_op jit(solution)/shard_map/ppermute | solution.py:46
  133.6 4.9 %collective-permute-start.17 = (bf16[128,256]{1,0:T(8,128)(2,1)S(1)}, bf16[128,256]{1,0:T(8,128)(2,1)S(1)}, u32[]{:S(2)}, u32[]{:S(2)}) collective-permute-start(bf16[128,256]{1,0:T(8,128)(2,1)S(1)} %collective-permute-done.13.refs_6_), channel_id=1, source_target_pairs={{0,1},{1,0},{2,3},{3,2},{4,5},{5,4},{6,7},{7,6},{8,9},{9,8},{10,11... | collective-permute-start | bytes 196616 | tf_op jit(solution)/shard_map/ppermute | solution.py:46
  134.1 4.4 %collective-permute-start.18 = (bf16[128,256]{1,0:T(8,128)(2,1)S(1)}, bf16[128,256]{1,0:T(8,128)(2,1)S(1)}, u32[]{:S(2)}, u32[]{:S(2)}) collective-permute-start(bf16[128,256]{1,0:T(8,128)(2,1)S(1)} %collective-permute-done.14.refs_7_), channel_id=1, source_target_pairs={{0,1},{1,0},{2,3},{3,2},{4,5},{5,4},{6,7},{7,6},{8,9},{9,8},{10,11... | collective-permute-start | bytes 196616 | tf_op jit(solution)/shard_map/ppermute | solution.py:46
  134.2 4.2 %collective-permute-start.9 = (bf16[112,256]{1,0:T(8,128)(2,1)S(1)}, bf16[112,256]{1,0:T(8,128)(2,1)S(1)}, u32[]{:S(2)}, u32[]{:S(2)}) collective-permute-start(bf16[112,256]{1,0:T(8,128)(2,1)S(1)} %get-tuple-element.34.refs_0_), channel_id=1, source_target_pairs={{0,64},{64,128},{128,192},{192,0},{1,65},{65,129},{129,193},{193,1... | collective-permute-start | bytes 172040 | tf_op jit(solution)/shard_map/ppermute | solution.py:51

commit v6 on v5

--- a/solution.py
+++ b/solution.py
@@ -31,19 +31,12 @@
 DOWN = [(i + 1, i) for i in range(NX * NZ * NC - 1)]
 
 
-def by_chips(copies):
-    near = lax.all_to_all(copies, "gz", split_axis=0, concat_axis=0, axis_index_groups=X_GROUPS, tiled=True)
-    return near, lax.ppermute(near, "gz", SWAP)
-
-
-def along_x(value, d):
-    n = NX * NZ * NC
-    return lax.ppermute(value, "gz", [(i, (i + 16 * d) % n) for i in range(n)])
-
-
-def over_chips(value):
-    near = [value] + [along_x(value, d) for d in range(1, NX)]
-    return near + [lax.ppermute(v, "gz", SWAP) for v in near]
+def by_x(copies):
+    return lax.all_to_all(copies, "gz", split_axis=0, concat_axis=0, axis_index_groups=X_GROUPS, tiled=True)
+
+
+def flip(value, bit):
+    return lax.ppermute(value, "gz", [(i, i ^ bit) for i in range(NX * NZ * NC)])
 
 
 def over_groups(value):
@@ -154,8 +147,7 @@
     return one_hot(rows == target), one_hot(rows == target + 4)
 
 
-def conv_body(feat_ref, prev_ref, next_ref, nbr_ref, rank_ref, cot_ref, weight, send_ref, ext, tab, wide):
-    weight_ref, weight_here = weight
+def conv_body(feat_ref, prev_ref, next_ref, nbr_ref, rank_ref, cot_ref, weight_ref, send_ref, ext, tab, wide):
     ext[:PTS] = feat_ref[...]
     ext[PTS : PTS + RIM] = prev_ref[...]
     ext[PTS + RIM : EXT] = next_ref[...]
@@ -168,7 +160,6 @@
     for k in range(OFFS):
         hit = one_hot(table[:, k : k + 1] == lanes)
         wide[:, k * FEAT : (k + 1) * FEAT] = mm(hit, rows).astype(BF)
-    weight_here()
     mixed = (feat_ref[...].astype(F32) + mm(wide[...], weight_ref[...])).astype(BF)
     rank_row = rank_ref[...]
     first, second = slot_hits(rank_row)
@@ -319,13 +310,11 @@
     out_ref[...] = (own_ref[...] + mm(hit, rims)).astype(BF)
 
 
-def kernel_grad_body(p0_ref, p1_ref, p2_ref, p3_ref, near_ref, far_ref, out_ref, tab, exts, terms, total):
+def kernel_grad_body(p0, p1_ref, p2_ref, p3_ref, near_ref, far_ref, out_ref, tab, exts, terms, total):
     x, core = position()
     base = x * 1728 + core * 108
     first_offset = jnp.minimum(lax.shift_right_logical(base, 8), OFFS - 8)
     first_row = base - first_offset * FEAT - core * 4
-    dense = p0_ref[...].astype(F32) + p1_ref[...].astype(F32) + p2_ref[...].astype(F32) + p3_ref[...].astype(F32)
-    dense = dense.astype(BF)
     gain = jnp.zeros((1, FEAT), F32)
     points = iota((EXT, PTS), 0).astype(F32)
     for s in range(NX * NC):
@@ -343,6 +332,10 @@
     for k in range(8):
         total[k * FEAT : (k + 1) * FEAT] = mm(ext_t, terms[k])
     total[8 * FEAT :] = jnp.zeros((16, FEAT), F32)
+    p0_ref, p0_here = p0
+    p0_here()
+    dense = p0_ref[...].astype(F32) + p1_ref[...].astype(F32) + p2_ref[...].astype(F32) + p3_ref[...].astype(F32)
+    dense = dense.astype(BF)
     at = iota((112, FEAT), 0)
     for z in range(NZ):
         wide = total[pl.ds(pl.multiple_of(first_row + z * 216, 8), 120), :]
@@ -361,18 +354,21 @@
         dense_ref[i * 16 : (i + 1) * 16] = got_ref[i, 112:]
 
 
-def last_body(factor, *refs):
-    groups, parts = refs[:4], refs[4 : 4 + NX * NC]
-    conv_ref, gain_ref, qkv_ref, proj_ref, rows = refs[4 + NX * NC :]
-    total = groups[0][...].astype(F32)
-    for group in groups[1:]:
-        total += group[...].astype(F32)
+def middle_body(conv_ref, other_ref, dense_ref, across_ref, pair_ref, two_ref):
+    pair_ref[...] = (conv_ref[...].astype(F32) + other_ref[...].astype(F32)).astype(BF)
+    two_ref[0] = dense_ref[...]
+    two_ref[1] = across_ref[...]
+
+
+def last_body(factor, pair_ref, other_ref, *refs):
+    parts, (conv_ref, gain_ref, qkv_ref, proj_ref, rows) = refs[:4], refs[4:]
+    total = pair_ref[...].astype(F32) + other_ref[...].astype(F32)
     conv_ref[...] = total[:108] * factor
     gain_ref[...] = total[108:109] * factor
     x, core = position()
     for s in range(NX * NC):
-        source = ((x + NX - s % NX) & (NX - 1)) + NX * (core if s < NX else 1 - core)
-        rows[source] = parts[s][...].astype(F32) * factor
+        source = (x ^ (s % 2 * 2) ^ (s // 2 % 2)) + NX * (core ^ (s // 4))
+        rows[source] = parts[s // 2][s % 2].astype(F32) * factor
     for b in range(NX * NC):
         part, at = b // 2, b % 2 * PTS
         if part < 3:
@@ -397,7 +393,7 @@
     gain_row = norm_gain.reshape(1, FEAT)
     table = neighbours.T
     to_prev, to_next = call(
-        pick_body, [sds((RIM, FEAT))] * 2, halo_rows, features, fetched=(0, 1), us=0.5, limit=8
+        pick_body, [sds((RIM, FEAT))] * 2, halo_rows, features, fetched=(0, 1), us=10.0, limit=8
     )
     from_prev = lax.ppermute(to_next, "gz", UP)
     from_next = lax.ppermute(to_prev, "gz", DOWN)
@@ -406,7 +402,7 @@
         sds((SLOTS, FEAT + PTS)),
         features, from_prev, from_next, table, rank_row, cotangent, conv_weight,
         scratch=[pltpu.VMEM((FEAT, FEAT), BF), pltpu.VMEM((PTS, PTS), F32), pltpu.VMEM((PTS, OFFS * FEAT), BF)],
-        fetched=(0, 3, 4, 5), late=(6,), us=3.0,
+        us=3.0,
     )
     got = lax.all_to_all(
         send.reshape(32, 16, FEAT + PTS), "gz", split_axis=0, concat_axis=0,
@@ -431,9 +427,9 @@
         unpack_body,
         [sds((PTS, FEAT)), sds((PTS, FEAT)), sds((NX, PAY, FEAT)), sds((16, FEAT))],
         returned, rank_row, grad_gain, features, from_prev, from_next, table,
-        fetched=(1, 3, 6), pinned=(1, 2, 3), us=1.5, limit=8,
-    )
-    near_grads, far_grads = by_chips(grad_copies)
+        pinned=(1, 2, 3), us=1.5, limit=8,
+    )
+    near_grads = by_x(grad_copies)
     dense_groups = over_groups(dense)
     own_part, rim_down, rim_up = call(
         spread_body,
@@ -442,6 +438,8 @@
         scratch=[pltpu.VMEM((OFFS * EXT, FEAT), BF), pltpu.VMEM((EXT, FEAT), F32)],
         fetched=(0, 1), late=(2,), pinned=(0, 1, 2), us=4.0,
     )
+    near_grads, own_part, dense_groups = lax.optimization_barrier((near_grads, own_part, dense_groups))
+    far_grads = lax.ppermute(near_grads, "gz", SWAP)
     got_down = lax.ppermute(rim_down, "gz", DOWN)
     got_up = lax.ppermute(rim_up, "gz", UP)
     parts = call(
@@ -454,23 +452,31 @@
             pltpu.VMEM((8, NX * NC * EXT, FEAT), BF),
             pltpu.VMEM((8 * FEAT + 16, FEAT), F32),
         ],
-        fetched=(0,), idle=(6,), pinned=(0,), us=5.0, limit=24,
-    )
+        late=(0,), idle=(6,), pinned=(0,), us=5.0, limit=24,
+    )
+    z_parts = lax.all_to_all(
+        parts, "gz", split_axis=0, concat_axis=0, axis_index_groups=Z_GROUPS, tiled=True
+    )
+    z_parts, got_up, got_down = lax.optimization_barrier((z_parts, got_up, got_down))
+    conv_part, dense_sum = call(
+        sum_body, [sds((112, FEAT)), sds((PTS, FEAT))], z_parts, us=1.0, limit=8,
+    )
+    conv_pair, dense_two = call(
+        middle_body, [sds((112, FEAT)), sds((2, PTS, FEAT))],
+        conv_part, lax.ppermute(conv_part, "grp", [(i, i ^ 1) for i in range(4)]), dense_sum, flip(dense_sum, 32),
+        us=0.5, limit=8,
+    )
+    conv_pair, dense_two, got_up, got_down = lax.optimization_barrier((conv_pair, dense_two, got_up, got_down))
     grad_features = call(
         rim_body, sds((PTS, FEAT)), own_part, got_up, got_down, halo_rows,
-        fetched=(0, 3), us=1.0, limit=8,
-    )
-    z_parts = lax.all_to_all(
-        parts, "gz", split_axis=0, concat_axis=0, axis_index_groups=Z_GROUPS, tiled=True
-    )
-    conv_part, dense_sum = call(
-        sum_body, [sds((112, FEAT)), sds((PTS, FEAT))], z_parts, grad_features,
-        idle=(1,), us=1.0, limit=8,
-    )
+        fetched=(0, 3), us=3.0, limit=8,
+    )
+    conv_other = lax.ppermute(conv_pair, "grp", [(i, i ^ 2) for i in range(4)])
+    dense_more = flip(dense_two, 16)
     grad_conv, gain_sum, grad_qkv, grad_proj = call(
         lambda *refs: last_body(factor, *refs),
         [sds((108, FEAT), F32), sds((1, FEAT), F32), sds((FEAT, 3 * FEAT), F32), sds((FEAT, FEAT), F32)],
-        *over_groups(conv_part), *over_chips(dense_sum),
+        conv_pair, conv_other, dense_two, dense_more, flip(dense_two, 1), flip(dense_more, 1),
         scratch=[pltpu.VMEM((NX * NC, PTS, FEAT), F32)],
         limit=8,
     )

time: 140 us -> 128 us (0.914)
  blocking collectives: 53.6 us -> 42.5 us
  Pallas kernels: 25.1 us -> 21.8 us
  starting transfers between devices: 41.2 us -> 42.9 us
    all_to_all x1 -> x0, blocking collectives: 11.1 us -> none  [by_chips(): lax.all_to_all(copies, 'gz', split_axis=0, concat_axis=0, axis_index_grou...]
    ppermute x6 -> x3, waiting for transfers between devices: 5.6 us -> 0.01 us  [over_groups(): lax.ppermute(value, 'grp', [(i, (i + d) % n) for i in range(n)])]
    ppermute x6 -> x3, starting transfers between devices: 8.17 us -> 3.85 us  [over_groups(): lax.ppermute(value, 'grp', [(i, (i + d) % n) for i in range(n)])]
    ppermute x8 -> x7, waiting for transfers between devices: 0.02 us -> 3.6 us  [the longest x1 1.86 us: shards(): lax.ppermute(conv_part, 'grp', [(i, i ^ 1) for i in range(4)])]
    all_to_all x0 -> x1, starting transfers between devices: none -> 3.5 us  [by_x(): lax.all_to_all(copies, 'gz', split_axis=0, concat_axis=0, axis_index_grou...]
    pallas_call x9 -> x10, Pallas kernels: 25.1 us -> 21.8 us  [call(): pl.pallas_call(outer, out_shape=shapes, in_specs=specs, out_specs=[pl.Blo...]
    ppermute x8 -> x7, starting transfers between devices: 11.4 us -> 14.6 us  [the longest x4 6 us: flip(): lax.ppermute(value, 'gz', [(i, i ^ bit) for i in range(NX * NZ * NC)])]
    all_to_all x1, waiting for transfers between devices: 1.53 us -> 4.02 us  [shards(): lax.all_to_all(parts, 'gz', split_axis=0, concat_axis=0, axis_index_group...]
  transfers between devices with their start and end apart: 20 -> 17, of which waited for: 7 -> 7; matrix products, arithmetic and copies ran while one was open for 0% -> 0% of each run, Pallas kernels for 4% -> 5%
where the time goes in v6:
time: 128 us
  starting transfers between devices  42.9 us (34%)
  blocking collectives  42.5 us (33%)
  Pallas kernels  21.8 us (17%)
  waiting for transfers between devices  19.8 us (15%)
    all_to_all x1, blocking collectives, shards(): lax.all_to_all(send.reshape(32, 16, FEAT + PTS), 'gz', split_axis=0, conc...  23.4 us
    pallas_call x10, Pallas kernels, call(): pl.pallas_call(outer, out_shape=shapes, in_specs=specs, out_specs=[pl.Blo...  21.8 us
    all_to_all x1, blocking collectives, shards(): lax.all_to_all(back, 'gz', split_axis=0, concat_axis=0, axis_index_groups...  19.1 us
    ppermute x4, starting transfers between devices, flip(): lax.ppermute(value, 'gz', [(i, i ^ bit) for i in range(NX * NZ * NC)])  6 us
    all_to_all x1, starting transfers between devices, shards(): lax.all_to_all(parts, 'gz', split_axis=0, concat_axis=0, axis_index_group...  5.65 us
    ppermute x1, waiting for transfers between devices, shards(): got_down = lax.ppermute(rim_down, 'gz', DOWN)  5.13 us
    ppermute x1, starting transfers between devices, shards(): from_prev = lax.ppermute(to_next, 'gz', UP)  4.94 us
    ppermute x1, starting transfers between devices, shards(): far_grads = lax.ppermute(near_grads, 'gz', SWAP)  4.48 us
  transfers between devices with their start and end apart: 17, of which 7 were waited for; matrix products, arithmetic and copies ran while one was open for 0% of the time, Pallas kernels for 5%

profile of v6, /device:TPU:1, one launch (start us, length us, event | category | flops | bytes accessed | tf_op | source)
XLA Modules:
  0.0 128.0 jit_solution(7696064739861670017)
XLA Ops:
  0.6 0.0 copy-start.4
  0.6 0.0 copy-start
  0.7 0.0 copy-start.3
  0.7 0.0 copy-start.5
  0.7 0.0 copy-start.7
  0.7 1.2 shard_map.136
  1.9 4.9 %collective-permute-start = (bf16[16,256]{1,0:T(8,128)(2,1)S(1)}, bf16[16,256]{1,0:T(8,128)(2,1)S(1)}, u32[]{:S(2)}, u32[]{:S(2)}) collective-permute-start(bf16[16,256]{1,0:T(8,128)(2,1)S(1)} %get-tuple-element.38), channel_id=1, source_target_pairs={{0,1},{1,2},{2,3},{3,4},{4,5},{5,6},{6,7},{7,8},{8,9},{9,10},{10,1... | collective-permute-start | bytes 24584 | tf_op jit(solution)/shard_map/ppermute | solution.py:398
  6.8 1.9 %collective-permute-start.1 = (bf16[16,256]{1,0:T(8,128)(2,1)S(1)}, bf16[16,256]{1,0:T(8,128)(2,1)S(1)}, u32[]{:S(2)}, u32[]{:S(2)}) collective-permute-start(bf16[16,256]{1,0:T(8,128)(2,1)S(1)} %get-tuple-element.39), channel_id=1, source_target_pairs={{1,0},{2,1},{3,2},{4,3},{5,4},{6,5},{7,6},{8,7},{9,8},{10,9},{11,1... | collective-permute-start | bytes 24584 | tf_op jit(solution)/shard_map/ppermute | solution.py:399
  8.8 0.0 collective-permute-done.refs_1_.refs_4_
  8.8 3.0 %collective-permute-done.1.refs_2_.refs_5_ = bf16[16,256]{1,0:T(8,128)(2,1)S(1)} collective-permute-done((bf16[16,256]{1,0:T(8,128)(2,1)S(1)}, bf16[16,256]{1,0:T(8,128)(2,1)S(1)}, u32[]{:S(2)}, u32[]{:S(2)}) %collective-permute-start.1) | collective-permute-done | bytes 8224 | tf_op jit(solution)/shard_map/ppermute | solution.py:399
  11.8 0.0 copy-done.4
  11.8 0.0 copy-done
  11.8 0.0 copy-done.3
  11.8 0.0 copy-done.5
  11.8 0.0 copy-done.7
  11.8 0.0 copy-start.1
  11.9 0.0 copy-start.2
  11.9 0.0 copy-start.6
  11.9 1.8 %shard_map.137 = bf16[512,384]{1,0:T(8,128)(2,1)S(1)} custom-call(bf16[128,256]{1,0:T(8,128)(2,1)S(1)} %copy-done.4, bf16[16,256]{1,0:T(8,128)(2,1)S(1)} %collective-permute-done.refs_1_.refs_4_, bf16[16,256]{1,0:T(8,128)(2,1)S(1)} %collective-permute-done.1.refs_2_.refs_5_, s32[27,128]{1,0:T(8,128)S(1)} %bitcast.10, s32[1,128]{1,0:T(1,128)S(1)} %bitcast.13, ...), custom_call_target="tpu_custom_call" | custom-call | flops 3300000000 | bytes 262144 | tf_op jit(solution)/shard_map/pallas_call | solution.py:110
  13.7 23.4 %all_to_all.20 = bf16[32,16,384]{2,1,0:T(8,128)(2,1)S(1)} all-to-all(bf16[32,16,384]{2,1,0:T(8,128)(2,1)S(1)} %bitcast.8), channel_id=1, replica_groups={{0,2,4,6,8,10,12,14,16,18,20,22,24,26,28,30,32,34,36,38,40,42,44,46,48,..., dimensions={0} | all-to-all | bytes 786432 | tf_op jit(solution)/shard_map/all_to_all | solution.py:407
  37.1 2.4 %collective-permute-start.2 = (bf16[512,384]{1,0:T(8,128)(2,1)S(1)}, bf16[512,384]{1,0:T(8,128)(2,1)S(1)}, u32[]{:S(2)}, u32[]{:S(2)}) collective-permute-start(bf16[512,384]{1,0:T(8,128)(2,1)S(1)} %bitcast.6), channel_id=1, source_target_pairs={{0,1},{1,0},{2,3},{3,2},{4,5},{5,4},{6,7},{7,6},{8,9},{9,8},{10,11... | collective-permute-start | bytes 1179656 | tf_op jit(solution)/shard_map/ppermute | solution.py:411
  39.6 1.3 %collective-permute-done.2.refs_1_ = bf16[512,384]{1,0:T(8,128)(2,1)S(1)} collective-permute-done((bf16[512,384]{1,0:T(8,128)(2,1)S(1)}, bf16[512,384]{1,0:T(8,128)(2,1)S(1)}, u32[]{:S(2)}, u32[]{:S(2)}) %collective-permute-start.2) | collective-permute-done | bytes 393248 | tf_op jit(solution)/shard_map/ppermute | solution.py:411
  40.9 0.0 copy-done.1
  40.9 0.0 copy-done.2
  40.9 0.0 copy-done.6
  40.9 6.0 %shard_map.138 = (bf16[32,32,256]{2,1,0:T(8,128)(2,1)S(1)}, f32[1,256]{1,0:T(1,128)S(1)}) custom-call(bf16[512,384]{1,0:T(8,128)(2,1)S(1)} %bitcast.7, bf16[512,384]{1,0:T(8,128)(2,1)S(1)} %collective-permute-done.2.refs_1_, bf16[256,768]{1,0:T(8,128)(2,1)S(1)} %copy-done.1, bf16[256,256]{1,0:T(8,128)(2,1)S(1)} %copy-done.2, f32[1,256]{1,0:T(1,128)S(1)} %bitcast.12), custom_call_target="tpu_custom_call" | custom-call | flops 6600000000 | bytes 262144 | tf_op jit(solution)/shard_map/pallas_call | solution.py:110
  46.9 19.1 %all_to_all.21.refs_0_ = bf16[32,32,256]{2,1,0:T(8,128)(2,1)S(1)} all-to-all(bf16[32,32,256]{2,1,0:T(8,128)(2,1)S(1)} %get-tuple-element.40), channel_id=1, replica_groups={{0,2,4,6,8,10,12,14,16,18,20,22,24,26,28,30,32,34,36,38,40,42,44,46,48,..., dimensions={0} | all-to-all | bytes 1048576 | tf_op jit(solution)/shard_map/all_to_all | solution.py:423
  66.0 1.9 %shard_map.139 = (bf16[128,256]{1,0:T(8,128)(2,1)}, bf16[128,256]{1,0:T(8,128)(2,1)}, bf16[4,320,256]{2,1,0:T(8,128)(2,1)}, bf16[16,256]{1,0:T(8,128)(2,1)}) custom-call(bf16[32,32,256]{2,1,0:T(8,128)(2,1)S(1)} %all_to_all.21.refs_0_, s32[1,128]{1,0:T(1,128)S(1)} %bitcast.14, f32[1,256]{1,0:T(1,128)S(1)} %get-tuple-element.41.refs_2_, ...), custom_call_target="tpu_custom_call" | custom-call | flops 1650000000 | bytes 262144 | tf_op jit(solution)/shard_map/pallas_call | solution.py:110
  67.9 3.5 %all-to-all-start.2 = ((bf16[4,320,256]{2,1,0:T(8,128)(2,1)}), bf16[4,320,256]{2,1,0:T(8,128)(2,1)S(1)}, u32[]{:S(2)}, u32[]{:S(2)}) async-start(bf16[4,320,256]{2,1,0:T(8,128)(2,1)} %get-tuple-element.43), calls=%async_computation.2 | async-start | bytes 1310720 | tf_op jit(solution)/shard_map/all_to_all | solution.py:35
  71.4 2.8 %collective-permute-start.5 = (bf16[16,256]{1,0:T(8,128)(2,1)}, bf16[16,256]{1,0:T(8,128)(2,1)S(1)}, u32[]{:S(2)}, u32[]{:S(2)}) collective-permute-start(bf16[16,256]{1,0:T(8,128)(2,1)} %get-tuple-element.48.refs_0_), channel_id=1, source_target_pairs={{0,192},{64,0},{128,64},{192,128},{1,193},{65,1},{129,65},{193,129... | collective-permute-start | bytes 24584 | tf_op jit(solution)/shard_map/ppermute | solution.py:44
  74.2 0.4 collective-permute-start.4
  74.6 0.7 collective-permute-start.3
  75.3 4.1 %shard_map.140 = (f32[128,256]{1,0:T(8,128)}, bf16[16,256]{1,0:T(8,128)(2,1)}, bf16[16,256]{1,0:T(8,128)(2,1)}) custom-call(bf16[128,256]{1,0:T(8,128)(2,1)} %get-tuple-element.44.refs_0_, s32[27,128]{1,0:T(8,128)} %bitcast.9, bf16[6912,256]{1,0:T(8,128)(2,1)} %refs_2_.3), custom_call_target="tpu_custom_call" | custom-call | flops 4400000000 | bytes 262144 | tf_op jit(solution)/shard_map/pallas_call | solution.py:110
  79.4 0.0 collective-permute-done.5.refs_3_
  79.4 0.0 collective-permute-done.4.refs_2_
  79.4 0.0 collective-permute-done.3.refs_1_
  79.4 0.0 all-to-all-done.2.refs_4_
  79.4 0.0 copy-start.9
  79.4 0.0 copy-start.8
  79.5 4.5 %collective-permute-start.6 = (bf16[4,320,256]{2,1,0:T(8,128)(2,1)S(1)}, bf16[4,320,256]{2,1,0:T(8,128)(2,1)S(1)}, u32[]{:S(2)}, u32[]{:S(2)}) collective-permute-start(bf16[4,320,256]{2,1,0:T(8,128)(2,1)S(1)} %all-to-all-done.2.refs_4_), channel_id=1, source_target_pairs={{0,1},{1,0},{2,3},{3,2},{4,5},{5,4},{6,7},{7,6},{8,9},{9,8},{10,11... | collective-permute-start | bytes 1966088 | tf_op jit(solution)/shard_map/ppermute | solution.py:442
  83.9 1.7 %collective-permute-done.6.refs_5_ = bf16[4,320,256]{2,1,0:T(8,128)(2,1)S(1)} collective-permute-done((bf16[4,320,256]{2,1,0:T(8,128)(2,1)S(1)}, bf16[4,320,256]{2,1,0:T(8,128)(2,1)S(1)}, u32[]{:S(2)}, u32[]{:S(2)}) %collective-permute-start.6) | collective-permute-done | bytes 655392 | tf_op jit(solution)/shard_map/ppermute | solution.py:442
  85.7 3.9 %shard_map.141 = bf16[8,128,256]{2,1,0:T(8,128)(2,1)} custom-call(bf16[16,256]{1,0:T(8,128)(2,1)} %get-tuple-element.48.refs_0_, bf16[16,256]{1,0:T(8,128)(2,1)S(1)} %collective-permute-done.3.refs_1_, bf16[16,256]{1,0:T(8,128)(2,1)S(1)} %collective-permute-done.4.refs_2_, bf16[16,256]{1,0:T(8,128)(2,1)S(1)} %collective-permute-done.5.refs_3_, ...), custom_call_target="tpu_custom_call" | custom-call | flops 5500000256 | bytes 262144 | tf_op jit(solution)/shard_map/pallas_call | solution.py:110
  89.5 5.7 %all-to-all-start.3 = ((bf16[8,128,256]{2,1,0:T(8,128)(2,1)}), bf16[8,128,256]{2,1,0:T(8,128)(2,1)S(1)}, u32[]{:S(2)}, u32[]{:S(2)}) async-start(bf16[8,128,256]{2,1,0:T(8,128)(2,1)} %shard_map.141), calls=%async_computation.3 | async-start | bytes 1048576 | tf_op jit(solution)/shard_map/all_to_all | solution.py:457
  95.2 0.0 copy-done.9
  95.2 4.2 %collective-permute-start.7 = (bf16[16,256]{1,0:T(8,128)(2,1)S(1)}, bf16[16,256]{1,0:T(8,128)(2,1)S(1)}, u32[]{:S(2)}, u32[]{:S(2)}) collective-permute-start(bf16[16,256]{1,0:T(8,128)(2,1)S(1)} %copy-done.9), channel_id=1, source_target_pairs={{0,1},{1,2},{2,3},{3,4},{4,5},{5,6},{6,7},{7,8},{8,9},{9,10},{10,1... | collective-permute-start | bytes 24584 | tf_op jit(solution)/shard_map/ppermute | solution.py:444
  99.4 1.9 %collective-permute-start.8 = (bf16[16,256]{1,0:T(8,128)(2,1)S(1)}, bf16[16,256]{1,0:T(8,128)(2,1)S(1)}, u32[]{:S(2)}, u32[]{:S(2)}) collective-permute-start(bf16[16,256]{1,0:T(8,128)(2,1)S(1)} %copy-done.8), channel_id=1, source_target_pairs={{1,0},{2,1},{3,2},{4,3},{5,4},{6,5},{7,6},{8,7},{9,8},{10,9},{11,1... | collective-permute-start | bytes 24584 | tf_op jit(solution)/shard_map/ppermute | solution.py:443
  101.3 2.7 %collective-permute-done.7.refs_1_ = bf16[16,256]{1,0:T(8,128)(2,1)S(1)} collective-permute-done((bf16[16,256]{1,0:T(8,128)(2,1)S(1)}, bf16[16,256]{1,0:T(8,128)(2,1)S(1)}, u32[]{:S(2)}, u32[]{:S(2)}) %collective-permute-start.7) | collective-permute-done | bytes 8224 | tf_op jit(solution)/shard_map/ppermute | solution.py:444
  104.0 5.1 %collective-permute-done.8.refs_2_ = bf16[16,256]{1,0:T(8,128)(2,1)S(1)} collective-permute-done((bf16[16,256]{1,0:T(8,128)(2,1)S(1)}, bf16[16,256]{1,0:T(8,128)(2,1)S(1)}, u32[]{:S(2)}, u32[]{:S(2)}) %collective-permute-start.8) | collective-permute-done | bytes 8224 | tf_op jit(solution)/shard_map/ppermute | solution.py:443
  109.1 4.0 %all-to-all-done.3.refs_0_ = bf16[8,128,256]{2,1,0:T(8,128)(2,1)S(1)} async-done(((bf16[8,128,256]{2,1,0:T(8,128)(2,1)}), bf16[8,128,256]{2,1,0:T(8,128)(2,1)S(1)}, u32[]{:S(2)}, u32[]{:S(2)}) %all-to-all-start.3) | async-done | bytes 524320 | tf_op jit(solution)/shard_map/all_to_all | solution.py:457
  113.1 0.1 shard_map.142
  113.2 1.8 %collective-permute-start.10 = (bf16[128,256]{1,0:T(8,128)(2,1)S(1)}, bf16[128,256]{1,0:T(8,128)(2,1)S(1)}, u32[]{:S(2)}, u32[]{:S(2)}) collective-permute-start(bf16[128,256]{1,0:T(8,128)(2,1)S(1)} %get-tuple-element.57.refs_2_), channel_id=1, source_target_pairs={{0,32},{1,33},{2,34},{3,35},{4,36},{5,37},{6,38},{7,39},{8,40},{9,... | collective-permute-start | bytes 196616 | tf_op jit(solution)/shard_map/ppermute | solution.py:39
  115.1 1.6 %collective-permute-start.9 = (bf16[112,256]{1,0:T(8,128)(2,1)S(1)}, bf16[112,256]{1,0:T(8,128)(2,1)S(1)}, u32[]{:S(2)}, u32[]{:S(2)}) collective-permute-start(bf16[112,256]{1,0:T(8,128)(2,1)S(1)} %get-tuple-element.56.refs_0_), channel_id=1, source_target_pairs={{0,64},{64,0},{128,192},{192,128},{1,65},{65,1},{129,193},{193,129... | collective-permute-start | bytes 172040 | tf_op jit(solution)/shard_map/ppermute | solution.py:466
  116.7 1.9 %collective-permute-done.9.refs_1_ = bf16[112,256]{1,0:T(8,128)(2,1)S(1)} collective-permute-done((bf16[112,256]{1,0:T(8,128)(2,1)S(1)}, bf16[112,256]{1,0:T(8,128)(2,1)S(1)}, u32[]{:S(2)}, u32[]{:S(2)}) %collective-permute-start.9) | collective-permute-done | bytes 57376 | tf_op jit(solution)/shard_map/ppermute | solution.py:466
  118.5 0.0 collective-permute-done.10.refs_3_
  118.5 0.1 collective-permute-start.12
  118.6 2.1 %collective-permute-start.13 = (bf16[2,128,256]{2,1,0:T(8,128)(2,1)S(1)}, bf16[2,128,256]{2,1,0:T(8,128)(2,1)S(1)}, u32[]{:S(2)}, u32[]{:S(2)}) collective-permute-start(bf16[2,128,256]{2,1,0:T(8,128)(2,1)S(1)} %get-tuple-element.65.refs_2_), channel_id=1, source_target_pairs={{0,1},{1,0},{2,3},{3,2},{4,5},{5,4},{6,7},{7,6},{8,9},{9,8},{10,11... | collective-permute-start | bytes 393224 | tf_op jit(solution)/shard_map/ppermute | solution.py:39
  120.8 2.5 %collective-permute-start.11 = (bf16[112,256]{1,0:T(8,128)(2,1)S(1)}, bf16[112,256]{1,0:T(8,128)(2,1)S(1)}, u32[]{:S(2)}, u32[]{:S(2)}) collective-permute-start(bf16[112,256]{1,0:T(8,128)(2,1)S(1)} %get-tuple-element.64.refs_0_), channel_id=1, source_target_pairs={{0,128},{64,192},{128,0},{192,64},{1,129},{65,193},{129,1},{193,65... | collective-permute-start | bytes 172040 | tf_op jit(solution)/shard_map/ppermute | solution.py:474
  123.2 0.0 collective-permute-done.12.refs_3_
  123.2 1.9 %collective-permute-start.14 = (bf16[2,128,256]{2,1,0:T(8,128)(2,1)S(1)}, bf16[2,128,256]{2,1,0:T(8,128)(2,1)S(1)}, u32[]{:S(2)}, u32[]{:S(2)}) collective-permute-start(bf16[2,128,256]{2,1,0:T(8,128)(2,1)S(1)} %collective-permute-done.12.refs_3_), channel_id=1, source_target_pairs={{0,1},{1,0},{2,3},{3,2},{4,5},{5,4},{6,7},{7,6},{8,9},{9,8},{10,11... | collective-permute-start | bytes 393224 | tf_op jit(solution)/shard_map/ppermute | solution.py:39
  125.2 1.7 %shard_map.144 = bf16[128,256]{1,0:T(8,128)(2,1)} custom-call(f32[128,256]{1,0:T(8,128)} %get-tuple-element.47.refs_6_.refs_0_, bf16[16,256]{1,0:T(8,128)(2,1)S(1)} %collective-permute-done.7.refs_1_, bf16[16,256]{1,0:T(8,128)(2,1)S(1)} %collective-permute-done.8.refs_2_, s32[1,32]{1,0:T(1,128)} %refs_3_.5), custom_call_target="tpu_custom_call" | custom-call | flops 3300000000 | bytes 262144 | tf_op jit(solution)/shard_map/pallas_call | solution.py:110
  126.9 0.0 collective-permute-done.11.refs_1_
  126.9 0.0 collective-permute-done.13.refs_4_
  126.9 0.0 collective-permute-done.14.refs_5_
  126.9 1.1 shard_map.145
  (2 shorter events, 0.0 us)
Async XLA Ops:
  0.6 11.2 %copy-start.4 = (bf16[128,256]{1,0:T(8,128)(2,1)S(1)}, bf16[128,256]{1,0:T(8,128)(2,1)}, u32[]{:S(2)}) copy-start(bf16[128,256]{1,0:T(8,128)(2,1)} %refs_3_.4) | copy-start | bytes 196612
  0.6 11.2 %copy-start = (bf16[6912,256]{1,0:T(8,128)(2,1)S(1)}, bf16[6912,256]{1,0:T(8,128)(2,1)}, u32[]{:S(2)}) copy-start(bf16[6912,256]{1,0:T(8,128)(2,1)} %refs_2_.3) | copy-start | bytes 10616836
  0.7 11.2 %copy-start.3 = (bf16[128,256]{1,0:T(8,128)(2,1)S(1)}, bf16[128,256]{1,0:T(8,128)(2,1)}, u32[]{:S(2)}) copy-start(bf16[128,256]{1,0:T(8,128)(2,1)} %refs_5_.1) | copy-start | bytes 196612
  0.7 11.2 %copy-start.5 = (s32[128,27]{0,1:T(8,128)S(1)}, s32[128,27]{0,1:T(8,128)}, u32[]{:S(2)}) copy-start(s32[128,27]{0,1:T(8,128)} %param.11) | copy-start | bytes 41476
  0.7 11.2 %copy-start.7 = (s32[128]{0:T(128)S(1)}, s32[128]{0:T(128)}, u32[]{:S(2)}) copy-start(s32[128]{0:T(128)} %param.10) | copy-start | bytes 1540
  1.9 6.9 %collective-permute-start = (bf16[16,256]{1,0:T(8,128)(2,1)S(1)}, bf16[16,256]{1,0:T(8,128)(2,1)S(1)}, u32[]{:S(2)}, u32[]{:S(2)}) collective-permute-start(bf16[16,256]{1,0:T(8,128)(2,1)S(1)} %get-tuple-element.38), channel_id=1, source_target_pairs={{0,1},{1,2},{2,3},{3,4},{4,5},{5,6},{6,7},{7,8},{8,9},{9,10},{10,1... | collective-permute-start | bytes 24584 | tf_op jit(solution)/shard_map/ppermute | solution.py:398
  6.8 5.0 %collective-permute-start.1 = (bf16[16,256]{1,0:T(8,128)(2,1)S(1)}, bf16[16,256]{1,0:T(8,128)(2,1)S(1)}, u32[]{:S(2)}, u32[]{:S(2)}) collective-permute-start(bf16[16,256]{1,0:T(8,128)(2,1)S(1)} %get-tuple-element.39), channel_id=1, source_target_pairs={{1,0},{2,1},{3,2},{4,3},{5,4},{6,5},{7,6},{8,7},{9,8},{10,9},{11,1... | collective-permute-start | bytes 24584 | tf_op jit(solution)/shard_map/ppermute | solution.py:399
  11.8 29.1 %copy-start.1 = (bf16[256,768]{1,0:T(8,128)(2,1)S(1)}, bf16[256,768]{1,0:T(8,128)(2,1)}, u32[]{:S(2)}) copy-start(bf16[256,768]{1,0:T(8,128)(2,1)} %refs_2_.2) | copy-start | bytes 1179652
  11.9 29.1 %copy-start.2 = (bf16[256,256]{1,0:T(8,128)(2,1)S(1)}, bf16[256,256]{1,0:T(8,128)(2,1)}, u32[]{:S(2)}) copy-start(bf16[256,256]{1,0:T(8,128)(2,1)} %refs_3_.3) | copy-start | bytes 393220
  11.9 29.0 %copy-start.6 = (f32[256]{0:T(256)S(1)}, f32[256]{0:T(256)}, u32[]{:S(2)}) copy-start(f32[256]{0:T(256)} %param.17) | copy-start | bytes 3076
  37.1 3.8 %collective-permute-start.2 = (bf16[512,384]{1,0:T(8,128)(2,1)S(1)}, bf16[512,384]{1,0:T(8,128)(2,1)S(1)}, u32[]{:S(2)}, u32[]{:S(2)}) collective-permute-start(bf16[512,384]{1,0:T(8,128)(2,1)S(1)} %bitcast.6), channel_id=1, source_target_pairs={{0,1},{1,0},{2,3},{3,2},{4,5},{5,4},{6,7},{7,6},{8,9},{9,8},{10,11... | collective-permute-start | bytes 1179656 | tf_op jit(solution)/shard_map/ppermute | solution.py:411
  67.9 11.5 %all-to-all-start.2 = ((bf16[4,320,256]{2,1,0:T(8,128)(2,1)}), bf16[4,320,256]{2,1,0:T(8,128)(2,1)S(1)}, u32[]{:S(2)}, u32[]{:S(2)}) async-start(bf16[4,320,256]{2,1,0:T(8,128)(2,1)} %get-tuple-element.43), calls=%async_computation.2 | async-start | bytes 1310720 | tf_op jit(solution)/shard_map/all_to_all | solution.py:35
  71.4 8.0 %collective-permute-start.5 = (bf16[16,256]{1,0:T(8,128)(2,1)}, bf16[16,256]{1,0:T(8,128)(2,1)S(1)}, u32[]{:S(2)}, u32[]{:S(2)}) collective-permute-start(bf16[16,256]{1,0:T(8,128)(2,1)} %get-tuple-element.48.refs_0_), channel_id=1, source_target_pairs={{0,192},{64,0},{128,64},{192,128},{1,193},{65,1},{129,65},{193,129... | collective-permute-start | bytes 24584 | tf_op jit(solution)/shard_map/ppermute | solution.py:44
  74.2 5.2 %collective-permute-start.4 = (bf16[16,256]{1,0:T(8,128)(2,1)}, bf16[16,256]{1,0:T(8,128)(2,1)S(1)}, u32[]{:S(2)}, u32[]{:S(2)}) collective-permute-start(bf16[16,256]{1,0:T(8,128)(2,1)} %get-tuple-element.48.refs_0_), channel_id=1, source_target_pairs={{0,128},{64,192},{128,0},{192,64},{1,129},{65,193},{129,1},{193,65... | collective-permute-start | bytes 24584 | tf_op jit(solution)/shard_map/ppermute | solution.py:44
  74.6 4.8 %collective-permute-start.3 = (bf16[16,256]{1,0:T(8,128)(2,1)}, bf16[16,256]{1,0:T(8,128)(2,1)S(1)}, u32[]{:S(2)}, u32[]{:S(2)}) collective-permute-start(bf16[16,256]{1,0:T(8,128)(2,1)} %get-tuple-element.48.refs_0_), channel_id=1, source_target_pairs={{0,64},{64,128},{128,192},{192,0},{1,65},{65,129},{129,193},{193,1... | collective-permute-start | bytes 24584 | tf_op jit(solution)/shard_map/ppermute | solution.py:44
  79.4 15.8 %copy-start.9 = (bf16[16,256]{1,0:T(8,128)(2,1)S(1)}, bf16[16,256]{1,0:T(8,128)(2,1)}, u32[]{:S(2)}) copy-start(bf16[16,256]{1,0:T(8,128)(2,1)} %get-tuple-element.53) | copy-start | bytes 24580
  79.4 19.9 %copy-start.8 = (bf16[16,256]{1,0:T(8,128)(2,1)S(1)}, bf16[16,256]{1,0:T(8,128)(2,1)}, u32[]{:S(2)}) copy-start(bf16[16,256]{1,0:T(8,128)(2,1)} %get-tuple-element.54) | copy-start | bytes 24580
  79.5 6.2 %collective-permute-start.6 = (bf16[4,320,256]{2,1,0:T(8,128)(2,1)S(1)}, bf16[4,320,256]{2,1,0:T(8,128)(2,1)S(1)}, u32[]{:S(2)}, u32[]{:S(2)}) collective-permute-start(bf16[4,320,256]{2,1,0:T(8,128)(2,1)S(1)} %all-to-all-done.2.refs_4_), channel_id=1, source_target_pairs={{0,1},{1,0},{2,3},{3,2},{4,5},{5,4},{6,7},{7,6},{8,9},{9,8},{10,11... | collective-permute-start | bytes 1966088 | tf_op jit(solution)/shard_map/ppermute | solution.py:442
  89.5 23.6 %all-to-all-start.3 = ((bf16[8,128,256]{2,1,0:T(8,128)(2,1)}), bf16[8,128,256]{2,1,0:T(8,128)(2,1)S(1)}, u32[]{:S(2)}, u32[]{:S(2)}) async-start(bf16[8,128,256]{2,1,0:T(8,128)(2,1)} %shard_map.141), calls=%async_computation.3 | async-start | bytes 1048576 | tf_op jit(solution)/shard_map/all_to_all | solution.py:457
  95.2 8.8 %collective-permute-start.7 = (bf16[16,256]{1,0:T(8,128)(2,1)S(1)}, bf16[16,256]{1,0:T(8,128)(2,1)S(1)}, u32[]{:S(2)}, u32[]{:S(2)}) collective-permute-start(bf16[16,256]{1,0:T(8,128)(2,1)S(1)} %copy-done.9), channel_id=1, source_target_pairs={{0,1},{1,2},{2,3},{3,4},{4,5},{5,6},{6,7},{7,8},{8,9},{9,10},{10,1... | collective-permute-start | bytes 24584 | tf_op jit(solution)/shard_map/ppermute | solution.py:444
  99.4 9.7 %collective-permute-start.8 = (bf16[16,256]{1,0:T(8,128)(2,1)S(1)}, bf16[16,256]{1,0:T(8,128)(2,1)S(1)}, u32[]{:S(2)}, u32[]{:S(2)}) collective-permute-start(bf16[16,256]{1,0:T(8,128)(2,1)S(1)} %copy-done.8), channel_id=1, source_target_pairs={{1,0},{2,1},{3,2},{4,3},{5,4},{6,5},{7,6},{8,7},{9,8},{10,9},{11,1... | collective-permute-start | bytes 24584 | tf_op jit(solution)/shard_map/ppermute | solution.py:443
  113.2 5.3 %collective-permute-start.10 = (bf16[128,256]{1,0:T(8,128)(2,1)S(1)}, bf16[128,256]{1,0:T(8,128)(2,1)S(1)}, u32[]{:S(2)}, u32[]{:S(2)}) collective-permute-start(bf16[128,256]{1,0:T(8,128)(2,1)S(1)} %get-tuple-element.57.refs_2_), channel_id=1, source_target_pairs={{0,32},{1,33},{2,34},{3,35},{4,36},{5,37},{6,38},{7,39},{8,40},{9,... | collective-permute-start | bytes 196616 | tf_op jit(solution)/shard_map/ppermute | solution.py:39
  115.1 3.5 %collective-permute-start.9 = (bf16[112,256]{1,0:T(8,128)(2,1)S(1)}, bf16[112,256]{1,0:T(8,128)(2,1)S(1)}, u32[]{:S(2)}, u32[]{:S(2)}) collective-permute-start(bf16[112,256]{1,0:T(8,128)(2,1)S(1)} %get-tuple-element.56.refs_0_), channel_id=1, source_target_pairs={{0,64},{64,0},{128,192},{192,128},{1,65},{65,1},{129,193},{193,129... | collective-permute-start | bytes 172040 | tf_op jit(solution)/shard_map/ppermute | solution.py:466
  118.5 4.7 %collective-permute-start.12 = (bf16[2,128,256]{2,1,0:T(8,128)(2,1)S(1)}, bf16[2,128,256]{2,1,0:T(8,128)(2,1)S(1)}, u32[]{:S(2)}, u32[]{:S(2)}) collective-permute-start(bf16[2,128,256]{2,1,0:T(8,128)(2,1)S(1)} %get-tuple-element.65.refs_2_), channel_id=1, source_target_pairs={{0,16},{1,17},{2,18},{3,19},{4,20},{5,21},{6,22},{7,23},{8,24},{9,... | collective-permute-start | bytes 393224 | tf_op jit(solution)/shard_map/ppermute | solution.py:39
  118.6 8.2 %collective-permute-start.13 = (bf16[2,128,256]{2,1,0:T(8,128)(2,1)S(1)}, bf16[2,128,256]{2,1,0:T(8,128)(2,1)S(1)}, u32[]{:S(2)}, u32[]{:S(2)}) collective-permute-start(bf16[2,128,256]{2,1,0:T(8,128)(2,1)S(1)} %get-tuple-element.65.refs_2_), channel_id=1, source_target_pairs={{0,1},{1,0},{2,3},{3,2},{4,5},{5,4},{6,7},{7,6},{8,9},{9,8},{10,11... | collective-permute-start | bytes 393224 | tf_op jit(solution)/shard_map/ppermute | solution.py:39
  120.8 6.1 %collective-permute-start.11 = (bf16[112,256]{1,0:T(8,128)(2,1)S(1)}, bf16[112,256]{1,0:T(8,128)(2,1)S(1)}, u32[]{:S(2)}, u32[]{:S(2)}) collective-permute-start(bf16[112,256]{1,0:T(8,128)(2,1)S(1)} %get-tuple-element.64.refs_0_), channel_id=1, source_target_pairs={{0,128},{64,192},{128,0},{192,64},{1,129},{65,193},{129,1},{193,65... | collective-permute-start | bytes 172040 | tf_op jit(solution)/shard_map/ppermute | solution.py:474
  123.2 3.7 %collective-permute-start.14 = (bf16[2,128,256]{2,1,0:T(8,128)(2,1)S(1)}, bf16[2,128,256]{2,1,0:T(8,128)(2,1)S(1)}, u32[]{:S(2)}, u32[]{:S(2)}) collective-permute-start(bf16[2,128,256]{2,1,0:T(8,128)(2,1)S(1)} %collective-permute-done.12.refs_3_), channel_id=1, source_target_pairs={{0,1},{1,0},{2,3},{3,2},{4,5},{5,4},{6,7},{7,6},{8,9},{9,8},{10,11... | collective-permute-start | bytes 393224 | tf_op jit(solution)/shard_map/ppermute | solution.py:39

commit v7 on v6

--- a/solution.py
+++ b/solution.py
@@ -29,10 +29,6 @@
 SWAP = [(i, i ^ 1) for i in range(NX * NZ * NC)]
 UP = [(i, i + 1) for i in range(NX * NZ * NC - 1)]
 DOWN = [(i + 1, i) for i in range(NX * NZ * NC - 1)]
-
-
-def by_x(copies):
-    return lax.all_to_all(copies, "gz", split_axis=0, concat_axis=0, axis_index_groups=X_GROUPS, tiled=True)
 
 
 def flip(value, bit):
@@ -274,27 +270,24 @@
     table = nbr_ref[...].astype(F32)
     table = jnp.concatenate([table, jnp.zeros((32 - OFFS, PTS), F32)], 0).astype(BF)
     grad_ref[...] = grad
-    for x in range(NX):
-        copies_ref[x, :AT_GAIN] = grad
-        copies_ref[x, AT_GAIN:AT_EXT] = gain
-        copies_ref[x, AT_EXT : AT_EXT + PTS] = feat_ref[...]
-        copies_ref[x, AT_EXT + PTS : AT_EXT + PTS + RIM] = prev_ref[...]
-        copies_ref[x, AT_EXT + PTS + RIM : AT_TAB] = next_ref[...]
-        copies_ref[x, AT_TAB:, :PTS] = table[:16]
-        copies_ref[x, AT_TAB:, PTS:] = table[16:]
+    copies_ref[:AT_GAIN] = grad
+    copies_ref[AT_GAIN:AT_EXT] = gain
+    copies_ref[AT_EXT : AT_EXT + PTS] = feat_ref[...]
+    copies_ref[AT_EXT + PTS : AT_EXT + PTS + RIM] = prev_ref[...]
+    copies_ref[AT_EXT + PTS + RIM : AT_TAB] = next_ref[...]
+    copies_ref[AT_TAB:, :PTS] = table[:16]
+    copies_ref[AT_TAB:, PTS:] = table[16:]
     dense_ref[...] = jnp.sum(back_ref[:, 16:].astype(F32), 0).astype(BF)
     block_ref[...] = t_mm(first, rows).astype(BF)
 
 
-def spread_body(grad_ref, nbr_ref, weight, own_ref, down_ref, up_ref, terms, acc):
-    weight_ref, weight_here = weight
+def spread_body(grad_ref, nbr_ref, weight_ref, own_ref, down_ref, up_ref, terms, acc):
     grad = grad_ref[...]
     table = nbr_ref[...].astype(F32)
     points = iota((EXT, PTS), 0).astype(F32)
     for k in range(OFFS):
         hit = one_hot(points == table[k : k + 1])
         terms[k * EXT : (k + 1) * EXT] = mm(hit, grad).astype(BF)
-    weight_here()
     acc[...] = jnp.zeros((EXT, FEAT), F32)
     for k in range(OFFS):
         acc[...] += mm_t(terms[k * EXT : (k + 1) * EXT], weight_ref[k * FEAT : (k + 1) * FEAT])
@@ -310,30 +303,48 @@
     out_ref[...] = (own_ref[...] + mm(hit, rims)).astype(BF)
 
 
-def kernel_grad_body(p0, p1_ref, p2_ref, p3_ref, near_ref, far_ref, out_ref, tab, exts, terms, total):
+def corner():
     x, core = position()
     base = x * 1728 + core * 108
     first_offset = jnp.minimum(lax.shift_right_logical(base, 8), OFFS - 8)
-    first_row = base - first_offset * FEAT - core * 4
+    return first_offset, base - first_offset * FEAT - core * 4, core
+
+
+def chip_terms(held, first_offset, tab, exts, terms):
     gain = jnp.zeros((1, FEAT), F32)
     points = iota((EXT, PTS), 0).astype(F32)
-    for s in range(NX * NC):
-        held = near_ref if s < NX else far_ref
-        rows = held[s % NX, AT_TAB:].astype(F32)
+    for s in range(NX):
+        rows = held[s][AT_TAB:].astype(F32)
         tab[s * 32 : s * 32 + 16] = rows[:, :PTS]
         tab[s * 32 + 16 : s * 32 + 32] = rows[:, PTS:]
-        exts[s * EXT : (s + 1) * EXT] = held[s % NX, AT_EXT:AT_TAB]
-        gain += held[s % NX, AT_GAIN : AT_GAIN + 1].astype(F32)
+        exts[s * EXT : (s + 1) * EXT] = held[s][AT_EXT:AT_TAB]
+        gain += held[s][AT_GAIN : AT_GAIN + 1].astype(F32)
         hits = [one_hot(points == tab[pl.ds(first_offset + (s * 32 + k), 1), :]) for k in range(8)]
-        found = mm(jnp.concatenate(hits, 0), held[s % NX, :PTS]).astype(BF)
+        found = mm(jnp.concatenate(hits, 0), held[s][:PTS]).astype(BF)
         for k in range(8):
             terms[k, s * EXT : (s + 1) * EXT] = found[k * EXT : (k + 1) * EXT]
-    ext_t = jnp.transpose(exts[...])
+    return gain, jnp.transpose(exts[...])
+
+
+def near_grad_body(h0, h1, h2, h3, total_ref, gain_ref, tab, exts, terms):
+    held = (h0, h1, h2, h3)
+    first_offset, _, _ = corner()
+    gain, ext_t = chip_terms(held, first_offset, tab, exts, terms)
+    gain_ref[...] = gain
     for k in range(8):
-        total[k * FEAT : (k + 1) * FEAT] = mm(ext_t, terms[k])
+        total_ref[k * FEAT : (k + 1) * FEAT] = mm(ext_t, terms[k])
+    total_ref[8 * FEAT :] = jnp.zeros((16, FEAT), F32)
+
+
+def kernel_grad_body(p0_ref, p1_ref, p2_ref, p3_ref, near_ref, gain_ref, h0, h1, h2, h3, out_ref, tab, exts, terms, total):
+    held = (h0, h1, h2, h3)
+    first_offset, first_row, core = corner()
+    gain, ext_t = chip_terms(held, first_offset, tab, exts, terms)
+    gain = gain + gain_ref[...]
+    for k in range(8):
+        span = slice(k * FEAT, (k + 1) * FEAT)
+        total[span] = near_ref[span] + mm(ext_t, terms[k])
     total[8 * FEAT :] = jnp.zeros((16, FEAT), F32)
-    p0_ref, p0_here = p0
-    p0_here()
     dense = p0_ref[...].astype(F32) + p1_ref[...].astype(F32) + p2_ref[...].astype(F32) + p3_ref[...].astype(F32)
     dense = dense.astype(BF)
     at = iota((112, FEAT), 0)
@@ -425,34 +436,39 @@
     )
     block_out, grad, grad_copies, dense = call(
         unpack_body,
-        [sds((PTS, FEAT)), sds((PTS, FEAT)), sds((NX, PAY, FEAT)), sds((16, FEAT))],
+        [sds((PTS, FEAT)), sds((PTS, FEAT)), sds((PAY, FEAT)), sds((16, FEAT))],
         returned, rank_row, grad_gain, features, from_prev, from_next, table,
-        pinned=(1, 2, 3), us=1.5, limit=8,
-    )
-    near_grads = by_x(grad_copies)
+        us=1.5, limit=8,
+    )
+    near_grads = [grad_copies] + [flip(grad_copies, 16 * d) for d in (1, 3, 2)]
     dense_groups = over_groups(dense)
     own_part, rim_down, rim_up = call(
         spread_body,
         [sds((PTS, FEAT), F32), sds((RIM, FEAT)), sds((RIM, FEAT))],
         grad, table, conv_weight,
         scratch=[pltpu.VMEM((OFFS * EXT, FEAT), BF), pltpu.VMEM((EXT, FEAT), F32)],
-        fetched=(0, 1), late=(2,), pinned=(0, 1, 2), us=4.0,
+        pinned=(0, 1, 2), us=3.0,
     )
     near_grads, own_part, dense_groups = lax.optimization_barrier((near_grads, own_part, dense_groups))
-    far_grads = lax.ppermute(near_grads, "gz", SWAP)
+    far_grads = [flip(v, 1) for v in near_grads]
     got_down = lax.ppermute(rim_down, "gz", DOWN)
     got_up = lax.ppermute(rim_up, "gz", UP)
+    held_scratch = [
+        pltpu.VMEM((NX * 32, PTS), F32),
+        pltpu.VMEM((NX * EXT, FEAT), BF),
+        pltpu.VMEM((8, NX * EXT, FEAT), BF),
+    ]
+    total_rows = 8 * FEAT + 16
+    near_total, near_gain = call(
+        near_grad_body, [sds((total_rows, FEAT), F32), sds((1, FEAT), F32)], *near_grads,
+        scratch=held_scratch, us=3.0, limit=16,
+    )
     parts = call(
         kernel_grad_body,
         sds((NZ, 128, FEAT)),
-        *dense_groups, near_grads, far_grads, own_part,
-        scratch=[
-            pltpu.VMEM((NX * NC * 32, PTS), F32),
-            pltpu.VMEM((NX * NC * EXT, FEAT), BF),
-            pltpu.VMEM((8, NX * NC * EXT, FEAT), BF),
-            pltpu.VMEM((8 * FEAT + 16, FEAT), F32),
-        ],
-        late=(0,), idle=(6,), pinned=(0,), us=5.0, limit=24,
+        *dense_groups, near_total, near_gain, *far_grads, own_part,
+        scratch=held_scratch + [pltpu.VMEM((total_rows, FEAT), F32)],
+        idle=(10,), pinned=(0,), us=5.0, limit=24,
     )
     z_parts = lax.all_to_all(
         parts, "gz", split_axis=0, concat_axis=0, axis_index_groups=Z_GROUPS, tiled=True

time: 128 us -> 125 us (0.977)
  Pallas kernels: 21.8 us -> 19.6 us
    ppermute x4 -> x11, starting transfers between devices: 6 us -> 15 us  [flip(): lax.ppermute(value, 'gz', [(i, i ^ bit) for i in range(NX * NZ * NC)])]
    ppermute x1 -> x0, starting transfers between devices: 4.48 us -> none  [shards(): far_grads = lax.ppermute(near_grads, 'gz', SWAP)]
    all_to_all x1 -> x0, starting transfers between devices: 3.5 us -> none  [by_x(): lax.all_to_all(copies, 'gz', split_axis=0, concat_axis=0, axis_index_grou...]
    pallas_call x10 -> x11, Pallas kernels: 21.8 us -> 19.6 us  [call(): pl.pallas_call(outer, out_shape=shapes, in_specs=specs, out_specs=[pl.Blo...]
    ppermute x1 -> x0, waiting for transfers between devices: 1.72 us -> none  [shards(): far_grads = lax.ppermute(near_grads, 'gz', SWAP)]
    all_to_all x1, starting transfers between devices: 5.65 us -> 4.28 us  [shards(): lax.all_to_all(parts, 'gz', split_axis=0, concat_axis=0, axis_index_group...]
  transfers between devices with their start and end apart: 17 -> 22, of which waited for: 7 -> 7; matrix products, arithmetic and copies ran while one was open for 0% -> 0% of each run, Pallas kernels for 5% -> 5%
where the time goes in v7:
time: 125 us
  blocking collectives  42.5 us (34%)
  starting transfers between devices  42.2 us (34%)
  Pallas kernels  19.6 us (16%)
  waiting for transfers between devices  19.3 us (15%)
    all_to_all x1, blocking collectives, shards(): lax.all_to_all(send.reshape(32, 16, FEAT + PTS), 'gz', split_axis=0, conc...  23.4 us
    pallas_call x11, Pallas kernels, call(): pl.pallas_call(outer, out_shape=shapes, in_specs=specs, out_specs=[pl.Blo...  19.6 us
    all_to_all x1, blocking collectives, shards(): lax.all_to_all(back, 'gz', split_axis=0, concat_axis=0, axis_index_groups...  19.1 us
    ppermute x11, starting transfers between devices, flip(): lax.ppermute(value, 'gz', [(i, i ^ bit) for i in range(NX * NZ * NC)])  15 us
    ppermute x1, waiting for transfers between devices, shards(): got_down = lax.ppermute(rim_down, 'gz', DOWN)  5.32 us
    ppermute x3, starting transfers between devices, over_groups(): lax.ppermute(value, 'grp', [(i, (i + d) % n) for i in range(n)])  4.99 us
    ppermute x1, starting transfers between devices, shards(): from_prev = lax.ppermute(to_next, 'gz', UP)  4.94 us
    all_to_all x1, starting transfers between devices, shards(): lax.all_to_all(parts, 'gz', split_axis=0, concat_axis=0, axis_index_group...  4.28 us
  transfers between devices with their start and end apart: 22, of which 7 were waited for; matrix products, arithmetic and copies ran while one was open for 0% of the time, Pallas kernels for 5%

profile of v7, /device:TPU:1, one launch (start us, length us, event | category | flops | bytes accessed | tf_op | source)
XLA Modules:
  0.0 124.7 jit_solution(25559076321791908)
XLA Ops:
  0.7 1.2 shard_map.136
  1.9 4.9 %collective-permute-start = (bf16[16,256]{1,0:T(8,128)(2,1)S(1)}, bf16[16,256]{1,0:T(8,128)(2,1)S(1)}, u32[]{:S(2)}, u32[]{:S(2)}) collective-permute-start(bf16[16,256]{1,0:T(8,128)(2,1)S(1)} %get-tuple-element.43), channel_id=1, source_target_pairs={{0,1},{1,2},{2,3},{3,4},{4,5},{5,6},{6,7},{7,8},{8,9},{9,10},{10,1... | collective-permute-start | bytes 24584 | tf_op jit(solution)/shard_map/ppermute | solution.py:409
  6.8 1.9 %collective-permute-start.1 = (bf16[16,256]{1,0:T(8,128)(2,1)S(1)}, bf16[16,256]{1,0:T(8,128)(2,1)S(1)}, u32[]{:S(2)}, u32[]{:S(2)}) collective-permute-start(bf16[16,256]{1,0:T(8,128)(2,1)S(1)} %get-tuple-element.44), channel_id=1, source_target_pairs={{1,0},{2,1},{3,2},{4,3},{5,4},{6,5},{7,6},{8,7},{9,8},{10,9},{11,1... | collective-permute-start | bytes 24584 | tf_op jit(solution)/shard_map/ppermute | solution.py:410
  8.8 0.0 collective-permute-done.refs_1_.refs_4_
  8.8 3.0 %collective-permute-done.1.refs_2_.refs_5_ = bf16[16,256]{1,0:T(8,128)(2,1)S(1)} collective-permute-done((bf16[16,256]{1,0:T(8,128)(2,1)S(1)}, bf16[16,256]{1,0:T(8,128)(2,1)S(1)}, u32[]{:S(2)}, u32[]{:S(2)}) %collective-permute-start.1) | collective-permute-done | bytes 8224 | tf_op jit(solution)/shard_map/ppermute | solution.py:410
  11.8 0.0 copy-done.3
  11.8 0.0 copy-done
  11.8 0.0 copy-start.1
  11.8 0.0 copy-start.2
  11.9 0.0 copy-start.6
  11.9 1.8 %shard_map.137 = bf16[512,384]{1,0:T(8,128)(2,1)S(1)} custom-call(bf16[128,256]{1,0:T(8,128)(2,1)S(1)} %copy-done.4, bf16[16,256]{1,0:T(8,128)(2,1)S(1)} %collective-permute-done.refs_1_.refs_4_, bf16[16,256]{1,0:T(8,128)(2,1)S(1)} %collective-permute-done.1.refs_2_.refs_5_, s32[27,128]{1,0:T(8,128)S(1)} %bitcast.9, s32[1,128]{1,0:T(1,128)S(1)} %bitcast.13, ...), custom_call_target="tpu_custom_call" | custom-call | flops 3300000000 | bytes 262144 | tf_op jit(solution)/shard_map/pallas_call | solution.py:106
  13.7 23.4 %all_to_all.15 = bf16[32,16,384]{2,1,0:T(8,128)(2,1)S(1)} all-to-all(bf16[32,16,384]{2,1,0:T(8,128)(2,1)S(1)} %bitcast.8), channel_id=1, replica_groups={{0,2,4,6,8,10,12,14,16,18,20,22,24,26,28,30,32,34,36,38,40,42,44,46,48,..., dimensions={0} | all-to-all | bytes 786432 | tf_op jit(solution)/shard_map/all_to_all | solution.py:418
  37.1 2.4 %collective-permute-start.2 = (bf16[512,384]{1,0:T(8,128)(2,1)S(1)}, bf16[512,384]{1,0:T(8,128)(2,1)S(1)}, u32[]{:S(2)}, u32[]{:S(2)}) collective-permute-start(bf16[512,384]{1,0:T(8,128)(2,1)S(1)} %bitcast.6), channel_id=1, source_target_pairs={{0,1},{1,0},{2,3},{3,2},{4,5},{5,4},{6,7},{7,6},{8,9},{9,8},{10,11... | collective-permute-start | bytes 1179656 | tf_op jit(solution)/shard_map/ppermute | solution.py:422
  39.5 1.3 %collective-permute-done.2.refs_1_ = bf16[512,384]{1,0:T(8,128)(2,1)S(1)} collective-permute-done((bf16[512,384]{1,0:T(8,128)(2,1)S(1)}, bf16[512,384]{1,0:T(8,128)(2,1)S(1)}, u32[]{:S(2)}, u32[]{:S(2)}) %collective-permute-start.2) | collective-permute-done | bytes 393248 | tf_op jit(solution)/shard_map/ppermute | solution.py:422
  40.9 6.0 %shard_map.138 = (bf16[32,32,256]{2,1,0:T(8,128)(2,1)S(1)}, f32[1,256]{1,0:T(1,128)S(1)}) custom-call(bf16[512,384]{1,0:T(8,128)(2,1)S(1)} %bitcast.7, bf16[512,384]{1,0:T(8,128)(2,1)S(1)} %collective-permute-done.2.refs_1_, bf16[256,768]{1,0:T(8,128)(2,1)S(1)} %copy-done.1, bf16[256,256]{1,0:T(8,128)(2,1)S(1)} %copy-done.2, f32[1,256]{1,0:T(1,128)S(1)} %bitcast.12), custom_call_target="tpu_custom_call" | custom-call | flops 6600000000 | bytes 262144 | tf_op jit(solution)/shard_map/pallas_call | solution.py:106
  46.9 19.1 %all_to_all.16.refs_0_ = bf16[32,32,256]{2,1,0:T(8,128)(2,1)S(1)} all-to-all(bf16[32,32,256]{2,1,0:T(8,128)(2,1)S(1)} %get-tuple-element.45), channel_id=1, replica_groups={{0,2,4,6,8,10,12,14,16,18,20,22,24,26,28,30,32,34,36,38,40,42,44,46,48,..., dimensions={0} | all-to-all | bytes 1048576 | tf_op jit(solution)/shard_map/all_to_all | solution.py:434
  66.0 1.0 shard_map.139
  67.0 1.3 %collective-permute-start.6 = (bf16[16,256]{1,0:T(8,128)(2,1)S(1)}, bf16[16,256]{1,0:T(8,128)(2,1)S(1)}, u32[]{:S(2)}, u32[]{:S(2)}) collective-permute-start(bf16[16,256]{1,0:T(8,128)(2,1)S(1)} %get-tuple-element.53.refs_0_), channel_id=1, source_target_pairs={{0,64},{64,128},{128,192},{192,0},{1,65},{65,129},{129,193},{193,1... | collective-permute-start | bytes 24584 | tf_op jit(solution)/shard_map/ppermute | solution.py:40
  68.3 0.4 collective-permute-start.3
  68.7 1.9 %collective-permute-start.4 = (bf16[320,256]{1,0:T(8,128)(2,1)S(1)}, bf16[320,256]{1,0:T(8,128)(2,1)S(1)}, u32[]{:S(2)}, u32[]{:S(2)}) collective-permute-start(bf16[320,256]{1,0:T(8,128)(2,1)S(1)} %get-tuple-element.57.refs_0_), channel_id=1, source_target_pairs={{0,48},{1,49},{2,50},{3,51},{4,52},{5,53},{6,54},{7,55},{8,56},{9,... | collective-permute-start | bytes 491528 | tf_op jit(solution)/shard_map/ppermute | solution.py:35
  70.6 1.0 collective-permute-start.5
  71.6 2.6 %collective-permute-start.7 = (bf16[16,256]{1,0:T(8,128)(2,1)S(1)}, bf16[16,256]{1,0:T(8,128)(2,1)S(1)}, u32[]{:S(2)}, u32[]{:S(2)}) collective-permute-start(bf16[16,256]{1,0:T(8,128)(2,1)S(1)} %get-tuple-element.53.refs_0_), channel_id=1, source_target_pairs={{0,128},{64,192},{128,0},{192,64},{1,129},{65,193},{129,1},{193,65... | collective-permute-start | bytes 24584 | tf_op jit(solution)/shard_map/ppermute | solution.py:40
  74.2 0.0 collective-permute-done.6.refs_1_
  74.2 1.1 collective-permute-start.8
  75.3 2.4 %shard_map.140 = (f32[128,256]{1,0:T(8,128)}, bf16[16,256]{1,0:T(8,128)(2,1)}, bf16[16,256]{1,0:T(8,128)(2,1)}) custom-call(bf16[128,256]{1,0:T(8,128)(2,1)S(1)} %get-tuple-element.49.refs_0_, s32[27,128]{1,0:T(8,128)S(1)} %bitcast.11, bf16[6912,256]{1,0:T(8,128)(2,1)S(1)} %copy-done), custom_call_target="tpu_custom_call" | custom-call | flops 3300000000 | bytes 262144 | tf_op jit(solution)/shard_map/pallas_call | solution.py:106
  77.7 0.0 collective-permute-done.7.refs_2_
  77.7 0.0 collective-permute-done.8.refs_3_
  77.7 0.0 collective-permute-done.3.refs_1_
  77.7 0.0 collective-permute-done.4.refs_2_
  77.7 0.0 collective-permute-done.5.refs_3_
  77.7 5.3 %collective-permute-start.9 = (bf16[320,256]{1,0:T(8,128)(2,1)S(1)}, bf16[320,256]{1,0:T(8,128)(2,1)S(1)}, u32[]{:S(2)}, u32[]{:S(2)}) collective-permute-start(bf16[320,256]{1,0:T(8,128)(2,1)S(1)} %get-tuple-element.57.refs_0_), channel_id=1, source_target_pairs={{0,1},{1,0},{2,3},{3,2},{4,5},{5,4},{6,7},{7,6},{8,9},{9,8},{10,11... | collective-permute-start | bytes 491528 | tf_op jit(solution)/shard_map/ppermute | solution.py:35
  83.0 0.1 collective-permute-start.10
  83.2 0.4 collective-permute-start.11
  83.6 0.1 collective-permute-start.12
  83.7 1.7 %shard_map.141 = (f32[2064,256]{1,0:T(8,128)S(1)}, f32[1,256]{1,0:T(1,128)S(1)}) custom-call(bf16[320,256]{1,0:T(8,128)(2,1)S(1)} %get-tuple-element.57.refs_0_, bf16[320,256]{1,0:T(8,128)(2,1)S(1)} %collective-permute-done.3.refs_1_, bf16[320,256]{1,0:T(8,128)(2,1)S(1)} %collective-permute-done.4.refs_2_, bf16[320,256]{1,0:T(8,128)(2,1)S(1)} %collective-permute-done.5.refs_3_), custom_call_target="tpu_custom_call" | custom-call | flops 3300000000 | bytes 262144 | tf_op jit(solution)/shard_map/pallas_call | solution.py:106
  85.3 0.0 collective-permute-done.9.refs_6_
  85.3 0.0 collective-permute-done.10.refs_7_
  85.3 0.0 collective-permute-done.11.refs_8_
  85.4 0.0 collective-permute-done.12.refs_9_
  85.4 0.0 copy-start.9
  85.4 0.0 copy-start.8
  85.4 2.6 %shard_map.142 = bf16[8,128,256]{2,1,0:T(8,128)(2,1)} custom-call(bf16[16,256]{1,0:T(8,128)(2,1)S(1)} %get-tuple-element.53.refs_0_, bf16[16,256]{1,0:T(8,128)(2,1)S(1)} %collective-permute-done.6.refs_1_, bf16[16,256]{1,0:T(8,128)(2,1)S(1)} %collective-permute-done.7.refs_2_, bf16[16,256]{1,0:T(8,128)(2,1)S(1)} %collective-permute-done.8.refs_3_, ...), custom_call_target="tpu_custom_call" | custom-call | flops 5500000256 | bytes 262144 | tf_op jit(solution)/shard_map/pallas_call | solution.py:106
  88.0 4.3 %all-to-all-start.2 = ((bf16[8,128,256]{2,1,0:T(8,128)(2,1)}), bf16[8,128,256]{2,1,0:T(8,128)(2,1)S(1)}, u32[]{:S(2)}, u32[]{:S(2)}) async-start(bf16[8,128,256]{2,1,0:T(8,128)(2,1)} %shard_map.142), calls=%async_computation.2 | async-start | bytes 1048576 | tf_op jit(solution)/shard_map/all_to_all | solution.py:473
  92.3 0.0 copy-done.9
  92.3 4.2 %collective-permute-start.13 = (bf16[16,256]{1,0:T(8,128)(2,1)S(1)}, bf16[16,256]{1,0:T(8,128)(2,1)S(1)}, u32[]{:S(2)}, u32[]{:S(2)}) collective-permute-start(bf16[16,256]{1,0:T(8,128)(2,1)S(1)} %copy-done.9), channel_id=1, source_target_pairs={{0,1},{1,2},{2,3},{3,4},{4,5},{5,6},{6,7},{7,8},{8,9},{9,10},{10,1... | collective-permute-start | bytes 24584 | tf_op jit(solution)/shard_map/ppermute | solution.py:455
  96.5 1.9 %collective-permute-start.14 = (bf16[16,256]{1,0:T(8,128)(2,1)S(1)}, bf16[16,256]{1,0:T(8,128)(2,1)S(1)}, u32[]{:S(2)}, u32[]{:S(2)}) collective-permute-start(bf16[16,256]{1,0:T(8,128)(2,1)S(1)} %copy-done.8), channel_id=1, source_target_pairs={{1,0},{2,1},{3,2},{4,3},{5,4},{6,5},{7,6},{8,7},{9,8},{10,9},{11,1... | collective-permute-start | bytes 24584 | tf_op jit(solution)/shard_map/ppermute | solution.py:454
  98.5 2.5 %collective-permute-done.13.refs_1_ = bf16[16,256]{1,0:T(8,128)(2,1)S(1)} collective-permute-done((bf16[16,256]{1,0:T(8,128)(2,1)S(1)}, bf16[16,256]{1,0:T(8,128)(2,1)S(1)}, u32[]{:S(2)}, u32[]{:S(2)}) %collective-permute-start.13) | collective-permute-done | bytes 8224 | tf_op jit(solution)/shard_map/ppermute | solution.py:455
  101.0 5.3 %collective-permute-done.14.refs_2_ = bf16[16,256]{1,0:T(8,128)(2,1)S(1)} collective-permute-done((bf16[16,256]{1,0:T(8,128)(2,1)S(1)}, bf16[16,256]{1,0:T(8,128)(2,1)S(1)}, u32[]{:S(2)}, u32[]{:S(2)}) %collective-permute-start.14) | collective-permute-done | bytes 8224 | tf_op jit(solution)/shard_map/ppermute | solution.py:454
  106.3 3.9 %all-to-all-done.2.refs_0_ = bf16[8,128,256]{2,1,0:T(8,128)(2,1)S(1)} async-done(((bf16[8,128,256]{2,1,0:T(8,128)(2,1)}), bf16[8,128,256]{2,1,0:T(8,128)(2,1)S(1)}, u32[]{:S(2)}, u32[]{:S(2)}) %all-to-all-start.2) | async-done | bytes 524320 | tf_op jit(solution)/shard_map/all_to_all | solution.py:473
  110.3 0.1 shard_map.143
  110.3 1.2 collective-permute-start.16
  111.5 0.4 collective-permute-start.15
  111.9 2.6 %collective-permute-done.15.refs_1_ = bf16[112,256]{1,0:T(8,128)(2,1)S(1)} collective-permute-done((bf16[112,256]{1,0:T(8,128)(2,1)S(1)}, bf16[112,256]{1,0:T(8,128)(2,1)S(1)}, u32[]{:S(2)}, u32[]{:S(2)}) %collective-permute-start.15) | collective-permute-done | bytes 57376 | tf_op jit(solution)/shard_map/ppermute | solution.py:482
  114.5 0.5 collective-permute-done.16.refs_3_
  115.0 0.4 collective-permute-start.18
  115.5 2.0 %collective-permute-start.19 = (bf16[2,128,256]{2,1,0:T(8,128)(2,1)S(1)}, bf16[2,128,256]{2,1,0:T(8,128)(2,1)S(1)}, u32[]{:S(2)}, u32[]{:S(2)}) collective-permute-start(bf16[2,128,256]{2,1,0:T(8,128)(2,1)S(1)} %get-tuple-element.75.refs_2_), channel_id=1, source_target_pairs={{0,1},{1,0},{2,3},{3,2},{4,5},{5,4},{6,7},{7,6},{8,9},{9,8},{10,11... | collective-permute-start | bytes 393224 | tf_op jit(solution)/shard_map/ppermute | solution.py:35
  117.5 2.2 %collective-permute-start.17 = (bf16[112,256]{1,0:T(8,128)(2,1)S(1)}, bf16[112,256]{1,0:T(8,128)(2,1)S(1)}, u32[]{:S(2)}, u32[]{:S(2)}) collective-permute-start(bf16[112,256]{1,0:T(8,128)(2,1)S(1)} %get-tuple-element.74.refs_0_), channel_id=1, source_target_pairs={{0,128},{64,192},{128,0},{192,64},{1,129},{65,193},{129,1},{193,65... | collective-permute-start | bytes 172040 | tf_op jit(solution)/shard_map/ppermute | solution.py:490
  119.6 0.0 collective-permute-done.18.refs_3_
  119.6 2.2 %collective-permute-start.20 = (bf16[2,128,256]{2,1,0:T(8,128)(2,1)S(1)}, bf16[2,128,256]{2,1,0:T(8,128)(2,1)S(1)}, u32[]{:S(2)}, u32[]{:S(2)}) collective-permute-start(bf16[2,128,256]{2,1,0:T(8,128)(2,1)S(1)} %collective-permute-done.18.refs_3_), channel_id=1, source_target_pairs={{0,1},{1,0},{2,3},{3,2},{4,5},{5,4},{6,7},{7,6},{8,9},{9,8},{10,11... | collective-permute-start | bytes 393224 | tf_op jit(solution)/shard_map/ppermute | solution.py:35
  121.8 1.7 %shard_map.145 = bf16[128,256]{1,0:T(8,128)(2,1)} custom-call(f32[128,256]{1,0:T(8,128)} %get-tuple-element.52.refs_10_.refs_0_, bf16[16,256]{1,0:T(8,128)(2,1)S(1)} %collective-permute-done.13.refs_1_, bf16[16,256]{1,0:T(8,128)(2,1)S(1)} %collective-permute-done.14.refs_2_, s32[1,32]{1,0:T(1,128)} %refs_3_.5), custom_call_target="tpu_custom_call" | custom-call | flops 3300000000 | bytes 262144 | tf_op jit(solution)/shard_map/pallas_call | solution.py:106
  123.5 0.0 collective-permute-done.17.refs_1_
  123.5 0.0 collective-permute-done.19.refs_4_
  123.6 0.0 collective-permute-done.20.refs_5_
  123.6 1.1 shard_map.146
  (13 shorter events, 0.0 us)
Async XLA Ops:
  0.6 11.2 %copy-start.4 = (bf16[128,256]{1,0:T(8,128)(2,1)S(1)}, bf16[128,256]{1,0:T(8,128)(2,1)}, u32[]{:S(2)}) copy-start(bf16[128,256]{1,0:T(8,128)(2,1)} %refs_3_.4) | copy-start | bytes 196612
  0.6 11.2 %copy-start.5 = (s32[128,27]{0,1:T(8,128)S(1)}, s32[128,27]{0,1:T(8,128)}, u32[]{:S(2)}) copy-start(s32[128,27]{0,1:T(8,128)} %param.11) | copy-start | bytes 41476
  0.7 11.2 %copy-start.7 = (s32[128]{0:T(128)S(1)}, s32[128]{0:T(128)}, u32[]{:S(2)}) copy-start(s32[128]{0:T(128)} %param.10) | copy-start | bytes 1540
  0.7 11.2 %copy-start.3 = (bf16[128,256]{1,0:T(8,128)(2,1)S(1)}, bf16[128,256]{1,0:T(8,128)(2,1)}, u32[]{:S(2)}) copy-start(bf16[128,256]{1,0:T(8,128)(2,1)} %refs_5_.1) | copy-start | bytes 196612
  0.7 11.2 %copy-start = (bf16[6912,256]{1,0:T(8,128)(2,1)S(1)}, bf16[6912,256]{1,0:T(8,128)(2,1)}, u32[]{:S(2)}) copy-start(bf16[6912,256]{1,0:T(8,128)(2,1)} %refs_2_.3) | copy-start | bytes 10616836
  1.9 6.9 %collective-permute-start = (bf16[16,256]{1,0:T(8,128)(2,1)S(1)}, bf16[16,256]{1,0:T(8,128)(2,1)S(1)}, u32[]{:S(2)}, u32[]{:S(2)}) collective-permute-start(bf16[16,256]{1,0:T(8,128)(2,1)S(1)} %get-tuple-element.43), channel_id=1, source_target_pairs={{0,1},{1,2},{2,3},{3,4},{4,5},{5,6},{6,7},{7,8},{8,9},{9,10},{10,1... | collective-permute-start | bytes 24584 | tf_op jit(solution)/shard_map/ppermute | solution.py:409
  6.8 5.0 %collective-permute-start.1 = (bf16[16,256]{1,0:T(8,128)(2,1)S(1)}, bf16[16,256]{1,0:T(8,128)(2,1)S(1)}, u32[]{:S(2)}, u32[]{:S(2)}) collective-permute-start(bf16[16,256]{1,0:T(8,128)(2,1)S(1)} %get-tuple-element.44), channel_id=1, source_target_pairs={{1,0},{2,1},{3,2},{4,3},{5,4},{6,5},{7,6},{8,7},{9,8},{10,9},{11,1... | collective-permute-start | bytes 24584 | tf_op jit(solution)/shard_map/ppermute | solution.py:410
  11.8 29.1 %copy-start.1 = (bf16[256,768]{1,0:T(8,128)(2,1)S(1)}, bf16[256,768]{1,0:T(8,128)(2,1)}, u32[]{:S(2)}) copy-start(bf16[256,768]{1,0:T(8,128)(2,1)} %refs_2_.2) | copy-start | bytes 1179652
  11.8 29.1 %copy-start.2 = (bf16[256,256]{1,0:T(8,128)(2,1)S(1)}, bf16[256,256]{1,0:T(8,128)(2,1)}, u32[]{:S(2)}) copy-start(bf16[256,256]{1,0:T(8,128)(2,1)} %refs_3_.3) | copy-start | bytes 393220
  11.9 29.0 %copy-start.6 = (f32[256]{0:T(256)S(1)}, f32[256]{0:T(256)}, u32[]{:S(2)}) copy-start(f32[256]{0:T(256)} %param.17) | copy-start | bytes 3076
  37.1 3.8 %collective-permute-start.2 = (bf16[512,384]{1,0:T(8,128)(2,1)S(1)}, bf16[512,384]{1,0:T(8,128)(2,1)S(1)}, u32[]{:S(2)}, u32[]{:S(2)}) collective-permute-start(bf16[512,384]{1,0:T(8,128)(2,1)S(1)} %bitcast.6), channel_id=1, source_target_pairs={{0,1},{1,0},{2,3},{3,2},{4,5},{5,4},{6,7},{7,6},{8,9},{9,8},{10,11... | collective-permute-start | bytes 1179656 | tf_op jit(solution)/shard_map/ppermute | solution.py:422
  67.0 7.2 %collective-permute-start.6 = (bf16[16,256]{1,0:T(8,128)(2,1)S(1)}, bf16[16,256]{1,0:T(8,128)(2,1)S(1)}, u32[]{:S(2)}, u32[]{:S(2)}) collective-permute-start(bf16[16,256]{1,0:T(8,128)(2,1)S(1)} %get-tuple-element.53.refs_0_), channel_id=1, source_target_pairs={{0,64},{64,128},{128,192},{192,0},{1,65},{65,129},{129,193},{193,1... | collective-permute-start | bytes 24584 | tf_op jit(solution)/shard_map/ppermute | solution.py:40
  68.3 9.4 %collective-permute-start.3 = (bf16[320,256]{1,0:T(8,128)(2,1)S(1)}, bf16[320,256]{1,0:T(8,128)(2,1)S(1)}, u32[]{:S(2)}, u32[]{:S(2)}) collective-permute-start(bf16[320,256]{1,0:T(8,128)(2,1)S(1)} %get-tuple-element.57.refs_0_), channel_id=1, source_target_pairs={{0,16},{1,17},{2,18},{3,19},{4,20},{5,21},{6,22},{7,23},{8,24},{9,... | collective-permute-start | bytes 491528 | tf_op jit(solution)/shard_map/ppermute | solution.py:35
  68.7 9.0 %collective-permute-start.4 = (bf16[320,256]{1,0:T(8,128)(2,1)S(1)}, bf16[320,256]{1,0:T(8,128)(2,1)S(1)}, u32[]{:S(2)}, u32[]{:S(2)}) collective-permute-start(bf16[320,256]{1,0:T(8,128)(2,1)S(1)} %get-tuple-element.57.refs_0_), channel_id=1, source_target_pairs={{0,48},{1,49},{2,50},{3,51},{4,52},{5,53},{6,54},{7,55},{8,56},{9,... | collective-permute-start | bytes 491528 | tf_op jit(solution)/shard_map/ppermute | solution.py:35
  70.6 7.1 %collective-permute-start.5 = (bf16[320,256]{1,0:T(8,128)(2,1)S(1)}, bf16[320,256]{1,0:T(8,128)(2,1)S(1)}, u32[]{:S(2)}, u32[]{:S(2)}) collective-permute-start(bf16[320,256]{1,0:T(8,128)(2,1)S(1)} %get-tuple-element.57.refs_0_), channel_id=1, source_target_pairs={{0,32},{1,33},{2,34},{3,35},{4,36},{5,37},{6,38},{7,39},{8,40},{9,... | collective-permute-start | bytes 491528 | tf_op jit(solution)/shard_map/ppermute | solution.py:35
  71.6 6.1 %collective-permute-start.7 = (bf16[16,256]{1,0:T(8,128)(2,1)S(1)}, bf16[16,256]{1,0:T(8,128)(2,1)S(1)}, u32[]{:S(2)}, u32[]{:S(2)}) collective-permute-start(bf16[16,256]{1,0:T(8,128)(2,1)S(1)} %get-tuple-element.53.refs_0_), channel_id=1, source_target_pairs={{0,128},{64,192},{128,0},{192,64},{1,129},{65,193},{129,1},{193,65... | collective-permute-start | bytes 24584 | tf_op jit(solution)/shard_map/ppermute | solution.py:40
  74.2 3.5 %collective-permute-start.8 = (bf16[16,256]{1,0:T(8,128)(2,1)S(1)}, bf16[16,256]{1,0:T(8,128)(2,1)S(1)}, u32[]{:S(2)}, u32[]{:S(2)}) collective-permute-start(bf16[16,256]{1,0:T(8,128)(2,1)S(1)} %get-tuple-element.53.refs_0_), channel_id=1, source_target_pairs={{0,192},{64,0},{128,64},{192,128},{1,193},{65,1},{129,65},{193,129... | collective-permute-start | bytes 24584 | tf_op jit(solution)/shard_map/ppermute | solution.py:40
  77.7 7.6 %collective-permute-start.9 = (bf16[320,256]{1,0:T(8,128)(2,1)S(1)}, bf16[320,256]{1,0:T(8,128)(2,1)S(1)}, u32[]{:S(2)}, u32[]{:S(2)}) collective-permute-start(bf16[320,256]{1,0:T(8,128)(2,1)S(1)} %get-tuple-element.57.refs_0_), channel_id=1, source_target_pairs={{0,1},{1,0},{2,3},{3,2},{4,5},{5,4},{6,7},{7,6},{8,9},{9,8},{10,11... | collective-permute-start | bytes 491528 | tf_op jit(solution)/shard_map/ppermute | solution.py:35
  83.0 2.3 %collective-permute-start.10 = (bf16[320,256]{1,0:T(8,128)(2,1)S(1)}, bf16[320,256]{1,0:T(8,128)(2,1)S(1)}, u32[]{:S(2)}, u32[]{:S(2)}) collective-permute-start(bf16[320,256]{1,0:T(8,128)(2,1)S(1)} %collective-permute-done.3.refs_1_), channel_id=1, source_target_pairs={{0,1},{1,0},{2,3},{3,2},{4,5},{5,4},{6,7},{7,6},{8,9},{9,8},{10,11... | collective-permute-start | bytes 491528 | tf_op jit(solution)/shard_map/ppermute | solution.py:35
  83.2 2.2 %collective-permute-start.11 = (bf16[320,256]{1,0:T(8,128)(2,1)S(1)}, bf16[320,256]{1,0:T(8,128)(2,1)S(1)}, u32[]{:S(2)}, u32[]{:S(2)}) collective-permute-start(bf16[320,256]{1,0:T(8,128)(2,1)S(1)} %collective-permute-done.4.refs_2_), channel_id=1, source_target_pairs={{0,1},{1,0},{2,3},{3,2},{4,5},{5,4},{6,7},{7,6},{8,9},{9,8},{10,11... | collective-permute-start | bytes 491528 | tf_op jit(solution)/shard_map/ppermute | solution.py:35
  83.6 1.8 %collective-permute-start.12 = (bf16[320,256]{1,0:T(8,128)(2,1)S(1)}, bf16[320,256]{1,0:T(8,128)(2,1)S(1)}, u32[]{:S(2)}, u32[]{:S(2)}) collective-permute-start(bf16[320,256]{1,0:T(8,128)(2,1)S(1)} %collective-permute-done.5.refs_3_), channel_id=1, source_target_pairs={{0,1},{1,0},{2,3},{3,2},{4,5},{5,4},{6,7},{7,6},{8,9},{9,8},{10,11... | collective-permute-start | bytes 491528 | tf_op jit(solution)/shard_map/ppermute | solution.py:35
  85.4 6.9 %copy-start.9 = (bf16[16,256]{1,0:T(8,128)(2,1)S(1)}, bf16[16,256]{1,0:T(8,128)(2,1)}, u32[]{:S(2)}) copy-start(bf16[16,256]{1,0:T(8,128)(2,1)} %get-tuple-element.63) | copy-start | bytes 24580
  85.4 11.2 %copy-start.8 = (bf16[16,256]{1,0:T(8,128)(2,1)S(1)}, bf16[16,256]{1,0:T(8,128)(2,1)}, u32[]{:S(2)}) copy-start(bf16[16,256]{1,0:T(8,128)(2,1)} %get-tuple-element.64) | copy-start | bytes 24580
  88.0 22.2 %all-to-all-start.2 = ((bf16[8,128,256]{2,1,0:T(8,128)(2,1)}), bf16[8,128,256]{2,1,0:T(8,128)(2,1)S(1)}, u32[]{:S(2)}, u32[]{:S(2)}) async-start(bf16[8,128,256]{2,1,0:T(8,128)(2,1)} %shard_map.142), calls=%async_computation.2 | async-start | bytes 1048576 | tf_op jit(solution)/shard_map/all_to_all | solution.py:473
  92.3 8.7 %collective-permute-start.13 = (bf16[16,256]{1,0:T(8,128)(2,1)S(1)}, bf16[16,256]{1,0:T(8,128)(2,1)S(1)}, u32[]{:S(2)}, u32[]{:S(2)}) collective-permute-start(bf16[16,256]{1,0:T(8,128)(2,1)S(1)} %copy-done.9), channel_id=1, source_target_pairs={{0,1},{1,2},{2,3},{3,4},{4,5},{5,6},{6,7},{7,8},{8,9},{9,10},{10,1... | collective-permute-start | bytes 24584 | tf_op jit(solution)/shard_map/ppermute | solution.py:455
  96.5 9.8 %collective-permute-start.14 = (bf16[16,256]{1,0:T(8,128)(2,1)S(1)}, bf16[16,256]{1,0:T(8,128)(2,1)S(1)}, u32[]{:S(2)}, u32[]{:S(2)}) collective-permute-start(bf16[16,256]{1,0:T(8,128)(2,1)S(1)} %copy-done.8), channel_id=1, source_target_pairs={{1,0},{2,1},{3,2},{4,3},{5,4},{6,5},{7,6},{8,7},{9,8},{10,9},{11,1... | collective-permute-start | bytes 24584 | tf_op jit(solution)/shard_map/ppermute | solution.py:454
  110.3 4.7 %collective-permute-start.16 = (bf16[128,256]{1,0:T(8,128)(2,1)S(1)}, bf16[128,256]{1,0:T(8,128)(2,1)S(1)}, u32[]{:S(2)}, u32[]{:S(2)}) collective-permute-start(bf16[128,256]{1,0:T(8,128)(2,1)S(1)} %get-tuple-element.67.refs_2_), channel_id=1, source_target_pairs={{0,32},{1,33},{2,34},{3,35},{4,36},{5,37},{6,38},{7,39},{8,40},{9,... | collective-permute-start | bytes 196616 | tf_op jit(solution)/shard_map/ppermute | solution.py:35
  111.5 3.0 %collective-permute-start.15 = (bf16[112,256]{1,0:T(8,128)(2,1)S(1)}, bf16[112,256]{1,0:T(8,128)(2,1)S(1)}, u32[]{:S(2)}, u32[]{:S(2)}) collective-permute-start(bf16[112,256]{1,0:T(8,128)(2,1)S(1)} %get-tuple-element.66.refs_0_), channel_id=1, source_target_pairs={{0,64},{64,0},{128,192},{192,128},{1,65},{65,1},{129,193},{193,129... | collective-permute-start | bytes 172040 | tf_op jit(solution)/shard_map/ppermute | solution.py:482
  115.0 4.6 %collective-permute-start.18 = (bf16[2,128,256]{2,1,0:T(8,128)(2,1)S(1)}, bf16[2,128,256]{2,1,0:T(8,128)(2,1)S(1)}, u32[]{:S(2)}, u32[]{:S(2)}) collective-permute-start(bf16[2,128,256]{2,1,0:T(8,128)(2,1)S(1)} %get-tuple-element.75.refs_2_), channel_id=1, source_target_pairs={{0,16},{1,17},{2,18},{3,19},{4,20},{5,21},{6,22},{7,23},{8,24},{9,... | collective-permute-start | bytes 393224 | tf_op jit(solution)/shard_map/ppermute | solution.py:35
  115.5 8.1 %collective-permute-start.19 = (bf16[2,128,256]{2,1,0:T(8,128)(2,1)S(1)}, bf16[2,128,256]{2,1,0:T(8,128)(2,1)S(1)}, u32[]{:S(2)}, u32[]{:S(2)}) collective-permute-start(bf16[2,128,256]{2,1,0:T(8,128)(2,1)S(1)} %get-tuple-element.75.refs_2_), channel_id=1, source_target_pairs={{0,1},{1,0},{2,3},{3,2},{4,5},{5,4},{6,7},{7,6},{8,9},{9,8},{10,11... | collective-permute-start | bytes 393224 | tf_op jit(solution)/shard_map/ppermute | solution.py:35
  117.5 6.1 %collective-permute-start.17 = (bf16[112,256]{1,0:T(8,128)(2,1)S(1)}, bf16[112,256]{1,0:T(8,128)(2,1)S(1)}, u32[]{:S(2)}, u32[]{:S(2)}) collective-permute-start(bf16[112,256]{1,0:T(8,128)(2,1)S(1)} %get-tuple-element.74.refs_0_), channel_id=1, source_target_pairs={{0,128},{64,192},{128,0},{192,64},{1,129},{65,193},{129,1},{193,65... | collective-permute-start | bytes 172040 | tf_op jit(solution)/shard_map/ppermute | solution.py:490
  119.6 3.9 %collective-permute-start.20 = (bf16[2,128,256]{2,1,0:T(8,128)(2,1)S(1)}, bf16[2,128,256]{2,1,0:T(8,128)(2,1)S(1)}, u32[]{:S(2)}, u32[]{:S(2)}) collective-permute-start(bf16[2,128,256]{2,1,0:T(8,128)(2,1)S(1)} %collective-permute-done.18.refs_3_), channel_id=1, source_target_pairs={{0,1},{1,0},{2,3},{3,2},{4,5},{5,4},{6,7},{7,6},{8,9},{9,8},{10,11... | collective-permute-start | bytes 393224 | tf_op jit(solution)/shard_map/ppermute | solution.py:35

commit v8 on v7

--- a/solution.py
+++ b/solution.py
@@ -19,7 +19,7 @@
 RIM = 16
 EXT = PTS + 2 * RIM
 SLOTS = 512
-AT_GAIN, AT_EXT, AT_TAB, PAY = 128, 144, 304, 320
+AT_EXT, AT_TAB, PAY = 128, 288, 304
 MIB = 1024 * 1024
 
 NX, NZ, NC = 4, 8, 2
@@ -266,17 +266,18 @@
     first, second = slot_hits(rank_ref[...])
     rows = back_ref[:, :16].reshape(SLOTS, FEAT)
     grad = t_mm(second, rows).astype(BF)
-    gain = jnp.broadcast_to(gg_ref[...], (16, FEAT)).astype(BF)
     table = nbr_ref[...].astype(F32)
-    table = jnp.concatenate([table, jnp.zeros((32 - OFFS, PTS), F32)], 0).astype(BF)
+    low = jnp.concatenate([table[16:], jnp.zeros((32 - OFFS, PTS), F32)], 0)
+    at = iota((16, PTS), 0)
+    gain = gg_ref[...]
+    low = jnp.where(at == 12, gain[:, :PTS], jnp.where(at == 14, gain[:, PTS:], low))
     grad_ref[...] = grad
-    copies_ref[:AT_GAIN] = grad
-    copies_ref[AT_GAIN:AT_EXT] = gain
+    copies_ref[:PTS] = grad
     copies_ref[AT_EXT : AT_EXT + PTS] = feat_ref[...]
     copies_ref[AT_EXT + PTS : AT_EXT + PTS + RIM] = prev_ref[...]
     copies_ref[AT_EXT + PTS + RIM : AT_TAB] = next_ref[...]
-    copies_ref[AT_TAB:, :PTS] = table[:16]
-    copies_ref[AT_TAB:, PTS:] = table[16:]
+    copies_ref[AT_TAB:, :PTS] = table[:16].astype(BF)
+    copies_ref[AT_TAB:, PTS:] = low.astype(BF)
     dense_ref[...] = jnp.sum(back_ref[:, 16:].astype(F32), 0).astype(BF)
     block_ref[...] = t_mm(first, rows).astype(BF)
 
@@ -318,7 +319,7 @@
         tab[s * 32 : s * 32 + 16] = rows[:, :PTS]
         tab[s * 32 + 16 : s * 32 + 32] = rows[:, PTS:]
         exts[s * EXT : (s + 1) * EXT] = held[s][AT_EXT:AT_TAB]
-        gain += held[s][AT_GAIN : AT_GAIN + 1].astype(F32)
+        gain += jnp.concatenate([rows[12:13, PTS:], rows[14:15, PTS:]], 1)
         hits = [one_hot(points == tab[pl.ds(first_offset + (s * 32 + k), 1), :]) for k in range(8)]
         found = mm(jnp.concatenate(hits, 0), held[s][:PTS]).astype(BF)
         for k in range(8):
@@ -485,7 +486,7 @@
     conv_pair, dense_two, got_up, got_down = lax.optimization_barrier((conv_pair, dense_two, got_up, got_down))
     grad_features = call(
         rim_body, sds((PTS, FEAT)), own_part, got_up, got_down, halo_rows,
-        fetched=(0, 3), us=3.0, limit=8,
+        us=3.0, limit=8,
     )
     conv_other = lax.ppermute(conv_pair, "grp", [(i, i ^ 2) for i in range(4)])
     dense_more = flip(dense_two, 16)

time: 125 us -> 124 us (level)
  transfers between devices with their start and end apart: 22 -> 22, of which waited for: 7 -> 8; matrix products, arithmetic and copies ran while one was open for 0% -> 0% of each run, Pallas kernels for 5% -> 4%
where the time goes in v8:
time: 124 us
  blocking collectives  42.5 us (34%)
  starting transfers between devices  42.4 us (34%)
  waiting for transfers between devices  19.5 us (16%)
  Pallas kernels  18.7 us (15%)
    all_to_all x1, blocking collectives, shards(): lax.all_to_all(send.reshape(32, 16, FEAT + PTS), 'gz', split_axis=0, conc...  23.4 us
    all_to_all x1, blocking collectives, shards(): lax.all_to_all(back, 'gz', split_axis=0, concat_axis=0, axis_index_groups...  19.1 us
    pallas_call x11, Pallas kernels, call(): pl.pallas_call(outer, out_shape=shapes, in_specs=specs, out_specs=[pl.Blo...  18.7 us
    ppermute x11, starting transfers between devices, flip(): lax.ppermute(value, 'gz', [(i, i ^ bit) for i in range(NX * NZ * NC)])  15.3 us
    ppermute x1, waiting for transfers between devices, shards(): got_down = lax.ppermute(rim_down, 'gz', DOWN)  5.31 us
    ppermute x3, starting transfers between devices, over_groups(): lax.ppermute(value, 'grp', [(i, (i + d) % n) for i in range(n)])  4.99 us
    ppermute x1, starting transfers between devices, shards(): from_prev = lax.ppermute(to_next, 'gz', UP)  4.94 us
    all_to_all x1, starting transfers between devices, shards(): lax.all_to_all(parts, 'gz', split_axis=0, concat_axis=0, axis_index_group...  4.41 us
  transfers between devices with their start and end apart: 22, of which 8 were waited for; matrix products, arithmetic and copies ran while one was open for 0% of the time, Pallas kernels for 4%

profile of v8, /device:TPU:1, one launch (start us, length us, event | category | flops | bytes accessed | tf_op | source)
XLA Modules:
  0.0 124.1 jit_solution(12873391173945139339)
XLA Ops:
  0.7 1.2 shard_map.136
  1.9 4.9 %collective-permute-start = (bf16[16,256]{1,0:T(8,128)(2,1)S(1)}, bf16[16,256]{1,0:T(8,128)(2,1)S(1)}, u32[]{:S(2)}, u32[]{:S(2)}) collective-permute-start(bf16[16,256]{1,0:T(8,128)(2,1)S(1)} %get-tuple-element.43), channel_id=1, source_target_pairs={{0,1},{1,2},{2,3},{3,4},{4,5},{5,6},{6,7},{7,8},{8,9},{9,10},{10,1... | collective-permute-start | bytes 24584 | tf_op jit(solution)/shard_map/ppermute | solution.py:410
  6.8 1.9 %collective-permute-start.1 = (bf16[16,256]{1,0:T(8,128)(2,1)S(1)}, bf16[16,256]{1,0:T(8,128)(2,1)S(1)}, u32[]{:S(2)}, u32[]{:S(2)}) collective-permute-start(bf16[16,256]{1,0:T(8,128)(2,1)S(1)} %get-tuple-element.44), channel_id=1, source_target_pairs={{1,0},{2,1},{3,2},{4,3},{5,4},{6,5},{7,6},{8,7},{9,8},{10,9},{11,1... | collective-permute-start | bytes 24584 | tf_op jit(solution)/shard_map/ppermute | solution.py:411
  8.8 0.0 collective-permute-done.refs_1_.refs_4_
  8.8 3.0 %collective-permute-done.1.refs_2_.refs_5_ = bf16[16,256]{1,0:T(8,128)(2,1)S(1)} collective-permute-done((bf16[16,256]{1,0:T(8,128)(2,1)S(1)}, bf16[16,256]{1,0:T(8,128)(2,1)S(1)}, u32[]{:S(2)}, u32[]{:S(2)}) %collective-permute-start.1) | collective-permute-done | bytes 8224 | tf_op jit(solution)/shard_map/ppermute | solution.py:411
  11.8 0.0 copy-done.5
  11.8 0.0 copy-start.1
  11.8 0.0 copy-start.2
  11.9 0.0 copy-start.6
  11.9 1.8 %shard_map.137 = bf16[512,384]{1,0:T(8,128)(2,1)S(1)} custom-call(bf16[128,256]{1,0:T(8,128)(2,1)S(1)} %copy-done.4, bf16[16,256]{1,0:T(8,128)(2,1)S(1)} %collective-permute-done.refs_1_.refs_4_, bf16[16,256]{1,0:T(8,128)(2,1)S(1)} %collective-permute-done.1.refs_2_.refs_5_, s32[27,128]{1,0:T(8,128)S(1)} %bitcast.9, s32[1,128]{1,0:T(1,128)S(1)} %bitcast.13, ...), custom_call_target="tpu_custom_call" | custom-call | flops 3300000000 | bytes 262144 | tf_op jit(solution)/shard_map/pallas_call | solution.py:106
  13.7 23.4 %all_to_all.15 = bf16[32,16,384]{2,1,0:T(8,128)(2,1)S(1)} all-to-all(bf16[32,16,384]{2,1,0:T(8,128)(2,1)S(1)} %bitcast.8), channel_id=1, replica_groups={{0,2,4,6,8,10,12,14,16,18,20,22,24,26,28,30,32,34,36,38,40,42,44,46,48,..., dimensions={0} | all-to-all | bytes 786432 | tf_op jit(solution)/shard_map/all_to_all | solution.py:419
  37.1 2.4 %collective-permute-start.2 = (bf16[512,384]{1,0:T(8,128)(2,1)S(1)}, bf16[512,384]{1,0:T(8,128)(2,1)S(1)}, u32[]{:S(2)}, u32[]{:S(2)}) collective-permute-start(bf16[512,384]{1,0:T(8,128)(2,1)S(1)} %bitcast.6), channel_id=1, source_target_pairs={{0,1},{1,0},{2,3},{3,2},{4,5},{5,4},{6,7},{7,6},{8,9},{9,8},{10,11... | collective-permute-start | bytes 1179656 | tf_op jit(solution)/shard_map/ppermute | solution.py:423
  39.5 1.3 %collective-permute-done.2.refs_1_ = bf16[512,384]{1,0:T(8,128)(2,1)S(1)} collective-permute-done((bf16[512,384]{1,0:T(8,128)(2,1)S(1)}, bf16[512,384]{1,0:T(8,128)(2,1)S(1)}, u32[]{:S(2)}, u32[]{:S(2)}) %collective-permute-start.2) | collective-permute-done | bytes 393248 | tf_op jit(solution)/shard_map/ppermute | solution.py:423
  40.9 6.0 %shard_map.138 = (bf16[32,32,256]{2,1,0:T(8,128)(2,1)S(1)}, f32[1,256]{1,0:T(1,128)S(1)}) custom-call(bf16[512,384]{1,0:T(8,128)(2,1)S(1)} %bitcast.7, bf16[512,384]{1,0:T(8,128)(2,1)S(1)} %collective-permute-done.2.refs_1_, bf16[256,768]{1,0:T(8,128)(2,1)S(1)} %copy-done.1, bf16[256,256]{1,0:T(8,128)(2,1)S(1)} %copy-done.2, f32[1,256]{1,0:T(1,128)S(1)} %bitcast.12), custom_call_target="tpu_custom_call" | custom-call | flops 6600000000 | bytes 262144 | tf_op jit(solution)/shard_map/pallas_call | solution.py:106
  46.9 19.1 %all_to_all.16.refs_0_ = bf16[32,32,256]{2,1,0:T(8,128)(2,1)S(1)} all-to-all(bf16[32,32,256]{2,1,0:T(8,128)(2,1)S(1)} %get-tuple-element.45), channel_id=1, replica_groups={{0,2,4,6,8,10,12,14,16,18,20,22,24,26,28,30,32,34,36,38,40,42,44,46,48,..., dimensions={0} | all-to-all | bytes 1048576 | tf_op jit(solution)/shard_map/all_to_all | solution.py:435
  66.0 1.0 shard_map.139
  67.0 1.3 %collective-permute-start.6 = (bf16[16,256]{1,0:T(8,128)(2,1)S(1)}, bf16[16,256]{1,0:T(8,128)(2,1)S(1)}, u32[]{:S(2)}, u32[]{:S(2)}) collective-permute-start(bf16[16,256]{1,0:T(8,128)(2,1)S(1)} %get-tuple-element.53.refs_0_), channel_id=1, source_target_pairs={{0,64},{64,128},{128,192},{192,0},{1,65},{65,129},{129,193},{193,1... | collective-permute-start | bytes 24584 | tf_op jit(solution)/shard_map/ppermute | solution.py:40
  68.3 0.4 collective-permute-start.3
  68.7 1.9 %collective-permute-start.4 = (bf16[304,256]{1,0:T(8,128)(2,1)S(1)}, bf16[304,256]{1,0:T(8,128)(2,1)S(1)}, u32[]{:S(2)}, u32[]{:S(2)}) collective-permute-start(bf16[304,256]{1,0:T(8,128)(2,1)S(1)} %get-tuple-element.57.refs_0_), channel_id=1, source_target_pairs={{0,48},{1,49},{2,50},{3,51},{4,52},{5,53},{6,54},{7,55},{8,56},{9,... | collective-permute-start | bytes 466952 | tf_op jit(solution)/shard_map/ppermute | solution.py:35
  70.6 1.0 collective-permute-start.5
  71.6 2.6 %collective-permute-start.7 = (bf16[16,256]{1,0:T(8,128)(2,1)S(1)}, bf16[16,256]{1,0:T(8,128)(2,1)S(1)}, u32[]{:S(2)}, u32[]{:S(2)}) collective-permute-start(bf16[16,256]{1,0:T(8,128)(2,1)S(1)} %get-tuple-element.53.refs_0_), channel_id=1, source_target_pairs={{0,128},{64,192},{128,0},{192,64},{1,129},{65,193},{129,1},{193,65... | collective-permute-start | bytes 24584 | tf_op jit(solution)/shard_map/ppermute | solution.py:40
  74.2 0.0 collective-permute-done.6.refs_1_
  74.2 1.1 collective-permute-start.8
  75.3 2.4 %shard_map.140 = (f32[128,256]{1,0:T(8,128)}, bf16[16,256]{1,0:T(8,128)(2,1)}, bf16[16,256]{1,0:T(8,128)(2,1)}) custom-call(bf16[128,256]{1,0:T(8,128)(2,1)S(1)} %get-tuple-element.49.refs_0_, s32[27,128]{1,0:T(8,128)S(1)} %bitcast.11, bf16[6912,256]{1,0:T(8,128)(2,1)S(1)} %copy-done), custom_call_target="tpu_custom_call" | custom-call | flops 3300000000 | bytes 262144 | tf_op jit(solution)/shard_map/pallas_call | solution.py:106
  77.7 0.0 collective-permute-done.7.refs_2_
  77.7 0.0 collective-permute-done.8.refs_3_
  77.7 0.0 collective-permute-done.3.refs_1_
  77.7 0.0 collective-permute-done.4.refs_2_
  77.7 0.0 collective-permute-done.5.refs_3_
  77.7 5.3 %collective-permute-start.9 = (bf16[304,256]{1,0:T(8,128)(2,1)S(1)}, bf16[304,256]{1,0:T(8,128)(2,1)S(1)}, u32[]{:S(2)}, u32[]{:S(2)}) collective-permute-start(bf16[304,256]{1,0:T(8,128)(2,1)S(1)} %get-tuple-element.57.refs_0_), channel_id=1, source_target_pairs={{0,1},{1,0},{2,3},{3,2},{4,5},{5,4},{6,7},{7,6},{8,9},{9,8},{10,11... | collective-permute-start | bytes 466952 | tf_op jit(solution)/shard_map/ppermute | solution.py:35
  83.0 0.1 collective-permute-start.10
  83.1 0.4 collective-permute-start.11
  83.6 0.1 collective-permute-start.12
  83.7 1.6 %shard_map.141 = (f32[2064,256]{1,0:T(8,128)S(1)}, f32[1,256]{1,0:T(1,128)S(1)}) custom-call(bf16[304,256]{1,0:T(8,128)(2,1)S(1)} %get-tuple-element.57.refs_0_, bf16[304,256]{1,0:T(8,128)(2,1)S(1)} %collective-permute-done.3.refs_1_, bf16[304,256]{1,0:T(8,128)(2,1)S(1)} %collective-permute-done.4.refs_2_, bf16[304,256]{1,0:T(8,128)(2,1)S(1)} %collective-permute-done.5.refs_3_), custom_call_target="tpu_custom_call" | custom-call | flops 3300000000 | bytes 262144 | tf_op jit(solution)/shard_map/pallas_call | solution.py:106
  85.3 0.0 collective-permute-done.9.refs_6_
  85.3 0.0 collective-permute-done.10.refs_7_
  85.3 0.0 collective-permute-done.11.refs_8_
  85.3 0.0 collective-permute-done.12.refs_9_
  85.4 0.0 copy-start.11
  85.4 0.0 copy-start.10
  85.4 2.6 %shard_map.142 = bf16[8,128,256]{2,1,0:T(8,128)(2,1)} custom-call(bf16[16,256]{1,0:T(8,128)(2,1)S(1)} %get-tuple-element.53.refs_0_, bf16[16,256]{1,0:T(8,128)(2,1)S(1)} %collective-permute-done.6.refs_1_, bf16[16,256]{1,0:T(8,128)(2,1)S(1)} %collective-permute-done.7.refs_2_, bf16[16,256]{1,0:T(8,128)(2,1)S(1)} %collective-permute-done.8.refs_3_, ...), custom_call_target="tpu_custom_call" | custom-call | flops 5500000256 | bytes 262144 | tf_op jit(solution)/shard_map/pallas_call | solution.py:106
  88.0 0.0 copy-start.8
  88.0 0.0 copy-start.9
  88.0 4.4 %all-to-all-start.2 = ((bf16[8,128,256]{2,1,0:T(8,128)(2,1)}), bf16[8,128,256]{2,1,0:T(8,128)(2,1)S(1)}, u32[]{:S(2)}, u32[]{:S(2)}) async-start(bf16[8,128,256]{2,1,0:T(8,128)(2,1)} %shard_map.142), calls=%async_computation.2 | async-start | bytes 1048576 | tf_op jit(solution)/shard_map/all_to_all | solution.py:474
  92.5 4.2 %collective-permute-start.13 = (bf16[16,256]{1,0:T(8,128)(2,1)S(1)}, bf16[16,256]{1,0:T(8,128)(2,1)S(1)}, u32[]{:S(2)}, u32[]{:S(2)}) collective-permute-start(bf16[16,256]{1,0:T(8,128)(2,1)S(1)} %copy-done.11), channel_id=1, source_target_pairs={{0,1},{1,2},{2,3},{3,4},{4,5},{5,6},{6,7},{7,8},{8,9},{9,10},{10,1... | collective-permute-start | bytes 24584 | tf_op jit(solution)/shard_map/ppermute | solution.py:456
  96.7 1.9 %collective-permute-start.14 = (bf16[16,256]{1,0:T(8,128)(2,1)S(1)}, bf16[16,256]{1,0:T(8,128)(2,1)S(1)}, u32[]{:S(2)}, u32[]{:S(2)}) collective-permute-start(bf16[16,256]{1,0:T(8,128)(2,1)S(1)} %copy-done.10), channel_id=1, source_target_pairs={{1,0},{2,1},{3,2},{4,3},{5,4},{6,5},{7,6},{8,7},{9,8},{10,9},{11,1... | collective-permute-start | bytes 24584 | tf_op jit(solution)/shard_map/ppermute | solution.py:455
  98.6 2.6 %collective-permute-done.13.refs_1_ = bf16[16,256]{1,0:T(8,128)(2,1)S(1)} collective-permute-done((bf16[16,256]{1,0:T(8,128)(2,1)S(1)}, bf16[16,256]{1,0:T(8,128)(2,1)S(1)}, u32[]{:S(2)}, u32[]{:S(2)}) %collective-permute-start.13) | collective-permute-done | bytes 8224 | tf_op jit(solution)/shard_map/ppermute | solution.py:456
  101.2 5.3 %collective-permute-done.14.refs_2_ = bf16[16,256]{1,0:T(8,128)(2,1)S(1)} collective-permute-done((bf16[16,256]{1,0:T(8,128)(2,1)S(1)}, bf16[16,256]{1,0:T(8,128)(2,1)S(1)}, u32[]{:S(2)}, u32[]{:S(2)}) %collective-permute-start.14) | collective-permute-done | bytes 8224 | tf_op jit(solution)/shard_map/ppermute | solution.py:455
  106.5 3.9 %all-to-all-done.2.refs_0_ = bf16[8,128,256]{2,1,0:T(8,128)(2,1)S(1)} async-done(((bf16[8,128,256]{2,1,0:T(8,128)(2,1)}), bf16[8,128,256]{2,1,0:T(8,128)(2,1)S(1)}, u32[]{:S(2)}, u32[]{:S(2)}) %all-to-all-start.2) | async-done | bytes 524320 | tf_op jit(solution)/shard_map/all_to_all | solution.py:474
  110.4 0.1 shard_map.143
  110.5 1.2 collective-permute-start.16
  111.7 0.4 collective-permute-start.15
  112.1 2.6 %collective-permute-done.15.refs_1_ = bf16[112,256]{1,0:T(8,128)(2,1)S(1)} collective-permute-done((bf16[112,256]{1,0:T(8,128)(2,1)S(1)}, bf16[112,256]{1,0:T(8,128)(2,1)S(1)}, u32[]{:S(2)}, u32[]{:S(2)}) %collective-permute-start.15) | collective-permute-done | bytes 57376 | tf_op jit(solution)/shard_map/ppermute | solution.py:483
  114.7 0.5 collective-permute-done.16.refs_3_
  115.2 0.4 collective-permute-start.18
  115.6 2.0 %collective-permute-start.19 = (bf16[2,128,256]{2,1,0:T(8,128)(2,1)S(1)}, bf16[2,128,256]{2,1,0:T(8,128)(2,1)S(1)}, u32[]{:S(2)}, u32[]{:S(2)}) collective-permute-start(bf16[2,128,256]{2,1,0:T(8,128)(2,1)S(1)} %get-tuple-element.75.refs_2_), channel_id=1, source_target_pairs={{0,1},{1,0},{2,3},{3,2},{4,5},{5,4},{6,7},{7,6},{8,9},{9,8},{10,11... | collective-permute-start | bytes 393224 | tf_op jit(solution)/shard_map/ppermute | solution.py:35
  117.6 1.8 %collective-permute-start.17 = (bf16[112,256]{1,0:T(8,128)(2,1)S(1)}, bf16[112,256]{1,0:T(8,128)(2,1)S(1)}, u32[]{:S(2)}, u32[]{:S(2)}) collective-permute-start(bf16[112,256]{1,0:T(8,128)(2,1)S(1)} %get-tuple-element.74.refs_0_), channel_id=1, source_target_pairs={{0,128},{64,192},{128,0},{192,64},{1,129},{65,193},{129,1},{193,65... | collective-permute-start | bytes 172040 | tf_op jit(solution)/shard_map/ppermute | solution.py:491
  119.5 0.0 collective-permute-done.18.refs_3_
  119.5 2.5 %collective-permute-start.20 = (bf16[2,128,256]{2,1,0:T(8,128)(2,1)S(1)}, bf16[2,128,256]{2,1,0:T(8,128)(2,1)S(1)}, u32[]{:S(2)}, u32[]{:S(2)}) collective-permute-start(bf16[2,128,256]{2,1,0:T(8,128)(2,1)S(1)} %collective-permute-done.18.refs_3_), channel_id=1, source_target_pairs={{0,1},{1,0},{2,3},{3,2},{4,5},{5,4},{6,7},{7,6},{8,9},{9,8},{10,11... | collective-permute-start | bytes 393224 | tf_op jit(solution)/shard_map/ppermute | solution.py:35
  122.0 0.8 shard_map.145
  122.8 0.0 collective-permute-done.17.refs_1_
  122.8 0.0 collective-permute-done.19.refs_4_
  122.8 0.2 collective-permute-done.20.refs_5_
  123.0 1.1 shard_map.146
  (17 shorter events, 0.1 us)
Async XLA Ops:
  0.6 11.2 %copy-start.4 = (bf16[128,256]{1,0:T(8,128)(2,1)S(1)}, bf16[128,256]{1,0:T(8,128)(2,1)}, u32[]{:S(2)}) copy-start(bf16[128,256]{1,0:T(8,128)(2,1)} %refs_3_.4) | copy-start | bytes 196612
  0.6 11.2 %copy-start.5 = (s32[128,27]{0,1:T(8,128)S(1)}, s32[128,27]{0,1:T(8,128)}, u32[]{:S(2)}) copy-start(s32[128,27]{0,1:T(8,128)} %param.11) | copy-start | bytes 41476
  0.7 11.2 %copy-start.7 = (s32[128]{0:T(128)S(1)}, s32[128]{0:T(128)}, u32[]{:S(2)}) copy-start(s32[128]{0:T(128)} %param.10) | copy-start | bytes 1540
  0.7 11.2 %copy-start.3 = (bf16[128,256]{1,0:T(8,128)(2,1)S(1)}, bf16[128,256]{1,0:T(8,128)(2,1)}, u32[]{:S(2)}) copy-start(bf16[128,256]{1,0:T(8,128)(2,1)} %refs_5_.1) | copy-start | bytes 196612
  0.7 11.2 %copy-start = (bf16[6912,256]{1,0:T(8,128)(2,1)S(1)}, bf16[6912,256]{1,0:T(8,128)(2,1)}, u32[]{:S(2)}) copy-start(bf16[6912,256]{1,0:T(8,128)(2,1)} %refs_2_.3) | copy-start | bytes 10616836
  1.9 6.9 %collective-permute-start = (bf16[16,256]{1,0:T(8,128)(2,1)S(1)}, bf16[16,256]{1,0:T(8,128)(2,1)S(1)}, u32[]{:S(2)}, u32[]{:S(2)}) collective-permute-start(bf16[16,256]{1,0:T(8,128)(2,1)S(1)} %get-tuple-element.43), channel_id=1, source_target_pairs={{0,1},{1,2},{2,3},{3,4},{4,5},{5,6},{6,7},{7,8},{8,9},{9,10},{10,1... | collective-permute-start | bytes 24584 | tf_op jit(solution)/shard_map/ppermute | solution.py:410
  6.8 5.0 %collective-permute-start.1 = (bf16[16,256]{1,0:T(8,128)(2,1)S(1)}, bf16[16,256]{1,0:T(8,128)(2,1)S(1)}, u32[]{:S(2)}, u32[]{:S(2)}) collective-permute-start(bf16[16,256]{1,0:T(8,128)(2,1)S(1)} %get-tuple-element.44), channel_id=1, source_target_pairs={{1,0},{2,1},{3,2},{4,3},{5,4},{6,5},{7,6},{8,7},{9,8},{10,9},{11,1... | collective-permute-start | bytes 24584 | tf_op jit(solution)/shard_map/ppermute | solution.py:411
  11.8 29.1 %copy-start.1 = (bf16[256,768]{1,0:T(8,128)(2,1)S(1)}, bf16[256,768]{1,0:T(8,128)(2,1)}, u32[]{:S(2)}) copy-start(bf16[256,768]{1,0:T(8,128)(2,1)} %refs_2_.2) | copy-start | bytes 1179652
  11.8 29.1 %copy-start.2 = (bf16[256,256]{1,0:T(8,128)(2,1)S(1)}, bf16[256,256]{1,0:T(8,128)(2,1)}, u32[]{:S(2)}) copy-start(bf16[256,256]{1,0:T(8,128)(2,1)} %refs_3_.3) | copy-start | bytes 393220
  11.9 29.0 %copy-start.6 = (f32[256]{0:T(256)S(1)}, f32[256]{0:T(256)}, u32[]{:S(2)}) copy-start(f32[256]{0:T(256)} %param.17) | copy-start | bytes 3076
  37.1 3.8 %collective-permute-start.2 = (bf16[512,384]{1,0:T(8,128)(2,1)S(1)}, bf16[512,384]{1,0:T(8,128)(2,1)S(1)}, u32[]{:S(2)}, u32[]{:S(2)}) collective-permute-start(bf16[512,384]{1,0:T(8,128)(2,1)S(1)} %bitcast.6), channel_id=1, source_target_pairs={{0,1},{1,0},{2,3},{3,2},{4,5},{5,4},{6,7},{7,6},{8,9},{9,8},{10,11... | collective-permute-start | bytes 1179656 | tf_op jit(solution)/shard_map/ppermute | solution.py:423
  67.0 7.2 %collective-permute-start.6 = (bf16[16,256]{1,0:T(8,128)(2,1)S(1)}, bf16[16,256]{1,0:T(8,128)(2,1)S(1)}, u32[]{:S(2)}, u32[]{:S(2)}) collective-permute-start(bf16[16,256]{1,0:T(8,128)(2,1)S(1)} %get-tuple-element.53.refs_0_), channel_id=1, source_target_pairs={{0,64},{64,128},{128,192},{192,0},{1,65},{65,129},{129,193},{193,1... | collective-permute-start | bytes 24584 | tf_op jit(solution)/shard_map/ppermute | solution.py:40
  68.3 9.3 %collective-permute-start.3 = (bf16[304,256]{1,0:T(8,128)(2,1)S(1)}, bf16[304,256]{1,0:T(8,128)(2,1)S(1)}, u32[]{:S(2)}, u32[]{:S(2)}) collective-permute-start(bf16[304,256]{1,0:T(8,128)(2,1)S(1)} %get-tuple-element.57.refs_0_), channel_id=1, source_target_pairs={{0,16},{1,17},{2,18},{3,19},{4,20},{5,21},{6,22},{7,23},{8,24},{9,... | collective-permute-start | bytes 466952 | tf_op jit(solution)/shard_map/ppermute | solution.py:35
  68.7 9.0 %collective-permute-start.4 = (bf16[304,256]{1,0:T(8,128)(2,1)S(1)}, bf16[304,256]{1,0:T(8,128)(2,1)S(1)}, u32[]{:S(2)}, u32[]{:S(2)}) collective-permute-start(bf16[304,256]{1,0:T(8,128)(2,1)S(1)} %get-tuple-element.57.refs_0_), channel_id=1, source_target_pairs={{0,48},{1,49},{2,50},{3,51},{4,52},{5,53},{6,54},{7,55},{8,56},{9,... | collective-permute-start | bytes 466952 | tf_op jit(solution)/shard_map/ppermute | solution.py:35
  70.6 7.1 %collective-permute-start.5 = (bf16[304,256]{1,0:T(8,128)(2,1)S(1)}, bf16[304,256]{1,0:T(8,128)(2,1)S(1)}, u32[]{:S(2)}, u32[]{:S(2)}) collective-permute-start(bf16[304,256]{1,0:T(8,128)(2,1)S(1)} %get-tuple-element.57.refs_0_), channel_id=1, source_target_pairs={{0,32},{1,33},{2,34},{3,35},{4,36},{5,37},{6,38},{7,39},{8,40},{9,... | collective-permute-start | bytes 466952 | tf_op jit(solution)/shard_map/ppermute | solution.py:35
  71.6 6.1 %collective-permute-start.7 = (bf16[16,256]{1,0:T(8,128)(2,1)S(1)}, bf16[16,256]{1,0:T(8,128)(2,1)S(1)}, u32[]{:S(2)}, u32[]{:S(2)}) collective-permute-start(bf16[16,256]{1,0:T(8,128)(2,1)S(1)} %get-tuple-element.53.refs_0_), channel_id=1, source_target_pairs={{0,128},{64,192},{128,0},{192,64},{1,129},{65,193},{129,1},{193,65... | collective-permute-start | bytes 24584 | tf_op jit(solution)/shard_map/ppermute | solution.py:40
  74.2 3.4 %collective-permute-start.8 = (bf16[16,256]{1,0:T(8,128)(2,1)S(1)}, bf16[16,256]{1,0:T(8,128)(2,1)S(1)}, u32[]{:S(2)}, u32[]{:S(2)}) collective-permute-start(bf16[16,256]{1,0:T(8,128)(2,1)S(1)} %get-tuple-element.53.refs_0_), channel_id=1, source_target_pairs={{0,192},{64,0},{128,64},{192,128},{1,193},{65,1},{129,65},{193,129... | collective-permute-start | bytes 24584 | tf_op jit(solution)/shard_map/ppermute | solution.py:40
  77.7 7.6 %collective-permute-start.9 = (bf16[304,256]{1,0:T(8,128)(2,1)S(1)}, bf16[304,256]{1,0:T(8,128)(2,1)S(1)}, u32[]{:S(2)}, u32[]{:S(2)}) collective-permute-start(bf16[304,256]{1,0:T(8,128)(2,1)S(1)} %get-tuple-element.57.refs_0_), channel_id=1, source_target_pairs={{0,1},{1,0},{2,3},{3,2},{4,5},{5,4},{6,7},{7,6},{8,9},{9,8},{10,11... | collective-permute-start | bytes 466952 | tf_op jit(solution)/shard_map/ppermute | solution.py:35
  83.0 2.3 %collective-permute-start.10 = (bf16[304,256]{1,0:T(8,128)(2,1)S(1)}, bf16[304,256]{1,0:T(8,128)(2,1)S(1)}, u32[]{:S(2)}, u32[]{:S(2)}) collective-permute-start(bf16[304,256]{1,0:T(8,128)(2,1)S(1)} %collective-permute-done.3.refs_1_), channel_id=1, source_target_pairs={{0,1},{1,0},{2,3},{3,2},{4,5},{5,4},{6,7},{7,6},{8,9},{9,8},{10,11... | collective-permute-start | bytes 466952 | tf_op jit(solution)/shard_map/ppermute | solution.py:35
  83.1 2.2 %collective-permute-start.11 = (bf16[304,256]{1,0:T(8,128)(2,1)S(1)}, bf16[304,256]{1,0:T(8,128)(2,1)S(1)}, u32[]{:S(2)}, u32[]{:S(2)}) collective-permute-start(bf16[304,256]{1,0:T(8,128)(2,1)S(1)} %collective-permute-done.4.refs_2_), channel_id=1, source_target_pairs={{0,1},{1,0},{2,3},{3,2},{4,5},{5,4},{6,7},{7,6},{8,9},{9,8},{10,11... | collective-permute-start | bytes 466952 | tf_op jit(solution)/shard_map/ppermute | solution.py:35
  83.6 1.8 %collective-permute-start.12 = (bf16[304,256]{1,0:T(8,128)(2,1)S(1)}, bf16[304,256]{1,0:T(8,128)(2,1)S(1)}, u32[]{:S(2)}, u32[]{:S(2)}) collective-permute-start(bf16[304,256]{1,0:T(8,128)(2,1)S(1)} %collective-permute-done.5.refs_3_), channel_id=1, source_target_pairs={{0,1},{1,0},{2,3},{3,2},{4,5},{5,4},{6,7},{7,6},{8,9},{9,8},{10,11... | collective-permute-start | bytes 466952 | tf_op jit(solution)/shard_map/ppermute | solution.py:35
  85.4 7.1 %copy-start.11 = (bf16[16,256]{1,0:T(8,128)(2,1)S(1)}, bf16[16,256]{1,0:T(8,128)(2,1)}, u32[]{:S(2)}) copy-start(bf16[16,256]{1,0:T(8,128)(2,1)} %get-tuple-element.63) | copy-start | bytes 24580
  85.4 11.3 %copy-start.10 = (bf16[16,256]{1,0:T(8,128)(2,1)S(1)}, bf16[16,256]{1,0:T(8,128)(2,1)}, u32[]{:S(2)}) copy-start(bf16[16,256]{1,0:T(8,128)(2,1)} %get-tuple-element.64) | copy-start | bytes 24580
  88.0 34.0 %copy-start.8 = (s32[1,32]{1,0:T(1,128)S(1)}, s32[1,32]{1,0:T(1,128)}, u32[]{:S(2)}) copy-start(s32[1,32]{1,0:T(1,128)} %refs_3_.5) | copy-start | bytes 388
  88.0 34.0 %copy-start.9 = (f32[128,256]{1,0:T(8,128)S(1)}, f32[128,256]{1,0:T(8,128)}, u32[]{:S(2)}) copy-start(f32[128,256]{1,0:T(8,128)} %get-tuple-element.52.refs_10_.refs_0_) | copy-start | bytes 393220
  88.0 22.4 %all-to-all-start.2 = ((bf16[8,128,256]{2,1,0:T(8,128)(2,1)}), bf16[8,128,256]{2,1,0:T(8,128)(2,1)S(1)}, u32[]{:S(2)}, u32[]{:S(2)}) async-start(bf16[8,128,256]{2,1,0:T(8,128)(2,1)} %shard_map.142), calls=%async_computation.2 | async-start | bytes 1048576 | tf_op jit(solution)/shard_map/all_to_all | solution.py:474
  92.5 8.7 %collective-permute-start.13 = (bf16[16,256]{1,0:T(8,128)(2,1)S(1)}, bf16[16,256]{1,0:T(8,128)(2,1)S(1)}, u32[]{:S(2)}, u32[]{:S(2)}) collective-permute-start(bf16[16,256]{1,0:T(8,128)(2,1)S(1)} %copy-done.11), channel_id=1, source_target_pairs={{0,1},{1,2},{2,3},{3,4},{4,5},{5,6},{6,7},{7,8},{8,9},{9,10},{10,1... | collective-permute-start | bytes 24584 | tf_op jit(solution)/shard_map/ppermute | solution.py:456
  96.7 9.8 %collective-permute-start.14 = (bf16[16,256]{1,0:T(8,128)(2,1)S(1)}, bf16[16,256]{1,0:T(8,128)(2,1)S(1)}, u32[]{:S(2)}, u32[]{:S(2)}) collective-permute-start(bf16[16,256]{1,0:T(8,128)(2,1)S(1)} %copy-done.10), channel_id=1, source_target_pairs={{1,0},{2,1},{3,2},{4,3},{5,4},{6,5},{7,6},{8,7},{9,8},{10,9},{11,1... | collective-permute-start | bytes 24584 | tf_op jit(solution)/shard_map/ppermute | solution.py:455
  110.5 4.7 %collective-permute-start.16 = (bf16[128,256]{1,0:T(8,128)(2,1)S(1)}, bf16[128,256]{1,0:T(8,128)(2,1)S(1)}, u32[]{:S(2)}, u32[]{:S(2)}) collective-permute-start(bf16[128,256]{1,0:T(8,128)(2,1)S(1)} %get-tuple-element.67.refs_2_), channel_id=1, source_target_pairs={{0,32},{1,33},{2,34},{3,35},{4,36},{5,37},{6,38},{7,39},{8,40},{9,... | collective-permute-start | bytes 196616 | tf_op jit(solution)/shard_map/ppermute | solution.py:35
  111.7 3.0 %collective-permute-start.15 = (bf16[112,256]{1,0:T(8,128)(2,1)S(1)}, bf16[112,256]{1,0:T(8,128)(2,1)S(1)}, u32[]{:S(2)}, u32[]{:S(2)}) collective-permute-start(bf16[112,256]{1,0:T(8,128)(2,1)S(1)} %get-tuple-element.66.refs_0_), channel_id=1, source_target_pairs={{0,64},{64,0},{128,192},{192,128},{1,65},{65,1},{129,193},{193,129... | collective-permute-start | bytes 172040 | tf_op jit(solution)/shard_map/ppermute | solution.py:483
  115.2 4.2 %collective-permute-start.18 = (bf16[2,128,256]{2,1,0:T(8,128)(2,1)S(1)}, bf16[2,128,256]{2,1,0:T(8,128)(2,1)S(1)}, u32[]{:S(2)}, u32[]{:S(2)}) collective-permute-start(bf16[2,128,256]{2,1,0:T(8,128)(2,1)S(1)} %get-tuple-element.75.refs_2_), channel_id=1, source_target_pairs={{0,16},{1,17},{2,18},{3,19},{4,20},{5,21},{6,22},{7,23},{8,24},{9,... | collective-permute-start | bytes 393224 | tf_op jit(solution)/shard_map/ppermute | solution.py:35
  115.6 7.2 %collective-permute-start.19 = (bf16[2,128,256]{2,1,0:T(8,128)(2,1)S(1)}, bf16[2,128,256]{2,1,0:T(8,128)(2,1)S(1)}, u32[]{:S(2)}, u32[]{:S(2)}) collective-permute-start(bf16[2,128,256]{2,1,0:T(8,128)(2,1)S(1)} %get-tuple-element.75.refs_2_), channel_id=1, source_target_pairs={{0,1},{1,0},{2,3},{3,2},{4,5},{5,4},{6,7},{7,6},{8,9},{9,8},{10,11... | collective-permute-start | bytes 393224 | tf_op jit(solution)/shard_map/ppermute | solution.py:35
  117.6 5.2 %collective-permute-start.17 = (bf16[112,256]{1,0:T(8,128)(2,1)S(1)}, bf16[112,256]{1,0:T(8,128)(2,1)S(1)}, u32[]{:S(2)}, u32[]{:S(2)}) collective-permute-start(bf16[112,256]{1,0:T(8,128)(2,1)S(1)} %get-tuple-element.74.refs_0_), channel_id=1, source_target_pairs={{0,128},{64,192},{128,0},{192,64},{1,129},{65,193},{129,1},{193,65... | collective-permute-start | bytes 172040 | tf_op jit(solution)/shard_map/ppermute | solution.py:491
  119.5 3.5 %collective-permute-start.20 = (bf16[2,128,256]{2,1,0:T(8,128)(2,1)S(1)}, bf16[2,128,256]{2,1,0:T(8,128)(2,1)S(1)}, u32[]{:S(2)}, u32[]{:S(2)}) collective-permute-start(bf16[2,128,256]{2,1,0:T(8,128)(2,1)S(1)} %collective-permute-done.18.refs_3_), channel_id=1, source_target_pairs={{0,1},{1,0},{2,3},{3,2},{4,5},{5,4},{6,7},{7,6},{8,9},{9,8},{10,11... | collective-permute-start | bytes 393224 | tf_op jit(solution)/shard_map/ppermute | solution.py:35

commit v9 on v8

--- a/solution.py
+++ b/solution.py
@@ -373,20 +373,35 @@
 
 
 def last_body(factor, pair_ref, other_ref, *refs):
-    parts, (conv_ref, gain_ref, qkv_ref, proj_ref, rows) = refs[:4], refs[4:]
+    parts, (conv_ref, gain_ref, qkv_ref, proj_ref) = refs[:4], refs[4:]
     total = pair_ref[...].astype(F32) + other_ref[...].astype(F32)
     conv_ref[...] = total[:108] * factor
     gain_ref[...] = total[108:109] * factor
     x, core = position()
-    for s in range(NX * NC):
-        source = (x ^ (s % 2 * 2) ^ (s // 2 % 2)) + NX * (core ^ (s // 4))
-        rows[source] = parts[s // 2][s % 2].astype(F32) * factor
-    for b in range(NX * NC):
-        part, at = b // 2, b % 2 * PTS
-        if part < 3:
-            qkv_ref[at : at + PTS, part * FEAT : (part + 1) * FEAT] = rows[b]
-        else:
-            proj_ref[at : at + PTS] = rows[b]
+
+    def fill(low_parts, high_parts):
+        for s in range(NX):
+            source = x ^ (s % 2 * 2) ^ (s // 2)
+            row = pl.ds(pl.multiple_of((source & 1) * PTS, PTS), PTS)
+            column = pl.multiple_of(lax.shift_right_logical(source, 1) * FEAT, FEAT)
+            qkv_ref[row, pl.ds(column, FEAT)] = low_parts[s // 2][s % 2].astype(F32) * factor
+            block = high_parts[s // 2][s % 2].astype(F32) * factor
+
+            @pl.when(source < 2)
+            def _():
+                qkv_ref[row, 2 * FEAT :] = block
+
+            @pl.when(source >= 2)
+            def _():
+                proj_ref[row, :] = block
+
+    @pl.when(core == 0)
+    def _():
+        fill(parts[:2], parts[2:])
+
+    @pl.when(core == 1)
+    def _():
+        fill(parts[2:], parts[:2])
 
 
 def shards(
@@ -494,7 +509,6 @@
         lambda *refs: last_body(factor, *refs),
         [sds((108, FEAT), F32), sds((1, FEAT), F32), sds((FEAT, 3 * FEAT), F32), sds((FEAT, FEAT), F32)],
         conv_pair, conv_other, dense_two, dense_more, flip(dense_two, 1), flip(dense_more, 1),
-        scratch=[pltpu.VMEM((NX * NC, PTS, FEAT), F32)],
         limit=8,
     )
     return (block_out, grad_features, grad_conv, grad_qkv, grad_proj, gain_sum.reshape(FEAT))

time: 124 us -> 124 us (level)
  no operation moved by 1% of the time
where the time goes in v9:
time: 124 us
  blocking collectives  42.5 us (34%)
  starting transfers between devices  42.4 us (34%)
  waiting for transfers between devices  19.5 us (16%)
  Pallas kernels  18.7 us (15%)
    all_to_all x1, blocking collectives, shards(): lax.all_to_all(send.reshape(32, 16, FEAT + PTS), 'gz', split_axis=0, conc...  23.4 us
    all_to_all x1, blocking collectives, shards(): lax.all_to_all(back, 'gz', split_axis=0, concat_axis=0, axis_index_groups...  19.1 us
    pallas_call x11, Pallas kernels, call(): pl.pallas_call(outer, out_shape=shapes, in_specs=specs, out_specs=[pl.Blo...  18.7 us
    ppermute x11, starting transfers between devices, flip(): lax.ppermute(value, 'gz', [(i, i ^ bit) for i in range(NX * NZ * NC)])  15.3 us
    ppermute x1, waiting for transfers between devices, shards(): got_down = lax.ppermute(rim_down, 'gz', DOWN)  5.31 us
    ppermute x3, starting transfers between devices, over_groups(): lax.ppermute(value, 'grp', [(i, (i + d) % n) for i in range(n)])  4.99 us
    ppermute x1, starting transfers between devices, shards(): from_prev = lax.ppermute(to_next, 'gz', UP)  4.94 us
    all_to_all x1, starting transfers between devices, shards(): lax.all_to_all(parts, 'gz', split_axis=0, concat_axis=0, axis_index_group...  4.41 us
  transfers between devices with their start and end apart: 22, of which 8 were waited for; matrix products, arithmetic and copies ran while one was open for 0% of the time, Pallas kernels for 4%

profile of v9, /device:TPU:1, one launch (start us, length us, event | category | flops | bytes accessed | tf_op | source)
XLA Modules:
  0.0 124.1 jit_solution(5155346736656804674)
XLA Ops:
  0.7 1.2 shard_map.136
  1.9 4.9 %collective-permute-start = (bf16[16,256]{1,0:T(8,128)(2,1)S(1)}, bf16[16,256]{1,0:T(8,128)(2,1)S(1)}, u32[]{:S(2)}, u32[]{:S(2)}) collective-permute-start(bf16[16,256]{1,0:T(8,128)(2,1)S(1)} %get-tuple-element.43), channel_id=1, source_target_pairs={{0,1},{1,2},{2,3},{3,4},{4,5},{5,6},{6,7},{7,8},{8,9},{9,10},{10,1... | collective-permute-start | bytes 24584 | tf_op jit(solution)/shard_map/ppermute | solution.py:425
  6.8 1.9 %collective-permute-start.1 = (bf16[16,256]{1,0:T(8,128)(2,1)S(1)}, bf16[16,256]{1,0:T(8,128)(2,1)S(1)}, u32[]{:S(2)}, u32[]{:S(2)}) collective-permute-start(bf16[16,256]{1,0:T(8,128)(2,1)S(1)} %get-tuple-element.44), channel_id=1, source_target_pairs={{1,0},{2,1},{3,2},{4,3},{5,4},{6,5},{7,6},{8,7},{9,8},{10,9},{11,1... | collective-permute-start | bytes 24584 | tf_op jit(solution)/shard_map/ppermute | solution.py:426
  8.8 0.0 collective-permute-done.refs_1_.refs_4_
  8.8 3.0 %collective-permute-done.1.refs_2_.refs_5_ = bf16[16,256]{1,0:T(8,128)(2,1)S(1)} collective-permute-done((bf16[16,256]{1,0:T(8,128)(2,1)S(1)}, bf16[16,256]{1,0:T(8,128)(2,1)S(1)}, u32[]{:S(2)}, u32[]{:S(2)}) %collective-permute-start.1) | collective-permute-done | bytes 8224 | tf_op jit(solution)/shard_map/ppermute | solution.py:426
  11.8 0.0 copy-start.1
  11.8 0.0 copy-start.2
  11.9 0.0 copy-start.6
  11.9 1.8 %shard_map.137 = bf16[512,384]{1,0:T(8,128)(2,1)S(1)} custom-call(bf16[128,256]{1,0:T(8,128)(2,1)S(1)} %copy-done.4, bf16[16,256]{1,0:T(8,128)(2,1)S(1)} %collective-permute-done.refs_1_.refs_4_, bf16[16,256]{1,0:T(8,128)(2,1)S(1)} %collective-permute-done.1.refs_2_.refs_5_, s32[27,128]{1,0:T(8,128)S(1)} %bitcast.9, s32[1,128]{1,0:T(1,128)S(1)} %bitcast.13, ...), custom_call_target="tpu_custom_call" | custom-call | flops 3300000000 | bytes 262144 | tf_op jit(solution)/shard_map/pallas_call | solution.py:106
  13.7 23.4 %all_to_all.15 = bf16[32,16,384]{2,1,0:T(8,128)(2,1)S(1)} all-to-all(bf16[32,16,384]{2,1,0:T(8,128)(2,1)S(1)} %bitcast.8), channel_id=1, replica_groups={{0,2,4,6,8,10,12,14,16,18,20,22,24,26,28,30,32,34,36,38,40,42,44,46,48,..., dimensions={0} | all-to-all | bytes 786432 | tf_op jit(solution)/shard_map/all_to_all | solution.py:434
  37.1 2.4 %collective-permute-start.2 = (bf16[512,384]{1,0:T(8,128)(2,1)S(1)}, bf16[512,384]{1,0:T(8,128)(2,1)S(1)}, u32[]{:S(2)}, u32[]{:S(2)}) collective-permute-start(bf16[512,384]{1,0:T(8,128)(2,1)S(1)} %bitcast.6), channel_id=1, source_target_pairs={{0,1},{1,0},{2,3},{3,2},{4,5},{5,4},{6,7},{7,6},{8,9},{9,8},{10,11... | collective-permute-start | bytes 1179656 | tf_op jit(solution)/shard_map/ppermute | solution.py:438
  39.5 1.3 %collective-permute-done.2.refs_1_ = bf16[512,384]{1,0:T(8,128)(2,1)S(1)} collective-permute-done((bf16[512,384]{1,0:T(8,128)(2,1)S(1)}, bf16[512,384]{1,0:T(8,128)(2,1)S(1)}, u32[]{:S(2)}, u32[]{:S(2)}) %collective-permute-start.2) | collective-permute-done | bytes 393248 | tf_op jit(solution)/shard_map/ppermute | solution.py:438
  40.9 6.0 %shard_map.138 = (bf16[32,32,256]{2,1,0:T(8,128)(2,1)S(1)}, f32[1,256]{1,0:T(1,128)S(1)}) custom-call(bf16[512,384]{1,0:T(8,128)(2,1)S(1)} %bitcast.7, bf16[512,384]{1,0:T(8,128)(2,1)S(1)} %collective-permute-done.2.refs_1_, bf16[256,768]{1,0:T(8,128)(2,1)S(1)} %copy-done.1, bf16[256,256]{1,0:T(8,128)(2,1)S(1)} %copy-done.2, f32[1,256]{1,0:T(1,128)S(1)} %bitcast.12), custom_call_target="tpu_custom_call" | custom-call | flops 6600000000 | bytes 262144 | tf_op jit(solution)/shard_map/pallas_call | solution.py:106
  46.9 19.1 %all_to_all.16.refs_0_ = bf16[32,32,256]{2,1,0:T(8,128)(2,1)S(1)} all-to-all(bf16[32,32,256]{2,1,0:T(8,128)(2,1)S(1)} %get-tuple-element.45), channel_id=1, replica_groups={{0,2,4,6,8,10,12,14,16,18,20,22,24,26,28,30,32,34,36,38,40,42,44,46,48,..., dimensions={0} | all-to-all | bytes 1048576 | tf_op jit(solution)/shard_map/all_to_all | solution.py:450
  66.0 1.0 shard_map.139
  67.0 1.3 %collective-permute-start.6 = (bf16[16,256]{1,0:T(8,128)(2,1)S(1)}, bf16[16,256]{1,0:T(8,128)(2,1)S(1)}, u32[]{:S(2)}, u32[]{:S(2)}) collective-permute-start(bf16[16,256]{1,0:T(8,128)(2,1)S(1)} %get-tuple-element.53.refs_0_), channel_id=1, source_target_pairs={{0,64},{64,128},{128,192},{192,0},{1,65},{65,129},{129,193},{193,1... | collective-permute-start | bytes 24584 | tf_op jit(solution)/shard_map/ppermute | solution.py:40
  68.3 0.4 collective-permute-start.3
  68.7 1.9 %collective-permute-start.4 = (bf16[304,256]{1,0:T(8,128)(2,1)S(1)}, bf16[304,256]{1,0:T(8,128)(2,1)S(1)}, u32[]{:S(2)}, u32[]{:S(2)}) collective-permute-start(bf16[304,256]{1,0:T(8,128)(2,1)S(1)} %get-tuple-element.57.refs_0_), channel_id=1, source_target_pairs={{0,48},{1,49},{2,50},{3,51},{4,52},{5,53},{6,54},{7,55},{8,56},{9,... | collective-permute-start | bytes 466952 | tf_op jit(solution)/shard_map/ppermute | solution.py:35
  70.6 1.0 collective-permute-start.5
  71.6 2.6 %collective-permute-start.7 = (bf16[16,256]{1,0:T(8,128)(2,1)S(1)}, bf16[16,256]{1,0:T(8,128)(2,1)S(1)}, u32[]{:S(2)}, u32[]{:S(2)}) collective-permute-start(bf16[16,256]{1,0:T(8,128)(2,1)S(1)} %get-tuple-element.53.refs_0_), channel_id=1, source_target_pairs={{0,128},{64,192},{128,0},{192,64},{1,129},{65,193},{129,1},{193,65... | collective-permute-start | bytes 24584 | tf_op jit(solution)/shard_map/ppermute | solution.py:40
  74.2 0.0 collective-permute-done.6.refs_1_
  74.2 1.1 collective-permute-start.8
  75.3 2.4 %shard_map.140 = (f32[128,256]{1,0:T(8,128)}, bf16[16,256]{1,0:T(8,128)(2,1)}, bf16[16,256]{1,0:T(8,128)(2,1)}) custom-call(bf16[128,256]{1,0:T(8,128)(2,1)S(1)} %get-tuple-element.49.refs_0_, s32[27,128]{1,0:T(8,128)S(1)} %bitcast.11, bf16[6912,256]{1,0:T(8,128)(2,1)S(1)} %copy-done), custom_call_target="tpu_custom_call" | custom-call | flops 3300000000 | bytes 262144 | tf_op jit(solution)/shard_map/pallas_call | solution.py:106
  77.7 0.0 collective-permute-done.7.refs_2_
  77.7 0.0 collective-permute-done.8.refs_3_
  77.7 0.0 collective-permute-done.3.refs_1_
  77.7 0.0 collective-permute-done.4.refs_2_
  77.7 0.0 collective-permute-done.5.refs_3_
  77.7 5.3 %collective-permute-start.9 = (bf16[304,256]{1,0:T(8,128)(2,1)S(1)}, bf16[304,256]{1,0:T(8,128)(2,1)S(1)}, u32[]{:S(2)}, u32[]{:S(2)}) collective-permute-start(bf16[304,256]{1,0:T(8,128)(2,1)S(1)} %get-tuple-element.57.refs_0_), channel_id=1, source_target_pairs={{0,1},{1,0},{2,3},{3,2},{4,5},{5,4},{6,7},{7,6},{8,9},{9,8},{10,11... | collective-permute-start | bytes 466952 | tf_op jit(solution)/shard_map/ppermute | solution.py:35
  83.0 0.1 collective-permute-start.10
  83.1 0.4 collective-permute-start.11
  83.6 0.1 collective-permute-start.12
  83.7 1.6 %shard_map.141 = (f32[2064,256]{1,0:T(8,128)S(1)}, f32[1,256]{1,0:T(1,128)S(1)}) custom-call(bf16[304,256]{1,0:T(8,128)(2,1)S(1)} %get-tuple-element.57.refs_0_, bf16[304,256]{1,0:T(8,128)(2,1)S(1)} %collective-permute-done.3.refs_1_, bf16[304,256]{1,0:T(8,128)(2,1)S(1)} %collective-permute-done.4.refs_2_, bf16[304,256]{1,0:T(8,128)(2,1)S(1)} %collective-permute-done.5.refs_3_), custom_call_target="tpu_custom_call" | custom-call | flops 3300000000 | bytes 262144 | tf_op jit(solution)/shard_map/pallas_call | solution.py:106
  85.3 0.0 collective-permute-done.9.refs_6_
  85.3 0.0 collective-permute-done.10.refs_7_
  85.3 0.0 collective-permute-done.11.refs_8_
  85.3 0.0 collective-permute-done.12.refs_9_
  85.4 0.0 copy-start.11
  85.4 0.0 copy-start.10
  85.4 2.6 %shard_map.142 = bf16[8,128,256]{2,1,0:T(8,128)(2,1)} custom-call(bf16[16,256]{1,0:T(8,128)(2,1)S(1)} %get-tuple-element.53.refs_0_, bf16[16,256]{1,0:T(8,128)(2,1)S(1)} %collective-permute-done.6.refs_1_, bf16[16,256]{1,0:T(8,128)(2,1)S(1)} %collective-permute-done.7.refs_2_, bf16[16,256]{1,0:T(8,128)(2,1)S(1)} %collective-permute-done.8.refs_3_, ...), custom_call_target="tpu_custom_call" | custom-call | flops 5500000256 | bytes 262144 | tf_op jit(solution)/shard_map/pallas_call | solution.py:106
  88.0 0.0 copy-start.8
  88.0 0.0 copy-start.9
  88.0 4.4 %all-to-all-start.2 = ((bf16[8,128,256]{2,1,0:T(8,128)(2,1)}), bf16[8,128,256]{2,1,0:T(8,128)(2,1)S(1)}, u32[]{:S(2)}, u32[]{:S(2)}) async-start(bf16[8,128,256]{2,1,0:T(8,128)(2,1)} %shard_map.142), calls=%async_computation.2 | async-start | bytes 1048576 | tf_op jit(solution)/shard_map/all_to_all | solution.py:489
  92.5 0.0 copy-done.11
  92.5 4.2 %collective-permute-start.13 = (bf16[16,256]{1,0:T(8,128)(2,1)S(1)}, bf16[16,256]{1,0:T(8,128)(2,1)S(1)}, u32[]{:S(2)}, u32[]{:S(2)}) collective-permute-start(bf16[16,256]{1,0:T(8,128)(2,1)S(1)} %copy-done.11), channel_id=1, source_target_pairs={{0,1},{1,2},{2,3},{3,4},{4,5},{5,6},{6,7},{7,8},{8,9},{9,10},{10,1... | collective-permute-start | bytes 24584 | tf_op jit(solution)/shard_map/ppermute | solution.py:471
  96.7 1.9 %collective-permute-start.14 = (bf16[16,256]{1,0:T(8,128)(2,1)S(1)}, bf16[16,256]{1,0:T(8,128)(2,1)S(1)}, u32[]{:S(2)}, u32[]{:S(2)}) collective-permute-start(bf16[16,256]{1,0:T(8,128)(2,1)S(1)} %copy-done.10), channel_id=1, source_target_pairs={{1,0},{2,1},{3,2},{4,3},{5,4},{6,5},{7,6},{8,7},{9,8},{10,9},{11,1... | collective-permute-start | bytes 24584 | tf_op jit(solution)/shard_map/ppermute | solution.py:470
  98.6 2.6 %collective-permute-done.13.refs_1_ = bf16[16,256]{1,0:T(8,128)(2,1)S(1)} collective-permute-done((bf16[16,256]{1,0:T(8,128)(2,1)S(1)}, bf16[16,256]{1,0:T(8,128)(2,1)S(1)}, u32[]{:S(2)}, u32[]{:S(2)}) %collective-permute-start.13) | collective-permute-done | bytes 8224 | tf_op jit(solution)/shard_map/ppermute | solution.py:471
  101.2 5.3 %collective-permute-done.14.refs_2_ = bf16[16,256]{1,0:T(8,128)(2,1)S(1)} collective-permute-done((bf16[16,256]{1,0:T(8,128)(2,1)S(1)}, bf16[16,256]{1,0:T(8,128)(2,1)S(1)}, u32[]{:S(2)}, u32[]{:S(2)}) %collective-permute-start.14) | collective-permute-done | bytes 8224 | tf_op jit(solution)/shard_map/ppermute | solution.py:470
  106.5 3.9 %all-to-all-done.2.refs_0_ = bf16[8,128,256]{2,1,0:T(8,128)(2,1)S(1)} async-done(((bf16[8,128,256]{2,1,0:T(8,128)(2,1)}), bf16[8,128,256]{2,1,0:T(8,128)(2,1)S(1)}, u32[]{:S(2)}, u32[]{:S(2)}) %all-to-all-start.2) | async-done | bytes 524320 | tf_op jit(solution)/shard_map/all_to_all | solution.py:489
  110.4 0.1 shard_map.143
  110.5 1.2 collective-permute-start.16
  111.7 0.4 collective-permute-start.15
  112.1 2.6 %collective-permute-done.15.refs_1_ = bf16[112,256]{1,0:T(8,128)(2,1)S(1)} collective-permute-done((bf16[112,256]{1,0:T(8,128)(2,1)S(1)}, bf16[112,256]{1,0:T(8,128)(2,1)S(1)}, u32[]{:S(2)}, u32[]{:S(2)}) %collective-permute-start.15) | collective-permute-done | bytes 57376 | tf_op jit(solution)/shard_map/ppermute | solution.py:498
  114.7 0.5 collective-permute-done.16.refs_3_
  115.2 0.4 collective-permute-start.18
  115.6 2.0 %collective-permute-start.19 = (bf16[2,128,256]{2,1,0:T(8,128)(2,1)S(1)}, bf16[2,128,256]{2,1,0:T(8,128)(2,1)S(1)}, u32[]{:S(2)}, u32[]{:S(2)}) collective-permute-start(bf16[2,128,256]{2,1,0:T(8,128)(2,1)S(1)} %get-tuple-element.75.refs_2_), channel_id=1, source_target_pairs={{0,1},{1,0},{2,3},{3,2},{4,5},{5,4},{6,7},{7,6},{8,9},{9,8},{10,11... | collective-permute-start | bytes 393224 | tf_op jit(solution)/shard_map/ppermute | solution.py:35
  117.6 1.8 %collective-permute-start.17 = (bf16[112,256]{1,0:T(8,128)(2,1)S(1)}, bf16[112,256]{1,0:T(8,128)(2,1)S(1)}, u32[]{:S(2)}, u32[]{:S(2)}) collective-permute-start(bf16[112,256]{1,0:T(8,128)(2,1)S(1)} %get-tuple-element.74.refs_0_), channel_id=1, source_target_pairs={{0,128},{64,192},{128,0},{192,64},{1,129},{65,193},{129,1},{193,65... | collective-permute-start | bytes 172040 | tf_op jit(solution)/shard_map/ppermute | solution.py:506
  119.5 0.0 collective-permute-done.18.refs_3_
  119.5 2.5 %collective-permute-start.20 = (bf16[2,128,256]{2,1,0:T(8,128)(2,1)S(1)}, bf16[2,128,256]{2,1,0:T(8,128)(2,1)S(1)}, u32[]{:S(2)}, u32[]{:S(2)}) collective-permute-start(bf16[2,128,256]{2,1,0:T(8,128)(2,1)S(1)} %collective-permute-done.18.refs_3_), channel_id=1, source_target_pairs={{0,1},{1,0},{2,3},{3,2},{4,5},{5,4},{6,7},{7,6},{8,9},{9,8},{10,11... | collective-permute-start | bytes 393224 | tf_op jit(solution)/shard_map/ppermute | solution.py:35
  122.0 0.8 shard_map.145
  122.8 0.0 collective-permute-done.17.refs_1_
  122.8 0.0 collective-permute-done.19.refs_4_
  122.8 0.2 collective-permute-done.20.refs_5_
  123.0 1.2 shard_map.146
  (17 shorter events, 0.1 us)
Async XLA Ops:
  0.6 11.2 %copy-start.4 = (bf16[128,256]{1,0:T(8,128)(2,1)S(1)}, bf16[128,256]{1,0:T(8,128)(2,1)}, u32[]{:S(2)}) copy-start(bf16[128,256]{1,0:T(8,128)(2,1)} %refs_3_.4) | copy-start | bytes 196612
  0.6 11.2 %copy-start.5 = (s32[128,27]{0,1:T(8,128)S(1)}, s32[128,27]{0,1:T(8,128)}, u32[]{:S(2)}) copy-start(s32[128,27]{0,1:T(8,128)} %param.11) | copy-start | bytes 41476
  0.7 11.2 %copy-start.7 = (s32[128]{0:T(128)S(1)}, s32[128]{0:T(128)}, u32[]{:S(2)}) copy-start(s32[128]{0:T(128)} %param.10) | copy-start | bytes 1540
  0.7 11.2 %copy-start.3 = (bf16[128,256]{1,0:T(8,128)(2,1)S(1)}, bf16[128,256]{1,0:T(8,128)(2,1)}, u32[]{:S(2)}) copy-start(bf16[128,256]{1,0:T(8,128)(2,1)} %refs_5_.1) | copy-start | bytes 196612
  0.7 11.2 %copy-start = (bf16[6912,256]{1,0:T(8,128)(2,1)S(1)}, bf16[6912,256]{1,0:T(8,128)(2,1)}, u32[]{:S(2)}) copy-start(bf16[6912,256]{1,0:T(8,128)(2,1)} %refs_2_.3) | copy-start | bytes 10616836
  1.9 6.9 %collective-permute-start = (bf16[16,256]{1,0:T(8,128)(2,1)S(1)}, bf16[16,256]{1,0:T(8,128)(2,1)S(1)}, u32[]{:S(2)}, u32[]{:S(2)}) collective-permute-start(bf16[16,256]{1,0:T(8,128)(2,1)S(1)} %get-tuple-element.43), channel_id=1, source_target_pairs={{0,1},{1,2},{2,3},{3,4},{4,5},{5,6},{6,7},{7,8},{8,9},{9,10},{10,1... | collective-permute-start | bytes 24584 | tf_op jit(solution)/shard_map/ppermute | solution.py:425
  6.8 5.0 %collective-permute-start.1 = (bf16[16,256]{1,0:T(8,128)(2,1)S(1)}, bf16[16,256]{1,0:T(8,128)(2,1)S(1)}, u32[]{:S(2)}, u32[]{:S(2)}) collective-permute-start(bf16[16,256]{1,0:T(8,128)(2,1)S(1)} %get-tuple-element.44), channel_id=1, source_target_pairs={{1,0},{2,1},{3,2},{4,3},{5,4},{6,5},{7,6},{8,7},{9,8},{10,9},{11,1... | collective-permute-start | bytes 24584 | tf_op jit(solution)/shard_map/ppermute | solution.py:426
  11.8 29.1 %copy-start.1 = (bf16[256,768]{1,0:T(8,128)(2,1)S(1)}, bf16[256,768]{1,0:T(8,128)(2,1)}, u32[]{:S(2)}) copy-start(bf16[256,768]{1,0:T(8,128)(2,1)} %refs_2_.2) | copy-start | bytes 1179652
  11.8 29.1 %copy-start.2 = (bf16[256,256]{1,0:T(8,128)(2,1)S(1)}, bf16[256,256]{1,0:T(8,128)(2,1)}, u32[]{:S(2)}) copy-start(bf16[256,256]{1,0:T(8,128)(2,1)} %refs_3_.3) | copy-start | bytes 393220
  11.9 29.0 %copy-start.6 = (f32[256]{0:T(256)S(1)}, f32[256]{0:T(256)}, u32[]{:S(2)}) copy-start(f32[256]{0:T(256)} %param.17) | copy-start | bytes 3076
  37.1 3.8 %collective-permute-start.2 = (bf16[512,384]{1,0:T(8,128)(2,1)S(1)}, bf16[512,384]{1,0:T(8,128)(2,1)S(1)}, u32[]{:S(2)}, u32[]{:S(2)}) collective-permute-start(bf16[512,384]{1,0:T(8,128)(2,1)S(1)} %bitcast.6), channel_id=1, source_target_pairs={{0,1},{1,0},{2,3},{3,2},{4,5},{5,4},{6,7},{7,6},{8,9},{9,8},{10,11... | collective-permute-start | bytes 1179656 | tf_op jit(solution)/shard_map/ppermute | solution.py:438
  67.0 7.2 %collective-permute-start.6 = (bf16[16,256]{1,0:T(8,128)(2,1)S(1)}, bf16[16,256]{1,0:T(8,128)(2,1)S(1)}, u32[]{:S(2)}, u32[]{:S(2)}) collective-permute-start(bf16[16,256]{1,0:T(8,128)(2,1)S(1)} %get-tuple-element.53.refs_0_), channel_id=1, source_target_pairs={{0,64},{64,128},{128,192},{192,0},{1,65},{65,129},{129,193},{193,1... | collective-permute-start | bytes 24584 | tf_op jit(solution)/shard_map/ppermute | solution.py:40
  68.3 9.3 %collective-permute-start.3 = (bf16[304,256]{1,0:T(8,128)(2,1)S(1)}, bf16[304,256]{1,0:T(8,128)(2,1)S(1)}, u32[]{:S(2)}, u32[]{:S(2)}) collective-permute-start(bf16[304,256]{1,0:T(8,128)(2,1)S(1)} %get-tuple-element.57.refs_0_), channel_id=1, source_target_pairs={{0,16},{1,17},{2,18},{3,19},{4,20},{5,21},{6,22},{7,23},{8,24},{9,... | collective-permute-start | bytes 466952 | tf_op jit(solution)/shard_map/ppermute | solution.py:35
  68.7 9.0 %collective-permute-start.4 = (bf16[304,256]{1,0:T(8,128)(2,1)S(1)}, bf16[304,256]{1,0:T(8,128)(2,1)S(1)}, u32[]{:S(2)}, u32[]{:S(2)}) collective-permute-start(bf16[304,256]{1,0:T(8,128)(2,1)S(1)} %get-tuple-element.57.refs_0_), channel_id=1, source_target_pairs={{0,48},{1,49},{2,50},{3,51},{4,52},{5,53},{6,54},{7,55},{8,56},{9,... | collective-permute-start | bytes 466952 | tf_op jit(solution)/shard_map/ppermute | solution.py:35
  70.6 7.1 %collective-permute-start.5 = (bf16[304,256]{1,0:T(8,128)(2,1)S(1)}, bf16[304,256]{1,0:T(8,128)(2,1)S(1)}, u32[]{:S(2)}, u32[]{:S(2)}) collective-permute-start(bf16[304,256]{1,0:T(8,128)(2,1)S(1)} %get-tuple-element.57.refs_0_), channel_id=1, source_target_pairs={{0,32},{1,33},{2,34},{3,35},{4,36},{5,37},{6,38},{7,39},{8,40},{9,... | collective-permute-start | bytes 466952 | tf_op jit(solution)/shard_map/ppermute | solution.py:35
  71.6 6.1 %collective-permute-start.7 = (bf16[16,256]{1,0:T(8,128)(2,1)S(1)}, bf16[16,256]{1,0:T(8,128)(2,1)S(1)}, u32[]{:S(2)}, u32[]{:S(2)}) collective-permute-start(bf16[16,256]{1,0:T(8,128)(2,1)S(1)} %get-tuple-element.53.refs_0_), channel_id=1, source_target_pairs={{0,128},{64,192},{128,0},{192,64},{1,129},{65,193},{129,1},{193,65... | collective-permute-start | bytes 24584 | tf_op jit(solution)/shard_map/ppermute | solution.py:40
  74.2 3.4 %collective-permute-start.8 = (bf16[16,256]{1,0:T(8,128)(2,1)S(1)}, bf16[16,256]{1,0:T(8,128)(2,1)S(1)}, u32[]{:S(2)}, u32[]{:S(2)}) collective-permute-start(bf16[16,256]{1,0:T(8,128)(2,1)S(1)} %get-tuple-element.53.refs_0_), channel_id=1, source_target_pairs={{0,192},{64,0},{128,64},{192,128},{1,193},{65,1},{129,65},{193,129... | collective-permute-start | bytes 24584 | tf_op jit(solution)/shard_map/ppermute | solution.py:40
  77.7 7.6 %collective-permute-start.9 = (bf16[304,256]{1,0:T(8,128)(2,1)S(1)}, bf16[304,256]{1,0:T(8,128)(2,1)S(1)}, u32[]{:S(2)}, u32[]{:S(2)}) collective-permute-start(bf16[304,256]{1,0:T(8,128)(2,1)S(1)} %get-tuple-element.57.refs_0_), channel_id=1, source_target_pairs={{0,1},{1,0},{2,3},{3,2},{4,5},{5,4},{6,7},{7,6},{8,9},{9,8},{10,11... | collective-permute-start | bytes 466952 | tf_op jit(solution)/shard_map/ppermute | solution.py:35
  83.0 2.3 %collective-permute-start.10 = (bf16[304,256]{1,0:T(8,128)(2,1)S(1)}, bf16[304,256]{1,0:T(8,128)(2,1)S(1)}, u32[]{:S(2)}, u32[]{:S(2)}) collective-permute-start(bf16[304,256]{1,0:T(8,128)(2,1)S(1)} %collective-permute-done.3.refs_1_), channel_id=1, source_target_pairs={{0,1},{1,0},{2,3},{3,2},{4,5},{5,4},{6,7},{7,6},{8,9},{9,8},{10,11... | collective-permute-start | bytes 466952 | tf_op jit(solution)/shard_map/ppermute | solution.py:35
  83.1 2.2 %collective-permute-start.11 = (bf16[304,256]{1,0:T(8,128)(2,1)S(1)}, bf16[304,256]{1,0:T(8,128)(2,1)S(1)}, u32[]{:S(2)}, u32[]{:S(2)}) collective-permute-start(bf16[304,256]{1,0:T(8,128)(2,1)S(1)} %collective-permute-done.4.refs_2_), channel_id=1, source_target_pairs={{0,1},{1,0},{2,3},{3,2},{4,5},{5,4},{6,7},{7,6},{8,9},{9,8},{10,11... | collective-permute-start | bytes 466952 | tf_op jit(solution)/shard_map/ppermute | solution.py:35
  83.6 1.8 %collective-permute-start.12 = (bf16[304,256]{1,0:T(8,128)(2,1)S(1)}, bf16[304,256]{1,0:T(8,128)(2,1)S(1)}, u32[]{:S(2)}, u32[]{:S(2)}) collective-permute-start(bf16[304,256]{1,0:T(8,128)(2,1)S(1)} %collective-permute-done.5.refs_3_), channel_id=1, source_target_pairs={{0,1},{1,0},{2,3},{3,2},{4,5},{5,4},{6,7},{7,6},{8,9},{9,8},{10,11... | collective-permute-start | bytes 466952 | tf_op jit(solution)/shard_map/ppermute | solution.py:35
  85.4 7.1 %copy-start.11 = (bf16[16,256]{1,0:T(8,128)(2,1)S(1)}, bf16[16,256]{1,0:T(8,128)(2,1)}, u32[]{:S(2)}) copy-start(bf16[16,256]{1,0:T(8,128)(2,1)} %get-tuple-element.63) | copy-start | bytes 24580
  85.4 11.3 %copy-start.10 = (bf16[16,256]{1,0:T(8,128)(2,1)S(1)}, bf16[16,256]{1,0:T(8,128)(2,1)}, u32[]{:S(2)}) copy-start(bf16[16,256]{1,0:T(8,128)(2,1)} %get-tuple-element.64) | copy-start | bytes 24580
  88.0 34.0 %copy-start.8 = (s32[1,32]{1,0:T(1,128)S(1)}, s32[1,32]{1,0:T(1,128)}, u32[]{:S(2)}) copy-start(s32[1,32]{1,0:T(1,128)} %refs_3_.5) | copy-start | bytes 388
  88.0 34.0 %copy-start.9 = (f32[128,256]{1,0:T(8,128)S(1)}, f32[128,256]{1,0:T(8,128)}, u32[]{:S(2)}) copy-start(f32[128,256]{1,0:T(8,128)} %get-tuple-element.52.refs_10_.refs_0_) | copy-start | bytes 393220
  88.0 22.4 %all-to-all-start.2 = ((bf16[8,128,256]{2,1,0:T(8,128)(2,1)}), bf16[8,128,256]{2,1,0:T(8,128)(2,1)S(1)}, u32[]{:S(2)}, u32[]{:S(2)}) async-start(bf16[8,128,256]{2,1,0:T(8,128)(2,1)} %shard_map.142), calls=%async_computation.2 | async-start | bytes 1048576 | tf_op jit(solution)/shard_map/all_to_all | solution.py:489
  92.5 8.7 %collective-permute-start.13 = (bf16[16,256]{1,0:T(8,128)(2,1)S(1)}, bf16[16,256]{1,0:T(8,128)(2,1)S(1)}, u32[]{:S(2)}, u32[]{:S(2)}) collective-permute-start(bf16[16,256]{1,0:T(8,128)(2,1)S(1)} %copy-done.11), channel_id=1, source_target_pairs={{0,1},{1,2},{2,3},{3,4},{4,5},{5,6},{6,7},{7,8},{8,9},{9,10},{10,1... | collective-permute-start | bytes 24584 | tf_op jit(solution)/shard_map/ppermute | solution.py:471
  96.7 9.8 %collective-permute-start.14 = (bf16[16,256]{1,0:T(8,128)(2,1)S(1)}, bf16[16,256]{1,0:T(8,128)(2,1)S(1)}, u32[]{:S(2)}, u32[]{:S(2)}) collective-permute-start(bf16[16,256]{1,0:T(8,128)(2,1)S(1)} %copy-done.10), channel_id=1, source_target_pairs={{1,0},{2,1},{3,2},{4,3},{5,4},{6,5},{7,6},{8,7},{9,8},{10,9},{11,1... | collective-permute-start | bytes 24584 | tf_op jit(solution)/shard_map/ppermute | solution.py:470
  110.5 4.7 %collective-permute-start.16 = (bf16[128,256]{1,0:T(8,128)(2,1)S(1)}, bf16[128,256]{1,0:T(8,128)(2,1)S(1)}, u32[]{:S(2)}, u32[]{:S(2)}) collective-permute-start(bf16[128,256]{1,0:T(8,128)(2,1)S(1)} %get-tuple-element.67.refs_2_), channel_id=1, source_target_pairs={{0,32},{1,33},{2,34},{3,35},{4,36},{5,37},{6,38},{7,39},{8,40},{9,... | collective-permute-start | bytes 196616 | tf_op jit(solution)/shard_map/ppermute | solution.py:35
  111.7 3.0 %collective-permute-start.15 = (bf16[112,256]{1,0:T(8,128)(2,1)S(1)}, bf16[112,256]{1,0:T(8,128)(2,1)S(1)}, u32[]{:S(2)}, u32[]{:S(2)}) collective-permute-start(bf16[112,256]{1,0:T(8,128)(2,1)S(1)} %get-tuple-element.66.refs_0_), channel_id=1, source_target_pairs={{0,64},{64,0},{128,192},{192,128},{1,65},{65,1},{129,193},{193,129... | collective-permute-start | bytes 172040 | tf_op jit(solution)/shard_map/ppermute | solution.py:498
  115.2 4.2 %collective-permute-start.18 = (bf16[2,128,256]{2,1,0:T(8,128)(2,1)S(1)}, bf16[2,128,256]{2,1,0:T(8,128)(2,1)S(1)}, u32[]{:S(2)}, u32[]{:S(2)}) collective-permute-start(bf16[2,128,256]{2,1,0:T(8,128)(2,1)S(1)} %get-tuple-element.75.refs_2_), channel_id=1, source_target_pairs={{0,16},{1,17},{2,18},{3,19},{4,20},{5,21},{6,22},{7,23},{8,24},{9,... | collective-permute-start | bytes 393224 | tf_op jit(solution)/shard_map/ppermute | solution.py:35
  115.6 7.2 %collective-permute-start.19 = (bf16[2,128,256]{2,1,0:T(8,128)(2,1)S(1)}, bf16[2,128,256]{2,1,0:T(8,128)(2,1)S(1)}, u32[]{:S(2)}, u32[]{:S(2)}) collective-permute-start(bf16[2,128,256]{2,1,0:T(8,128)(2,1)S(1)} %get-tuple-element.75.refs_2_), channel_id=1, source_target_pairs={{0,1},{1,0},{2,3},{3,2},{4,5},{5,4},{6,7},{7,6},{8,9},{9,8},{10,11... | collective-permute-start | bytes 393224 | tf_op jit(solution)/shard_map/ppermute | solution.py:35
  117.6 5.2 %collective-permute-start.17 = (bf16[112,256]{1,0:T(8,128)(2,1)S(1)}, bf16[112,256]{1,0:T(8,128)(2,1)S(1)}, u32[]{:S(2)}, u32[]{:S(2)}) collective-permute-start(bf16[112,256]{1,0:T(8,128)(2,1)S(1)} %get-tuple-element.74.refs_0_), channel_id=1, source_target_pairs={{0,128},{64,192},{128,0},{192,64},{1,129},{65,193},{129,1},{193,65... | collective-permute-start | bytes 172040 | tf_op jit(solution)/shard_map/ppermute | solution.py:506
  119.5 3.5 %collective-permute-start.20 = (bf16[2,128,256]{2,1,0:T(8,128)(2,1)S(1)}, bf16[2,128,256]{2,1,0:T(8,128)(2,1)S(1)}, u32[]{:S(2)}, u32[]{:S(2)}) collective-permute-start(bf16[2,128,256]{2,1,0:T(8,128)(2,1)S(1)} %collective-permute-done.18.refs_3_), channel_id=1, source_target_pairs={{0,1},{1,0},{2,3},{3,2},{4,5},{5,4},{6,7},{7,6},{8,9},{9,8},{10,11... | collective-permute-start | bytes 393224 | tf_op jit(solution)/shard_map/ppermute | solution.py:35

commit v10 on v9

--- a/solution.py
+++ b/solution.py
@@ -457,7 +457,6 @@
         us=1.5, limit=8,
     )
     near_grads = [grad_copies] + [flip(grad_copies, 16 * d) for d in (1, 3, 2)]
-    dense_groups = over_groups(dense)
     own_part, rim_down, rim_up = call(
         spread_body,
         [sds((PTS, FEAT), F32), sds((RIM, FEAT)), sds((RIM, FEAT))],
@@ -465,7 +464,9 @@
         scratch=[pltpu.VMEM((OFFS * EXT, FEAT), BF), pltpu.VMEM((EXT, FEAT), F32)],
         pinned=(0, 1, 2), us=3.0,
     )
-    near_grads, own_part, dense_groups = lax.optimization_barrier((near_grads, own_part, dense_groups))
+    dense, own_part = lax.optimization_barrier((dense, own_part))
+    dense_groups = over_groups(dense)
+    near_grads, own_part = lax.optimization_barrier((near_grads, own_part))
     far_grads = [flip(v, 1) for v in near_grads]
     got_down = lax.ppermute(rim_down, "gz", DOWN)
     got_up = lax.ppermute(rim_up, "gz", UP)

time: 124 us -> 125 us (level)
  no operation moved by 1% of the time
where the time goes in v10:
time: 125 us; the launch traced here: 124 us
  starting transfers between devices  43.3 us (35%)
  blocking collectives  42.5 us (34%)
  waiting for transfers between devices  18.8 us (15%)
  Pallas kernels  18.7 us (15%)
    all_to_all x1, blocking collectives, shards(): lax.all_to_all(send.reshape(32, 16, FEAT + PTS), 'gz', split_axis=0, conc...  23.4 us
    all_to_all x1, blocking collectives, shards(): lax.all_to_all(back, 'gz', split_axis=0, concat_axis=0, axis_index_groups...  19.1 us
    pallas_call x11, Pallas kernels, call(): pl.pallas_call(outer, out_shape=shapes, in_specs=specs, out_specs=[pl.Blo...  18.7 us
    ppermute x11, starting transfers between devices, flip(): lax.ppermute(value, 'gz', [(i, i ^ bit) for i in range(NX * NZ * NC)])  14.7 us
    ppermute x3, starting transfers between devices, over_groups(): lax.ppermute(value, 'grp', [(i, (i + d) % n) for i in range(n)])  5.07 us
    ppermute x1, starting transfers between devices, shards(): from_prev = lax.ppermute(to_next, 'gz', UP)  4.94 us
    ppermute x1, waiting for transfers between devices, shards(): got_down = lax.ppermute(rim_down, 'gz', DOWN)  4.5 us
    all_to_all x1, starting transfers between devices, shards(): lax.all_to_all(parts, 'gz', split_axis=0, concat_axis=0, axis_index_group...  4.41 us
  transfers between devices with their start and end apart: 22, of which 8 were waited for; matrix products, arithmetic and copies ran while one was open for 0% of the time, Pallas kernels for 4%

profile of v10, /device:TPU:1, one launch (start us, length us, event | category | flops | bytes accessed | tf_op | source)
XLA Modules:
  0.0 124.4 jit_solution(15698347163732632525)
XLA Ops:
  0.7 1.2 shard_map.136
  1.9 4.9 %collective-permute-start = (bf16[16,256]{1,0:T(8,128)(2,1)S(1)}, bf16[16,256]{1,0:T(8,128)(2,1)S(1)}, u32[]{:S(2)}, u32[]{:S(2)}) collective-permute-start(bf16[16,256]{1,0:T(8,128)(2,1)S(1)} %get-tuple-element.41), channel_id=1, source_target_pairs={{0,1},{1,2},{2,3},{3,4},{4,5},{5,6},{6,7},{7,8},{8,9},{9,10},{10,1... | collective-permute-start | bytes 24584 | tf_op jit(solution)/shard_map/ppermute | solution.py:425
  6.8 1.9 %collective-permute-start.1 = (bf16[16,256]{1,0:T(8,128)(2,1)S(1)}, bf16[16,256]{1,0:T(8,128)(2,1)S(1)}, u32[]{:S(2)}, u32[]{:S(2)}) collective-permute-start(bf16[16,256]{1,0:T(8,128)(2,1)S(1)} %get-tuple-element.42), channel_id=1, source_target_pairs={{1,0},{2,1},{3,2},{4,3},{5,4},{6,5},{7,6},{8,7},{9,8},{10,9},{11,1... | collective-permute-start | bytes 24584 | tf_op jit(solution)/shard_map/ppermute | solution.py:426
  8.8 0.0 collective-permute-done.refs_1_.refs_4_
  8.8 3.0 %collective-permute-done.1.refs_2_.refs_5_ = bf16[16,256]{1,0:T(8,128)(2,1)S(1)} collective-permute-done((bf16[16,256]{1,0:T(8,128)(2,1)S(1)}, bf16[16,256]{1,0:T(8,128)(2,1)S(1)}, u32[]{:S(2)}, u32[]{:S(2)}) %collective-permute-start.1) | collective-permute-done | bytes 8224 | tf_op jit(solution)/shard_map/ppermute | solution.py:426
  11.8 0.0 copy-done.4
  11.8 0.0 copy-start.1
  11.8 0.0 copy-start.2
  11.9 0.0 copy-start.6
  11.9 1.8 %shard_map.137 = bf16[512,384]{1,0:T(8,128)(2,1)S(1)} custom-call(bf16[128,256]{1,0:T(8,128)(2,1)S(1)} %copy-done.4, bf16[16,256]{1,0:T(8,128)(2,1)S(1)} %collective-permute-done.refs_1_.refs_4_, bf16[16,256]{1,0:T(8,128)(2,1)S(1)} %collective-permute-done.1.refs_2_.refs_5_, s32[27,128]{1,0:T(8,128)S(1)} %bitcast.9, s32[1,128]{1,0:T(1,128)S(1)} %bitcast.13, ...), custom_call_target="tpu_custom_call" | custom-call | flops 3300000000 | bytes 262144 | tf_op jit(solution)/shard_map/pallas_call | solution.py:106
  13.7 23.4 %all_to_all.15 = bf16[32,16,384]{2,1,0:T(8,128)(2,1)S(1)} all-to-all(bf16[32,16,384]{2,1,0:T(8,128)(2,1)S(1)} %bitcast.8), channel_id=1, replica_groups={{0,2,4,6,8,10,12,14,16,18,20,22,24,26,28,30,32,34,36,38,40,42,44,46,48,..., dimensions={0} | all-to-all | bytes 786432 | tf_op jit(solution)/shard_map/all_to_all | solution.py:434
  37.1 2.4 %collective-permute-start.2 = (bf16[512,384]{1,0:T(8,128)(2,1)S(1)}, bf16[512,384]{1,0:T(8,128)(2,1)S(1)}, u32[]{:S(2)}, u32[]{:S(2)}) collective-permute-start(bf16[512,384]{1,0:T(8,128)(2,1)S(1)} %bitcast.6), channel_id=1, source_target_pairs={{0,1},{1,0},{2,3},{3,2},{4,5},{5,4},{6,7},{7,6},{8,9},{9,8},{10,11... | collective-permute-start | bytes 1179656 | tf_op jit(solution)/shard_map/ppermute | solution.py:438
  39.5 1.3 %collective-permute-done.2.refs_1_ = bf16[512,384]{1,0:T(8,128)(2,1)S(1)} collective-permute-done((bf16[512,384]{1,0:T(8,128)(2,1)S(1)}, bf16[512,384]{1,0:T(8,128)(2,1)S(1)}, u32[]{:S(2)}, u32[]{:S(2)}) %collective-permute-start.2) | collective-permute-done | bytes 393248 | tf_op jit(solution)/shard_map/ppermute | solution.py:438
  40.9 6.0 %shard_map.138 = (bf16[32,32,256]{2,1,0:T(8,128)(2,1)S(1)}, f32[1,256]{1,0:T(1,128)S(1)}) custom-call(bf16[512,384]{1,0:T(8,128)(2,1)S(1)} %bitcast.7, bf16[512,384]{1,0:T(8,128)(2,1)S(1)} %collective-permute-done.2.refs_1_, bf16[256,768]{1,0:T(8,128)(2,1)S(1)} %copy-done.1, bf16[256,256]{1,0:T(8,128)(2,1)S(1)} %copy-done.2, f32[1,256]{1,0:T(1,128)S(1)} %bitcast.12), custom_call_target="tpu_custom_call" | custom-call | flops 6600000000 | bytes 262144 | tf_op jit(solution)/shard_map/pallas_call | solution.py:106
  46.9 19.1 %all_to_all.16.refs_0_ = bf16[32,32,256]{2,1,0:T(8,128)(2,1)S(1)} all-to-all(bf16[32,32,256]{2,1,0:T(8,128)(2,1)S(1)} %get-tuple-element.43), channel_id=1, replica_groups={{0,2,4,6,8,10,12,14,16,18,20,22,24,26,28,30,32,34,36,38,40,42,44,46,48,..., dimensions={0} | all-to-all | bytes 1048576 | tf_op jit(solution)/shard_map/all_to_all | solution.py:450
  66.0 1.0 shard_map.139
  67.0 0.4 collective-permute-start.3
  67.4 1.9 %collective-permute-start.4 = (bf16[304,256]{1,0:T(8,128)(2,1)S(1)}, bf16[304,256]{1,0:T(8,128)(2,1)S(1)}, u32[]{:S(2)}, u32[]{:S(2)}) collective-permute-start(bf16[304,256]{1,0:T(8,128)(2,1)S(1)} %get-tuple-element.53.refs_0_), channel_id=1, source_target_pairs={{0,48},{1,49},{2,50},{3,51},{4,52},{5,53},{6,54},{7,55},{8,56},{9,... | collective-permute-start | bytes 466952 | tf_op jit(solution)/shard_map/ppermute | solution.py:35
  69.3 1.0 collective-permute-start.5
  70.3 2.4 %shard_map.140 = (f32[128,256]{1,0:T(8,128)}, bf16[16,256]{1,0:T(8,128)(2,1)}, bf16[16,256]{1,0:T(8,128)(2,1)}) custom-call(bf16[128,256]{1,0:T(8,128)(2,1)S(1)} %get-tuple-element.48.refs_0_, s32[27,128]{1,0:T(8,128)S(1)} %bitcast.11, bf16[6912,256]{1,0:T(8,128)(2,1)S(1)} %copy-done), custom_call_target="tpu_custom_call" | custom-call | flops 3300000000 | bytes 262144 | tf_op jit(solution)/shard_map/pallas_call | solution.py:106
  72.7 1.4 %collective-permute-start.6 = (bf16[16,256]{1,0:T(8,128)(2,1)S(1)}, bf16[16,256]{1,0:T(8,128)(2,1)S(1)}, u32[]{:S(2)}, u32[]{:S(2)}) collective-permute-start(bf16[16,256]{1,0:T(8,128)(2,1)S(1)} %get-tuple-element.52.refs_0_), channel_id=1, source_target_pairs={{0,64},{64,128},{128,192},{192,0},{1,65},{65,129},{129,193},{193,1... | collective-permute-start | bytes 24584 | tf_op jit(solution)/shard_map/ppermute | solution.py:40
  74.0 2.6 %collective-permute-start.7 = (bf16[16,256]{1,0:T(8,128)(2,1)S(1)}, bf16[16,256]{1,0:T(8,128)(2,1)S(1)}, u32[]{:S(2)}, u32[]{:S(2)}) collective-permute-start(bf16[16,256]{1,0:T(8,128)(2,1)S(1)} %get-tuple-element.52.refs_0_), channel_id=1, source_target_pairs={{0,128},{64,192},{128,0},{192,64},{1,129},{65,193},{129,1},{193,65... | collective-permute-start | bytes 24584 | tf_op jit(solution)/shard_map/ppermute | solution.py:40
  76.7 0.0 collective-permute-done.3.refs_1_
  76.7 1.1 collective-permute-start.8
  77.7 0.0 collective-permute-done.4.refs_2_
  77.7 0.0 collective-permute-done.5.refs_3_
  77.7 5.2 %collective-permute-start.9 = (bf16[304,256]{1,0:T(8,128)(2,1)S(1)}, bf16[304,256]{1,0:T(8,128)(2,1)S(1)}, u32[]{:S(2)}, u32[]{:S(2)}) collective-permute-start(bf16[304,256]{1,0:T(8,128)(2,1)S(1)} %get-tuple-element.53.refs_0_), channel_id=1, source_target_pairs={{0,1},{1,0},{2,3},{3,2},{4,5},{5,4},{6,7},{7,6},{8,9},{9,8},{10,11... | collective-permute-start | bytes 466952 | tf_op jit(solution)/shard_map/ppermute | solution.py:35
  83.0 0.1 collective-permute-start.10
  83.1 0.0 collective-permute-done.6.refs_1_
  83.1 0.4 collective-permute-start.11
  83.5 0.0 collective-permute-done.7.refs_2_
  83.5 0.4 collective-permute-start.12
  83.9 1.7 %shard_map.141 = (f32[2064,256]{1,0:T(8,128)S(1)}, f32[1,256]{1,0:T(1,128)S(1)}) custom-call(bf16[304,256]{1,0:T(8,128)(2,1)S(1)} %get-tuple-element.53.refs_0_, bf16[304,256]{1,0:T(8,128)(2,1)S(1)} %collective-permute-done.3.refs_1_, bf16[304,256]{1,0:T(8,128)(2,1)S(1)} %collective-permute-done.4.refs_2_, bf16[304,256]{1,0:T(8,128)(2,1)S(1)} %collective-permute-done.5.refs_3_), custom_call_target="tpu_custom_call" | custom-call | flops 3300000000 | bytes 262144 | tf_op jit(solution)/shard_map/pallas_call | solution.py:106
  85.5 0.0 collective-permute-done.8.refs_3_
  85.6 0.0 collective-permute-done.9.refs_6_
  85.6 0.0 collective-permute-done.10.refs_7_
  85.6 0.0 collective-permute-done.11.refs_8_
  85.6 0.0 collective-permute-done.12.refs_9_
  85.6 0.0 copy-start.11
  85.6 0.0 copy-start.10
  85.6 2.6 %shard_map.142 = bf16[8,128,256]{2,1,0:T(8,128)(2,1)} custom-call(bf16[16,256]{1,0:T(8,128)(2,1)S(1)} %get-tuple-element.52.refs_0_, bf16[16,256]{1,0:T(8,128)(2,1)S(1)} %collective-permute-done.6.refs_1_, bf16[16,256]{1,0:T(8,128)(2,1)S(1)} %collective-permute-done.7.refs_2_, bf16[16,256]{1,0:T(8,128)(2,1)S(1)} %collective-permute-done.8.refs_3_, ...), custom_call_target="tpu_custom_call" | custom-call | flops 5500000256 | bytes 262144 | tf_op jit(solution)/shard_map/pallas_call | solution.py:106
  88.3 0.0 copy-start.8
  88.3 0.0 copy-start.9
  88.3 4.4 %all-to-all-start.2 = ((bf16[8,128,256]{2,1,0:T(8,128)(2,1)}), bf16[8,128,256]{2,1,0:T(8,128)(2,1)S(1)}, u32[]{:S(2)}, u32[]{:S(2)}) async-start(bf16[8,128,256]{2,1,0:T(8,128)(2,1)} %shard_map.142), calls=%async_computation.2 | async-start | bytes 1048576 | tf_op jit(solution)/shard_map/all_to_all | solution.py:490
  92.7 3.9 %collective-permute-start.13 = (bf16[16,256]{1,0:T(8,128)(2,1)S(1)}, bf16[16,256]{1,0:T(8,128)(2,1)S(1)}, u32[]{:S(2)}, u32[]{:S(2)}) collective-permute-start(bf16[16,256]{1,0:T(8,128)(2,1)S(1)} %copy-done.11), channel_id=1, source_target_pairs={{0,1},{1,2},{2,3},{3,4},{4,5},{5,6},{6,7},{7,8},{8,9},{9,10},{10,1... | collective-permute-start | bytes 24584 | tf_op jit(solution)/shard_map/ppermute | solution.py:472
  96.7 1.9 %collective-permute-start.14 = (bf16[16,256]{1,0:T(8,128)(2,1)S(1)}, bf16[16,256]{1,0:T(8,128)(2,1)S(1)}, u32[]{:S(2)}, u32[]{:S(2)}) collective-permute-start(bf16[16,256]{1,0:T(8,128)(2,1)S(1)} %copy-done.10), channel_id=1, source_target_pairs={{1,0},{2,1},{3,2},{4,3},{5,4},{6,5},{7,6},{8,7},{9,8},{10,9},{11,1... | collective-permute-start | bytes 24584 | tf_op jit(solution)/shard_map/ppermute | solution.py:471
  98.6 3.6 %collective-permute-done.13.refs_1_ = bf16[16,256]{1,0:T(8,128)(2,1)S(1)} collective-permute-done((bf16[16,256]{1,0:T(8,128)(2,1)S(1)}, bf16[16,256]{1,0:T(8,128)(2,1)S(1)}, u32[]{:S(2)}, u32[]{:S(2)}) %collective-permute-start.13) | collective-permute-done | bytes 8224 | tf_op jit(solution)/shard_map/ppermute | solution.py:472
  102.2 4.5 %collective-permute-done.14.refs_2_ = bf16[16,256]{1,0:T(8,128)(2,1)S(1)} collective-permute-done((bf16[16,256]{1,0:T(8,128)(2,1)S(1)}, bf16[16,256]{1,0:T(8,128)(2,1)S(1)}, u32[]{:S(2)}, u32[]{:S(2)}) %collective-permute-start.14) | collective-permute-done | bytes 8224 | tf_op jit(solution)/shard_map/ppermute | solution.py:471
  106.7 3.9 %all-to-all-done.2.refs_0_ = bf16[8,128,256]{2,1,0:T(8,128)(2,1)S(1)} async-done(((bf16[8,128,256]{2,1,0:T(8,128)(2,1)}), bf16[8,128,256]{2,1,0:T(8,128)(2,1)S(1)}, u32[]{:S(2)}, u32[]{:S(2)}) %all-to-all-start.2) | async-done | bytes 524320 | tf_op jit(solution)/shard_map/all_to_all | solution.py:490
  110.7 0.1 shard_map.143
  110.7 1.2 collective-permute-start.16
  111.9 1.4 %collective-permute-start.15 = (bf16[112,256]{1,0:T(8,128)(2,1)S(1)}, bf16[112,256]{1,0:T(8,128)(2,1)S(1)}, u32[]{:S(2)}, u32[]{:S(2)}) collective-permute-start(bf16[112,256]{1,0:T(8,128)(2,1)S(1)} %get-tuple-element.62.refs_0_), channel_id=1, source_target_pairs={{0,64},{64,0},{128,192},{192,128},{1,65},{65,1},{129,193},{193,129... | collective-permute-start | bytes 172040 | tf_op jit(solution)/shard_map/ppermute | solution.py:499
  113.3 1.7 %collective-permute-done.15.refs_1_ = bf16[112,256]{1,0:T(8,128)(2,1)S(1)} collective-permute-done((bf16[112,256]{1,0:T(8,128)(2,1)S(1)}, bf16[112,256]{1,0:T(8,128)(2,1)S(1)}, u32[]{:S(2)}, u32[]{:S(2)}) %collective-permute-start.15) | collective-permute-done | bytes 57376 | tf_op jit(solution)/shard_map/ppermute | solution.py:499
  114.9 0.5 collective-permute-done.16.refs_3_
  115.5 0.4 collective-permute-start.18
  115.9 2.0 %collective-permute-start.19 = (bf16[2,128,256]{2,1,0:T(8,128)(2,1)S(1)}, bf16[2,128,256]{2,1,0:T(8,128)(2,1)S(1)}, u32[]{:S(2)}, u32[]{:S(2)}) collective-permute-start(bf16[2,128,256]{2,1,0:T(8,128)(2,1)S(1)} %get-tuple-element.71.refs_2_), channel_id=1, source_target_pairs={{0,1},{1,0},{2,3},{3,2},{4,5},{5,4},{6,7},{7,6},{8,9},{9,8},{10,11... | collective-permute-start | bytes 393224 | tf_op jit(solution)/shard_map/ppermute | solution.py:35
  117.9 2.6 %collective-permute-start.17 = (bf16[112,256]{1,0:T(8,128)(2,1)S(1)}, bf16[112,256]{1,0:T(8,128)(2,1)S(1)}, u32[]{:S(2)}, u32[]{:S(2)}) collective-permute-start(bf16[112,256]{1,0:T(8,128)(2,1)S(1)} %get-tuple-element.70.refs_0_), channel_id=1, source_target_pairs={{0,128},{64,192},{128,0},{192,64},{1,129},{65,193},{129,1},{193,65... | collective-permute-start | bytes 172040 | tf_op jit(solution)/shard_map/ppermute | solution.py:507
  120.5 0.0 collective-permute-done.18.refs_3_
  120.5 1.7 %collective-permute-start.20 = (bf16[2,128,256]{2,1,0:T(8,128)(2,1)S(1)}, bf16[2,128,256]{2,1,0:T(8,128)(2,1)S(1)}, u32[]{:S(2)}, u32[]{:S(2)}) collective-permute-start(bf16[2,128,256]{2,1,0:T(8,128)(2,1)S(1)} %collective-permute-done.18.refs_3_), channel_id=1, source_target_pairs={{0,1},{1,0},{2,3},{3,2},{4,5},{5,4},{6,7},{7,6},{8,9},{9,8},{10,11... | collective-permute-start | bytes 393224 | tf_op jit(solution)/shard_map/ppermute | solution.py:35
  122.2 0.8 shard_map.145
  123.0 0.0 collective-permute-done.17.refs_1_
  123.0 0.0 collective-permute-done.19.refs_4_
  123.0 0.2 collective-permute-done.20.refs_5_
  123.2 1.2 shard_map.146
  (17 shorter events, 0.1 us)
Async XLA Ops:
  0.6 11.2 %copy-start.4 = (bf16[128,256]{1,0:T(8,128)(2,1)S(1)}, bf16[128,256]{1,0:T(8,128)(2,1)}, u32[]{:S(2)}) copy-start(bf16[128,256]{1,0:T(8,128)(2,1)} %refs_3_.4) | copy-start | bytes 196612
  0.6 11.2 %copy-start.5 = (s32[128,27]{0,1:T(8,128)S(1)}, s32[128,27]{0,1:T(8,128)}, u32[]{:S(2)}) copy-start(s32[128,27]{0,1:T(8,128)} %param.11) | copy-start | bytes 41476
  0.7 11.2 %copy-start.7 = (s32[128]{0:T(128)S(1)}, s32[128]{0:T(128)}, u32[]{:S(2)}) copy-start(s32[128]{0:T(128)} %param.10) | copy-start | bytes 1540
  0.7 11.2 %copy-start.3 = (bf16[128,256]{1,0:T(8,128)(2,1)S(1)}, bf16[128,256]{1,0:T(8,128)(2,1)}, u32[]{:S(2)}) copy-start(bf16[128,256]{1,0:T(8,128)(2,1)} %refs_5_.1) | copy-start | bytes 196612
  0.7 11.2 %copy-start = (bf16[6912,256]{1,0:T(8,128)(2,1)S(1)}, bf16[6912,256]{1,0:T(8,128)(2,1)}, u32[]{:S(2)}) copy-start(bf16[6912,256]{1,0:T(8,128)(2,1)} %refs_2_.3) | copy-start | bytes 10616836
  1.9 6.9 %collective-permute-start = (bf16[16,256]{1,0:T(8,128)(2,1)S(1)}, bf16[16,256]{1,0:T(8,128)(2,1)S(1)}, u32[]{:S(2)}, u32[]{:S(2)}) collective-permute-start(bf16[16,256]{1,0:T(8,128)(2,1)S(1)} %get-tuple-element.41), channel_id=1, source_target_pairs={{0,1},{1,2},{2,3},{3,4},{4,5},{5,6},{6,7},{7,8},{8,9},{9,10},{10,1... | collective-permute-start | bytes 24584 | tf_op jit(solution)/shard_map/ppermute | solution.py:425
  6.8 5.0 %collective-permute-start.1 = (bf16[16,256]{1,0:T(8,128)(2,1)S(1)}, bf16[16,256]{1,0:T(8,128)(2,1)S(1)}, u32[]{:S(2)}, u32[]{:S(2)}) collective-permute-start(bf16[16,256]{1,0:T(8,128)(2,1)S(1)} %get-tuple-element.42), channel_id=1, source_target_pairs={{1,0},{2,1},{3,2},{4,3},{5,4},{6,5},{7,6},{8,7},{9,8},{10,9},{11,1... | collective-permute-start | bytes 24584 | tf_op jit(solution)/shard_map/ppermute | solution.py:426
  11.8 29.1 %copy-start.1 = (bf16[256,768]{1,0:T(8,128)(2,1)S(1)}, bf16[256,768]{1,0:T(8,128)(2,1)}, u32[]{:S(2)}) copy-start(bf16[256,768]{1,0:T(8,128)(2,1)} %refs_2_.2) | copy-start | bytes 1179652
  11.8 29.1 %copy-start.2 = (bf16[256,256]{1,0:T(8,128)(2,1)S(1)}, bf16[256,256]{1,0:T(8,128)(2,1)}, u32[]{:S(2)}) copy-start(bf16[256,256]{1,0:T(8,128)(2,1)} %refs_3_.3) | copy-start | bytes 393220
  11.9 29.0 %copy-start.6 = (f32[256]{0:T(256)S(1)}, f32[256]{0:T(256)}, u32[]{:S(2)}) copy-start(f32[256]{0:T(256)} %param.17) | copy-start | bytes 3076
  37.1 3.8 %collective-permute-start.2 = (bf16[512,384]{1,0:T(8,128)(2,1)S(1)}, bf16[512,384]{1,0:T(8,128)(2,1)S(1)}, u32[]{:S(2)}, u32[]{:S(2)}) collective-permute-start(bf16[512,384]{1,0:T(8,128)(2,1)S(1)} %bitcast.6), channel_id=1, source_target_pairs={{0,1},{1,0},{2,3},{3,2},{4,5},{5,4},{6,7},{7,6},{8,9},{9,8},{10,11... | collective-permute-start | bytes 1179656 | tf_op jit(solution)/shard_map/ppermute | solution.py:438
  67.0 9.6 %collective-permute-start.3 = (bf16[304,256]{1,0:T(8,128)(2,1)S(1)}, bf16[304,256]{1,0:T(8,128)(2,1)S(1)}, u32[]{:S(2)}, u32[]{:S(2)}) collective-permute-start(bf16[304,256]{1,0:T(8,128)(2,1)S(1)} %get-tuple-element.53.refs_0_), channel_id=1, source_target_pairs={{0,16},{1,17},{2,18},{3,19},{4,20},{5,21},{6,22},{7,23},{8,24},{9,... | collective-permute-start | bytes 466952 | tf_op jit(solution)/shard_map/ppermute | solution.py:35
  67.4 10.3 %collective-permute-start.4 = (bf16[304,256]{1,0:T(8,128)(2,1)S(1)}, bf16[304,256]{1,0:T(8,128)(2,1)S(1)}, u32[]{:S(2)}, u32[]{:S(2)}) collective-permute-start(bf16[304,256]{1,0:T(8,128)(2,1)S(1)} %get-tuple-element.53.refs_0_), channel_id=1, source_target_pairs={{0,48},{1,49},{2,50},{3,51},{4,52},{5,53},{6,54},{7,55},{8,56},{9,... | collective-permute-start | bytes 466952 | tf_op jit(solution)/shard_map/ppermute | solution.py:35
  69.3 8.4 %collective-permute-start.5 = (bf16[304,256]{1,0:T(8,128)(2,1)S(1)}, bf16[304,256]{1,0:T(8,128)(2,1)S(1)}, u32[]{:S(2)}, u32[]{:S(2)}) collective-permute-start(bf16[304,256]{1,0:T(8,128)(2,1)S(1)} %get-tuple-element.53.refs_0_), channel_id=1, source_target_pairs={{0,32},{1,33},{2,34},{3,35},{4,36},{5,37},{6,38},{7,39},{8,40},{9,... | collective-permute-start | bytes 466952 | tf_op jit(solution)/shard_map/ppermute | solution.py:35
  72.7 10.4 %collective-permute-start.6 = (bf16[16,256]{1,0:T(8,128)(2,1)S(1)}, bf16[16,256]{1,0:T(8,128)(2,1)S(1)}, u32[]{:S(2)}, u32[]{:S(2)}) collective-permute-start(bf16[16,256]{1,0:T(8,128)(2,1)S(1)} %get-tuple-element.52.refs_0_), channel_id=1, source_target_pairs={{0,64},{64,128},{128,192},{192,0},{1,65},{65,129},{129,193},{193,1... | collective-permute-start | bytes 24584 | tf_op jit(solution)/shard_map/ppermute | solution.py:40
  74.0 9.5 %collective-permute-start.7 = (bf16[16,256]{1,0:T(8,128)(2,1)S(1)}, bf16[16,256]{1,0:T(8,128)(2,1)S(1)}, u32[]{:S(2)}, u32[]{:S(2)}) collective-permute-start(bf16[16,256]{1,0:T(8,128)(2,1)S(1)} %get-tuple-element.52.refs_0_), channel_id=1, source_target_pairs={{0,128},{64,192},{128,0},{192,64},{1,129},{65,193},{129,1},{193,65... | collective-permute-start | bytes 24584 | tf_op jit(solution)/shard_map/ppermute | solution.py:40
  76.7 8.9 %collective-permute-start.8 = (bf16[16,256]{1,0:T(8,128)(2,1)S(1)}, bf16[16,256]{1,0:T(8,128)(2,1)S(1)}, u32[]{:S(2)}, u32[]{:S(2)}) collective-permute-start(bf16[16,256]{1,0:T(8,128)(2,1)S(1)} %get-tuple-element.52.refs_0_), channel_id=1, source_target_pairs={{0,192},{64,0},{128,64},{192,128},{1,193},{65,1},{129,65},{193,129... | collective-permute-start | bytes 24584 | tf_op jit(solution)/shard_map/ppermute | solution.py:40
  77.7 7.8 %collective-permute-start.9 = (bf16[304,256]{1,0:T(8,128)(2,1)S(1)}, bf16[304,256]{1,0:T(8,128)(2,1)S(1)}, u32[]{:S(2)}, u32[]{:S(2)}) collective-permute-start(bf16[304,256]{1,0:T(8,128)(2,1)S(1)} %get-tuple-element.53.refs_0_), channel_id=1, source_target_pairs={{0,1},{1,0},{2,3},{3,2},{4,5},{5,4},{6,7},{7,6},{8,9},{9,8},{10,11... | collective-permute-start | bytes 466952 | tf_op jit(solution)/shard_map/ppermute | solution.py:35
  83.0 2.6 %collective-permute-start.10 = (bf16[304,256]{1,0:T(8,128)(2,1)S(1)}, bf16[304,256]{1,0:T(8,128)(2,1)S(1)}, u32[]{:S(2)}, u32[]{:S(2)}) collective-permute-start(bf16[304,256]{1,0:T(8,128)(2,1)S(1)} %collective-permute-done.3.refs_1_), channel_id=1, source_target_pairs={{0,1},{1,0},{2,3},{3,2},{4,5},{5,4},{6,7},{7,6},{8,9},{9,8},{10,11... | collective-permute-start | bytes 466952 | tf_op jit(solution)/shard_map/ppermute | solution.py:35
  83.1 2.5 %collective-permute-start.11 = (bf16[304,256]{1,0:T(8,128)(2,1)S(1)}, bf16[304,256]{1,0:T(8,128)(2,1)S(1)}, u32[]{:S(2)}, u32[]{:S(2)}) collective-permute-start(bf16[304,256]{1,0:T(8,128)(2,1)S(1)} %collective-permute-done.4.refs_2_), channel_id=1, source_target_pairs={{0,1},{1,0},{2,3},{3,2},{4,5},{5,4},{6,7},{7,6},{8,9},{9,8},{10,11... | collective-permute-start | bytes 466952 | tf_op jit(solution)/shard_map/ppermute | solution.py:35
  83.5 2.1 %collective-permute-start.12 = (bf16[304,256]{1,0:T(8,128)(2,1)S(1)}, bf16[304,256]{1,0:T(8,128)(2,1)S(1)}, u32[]{:S(2)}, u32[]{:S(2)}) collective-permute-start(bf16[304,256]{1,0:T(8,128)(2,1)S(1)} %collective-permute-done.5.refs_3_), channel_id=1, source_target_pairs={{0,1},{1,0},{2,3},{3,2},{4,5},{5,4},{6,7},{7,6},{8,9},{9,8},{10,11... | collective-permute-start | bytes 466952 | tf_op jit(solution)/shard_map/ppermute | solution.py:35
  85.6 7.1 %copy-start.11 = (bf16[16,256]{1,0:T(8,128)(2,1)S(1)}, bf16[16,256]{1,0:T(8,128)(2,1)}, u32[]{:S(2)}) copy-start(bf16[16,256]{1,0:T(8,128)(2,1)} %get-tuple-element.59) | copy-start | bytes 24580
  85.6 11.1 %copy-start.10 = (bf16[16,256]{1,0:T(8,128)(2,1)S(1)}, bf16[16,256]{1,0:T(8,128)(2,1)}, u32[]{:S(2)}) copy-start(bf16[16,256]{1,0:T(8,128)(2,1)} %get-tuple-element.60) | copy-start | bytes 24580
  88.3 34.0 %copy-start.8 = (s32[1,32]{1,0:T(1,128)S(1)}, s32[1,32]{1,0:T(1,128)}, u32[]{:S(2)}) copy-start(s32[1,32]{1,0:T(1,128)} %refs_3_.5) | copy-start | bytes 388
  88.3 34.0 %copy-start.9 = (f32[128,256]{1,0:T(8,128)S(1)}, f32[128,256]{1,0:T(8,128)}, u32[]{:S(2)}) copy-start(f32[128,256]{1,0:T(8,128)} %get-tuple-element.51.refs_10_.refs_0_) | copy-start | bytes 393220
  88.3 22.4 %all-to-all-start.2 = ((bf16[8,128,256]{2,1,0:T(8,128)(2,1)}), bf16[8,128,256]{2,1,0:T(8,128)(2,1)S(1)}, u32[]{:S(2)}, u32[]{:S(2)}) async-start(bf16[8,128,256]{2,1,0:T(8,128)(2,1)} %shard_map.142), calls=%async_computation.2 | async-start | bytes 1048576 | tf_op jit(solution)/shard_map/all_to_all | solution.py:490
  92.7 9.5 %collective-permute-start.13 = (bf16[16,256]{1,0:T(8,128)(2,1)S(1)}, bf16[16,256]{1,0:T(8,128)(2,1)S(1)}, u32[]{:S(2)}, u32[]{:S(2)}) collective-permute-start(bf16[16,256]{1,0:T(8,128)(2,1)S(1)} %copy-done.11), channel_id=1, source_target_pairs={{0,1},{1,2},{2,3},{3,4},{4,5},{5,6},{6,7},{7,8},{8,9},{9,10},{10,1... | collective-permute-start | bytes 24584 | tf_op jit(solution)/shard_map/ppermute | solution.py:472
  96.7 10.1 %collective-permute-start.14 = (bf16[16,256]{1,0:T(8,128)(2,1)S(1)}, bf16[16,256]{1,0:T(8,128)(2,1)S(1)}, u32[]{:S(2)}, u32[]{:S(2)}) collective-permute-start(bf16[16,256]{1,0:T(8,128)(2,1)S(1)} %copy-done.10), channel_id=1, source_target_pairs={{1,0},{2,1},{3,2},{4,3},{5,4},{6,5},{7,6},{8,7},{9,8},{10,9},{11,1... | collective-permute-start | bytes 24584 | tf_op jit(solution)/shard_map/ppermute | solution.py:471
  110.7 4.7 %collective-permute-start.16 = (bf16[128,256]{1,0:T(8,128)(2,1)S(1)}, bf16[128,256]{1,0:T(8,128)(2,1)S(1)}, u32[]{:S(2)}, u32[]{:S(2)}) collective-permute-start(bf16[128,256]{1,0:T(8,128)(2,1)S(1)} %get-tuple-element.63.refs_2_), channel_id=1, source_target_pairs={{0,32},{1,33},{2,34},{3,35},{4,36},{5,37},{6,38},{7,39},{8,40},{9,... | collective-permute-start | bytes 196616 | tf_op jit(solution)/shard_map/ppermute | solution.py:35
  111.9 3.0 %collective-permute-start.15 = (bf16[112,256]{1,0:T(8,128)(2,1)S(1)}, bf16[112,256]{1,0:T(8,128)(2,1)S(1)}, u32[]{:S(2)}, u32[]{:S(2)}) collective-permute-start(bf16[112,256]{1,0:T(8,128)(2,1)S(1)} %get-tuple-element.62.refs_0_), channel_id=1, source_target_pairs={{0,64},{64,0},{128,192},{192,128},{1,65},{65,1},{129,193},{193,129... | collective-permute-start | bytes 172040 | tf_op jit(solution)/shard_map/ppermute | solution.py:499
  115.5 5.0 %collective-permute-start.18 = (bf16[2,128,256]{2,1,0:T(8,128)(2,1)S(1)}, bf16[2,128,256]{2,1,0:T(8,128)(2,1)S(1)}, u32[]{:S(2)}, u32[]{:S(2)}) collective-permute-start(bf16[2,128,256]{2,1,0:T(8,128)(2,1)S(1)} %get-tuple-element.71.refs_2_), channel_id=1, source_target_pairs={{0,16},{1,17},{2,18},{3,19},{4,20},{5,21},{6,22},{7,23},{8,24},{9,... | collective-permute-start | bytes 393224 | tf_op jit(solution)/shard_map/ppermute | solution.py:35
  115.9 7.2 %collective-permute-start.19 = (bf16[2,128,256]{2,1,0:T(8,128)(2,1)S(1)}, bf16[2,128,256]{2,1,0:T(8,128)(2,1)S(1)}, u32[]{:S(2)}, u32[]{:S(2)}) collective-permute-start(bf16[2,128,256]{2,1,0:T(8,128)(2,1)S(1)} %get-tuple-element.71.refs_2_), channel_id=1, source_target_pairs={{0,1},{1,0},{2,3},{3,2},{4,5},{5,4},{6,7},{7,6},{8,9},{9,8},{10,11... | collective-permute-start | bytes 393224 | tf_op jit(solution)/shard_map/ppermute | solution.py:35
  117.9 5.2 %collective-permute-start.17 = (bf16[112,256]{1,0:T(8,128)(2,1)S(1)}, bf16[112,256]{1,0:T(8,128)(2,1)S(1)}, u32[]{:S(2)}, u32[]{:S(2)}) collective-permute-start(bf16[112,256]{1,0:T(8,128)(2,1)S(1)} %get-tuple-element.70.refs_0_), channel_id=1, source_target_pairs={{0,128},{64,192},{128,0},{192,64},{1,129},{65,193},{129,1},{193,65... | collective-permute-start | bytes 172040 | tf_op jit(solution)/shard_map/ppermute | solution.py:507
  120.5 2.7 %collective-permute-start.20 = (bf16[2,128,256]{2,1,0:T(8,128)(2,1)S(1)}, bf16[2,128,256]{2,1,0:T(8,128)(2,1)S(1)}, u32[]{:S(2)}, u32[]{:S(2)}) collective-permute-start(bf16[2,128,256]{2,1,0:T(8,128)(2,1)S(1)} %collective-permute-done.18.refs_3_), channel_id=1, source_target_pairs={{0,1},{1,0},{2,3},{3,2},{4,5},{5,4},{6,7},{7,6},{8,9},{9,8},{10,11... | collective-permute-start | bytes 393224 | tf_op jit(solution)/shard_map/ppermute | solution.py:35
